TPU v7x, 256 devices: a whole 4x4x8 slice. The times are simulated.
256 devices in a mesh: blk: 64 (over z, x, core), gz: 4 (over y).
Axes of the slice: x: 4, y: 4, z: 8, core: 2. Of those that a mesh axis runs over, the one named last changes fastest.
Arguments:
- sqrt_density: float32 [384, 64, 512], P('blk', None, 'gz'), may hold values from 0.25 to 4, as said below
- ion_charge: float32 [384, 64, 512], P('blk', None, 'gz'), may hold values from 0.2 to 2
- ion_potential: float32 [384, 64, 512], P('blk', None, 'gz'), may hold values from -6 to 6
- hartree_prev: float32 [384, 64, 512], P('blk', None, 'gz'), may hold values from -6 to 6
- hist_steps: float32 [8, 384, 64, 512], P(None, 'blk', None, 'gz'), may hold values from -16 to 16
- hist_changes: float32 [8, 384, 64, 512], P(None, 'blk', None, 'gz'), may hold values from -32 to 32
Outputs:
- new_density: float32 [384, 64, 512], P('blk', None, 'gz')
- hartree: float32 [384, 64, 512], P('blk', None, 'gz')
Inputs may be any that keep to these rules, and one draw needn't show every extreme that they name: `sqrt_density`: positive everywhere.
All inputs are finite; a program needn't handle non-finite values.
Results may differ from a plain program's by a relative error of at most 0.006.
Values sent between devices are 32-bit elements; how exact they have to be, the bound alone decides.
No kernel may reach another device: no remote copies, remote signals or barrier semaphores. Data moves between devices by JAX's collectives and lax.ppermute only.
A program may use at most 128 MiB of HBM per device.

v0:
```python
import math

import jax
import jax.numpy as jnp
from jax import lax
from jax.sharding import PartitionSpec as P

ITERS = 4


center = -5369.0 / 1800.0
coeffs = (12.0 / 7.0, -15.0 / 56.0, 10.0 / 189.0, -1.0 / 112.0, 2.0 / 825.0, -1.0 / 4752.0)
screen = 0.0025
spacing = 0.28
source_scale = 4.0 * math.pi * spacing * spacing
tf_scale = 5.0 / 3.0 * 2.871234
step_length = 0.01
damp_floor = 0.2


def with_halo(x, sides, width):
    for axis, dim in sides:
        size, length = (lax.axis_size(axis), x.shape[dim])
        up = [(i, (i + 1) % size) for i in range(size)]
        down = [(j, i) for i, j in up]
        last = lax.slice_in_dim(x, length - width, length, axis=dim)
        first = lax.slice_in_dim(x, 0, width, axis=dim)
        before = lax.ppermute(last, axis, up)
        after = lax.ppermute(first, axis, down)
        x = jnp.concatenate([before, x, after], axis=dim)
    return x


def shifted_sum(padded, grid_axis, length):
    summed = 0.0
    for offset, weight in enumerate(coeffs, 1):
        upper_cells = lax.slice_in_dim(padded, 6 + offset, 6 + offset + length, axis=grid_axis)
        lower_cells = lax.slice_in_dim(padded, 6 - offset, 6 - offset + length, axis=grid_axis)
        summed = summed + weight * (upper_cells + lower_cells)
    return summed


def rolled_sum(values, grid_axis):
    summed = 0.0
    for offset, weight in enumerate(coeffs, 1):
        summed = summed + weight * (
            jnp.roll(values, offset, grid_axis) + jnp.roll(values, -offset, grid_axis)
        )
    return summed


def laplace(values):
    depth_x, width_y, depth_z = values.shape
    padded = with_halo(values, (("blk", 0), ("gz", 2)), 6)
    x_part = shifted_sum(padded[:, :, 6 : 6 + depth_z], 0, depth_x)
    z_part = shifted_sum(padded[6 : 6 + depth_x], 2, depth_z)
    return 3.0 * center * values + x_part + rolled_sum(values, 1) + z_part


def operate(values):
    return screen * values - laplace(values)


def residual_norm(residual):
    return lax.psum(jnp.sum(residual * residual), ("blk", "gz"))


def pair_terms(step_curv, step_norms, last_norm):
    damping = jnp.where(
        step_curv >= damp_floor * step_norms,
        1.0,
        (1.0 - damp_floor)
        * step_norms
        / jnp.maximum(step_norms - step_curv, (1.0 - damp_floor) * step_norms),
    )
    curvature = damping * step_curv + (1.0 - damping) * step_norms
    last_damp = damping[-1]
    last_bar = (
        last_damp * last_damp * last_norm
        + 2.0 * last_damp * (1.0 - last_damp) * step_curv[-1]
        + (1.0 - last_damp) * (1.0 - last_damp) * step_norms[-1]
    )
    return (damping, 1.0 / curvature, curvature[-1] / last_bar)


def on_device(sqrt_density, ion_charge, ion_potential, hartree_prev, hist_steps, hist_changes):
    source = source_scale * (sqrt_density * sqrt_density - ion_charge)
    hartree = hartree_prev
    residual = source - operate(hartree)
    direction = residual
    norm_now = residual_norm(residual)
    for sweep in range(ITERS):
        applied = operate(direction)
        step_size = norm_now / lax.psum(jnp.sum(direction * applied), ("blk", "gz"))
        hartree = hartree + step_size * direction
        residual = residual - step_size * applied
        if sweep + 1 < ITERS:
            norm_next = residual_norm(residual)
            direction = residual + norm_next / norm_now * direction
            norm_now = norm_next
    density_lap = laplace(sqrt_density)
    tf_power = jnp.exp(jnp.log(sqrt_density) * (4.0 / 3.0))
    energy_grad = 2.0 * sqrt_density * (
        hartree + ion_potential + tf_scale * tf_power
    ) - density_lap / (spacing * spacing)
    pair_count = hist_steps.shape[0]
    chem_top, chem_base = lax.psum(
        (jnp.sum(sqrt_density * energy_grad), jnp.sum(sqrt_density * sqrt_density)), ("blk", "gz")
    )
    chem_pot = chem_top / (2.0 * chem_base)
    gradient = energy_grad - 2.0 * chem_pot * sqrt_density
    step_curv, step_norms, last_norm = lax.psum(
        (
            jnp.sum(hist_steps * hist_changes, axis=(1, 2, 3)),
            jnp.sum(hist_steps * hist_steps, axis=(1, 2, 3)),
            jnp.sum(hist_changes[-1] * hist_changes[-1]),
        ),
        ("blk", "gz"),
    )
    damping, inverse_curv, scaling = pair_terms(step_curv, step_norms, last_norm)
    search = gradient
    first_coeffs = [None] * pair_count
    for pair_idx in reversed(range(pair_count)):
        partial_dot = lax.psum(jnp.sum(hist_steps[pair_idx] * search), ("blk", "gz"))
        first_coeffs[pair_idx] = inverse_curv[pair_idx] * partial_dot
        search = search - first_coeffs[pair_idx] * (
            damping[pair_idx] * hist_changes[pair_idx]
            + (1.0 - damping[pair_idx]) * hist_steps[pair_idx]
        )
    result = scaling * search
    for pair_idx in range(pair_count):
        damped_change = (
            damping[pair_idx] * hist_changes[pair_idx]
            + (1.0 - damping[pair_idx]) * hist_steps[pair_idx]
        )
        second = inverse_curv[pair_idx] * lax.psum(jnp.sum(damped_change * result), ("blk", "gz"))
        result = result + (first_coeffs[pair_idx] - second) * hist_steps[pair_idx]
    new_density = sqrt_density - step_length * result
    return (new_density, hartree)


def solution(mesh):
    placed = (
        P("blk", None, "gz"),
        P("blk", None, "gz"),
        P("blk", None, "gz"),
        P("blk", None, "gz"),
        P(None, "blk", None, "gz"),
        P(None, "blk", None, "gz"),
    )
    return jax.shard_map(
        on_device,
        mesh=mesh,
        in_specs=placed,
        out_specs=(P("blk", None, "gz"), P("blk", None, "gz")),
        check_vma=False,
    )
```

profile of v0, /device:TPU:1, one launch (start us, length us, event | category | flops | bytes accessed | tf_op | source)
XLA Modules:
  0.0 2058.6 jit_solution(15447510162628300889)
XLA Ops:
  1.7 3.3 collective-permute-start
  6.2 5.8 collective-permute-start.20
  76.9 2.8 collective-permute-start.2
  81.1 3.2 collective-permute-done.3
  85.8 4.2 fusion.137
  90.0 6.6 collective-permute-start.4
  98.6 2.8 collective-permute-done.5
  106.5 3.1 multiply_reduce_fusion.16
  109.7 80.9 %all-reduce.3 = (f32[]{:T(128)}, f32[]{:T(128)}) all-reduce(f32[]{:T(128)} %get-tuple-element.9, f32[]{:T(128)} %get-tuple-element.8), channel_id=1, replica_groups=mesh['blk'=64,'gz'=4] {'blk','gz'}, use_global_device_ids=true, to_apply=%region_7.8 | all-reduce | flops 2 | bytes 16 | tf_op jit(solution)/shard_map/psum | solution.py:65
  195.2 73.5 %psum.208 = f32[]{:T(128)} all-reduce(f32[]{:T(128)} %multiply_reduce_fusion.15), channel_id=1, replica_groups=mesh['blk'=64,'gz'=4] {'blk','gz'}, use_global_device_ids=true, to_apply=%region_11.12 | all-reduce | flops 1 | bytes 8 | tf_op jit(solution)/shard_map/psum | solution.py:65
  274.3 3.1 collective-permute-done.8
  283.3 3.8 multiply_reduce_fusion.14
  287.0 76.8 %psum.209 = f32[]{:T(128)} all-reduce(f32[]{:T(128)} %get-tuple-element.50), channel_id=1, replica_groups=mesh['blk'=64,'gz'=4] {'blk','gz'}, use_global_device_ids=true, to_apply=%region_13.14 | all-reduce | flops 1 | bytes 8 | tf_op jit(solution)/shard_map/psum | solution.py:94
  367.0 74.3 %psum.210 = f32[]{:T(128)} all-reduce(f32[]{:T(128)} %get-tuple-element.48), channel_id=1, replica_groups=mesh['blk'=64,'gz'=4] {'blk','gz'}, use_global_device_ids=true, to_apply=%region_15.16 | all-reduce | flops 1 | bytes 8 | tf_op jit(solution)/shard_map/psum | solution.py:65
  446.6 3.4 collective-permute-done.12
  450.0 2.7 collective-permute-start.14
  454.2 3.2 collective-permute-done.15
  457.5 3.8 multiply_reduce_fusion.12
  461.3 76.0 %psum.211 = f32[]{:T(128)} all-reduce(f32[]{:T(128)} %get-tuple-element.46), channel_id=1, replica_groups=mesh['blk'=64,'gz'=4] {'blk','gz'}, use_global_device_ids=true, to_apply=%region_17.18 | all-reduce | flops 1 | bytes 8 | tf_op jit(solution)/shard_map/psum | solution.py:94
  541.4 75.4 %psum.212 = f32[]{:T(128)} all-reduce(f32[]{:T(128)} %multiply_reduce_fusion.11), channel_id=1, replica_groups=mesh['blk'=64,'gz'=4] {'blk','gz'}, use_global_device_ids=true, to_apply=%region_19.20 | all-reduce | flops 1 | bytes 8 | tf_op jit(solution)/shard_map/psum | solution.py:65
  623.2 3.4 collective-permute-done.16
  631.9 3.0 fusion.315
  637.5 77.3 %psum.213 = f32[]{:T(128)} all-reduce(f32[]{:T(128)} %fusion.315), channel_id=1, replica_groups=mesh['blk'=64,'gz'=4] {'blk','gz'}, use_global_device_ids=true, to_apply=%region_21.22 | all-reduce | flops 1 | bytes 8 | tf_op jit(solution)/shard_map/psum | solution.py:94
  716.1 9.6 multiply_reduce_fusion.19
  725.8 74.4 %all-reduce.2 = (f32[]{:T(128)}, f32[]{:T(128)}) all-reduce(f32[]{:T(128)} %get-tuple-element.7, f32[]{:T(128)} %get-tuple-element.6), channel_id=1, replica_groups=mesh['blk'=64,'gz'=4] {'blk','gz'}, use_global_device_ids=true, to_apply=%region_23.24 | all-reduce | flops 2 | bytes 16 | tf_op jit(solution)/shard_map/psum | solution.py:107
  803.2 73.4 %all-reduce.1 = (f32[8]{0:T(128)S(1)}, f32[8]{0:T(128)S(1)}, f32[]{:T(128)}) all-reduce(f32[8]{0:T(128)S(1)} %get-tuple-element.5, f32[8]{0:T(128)S(1)} %get-tuple-element.4, f32[]{:T(128)} %fusion.311), channel_id=1, replica_groups=mesh['blk'=64,'gz'=4] {'blk','gz'}, use_global_device_ids=true, to_apply=%region_3.4 | all-reduce | flops 17 | bytes 136 | tf_op jit(solution)/shard_map/psum | solution.py:112
  884.1 74.3 %psum.217 = f32[]{:T(128)} all-reduce(f32[]{:T(128)} %get-tuple-element.39), channel_id=1, replica_groups=mesh['blk'=64,'gz'=4] {'blk','gz'}, use_global_device_ids=true, to_apply=%region_29.30 | all-reduce | flops 1 | bytes 8 | tf_op jit(solution)/shard_map/psum | solution.py:124
  960.2 3.1 fusion.307
  963.3 73.3 %psum.218 = f32[]{:T(128)} all-reduce(f32[]{:T(128)} %get-tuple-element.37), channel_id=1, replica_groups=mesh['blk'=64,'gz'=4] {'blk','gz'}, use_global_device_ids=true, to_apply=%region_31.32 | all-reduce | flops 1 | bytes 8 | tf_op jit(solution)/shard_map/psum | solution.py:124
  1038.6 3.3 fusion.305
  1042.0 74.2 %psum.219 = f32[]{:T(128)} all-reduce(f32[]{:T(128)} %get-tuple-element.35), channel_id=1, replica_groups=mesh['blk'=64,'gz'=4] {'blk','gz'}, use_global_device_ids=true, to_apply=%region_33.34 | all-reduce | flops 1 | bytes 8 | tf_op jit(solution)/shard_map/psum | solution.py:124
  1118.1 3.3 fusion.303
  1121.4 73.4 %psum.220 = f32[]{:T(128)} all-reduce(f32[]{:T(128)} %get-tuple-element.33), channel_id=1, replica_groups=mesh['blk'=64,'gz'=4] {'blk','gz'}, use_global_device_ids=true, to_apply=%region_35.36 | all-reduce | flops 1 | bytes 8 | tf_op jit(solution)/shard_map/psum | solution.py:124
  1196.6 3.3 fusion.301
  1199.8 74.2 %psum.221 = f32[]{:T(128)} all-reduce(f32[]{:T(128)} %get-tuple-element.31), channel_id=1, replica_groups=mesh['blk'=64,'gz'=4] {'blk','gz'}, use_global_device_ids=true, to_apply=%region_37.38 | all-reduce | flops 1 | bytes 8 | tf_op jit(solution)/shard_map/psum | solution.py:124
  1275.8 3.1 fusion.299
  1278.9 73.5 %psum.222 = f32[]{:T(128)} all-reduce(f32[]{:T(128)} %get-tuple-element.29), channel_id=1, replica_groups=mesh['blk'=64,'gz'=4] {'blk','gz'}, use_global_device_ids=true, to_apply=%region_39.40 | all-reduce | flops 1 | bytes 8 | tf_op jit(solution)/shard_map/psum | solution.py:124
  1356.8 3.4 fusion.297
  1360.2 74.2 %all-reduce = (f32[]{:T(128)}, f32[]{:T(128)}) all-reduce(f32[]{:T(128)} %get-tuple-element.27, f32[]{:T(128)} %multiply_reduce_fusion.18), channel_id=1, replica_groups=mesh['blk'=64,'gz'=4] {'blk','gz'}, use_global_device_ids=true, to_apply=%region_41.42 | all-reduce | flops 2 | bytes 16 | tf_op jit(solution)/shard_map/psum | solution.py:124
  1439.7 73.7 %psum.224 = f32[]{:T(128)} all-reduce(f32[]{:T(128)} %multiply_reduce_fusion.9), channel_id=1, replica_groups=mesh['blk'=64,'gz'=4] {'blk','gz'}, use_global_device_ids=true, to_apply=%region_43.44 | all-reduce | flops 1 | bytes 8 | tf_op jit(solution)/shard_map/psum | solution.py:136
  1514.7 4.2 multiply_reduce_fusion.8
  1518.9 74.1 %psum.225 = f32[]{:T(128)} all-reduce(f32[]{:T(128)} %get-tuple-element.25), channel_id=1, replica_groups=mesh['blk'=64,'gz'=4] {'blk','gz'}, use_global_device_ids=true, to_apply=%region_45.46 | all-reduce | flops 1 | bytes 8 | tf_op jit(solution)/shard_map/psum | solution.py:136
  1596.7 73.5 %psum.226 = f32[]{:T(128)} all-reduce(f32[]{:T(128)} %get-tuple-element.23), channel_id=1, replica_groups=mesh['blk'=64,'gz'=4] {'blk','gz'}, use_global_device_ids=true, to_apply=%region_47.48 | all-reduce | flops 1 | bytes 8 | tf_op jit(solution)/shard_map/psum | solution.py:136
  1673.8 74.1 %psum.227 = f32[]{:T(128)} all-reduce(f32[]{:T(128)} %multiply_reduce_fusion.6), channel_id=1, replica_groups=mesh['blk'=64,'gz'=4] {'blk','gz'}, use_global_device_ids=true, to_apply=%region_49.50 | all-reduce | flops 1 | bytes 8 | tf_op jit(solution)/shard_map/psum | solution.py:136
  1751.7 73.5 %psum.228 = f32[]{:T(128)} all-reduce(f32[]{:T(128)} %get-tuple-element.21), channel_id=1, replica_groups=mesh['blk'=64,'gz'=4] {'blk','gz'}, use_global_device_ids=true, to_apply=%region_51.52 | all-reduce | flops 1 | bytes 8 | tf_op jit(solution)/shard_map/psum | solution.py:136
  1828.8 74.1 %psum.229 = f32[]{:T(128)} all-reduce(f32[]{:T(128)} %multiply_reduce_fusion.4), channel_id=1, replica_groups=mesh['blk'=64,'gz'=4] {'blk','gz'}, use_global_device_ids=true, to_apply=%region_53.54 | all-reduce | flops 1 | bytes 8 | tf_op jit(solution)/shard_map/psum | solution.py:136
  1904.9 73.5 %psum.230 = f32[]{:T(128)} all-reduce(f32[]{:T(128)} %get-tuple-element.19), channel_id=1, replica_groups=mesh['blk'=64,'gz'=4] {'blk','gz'}, use_global_device_ids=true, to_apply=%region_55.56 | all-reduce | flops 1 | bytes 8 | tf_op jit(solution)/shard_map/psum | solution.py:136
  1981.0 74.1 %psum.231 = f32[]{:T(128)} all-reduce(f32[]{:T(128)} %multiply_reduce_fusion.2), channel_id=1, replica_groups=mesh['blk'=64,'gz'=4] {'blk','gz'}, use_global_device_ids=true, to_apply=%region_57.58 | all-reduce | flops 1 | bytes 8 | tf_op jit(solution)/shard_map/psum | solution.py:136
  (276 shorter events, 135.3 us)
Async XLA Ops:
  1.7 74.3 %collective-permute-start = (f32[6,64,128]{1,2,0:T(8,128)S(1)}, f32[6,64,128]{1,2,0:T(8,128)S(1)}, u32[]{:S(2)}, u32[]{:S(2)}) collective-permute-start(f32[6,64,128]{1,2,0:T(8,128)S(1)} %copy.44), channel_id=1, source_target_pairs={{4,0},{8,4},{12,8},{16,12},{20,16},{24,20},{28,24},{32,28},{36,32}... | collective-permute-start | bytes 589832 | tf_op jit(solution)/shard_map/ppermute | solution.py:29
  5.0 71.0 %collective-permute-start.1 = (f32[6,64,128]{1,2,0:T(8,128)S(1)}, f32[6,64,128]{1,2,0:T(8,128)}, u32[]{:S(2)}, u32[]{:S(2)}) collective-permute-start(f32[6,64,128]{1,2,0:T(8,128)S(1)} %copy.44), channel_id=1, source_target_pairs={{0,4},{4,8},{8,12},{12,16},{16,20},{20,24},{24,28},{28,32},{32,36}... | collective-permute-start | bytes 589832 | tf_op jit(solution)/shard_map/ppermute | solution.py:28
  6.2 73.8 %collective-permute-start.20 = (f32[6,64,128]{1,2,0:T(8,128)S(1)}, f32[6,64,128]{1,2,0:T(8,128)S(1)}, u32[]{:S(2)}, u32[]{:S(2)}) collective-permute-start(f32[6,64,128]{1,2,0:T(8,128)S(1)} %copy.94), channel_id=1, source_target_pairs={{4,0},{8,4},{12,8},{16,12},{20,16},{24,20},{28,24},{32,28},{36,32}... | collective-permute-start | bytes 589832 | tf_op jit(solution)/shard_map/ppermute | solution.py:29
  12.0 68.0 %collective-permute-start.21 = (f32[6,64,128]{1,2,0:T(8,128)S(1)}, f32[6,64,128]{1,2,0:T(8,128)S(1)}, u32[]{:S(2)}, u32[]{:S(2)}) collective-permute-start(f32[6,64,128]{1,2,0:T(8,128)S(1)} %copy.94), channel_id=1, source_target_pairs={{0,4},{4,8},{8,12},{12,16},{16,20},{20,24},{24,28},{28,32},{32,36}... | collective-permute-start | bytes 589832 | tf_op jit(solution)/shard_map/ppermute | solution.py:28
  33.9 5.7 copy-start.40
  54.4 20.9 %copy-start.6 = (f32[1,6,64,128]{2,3,1,0:T(8,128)}, f32[1,6,64,128]{2,3,1,0:T(8,128)S(1)}, u32[]{:S(2)}) copy-start(f32[1,6,64,128]{2,3,1,0:T(8,128)S(1)} %copy.97) | copy-start | bytes 589828
  75.2 10.4 copy-start.36
  76.0 9.7 copy-start.33
  76.0 9.7 copy-start.34
  76.0 9.7 copy-start.35
  76.9 4.2 collective-permute-start.2
  79.7 4.6 collective-permute-start.3
  79.9 5.7 copy-start.14
  79.9 5.7 copy-start.16
  80.0 5.8 copy-start.29
  80.0 5.8 copy-start.30
  80.0 5.8 copy-start.31
  80.0 5.8 copy-start.32
  90.0 8.6 collective-permute-start.4
  96.6 4.8 collective-permute-start.5
  101.5 3.3 collective-permute-start.6
  101.7 4.7 collective-permute-start.7
  192.6 442.3 %collective-permute-start.22 = (f32[18,64,6]{1,2,0:T(8,128)}, f32[18,64,6]{1,2,0:T(8,128)}, u32[]{:S(2)}, u32[]{:S(2)}) collective-permute-start(f32[18,64,6]{1,2,0:T(8,128)} %get-tuple-element.91), channel_id=1, source_target_pairs={{1,0},{2,1},{3,2},{0,3},{5,4},{6,5},{7,6},{4,7},{9,8},{10,9},{11,1... | collective-permute-start | bytes 82952 | tf_op jit(solution)/shard_map/ppermute | solution.py:29
  270.1 7.3 collective-permute-start.8
  270.8 6.5 collective-permute-start.9
  277.4 3.6 collective-permute-start.10
  278.7 4.4 collective-permute-start.11
  366.9 171.7 %copy-start.8 = (f32[6,64,128]{1,2,0:T(8,128)}, f32[6,64,128]{1,2,0:T(8,128)S(1)}, u32[]{:S(2)}) copy-start(f32[6,64,128]{1,2,0:T(8,128)S(1)} %get-tuple-element.49) | copy-start | bytes 589828
  442.7 7.3 collective-permute-start.12
  443.4 6.5 collective-permute-start.13
  450.0 4.1 collective-permute-start.14
  452.8 4.6 collective-permute-start.15
  540.4 94.5 %collective-permute-start.23 = (f32[18,64,6]{1,2,0:T(8,128)}, f32[18,64,6]{1,2,0:T(8,128)}, u32[]{:S(2)}, u32[]{:S(2)}) collective-permute-start(f32[18,64,6]{1,2,0:T(8,128)} %get-tuple-element.92), channel_id=1, source_target_pairs={{0,1},{1,2},{2,3},{3,0},{4,5},{5,6},{6,7},{7,4},{8,9},{9,10},{10,1... | collective-permute-start | bytes 82952 | tf_op jit(solution)/shard_map/ppermute | solution.py:28
  619.3 7.3 collective-permute-start.16
  620.4 6.3 collective-permute-start.17
  626.6 3.6 collective-permute-start.18
  627.3 4.4 collective-permute-start.19
  725.8 156.9 %copy-start.7 = (f32[1,6,64,128]{2,3,1,0:T(8,128)S(1)}, f32[1,6,64,128]{2,3,1,0:T(8,128)}, u32[]{:S(2)}) copy-start(f32[1,6,64,128]{2,3,1,0:T(8,128)} %copy-done.6) | copy-start | bytes 589828
  725.8 156.9 %copy-start.18 = (f32[6,64,128]{1,2,0:T(8,128)S(1)}, f32[6,64,128]{1,2,0:T(8,128)}, u32[]{:S(2)}) copy-start(f32[6,64,128]{1,2,0:T(8,128)} %get-tuple-element.44) | copy-start | bytes 589828
  803.2 157.0 %copy-start.2 = (f32[1,6,64,128]{2,3,1,0:T(8,128)S(1)}, f32[1,6,64,128]{2,3,1,0:T(8,128)}, u32[]{:S(2)}) copy-start(f32[1,6,64,128]{2,3,1,0:T(8,128)} %copy.101) | copy-start | bytes 589828
  884.1 76.1 %copy-start.13 = (f32[6,64,128]{1,2,0:T(8,128)}, f32[6,64,128]{1,2,0:T(8,128)S(1)}, u32[]{:S(2)}) copy-start(f32[6,64,128]{1,2,0:T(8,128)S(1)} %get-tuple-element.40) | copy-start | bytes 589828
  884.1 154.5 %copy-start = (f32[1,6,64,128]{2,3,1,0:T(8,128)S(1)}, f32[1,6,64,128]{2,3,1,0:T(8,128)}, u32[]{:S(2)}) copy-start(f32[1,6,64,128]{2,3,1,0:T(8,128)} %copy.103) | copy-start | bytes 589828
  884.1 154.5 %copy-start.9 = (f32[1,6,64,128]{2,3,1,0:T(8,128)S(1)}, f32[1,6,64,128]{2,3,1,0:T(8,128)}, u32[]{:S(2)}) copy-start(f32[1,6,64,128]{2,3,1,0:T(8,128)} %copy.102) | copy-start | bytes 589828
  963.3 154.8 %copy-start.3 = (f32[1,6,64,128]{2,3,1,0:T(8,128)S(1)}, f32[1,6,64,128]{2,3,1,0:T(8,128)}, u32[]{:S(2)}) copy-start(f32[1,6,64,128]{2,3,1,0:T(8,128)} %copy.105) | copy-start | bytes 589828
  1042.0 154.6 %copy-start.1 = (f32[1,6,64,128]{2,3,1,0:T(8,128)S(1)}, f32[1,6,64,128]{2,3,1,0:T(8,128)}, u32[]{:S(2)}) copy-start(f32[1,6,64,128]{2,3,1,0:T(8,128)} %copy.107) | copy-start | bytes 589828
  1673.8 152.6 %copy-start.10 = (f32[1,6,64,128]{2,3,1,0:T(8,128)S(1)}, f32[1,6,64,128]{2,3,1,0:T(8,128)}, u32[]{:S(2)}) copy-start(f32[1,6,64,128]{2,3,1,0:T(8,128)} %copy.102) | copy-start | bytes 589828
  1751.7 152.5 %copy-start.11 = (f32[6,64,128]{1,2,0:T(8,128)S(1)}, f32[6,64,128]{1,2,0:T(8,128)}, u32[]{:S(2)}) copy-start(f32[6,64,128]{1,2,0:T(8,128)} %get-tuple-element.38) | copy-start | bytes 589828
  1751.7 152.5 %copy-start.12 = (f32[6,64,128]{1,2,0:T(8,128)S(1)}, f32[6,64,128]{1,2,0:T(8,128)}, u32[]{:S(2)}) copy-start(f32[6,64,128]{1,2,0:T(8,128)} %get-tuple-element.22) | copy-start | bytes 589828
  (18 other events, 68.9 us)
where the time goes:
time: 2070 us; the launch traced here: 2060 us
  blocking collectives  1790 us (86%)
  other arithmetic  82 us (4%)
  local copies, waits for them, and re-layouts  78.1 us (4%)
  between operations  42.3 us (2%)
  starting transfers between devices  35.7 us (2%)
  waiting for transfers between devices  31 us (1%)
    psum x8, blocking collectives, on_device(): lax.psum(jnp.sum(damped_change * result), ('blk', 'gz'))  590 us
    psum x7, blocking collectives, on_device(): lax.psum(jnp.sum(hist_steps[pair_idx] * search), ('blk', 'gz'))  517 us
    psum x4, blocking collectives, residual_norm(): return lax.psum(jnp.sum(residual * residual), ('blk', 'gz'))  304 us
    psum x3, blocking collectives, on_device(): step_size = norm_now / lax.psum(jnp.sum(direction * applied), ('blk', 'gz'))  230 us
    psum x1, blocking collectives, on_device(): lax.psum((jnp.sum(sqrt_density * energy_grad), jnp.sum(sqrt_density * sqr...  74.4 us
    psum x1, blocking collectives, on_device(): lax.psum((jnp.sum(hist_steps * hist_changes, axis=(1, 2, 3)), jnp.sum(his...  73.4 us
  transfers between devices with their start and end apart: 24, of which 14 were waited for; matrix products, arithmetic and copies ran while one was open for 4% of the time, Pallas kernels for 0%

commit v1 on v0

v1 whole, which is shorter than its diff:
```python
import functools
import math

import jax
import jax.numpy as jnp
from jax import lax
from jax.experimental import pallas as pl
from jax.experimental.pallas import tpu as pltpu
from jax.sharding import PartitionSpec as P

center = -5369.0 / 1800.0
coeffs = (12.0 / 7.0, -15.0 / 56.0, 10.0 / 189.0, -1.0 / 112.0, 2.0 / 825.0, -1.0 / 4752.0)
screen = 0.0025
spacing = 0.28
source_scale = 4.0 * math.pi * spacing * spacing
tf_scale = 5.0 / 3.0 * 2.871234
step_length = 0.01
damp_floor = 0.2

SHIFT = 2.0
HIST = 8
REACH = 6
LANES = 128
VMEM_LIMIT = 24 * 1024 * 1024

ROW_GRAM = 0
ROW_BASE = 136
ROW_W = 170
ROW_MOM = 238
PAIRS = tuple((i, j) for i in range(HIST) for j in range(i, HIST))
PAIR_ROW = {pair: row for row, pair in enumerate(PAIRS)}


def two_sum(a, b):
    s = a + b
    bb = s - a
    return s, (a - (s - bb)) + (b - bb)


def quick_sum(a, b):
    s = a + b
    return s, b - (s - a)


def split(a):
    t = 4097.0 * a
    hi = t - (t - a)
    return hi, a - hi


def two_prod(a, b):
    p = a * b
    ah, al = split(a)
    bh, bl = split(b)
    return p, ((ah * bh - p) + ah * bl + al * bh) + al * bl


def df_add(a, b):
    s, e = two_sum(a[0], b[0])
    return quick_sum(s, e + (a[1] + b[1]))


def df_neg(a):
    return (-a[0], -a[1])


def df_sub(a, b):
    return df_add(a, df_neg(b))


def df_scale(a, factor):
    return (a[0] * factor, a[1] * factor)


def df_mul(a, b):
    p, e = two_prod(a[0], b[0])
    return quick_sum(p, e + (a[0] * b[1] + a[1] * b[0]))


def df_div(a, b):
    q1 = a[0] / b[0]
    r = df_sub(a, df_mul(b, (q1, jnp.zeros_like(q1))))
    q2 = r[0] / b[0]
    return quick_sum(q1, q2)


def lane_ids(shape):
    return lax.broadcasted_iota(jnp.int32, shape, len(shape) - 1)


def stencil_plane(i, own, left, right, ext, z_left, z_right):
    def layer(k):
        if k < 0:
            return left[k + REACH]
        if k >= REACH:
            return right[k - REACH]
        return own[k]

    values = own[i]
    rows = values.shape[0]
    lane = lane_ids((rows, LANES))
    tile_lane = lane_ids((8, LANES))
    from_right = z_right[8 * (i // 2) : 8 * (i // 2) + 8, :]
    from_left = z_left[8 * (i // 2) : 8 * (i // 2) + 8, :]
    wraps = []
    for b in range(rows // 8):
        j = 8 * (i % 2) + b
        upper = pltpu.roll(from_right, (LANES - 8 * j) % LANES, 1)
        lower = pltpu.roll(from_left, (2 * LANES - 8 * j - 8) % LANES, 1)
        wraps.append(jnp.where(tile_lane < 64, upper, lower))
    wrap = jnp.concatenate(wraps, axis=0)
    total = (3.0 * center) * values
    for k, weight in enumerate(coeffs, 1):
        pair = layer(i + k) + layer(i - k)
        pair = pair + (ext[i, 8 + k : 8 + k + rows, :] + ext[i, 8 - k : 8 - k + rows, :])
        up = pltpu.roll(jnp.where(lane < k, wrap, values), LANES - k, 1)
        down = pltpu.roll(jnp.where(lane >= LANES - k, wrap, values), k, 1)
        total = total + weight * (pair + (up + down))
    return total, values


def fill_ext(own, ext):
    rows = own.shape[1]
    ext[:, 8 : 8 + rows, :] = own[...]
    ext[:, 0:8, :] = own[:, rows - 8 : rows, :]
    ext[:, 8 + rows : 16 + rows, :] = own[:, 0:8, :]


def pack_faces(src, first_ref, last_ref, base):
    lane = lane_ids((8, LANES))
    for m in range(3):
        first = jnp.zeros((8, LANES), jnp.float32)
        last = jnp.zeros((8, LANES), jnp.float32)
        for j in range(16):
            n = 16 * m + j
            tile = src[n // 8, 8 * (n % 8) : 8 * (n % 8) + 8, :]
            here = (lane >= 8 * j) & (lane < 8 * j + 8)
            first = jnp.where(here, pltpu.roll(tile, 8 * j, 1) if j else tile, first)
            last = jnp.where(here, pltpu.roll(tile, (8 * j + 8) % LANES, 1) if j < 15 else tile, last)
        first_ref[base + 8 * m : base + 8 * m + 8, :] = first
        last_ref[base + 8 * m : base + 8 * m + 8, :] = last


def exact_total(hi, lo):
    for step in (4, 2, 1):
        hi, err = two_sum(hi, pltpu.roll(hi, step, 0))
        lo = lo + pltpu.roll(lo, step, 0) + err
    hi, lo = hi[0:1], lo[0:1]
    for step in (64, 32, 16, 8, 4, 2, 1):
        hi, err = two_sum(hi, pltpu.roll(hi, step, 1))
        lo = lo + pltpu.roll(lo, step, 1) + err
    return quick_sum(hi, lo)


def add_tile(acc, product):
    hi, err = two_sum(acc[0], product)
    return hi, acc[1] + err


def tile_of(ref, i, b):
    return ref[i, pl.ds(pl.multiple_of(8 * b, 8), 8), :]


def exact_dots(pairs):
    zero = jnp.zeros((8, LANES), jnp.float32)

    def body(i, accs):
        for b in range(8):
            accs = tuple(
                add_tile(acc, tile_of(a, i, b) * tile_of(c, i, b)) for acc, (a, c) in zip(accs, pairs)
            )
        return accs

    accs = lax.fori_loop(0, REACH, body, tuple((zero, zero) for _ in pairs))
    return [exact_total(*acc) for acc in accs]


def collapse(acc):
    return jnp.sum(acc, axis=0, keepdims=True)


def pack_kernel(hartree, density, first, last):
    pack_faces(hartree, first, last, 0)
    pack_faces(density, first, last, 24)


def residual_kernel(hartree, left, right, z_left, z_right, density, charge, out, first, last, ext):
    fill_ext(hartree, ext)
    for i in range(REACH):
        lap, values = stencil_plane(i, hartree, left, right, ext, z_left, z_right)
        rho = density[i]
        out[i] = source_scale * (rho * rho - charge[i]) - (screen * values - lap)
    pack_faces(out, first, last, 0)


def basis_kernel(has_prior, *refs):
    if has_prior:
        own, left, right, z_left, z_right, prior, out, first, last, ext = refs
    else:
        own, left, right, z_left, z_right, out, first, last, ext = refs
    fill_ext(own, ext)
    for i in range(REACH):
        lap, values = stencil_plane(i, own, left, right, ext, z_left, z_right)
        moved = (screen / SHIFT - 1.0) * values - (1.0 / SHIFT) * lap
        out[i] = 2.0 * moved - prior[i] if has_prior else moved
    pack_faces(out, first, last, 0)


def gram_kernel(steps, changes, rows):
    zero = jnp.zeros((8, LANES), jnp.float32)

    def run(base, left, right, pairs):
        def body(n, accs):
            i, b = n // 8, n % 8
            at = pl.ds(pl.multiple_of(8 * b, 8), 8)
            l_need = sorted({p for p, _ in pairs})
            r_need = sorted({q for _, q in pairs})
            l_tiles = {p: left[p, i, at, :] for p in l_need}
            r_tiles = l_tiles if left is right else {}
            r_tiles = {q: r_tiles[q] if q in r_tiles else right[q, i, at, :] for q in r_need}
            return tuple(acc + l_tiles[p] * r_tiles[q] for acc, (p, q) in zip(accs, pairs))

        accs = lax.fori_loop(0, 48, body, tuple(zero for _ in pairs))
        for n, acc in enumerate(accs):
            rows[base + n : base + n + 1, :] = collapse(acc)

    run(0, steps, steps, PAIRS)
    run(36, changes, changes, PAIRS)
    run(72, steps, changes, tuple((i, j) for i in range(4) for j in range(8)))
    run(104, steps, changes, tuple((i, j) for i in range(4, 8) for j in range(8)))


def field_dots(steps, changes, others):
    zero = jnp.zeros((8, LANES), jnp.float32)
    count = 2 * HIST

    def body(i, accs):
        accs = list(accs)
        for b in range(8):
            at = pl.ds(8 * b, 8)
            tiles = [other(i, b) for other in others]
            for f in range(count):
                field = steps[f, i, at, :] if f < HIST else changes[f - HIST, i, at, :]
                for o, tile in enumerate(tiles):
                    accs[o * count + f] = accs[o * count + f] + field * tile
        return tuple(accs)

    accs = lax.fori_loop(0, REACH, body, tuple(zero for _ in range(count * len(others))))
    return [collapse(acc) for acc in accs]


def plain_dots(pairs):
    zero = jnp.zeros((8, LANES), jnp.float32)

    def body(i, accs):
        for b in range(8):
            accs = tuple(acc + a(i, b) * c(i, b) for acc, (a, c) in zip(accs, pairs))
        return accs

    return [collapse(acc) for acc in lax.fori_loop(0, REACH, body, tuple(zero for _ in pairs))]


def base_kernel(density, left, right, z_left, z_right, hartree, potential, steps, changes, grad, rows, ext):
    fill_ext(density, ext)
    for i in range(REACH):
        lap, rho = stencil_plane(i, density, left, right, ext, z_left.at[24:48], z_right.at[24:48])
        power = jnp.exp(jnp.log(rho) * (4.0 / 3.0))
        grad[i] = 2.0 * rho * (hartree[i] + potential[i] + tf_scale * power) - lap * (
            1.0 / (spacing * spacing)
        )
    g_tile = lambda i, b: tile_of(grad, i, b)
    r_tile = lambda i, b: tile_of(density, i, b)
    dots = field_dots(steps, changes, [g_tile, r_tile]) + plain_dots([(r_tile, g_tile), (r_tile, r_tile)])
    for n, row in enumerate(dots):
        rows[n : n + 1, :] = row


def basis_dots(vector, density, steps, changes, rows):
    w_tile = lambda i, b: 2.0 * tile_of(density, i, b) * tile_of(vector, i, b)
    r_tile = lambda i, b: tile_of(density, i, b)
    dots = field_dots(steps, changes, [w_tile]) + plain_dots([(r_tile, w_tile)])
    for n, row in enumerate(dots):
        rows[n : n + 1, :] = row


def store_moments(pairs, moments):
    for n, (hi, lo) in enumerate(exact_dots(pairs)):
        moments[2 * n : 2 * n + 1, :] = hi
        moments[2 * n + 1 : 2 * n + 2, :] = lo


def first_dots_kernel(vector, density, steps, changes, rows, moments):
    basis_dots(vector, density, steps, changes, rows)
    store_moments([(vector, vector)], moments)


def dots_kernel(prior, vector, density, steps, changes, rows, moments):
    basis_dots(vector, density, steps, changes, rows)
    store_moments([(prior, vector), (vector, vector)], moments)


def last_dots_kernel(
    prior, vector, density, steps, changes, gram, base, d0, d1, d2, m0, m1, m2, out, rows, own_rows, moments
):
    basis_dots(vector, density, steps, changes, own_rows)
    store_moments([(prior, vector), (vector, vector)], moments)
    rows[ROW_GRAM : ROW_GRAM + 136, :] = gram[0:136, :]
    rows[ROW_BASE : ROW_BASE + 34, :] = base[0:34, :]
    for n, d in enumerate((d0, d1, d2, own_rows)):
        rows[ROW_W + 17 * n : ROW_W + 17 * n + 17, :] = d[0:17, :]
    rows[ROW_MOM:256, :] = jnp.zeros((256 - ROW_MOM, LANES), jnp.float32)
    lane = lane_ids((1, LANES))
    out[0:1, :] = jnp.sum(jnp.transpose(rows[0:128, :]), axis=0, keepdims=True)
    second = jnp.sum(jnp.transpose(rows[128:256, :]), axis=0, keepdims=True)
    at = ROW_MOM - 128
    order = [(m0, 0), (m1, 0), (m1, 1), (m2, 0), (m2, 1), (moments, 0), (moments, 1)]
    for n, (ref, which) in enumerate(order):
        second = jnp.where(lane == at + n, ref[2 * which : 2 * which + 1, :], second)
        second = jnp.where(lane == at + 8 + n, ref[2 * which + 1 : 2 * which + 2, :], second)
    out[1:2, :] = second


def send_kernel(own, left, right, z_left, z_right, sums, out, ext):
    fill_ext(own, ext)
    zero = jnp.zeros((8, LANES), jnp.float32)
    accs = [(zero, zero) for _ in range(2)]
    for i in range(REACH):
        lap, values = stencil_plane(i, own, left, right, ext, z_left, z_right)
        product = values * ((screen / SHIFT - 1.0) * values - (1.0 / SHIFT) * lap)
        for b in range(8):
            accs[b % 2] = add_tile(accs[b % 2], product[8 * b : 8 * b + 8])
    hi, err = two_sum(accs[0][0], accs[1][0])
    hi, lo = exact_total(hi, accs[0][1] + accs[1][1] + err)
    lane = lane_ids((1, LANES))
    at = ROW_MOM - 128
    second = jnp.where(lane == at + 7, hi, jnp.where(lane == at + 15, lo, sums[1:2, :]))
    both = jnp.concatenate([sums[0:1, :], second], axis=0)
    out[...] = jnp.broadcast_to(both[None], out.shape)


def solve_krylov(moment):
    n00, n01, n11, n12, n22, n23, n33, n34 = moment
    nu = [n00, n01]
    nu.append(df_sub(df_scale(n11, 2.0), n00))
    nu.append(df_sub(df_scale(n12, 2.0), n01))
    nu.append(df_sub(df_scale(n22, 2.0), n00))
    nu.append(df_sub(df_scale(n23, 2.0), n01))
    nu.append(df_sub(df_scale(n33, 2.0), n00))

    def gram(i, j):
        if i == j == 0:
            return n00
        return df_scale(df_add(nu[i + j], nu[abs(i - j)]), 0.5)

    def moved(i, j):
        if i == 3 and j == 3:
            return n34
        if j == 0:
            return gram(i, 1)
        return df_scale(df_add(gram(i, j + 1), gram(i, j - 1)), 0.5)

    mat = {(i, j): df_add(moved(i, j), gram(i, j)) for i in range(4) for j in range(i + 1)}
    rhs = [df_scale(gram(i, 0), 1.0 / SHIFT) for i in range(4)]
    low = {}
    for k in range(4):
        for i in range(k + 1, 4):
            low[i, k] = df_div(mat[i, k], mat[k, k])
        for i in range(k + 1, 4):
            for j in range(k + 1, i + 1):
                mat[i, j] = df_sub(mat[i, j], df_mul(low[i, k], mat[j, k]))
            rhs[i] = df_sub(rhs[i], df_mul(low[i, k], rhs[k]))
    sol = [None] * 4
    for k in reversed(range(4)):
        value = df_div(rhs[k], mat[k, k])
        for i in range(k + 1, 4):
            value = df_sub(value, df_mul(low[i, k], sol[i]))
        sol[k] = value
    return [hi + lo for hi, lo in sol]


def final_kernel(received, density, hartree, grad, v0, v1, v2, v3, steps, changes, new_density, new_hartree, spread):
    chains = 8
    parts = [(received[n], jnp.zeros((2, LANES), jnp.float32)) for n in range(chains)]
    for n in range(chains, received.shape[0]):
        parts[n % chains] = add_tile(parts[n % chains], received[n])
    while len(parts) > 1:
        half = len(parts) // 2
        merged = []
        for a, b in zip(parts[:half], parts[half:]):
            hi, err = two_sum(a[0], b[0])
            merged.append((hi, a[1] + b[1] + err))
        parts = merged
    hi, lo = quick_sum(*parts[0])
    spread[0:128, :] = jnp.transpose(jnp.broadcast_to(hi[0:1], (LANES, LANES)))
    spread[128:256, :] = jnp.transpose(jnp.broadcast_to(hi[1:2], (LANES, LANES)))
    spread[256:384, :] = jnp.transpose(jnp.broadcast_to(lo[1:2], (LANES, LANES)))

    def row(n):
        return spread[n : n + 1, :]

    def moment(n):
        low = 128 + ROW_MOM
        a = df_add((row(ROW_MOM + n), row(low + n)), (row(ROW_MOM + 8 + n), row(low + 8 + n)))
        return a

    mix = solve_krylov([moment(n) for n in range(8)])

    def s_s(i, j):
        return row(ROW_GRAM + PAIR_ROW[min(i, j), max(i, j)])

    def y_y(i, j):
        return row(ROW_GRAM + 36 + PAIR_ROW[min(i, j), max(i, j)])

    def s_y(i, j):
        return row(ROW_GRAM + 72 + 8 * i + j)

    pairs = range(HIST)
    theta, rest, inverse = [], [], []
    for i in pairs:
        curv, norm = s_y(i, i), s_s(i, i)
        kept = (1.0 - damp_floor) * norm
        damp = jnp.where(curv >= damp_floor * norm, 1.0, kept / jnp.maximum(norm - curv, kept))
        theta.append(damp)
        rest.append(1.0 - damp)
        inverse.append(1.0 / (damp * curv + (1.0 - damp) * norm))

    def s_bar(i, j):
        return theta[j] * s_y(i, j) + rest[j] * s_s(i, j)

    def bar_bar(i, j):
        return theta[i] * (theta[j] * y_y(i, j) + rest[j] * s_y(j, i)) + rest[i] * s_bar(i, j)

    last = HIST - 1
    scaling = s_bar(last, last) / bar_bar(last, last)

    def energy(n):
        value = row(ROW_BASE + n) if n < 16 else row(ROW_BASE + 32)
        for j in range(4):
            value = value + mix[j] * row(ROW_W + 17 * j + n)
        return value

    chem = energy(16) / row(ROW_BASE + 33)

    def gradient(n):
        return energy(n) - chem * row(ROW_BASE + 16 + n)

    s_grad = [gradient(i) for i in pairs]
    bar_grad = [theta[i] * gradient(HIST + i) + rest[i] * s_grad[i] for i in pairs]

    first = [None] * HIST
    pending = list(s_grad)
    for j in reversed(pairs):
        first[j] = inverse[j] * pending[j]
        for i in range(j):
            pending[i] = pending[i] - first[j] * s_bar(i, j)
    pending = list(bar_grad)
    for j in pairs:
        for i in pairs:
            pending[i] = pending[i] - first[j] * bar_bar(i, j)
    pending = [scaling * value for value in pending]
    step_mix, change_mix = [], []
    for j in pairs:
        net = first[j] - inverse[j] * pending[j]
        for i in range(j + 1, HIST):
            pending[i] = pending[i] + net * s_bar(j, i)
        change_mix.append((-step_length) * (-scaling * first[j] * theta[j]))
        step_mix.append((-step_length) * (net - scaling * first[j] * rest[j]))

    wide = lambda value: jnp.broadcast_to(value, (8, LANES))
    mix = [wide(value) for value in mix]
    chem, gain = wide(chem), wide((-step_length) * scaling)
    step_mix = [wide(value) for value in step_mix]
    change_mix = [wide(value) for value in change_mix]
    basis = (v0, v1, v2, v3)

    @pl.loop(0, REACH)
    def _(i):
        for b in range(8):
            at = pl.ds(8 * b, 8)
            rho = density[i, at, :]
            lift = mix[0] * v0[i, at, :]
            for j in range(1, 4):
                lift = lift + mix[j] * basis[j][i, at, :]
            new_hartree[i, at, :] = hartree[i, at, :] + lift
            slope = grad[i, at, :] + 2.0 * rho * lift - chem * rho
            parts = [rho, gain * slope, step_mix[0] * steps[0, i, at, :], change_mix[0] * changes[0, i, at, :]]
            for f in range(1, HIST):
                parts[2] = parts[2] + step_mix[f] * steps[f, i, at, :]
                parts[3] = parts[3] + change_mix[f] * changes[f, i, at, :]
            new_density[i, at, :] = parts[0] + (parts[1] + (parts[2] + parts[3]))


def call(kernel, outs, args, scratch=(), flops=0):
    whole = pl.BlockSpec(memory_space=pltpu.VMEM)
    shapes = [jax.ShapeDtypeStruct(shape, jnp.float32) for shape in outs]
    size = sum(4 * math.prod(a.shape) for a in (*args, *shapes))
    return pl.pallas_call(
        kernel,
        out_shape=shapes,
        in_specs=[whole] * len(args),
        out_specs=[whole] * len(outs),
        scratch_shapes=[pltpu.VMEM(shape, jnp.float32) for shape in scratch],
        cost_estimate=pl.CostEstimate(flops=flops, bytes_accessed=size, transcendentals=0),
        compiler_params=pltpu.CompilerParams(vmem_limit_bytes=VMEM_LIMIT),
    )(*args)


def ring(axis, step):
    size = lax.axis_size(axis)
    return [(i, (i + step) % size) for i in range(size)]


def x_halo(block):
    return (lax.ppermute(block, "blk", ring("blk", 1)), lax.ppermute(block, "blk", ring("blk", -1)))


def z_halo(first, last):
    return (lax.ppermute(last, "gz", ring("gz", 1)), lax.ppermute(first, "gz", ring("gz", -1)))


def after(values, *earlier):
    return lax.optimization_barrier((tuple(values), earlier))[0]


def on_device(sqrt_density, ion_charge, ion_potential, hartree_prev, hist_steps, hist_changes):
    block = sqrt_density.shape
    ext = (block[0], block[1] + 16, block[2])
    face = (24, LANES)
    stencil_flops = 60 * math.prod(block)
    h_sides = x_halo(hartree_prev)
    faces = call(pack_kernel, [(48, LANES)] * 2, [hartree_prev, sqrt_density])
    h_ends = z_halo(*faces)
    (gram,) = call(gram_kernel, [(136, LANES)], [hist_steps, hist_changes], flops=272 * math.prod(block))
    h_sides = after(h_sides, gram)
    v0, first, last = call(
        residual_kernel,
        [block, face, face],
        [hartree_prev, *h_sides, *h_ends, sqrt_density, ion_charge],
        [ext],
        stencil_flops,
    )
    basis = [v0]
    dots, moments = [], []
    for n in range(3):
        halo = (*x_halo(basis[n]), *z_halo(first, last))
        prior = [basis[n - 1]] if n else []
        rows, moment = call(
            dots_kernel if n else first_dots_kernel,
            [(24, LANES), (8, LANES)],
            [*prior, basis[n], sqrt_density, hist_steps, hist_changes],
            flops=50 * math.prod(block),
        )
        dots.append(rows)
        moments.append(moment)
        done = [rows]
        if n == 1:
            rho_sides = x_halo(after([sqrt_density], v0)[0])
        if n == 2:
            grad, base = call(
                base_kernel,
                [block, (40, LANES)],
                [sqrt_density, *rho_sides, *h_ends, hartree_prev, ion_potential, hist_steps, hist_changes],
                [ext],
                2 * stencil_flops,
            )
            done.append(base)
        halo = after(halo, *done)
        fresh, first, last = call(
            functools.partial(basis_kernel, n > 0),
            [block, face, face],
            [basis[n], *halo, *prior],
            [ext],
            stencil_flops,
        )
        basis.append(fresh)
    halo = (*x_halo(basis[3]), *z_halo(first, last))
    (sums,) = call(
        last_dots_kernel,
        [(2, LANES)],
        [basis[2], basis[3], sqrt_density, hist_steps, hist_changes, gram, base, *dots, *moments],
        [(256, LANES), (24, LANES), (8, LANES)],
        50 * math.prod(block),
    )
    devices = lax.axis_size("blk") * lax.axis_size("gz")
    (outgoing,) = call(send_kernel, [(devices, 2, LANES)], [basis[3], *halo, sums], [ext], stencil_flops)
    received = lax.all_to_all(outgoing, ("blk", "gz"), 0, 0, tiled=True)
    return tuple(
        call(
            final_kernel,
            [block, block],
            [received, sqrt_density, hartree_prev, grad, *basis, hist_steps, hist_changes],
            [(384, LANES)],
            50 * math.prod(block),
        )
    )


def solution(mesh):
    placed = (
        P("blk", None, "gz"),
        P("blk", None, "gz"),
        P("blk", None, "gz"),
        P("blk", None, "gz"),
        P(None, "blk", None, "gz"),
        P(None, "blk", None, "gz"),
    )
    return jax.shard_map(
        on_device,
        mesh=mesh,
        in_specs=placed,
        out_specs=(P("blk", None, "gz"), P("blk", None, "gz")),
        check_vma=False,
    )
```

time: 2070 us -> 98.9 us (0.05)
  blocking collectives: 1790 us -> 26.9 us
  other arithmetic: 82 us -> 0 us
  local copies, waits for them, and re-layouts: 78.1 us -> 4.69 us
  between operations: 42.3 us -> 0.82 us
  waiting for transfers between devices: 31 us -> 2.48 us
    psum x24 -> x0, blocking collectives: 1790 us -> none  [the longest x8 590 us: on_device(): lax.psum(jnp.sum(damped_change * result), ('blk', 'gz'))]
    reduce_sum x26 -> x0, other arithmetic: 70.3 us -> none  [the longest x8 22.6 us: on_device(): jnp.sum(hist_steps[pair_idx] * search)]
    slice x102 -> x0, local copies, waits for them, and re-layouts: 48.5 us -> none  [the longest x72 26.2 us: rolled_sum(): jnp.roll(values, offset, grid_axis) + jnp.roll(values, -offset, grid_axis)]
    ppermute x24 -> x22, waiting for transfers between devices: 31 us -> 2.48 us  [the longest x6 2.28 us: x_halo(): lax.ppermute(block, 'blk', ring('blk', 1))]
    all_to_all x0 -> x1, blocking collectives: none -> 26.9 us  [on_device(): received = lax.all_to_all(outgoing, ('blk', 'gz'), 0, 0, tiled=True)]
    unnamed x106 -> x18, local copies, waits for them, and re-layouts: 29.6 us -> 4.69 us
    ppermute x24 -> x22, starting transfers between devices: 35.7 us -> 43.9 us  [the longest x6 29.7 us: x_halo(): lax.ppermute(block, 'blk', ring('blk', -1))]
  transfers between devices with their start and end apart: 24 -> 22, of which waited for: 14 -> 3; matrix products, arithmetic and copies ran while one was open for 4% -> 0% of each run, Pallas kernels for 0% -> 13%
where the time goes in v1:
time: 98.9 us; the launch traced here: 98.7 us
  starting transfers between devices  43.9 us (44%)
  blocking collectives  26.9 us (27%)
  Pallas kernels  19.9 us (20%)
  local copies, waits for them, and re-layouts  4.69 us (5%)
  waiting for transfers between devices  2.48 us (3%)
    ppermute x6, starting transfers between devices, x_halo(): lax.ppermute(block, 'blk', ring('blk', -1))  29.7 us
    all_to_all x1, blocking collectives, on_device(): received = lax.all_to_all(outgoing, ('blk', 'gz'), 0, 0, tiled=True)  26.9 us
    pallas_call x13, Pallas kernels, call(): pl.pallas_call(kernel, out_shape=shapes, in_specs=[whole] * len(args), ou...  19.9 us
    ppermute x5, starting transfers between devices, z_halo(): lax.ppermute(first, 'gz', ring('gz', -1))  12.5 us
    unnamed x18, local copies, waits for them, and re-layouts  4.69 us
    ppermute x6, waiting for transfers between devices, x_halo(): lax.ppermute(block, 'blk', ring('blk', 1))  2.28 us
  transfers between devices with their start and end apart: 22, of which 3 were waited for; matrix products, arithmetic and copies ran while one was open for 0% of the time, Pallas kernels for 13%

profile of v1, /device:TPU:1, one launch (start us, length us, event | category | flops | bytes accessed | tf_op | source)
XLA Modules:
  0.0 98.7 jit_solution(5834192165887677421)
XLA Ops:
  0.6 3.3 %collective-permute-start.1 = (f32[6,64,128]{2,1,0:T(8,128)}, f32[6,64,128]{2,1,0:T(8,128)S(1)}, u32[]{:S(2)}, u32[]{:S(2)}) collective-permute-start(f32[6,64,128]{2,1,0:T(8,128)} %hartree.7), channel_id=1, source_target_pairs={{0,252},{4,0},{8,4},{12,8},{16,12},{20,16},{24,20},{28,24},{32,28}... | collective-permute-start | bytes 589832 | tf_op jit(solution)/shard_map/ppermute | solution.py:514
  3.9 0.0 collective-permute-start
  4.0 0.9 copy-done.3
  4.9 0.9 copy-done.5
  5.8 0.2 shard_map.78
  6.1 0.8 collective-permute-start.2
  6.9 1.9 %collective-permute-start.3 = (f32[48,128]{1,0:T(8,128)S(1)}, f32[48,128]{1,0:T(8,128)S(1)}, u32[]{:S(2)}, u32[]{:S(2)}) collective-permute-start(f32[48,128]{1,0:T(8,128)S(1)} %get-tuple-element.42), channel_id=1, source_target_pairs={{0,3},{1,0},{2,1},{3,2},{4,7},{5,4},{6,5},{7,6},{8,11},{9,8},{10,9... | collective-permute-start | bytes 73736 | tf_op jit(solution)/shard_map/ppermute | solution.py:518
  8.8 1.4 %copy-done = f32[8,6,64,128]{3,2,1,0:T(8,128)S(1)} copy-done((f32[8,6,64,128]{3,2,1,0:T(8,128)S(1)}, f32[8,6,64,128]{3,2,1,0:T(8,128)}, u32[]{:S(2)}) %copy-start) | copy-done | bytes 1572888
  10.2 1.4 %copy-done.2 = f32[8,6,64,128]{3,2,1,0:T(8,128)S(1)} copy-done((f32[8,6,64,128]{3,2,1,0:T(8,128)S(1)}, f32[8,6,64,128]{3,2,1,0:T(8,128)}, u32[]{:S(2)}) %copy-start.2) | copy-done | bytes 1572888
  11.6 5.1 %shard_map.77.gram = f32[136,128]{1,0:T(8,128)S(1)} custom-call(f32[8,6,64,128]{3,2,1,0:T(8,128)S(1)} %copy-done, f32[8,6,64,128]{3,2,1,0:T(8,128)S(1)} %copy-done.2), custom_call_target="tpu_custom_call" | custom-call | flops 13369344 | bytes 3215360 | tf_op jit(solution)/shard_map/pallas_call | solution.py:497
  16.8 0.0 collective-permute-done.left
  16.8 0.0 collective-permute-done.2.z_left
  16.9 1.3 %shard_map.79 = (f32[6,64,128]{2,1,0:T(8,128)S(1)}, f32[24,128]{1,0:T(8,128)S(1)}, f32[24,128]{1,0:T(8,128)S(1)}) custom-call(f32[6,64,128]{2,1,0:T(8,128)S(1)} %copy-done.6, f32[6,64,128]{2,1,0:T(8,128)S(1)} %collective-permute-done.left, f32[6,64,128]{2,1,0:T(8,128)S(1)} %collective-permute-done.1.right, f32[48,128]{1,0:T(8,128)S(1)} %collective-permute-done.2.z_left, ...), custom_call_target="tpu_custom_call" | custom-call | flops 2949120 | bytes 1253376 | tf_op jit(solution)/shard_map/pallas_call | solution.py:497
  18.2 6.4 %collective-permute-start.5 = (f32[6,64,128]{2,1,0:T(8,128)S(1)}, f32[6,64,128]{2,1,0:T(8,128)S(1)}, u32[]{:S(2)}, u32[]{:S(2)}) collective-permute-start(f32[6,64,128]{2,1,0:T(8,128)S(1)} %get-tuple-element.43.vector.refs_0_.prior.refs_5_.v0), channel_id=1, source_target_pairs={{0,252},{4,0},{8,4},{12,8},{16,12},{20,16},{24,20},{28,24},{32,28}... | collective-permute-start | bytes 589832 | tf_op jit(solution)/shard_map/ppermute | solution.py:514
  24.6 0.0 collective-permute-start.4
  24.6 0.1 collective-permute-start.6
  24.7 2.6 %collective-permute-start.7 = (f32[24,128]{1,0:T(8,128)S(1)}, f32[24,128]{1,0:T(8,128)S(1)}, u32[]{:S(2)}, u32[]{:S(2)}) collective-permute-start(f32[24,128]{1,0:T(8,128)S(1)} %get-tuple-element.45), channel_id=1, source_target_pairs={{0,3},{1,0},{2,1},{3,2},{4,7},{5,4},{6,5},{7,6},{8,11},{9,8},{10,9... | collective-permute-start | bytes 36872 | tf_op jit(solution)/shard_map/ppermute | solution.py:518
  27.3 1.0 shard_map.80
  28.2 0.1 collective-permute-done.6.refs_3_
  28.4 0.0 collective-permute-done.7.refs_4_
  28.4 0.0 collective-permute-done.5.refs_2_
  28.4 1.8 %collective-permute-done.4.refs_1_ = f32[6,64,128]{2,1,0:T(8,128)S(1)} collective-permute-done((f32[6,64,128]{2,1,0:T(8,128)S(1)}, f32[6,64,128]{2,1,0:T(8,128)S(1)}, u32[]{:S(2)}, u32[]{:S(2)}) %collective-permute-start.4) | collective-permute-done | bytes 196640 | tf_op jit(solution)/shard_map/ppermute | solution.py:514
  30.2 1.3 %shard_map.81 = (f32[6,64,128]{2,1,0:T(8,128)S(1)}, f32[24,128]{1,0:T(8,128)S(1)}, f32[24,128]{1,0:T(8,128)S(1)}) custom-call(f32[6,64,128]{2,1,0:T(8,128)S(1)} %get-tuple-element.43.vector.refs_0_.prior.refs_5_.v0, f32[6,64,128]{2,1,0:T(8,128)S(1)} %collective-permute-done.4.refs_1_, f32[6,64,128]{2,1,0:T(8,128)S(1)} %collective-permute-done.5.refs_2_, ...), custom_call_target="tpu_custom_call" | custom-call | flops 2949120 | bytes 835584 | tf_op jit(solution)/shard_map/pallas_call | solution.py:497
  31.4 7.6 %collective-permute-start.9 = (f32[6,64,128]{2,1,0:T(8,128)S(1)}, f32[6,64,128]{2,1,0:T(8,128)S(1)}, u32[]{:S(2)}, u32[]{:S(2)}) collective-permute-start(f32[6,64,128]{2,1,0:T(8,128)S(1)} %get-tuple-element.51.vector.refs_0_.prior.refs_5_.v1), channel_id=1, source_target_pairs={{0,252},{4,0},{8,4},{12,8},{16,12},{20,16},{24,20},{28,24},{32,28}... | collective-permute-start | bytes 589832 | tf_op jit(solution)/shard_map/ppermute | solution.py:514
  39.0 0.0 collective-permute-start.8
  39.0 2.7 %collective-permute-start.11 = (f32[24,128]{1,0:T(8,128)S(1)}, f32[24,128]{1,0:T(8,128)S(1)}, u32[]{:S(2)}, u32[]{:S(2)}) collective-permute-start(f32[24,128]{1,0:T(8,128)S(1)} %get-tuple-element.53), channel_id=1, source_target_pairs={{0,3},{1,0},{2,1},{3,2},{4,7},{5,4},{6,5},{7,6},{8,11},{9,8},{10,9... | collective-permute-start | bytes 36872 | tf_op jit(solution)/shard_map/ppermute | solution.py:518
  41.7 1.1 %collective-permute-start.17 = (f32[6,64,128]{2,1,0:T(8,128)S(1)}, f32[6,64,128]{2,1,0:T(8,128)S(1)}, u32[]{:S(2)}, u32[]{:S(2)}) collective-permute-start(f32[6,64,128]{2,1,0:T(8,128)S(1)} %copy-done.4), channel_id=1, source_target_pairs={{0,252},{4,0},{8,4},{12,8},{16,12},{20,16},{24,20},{28,24},{32,28}... | collective-permute-start | bytes 589832 | tf_op jit(solution)/shard_map/ppermute | solution.py:514
  42.8 0.0 collective-permute-done.10.refs_3_
  42.8 0.7 collective-permute-start.16
  43.4 1.0 %shard_map.82 = (f32[24,128]{1,0:T(8,128)S(1)}, f32[8,128]{1,0:T(8,128)S(1)}) custom-call(f32[6,64,128]{2,1,0:T(8,128)S(1)} %get-tuple-element.43.vector.refs_0_.prior.refs_5_.v0, f32[6,64,128]{2,1,0:T(8,128)S(1)} %get-tuple-element.51.vector.refs_0_.prior.refs_5_.v1, f32[6,64,128]{2,1,0:T(8,128)S(1)} %copy-done.4, f32[8,6,64,128]{3,2,1,0:T(8,128)S(1)} %copy-done.1, ...), custom_call_target="tpu_custom_call" | custom-call | flops 2457600 | bytes 3751936 | tf_op jit(solution)/shard_map/pallas_call | solution.py:497
  44.4 0.0 collective-permute-done.11.refs_4_
  44.4 0.0 collective-permute-done.8.refs_1_
  44.5 1.3 %shard_map.83 = (f32[6,64,128]{2,1,0:T(8,128)S(1)}, f32[24,128]{1,0:T(8,128)S(1)}, f32[24,128]{1,0:T(8,128)S(1)}) custom-call(f32[6,64,128]{2,1,0:T(8,128)S(1)} %get-tuple-element.51.vector.refs_0_.prior.refs_5_.v1, f32[6,64,128]{2,1,0:T(8,128)S(1)} %collective-permute-done.8.refs_1_, f32[6,64,128]{2,1,0:T(8,128)S(1)} %collective-permute-done.9.refs_2_, ...), custom_call_target="tpu_custom_call" | custom-call | flops 2949120 | bytes 1032192 | tf_op jit(solution)/shard_map/pallas_call | solution.py:497
  45.7 3.8 %collective-permute-start.13 = (f32[6,64,128]{2,1,0:T(8,128)S(1)}, f32[6,64,128]{2,1,0:T(8,128)S(1)}, u32[]{:S(2)}, u32[]{:S(2)}) collective-permute-start(f32[6,64,128]{2,1,0:T(8,128)S(1)} %get-tuple-element.59.vector.refs_0_.prior.v2), channel_id=1, source_target_pairs={{0,252},{4,0},{8,4},{12,8},{16,12},{20,16},{24,20},{28,24},{32,28}... | collective-permute-start | bytes 589832 | tf_op jit(solution)/shard_map/ppermute | solution.py:514
  49.5 0.0 collective-permute-start.12
  49.5 0.0 collective-permute-start.14
  49.6 2.7 %collective-permute-start.15 = (f32[24,128]{1,0:T(8,128)S(1)}, f32[24,128]{1,0:T(8,128)S(1)}, u32[]{:S(2)}, u32[]{:S(2)}) collective-permute-start(f32[24,128]{1,0:T(8,128)S(1)} %get-tuple-element.61), channel_id=1, source_target_pairs={{0,3},{1,0},{2,1},{3,2},{4,7},{5,4},{6,5},{7,6},{8,11},{9,8},{10,9... | collective-permute-start | bytes 36872 | tf_op jit(solution)/shard_map/ppermute | solution.py:518
  52.2 1.8 %shard_map.85 = (f32[6,64,128]{2,1,0:T(8,128)S(1)}, f32[40,128]{1,0:T(8,128)S(1)}) custom-call(f32[6,64,128]{2,1,0:T(8,128)S(1)} %copy-done.4, f32[6,64,128]{2,1,0:T(8,128)S(1)} %collective-permute-done.16.left, f32[6,64,128]{2,1,0:T(8,128)S(1)} %collective-permute-done.17.right, f32[48,128]{1,0:T(8,128)S(1)} %collective-permute-done.2.z_left, ...), custom_call_target="tpu_custom_call" | custom-call | flops 5898240 | bytes 4395008 | tf_op jit(solution)/shard_map/pallas_call | solution.py:497
  54.1 1.0 %shard_map.84 = (f32[24,128]{1,0:T(8,128)S(1)}, f32[8,128]{1,0:T(8,128)S(1)}) custom-call(f32[6,64,128]{2,1,0:T(8,128)S(1)} %get-tuple-element.51.vector.refs_0_.prior.refs_5_.v1, f32[6,64,128]{2,1,0:T(8,128)S(1)} %get-tuple-element.59.vector.refs_0_.prior.v2, f32[6,64,128]{2,1,0:T(8,128)S(1)} %copy-done.4, f32[8,6,64,128]{3,2,1,0:T(8,128)S(1)} %copy-done.1, ...), custom_call_target="tpu_custom_call" | custom-call | flops 2457600 | bytes 3751936 | tf_op jit(solution)/shard_map/pallas_call | solution.py:497
  55.1 0.5 collective-permute-done.12.refs_1_
  55.5 1.3 %shard_map.86 = (f32[6,64,128]{2,1,0:T(8,128)S(1)}, f32[24,128]{1,0:T(8,128)S(1)}, f32[24,128]{1,0:T(8,128)S(1)}) custom-call(f32[6,64,128]{2,1,0:T(8,128)S(1)} %get-tuple-element.59.vector.refs_0_.prior.v2, f32[6,64,128]{2,1,0:T(8,128)S(1)} %collective-permute-done.12.refs_1_, f32[6,64,128]{2,1,0:T(8,128)S(1)} %collective-permute-done.13.refs_2_, ...), custom_call_target="tpu_custom_call" | custom-call | flops 2949120 | bytes 1032192 | tf_op jit(solution)/shard_map/pallas_call | solution.py:497
  56.8 7.6 %collective-permute-start.19 = (f32[6,64,128]{2,1,0:T(8,128)S(1)}, f32[6,64,128]{2,1,0:T(8,128)S(1)}, u32[]{:S(2)}, u32[]{:S(2)}) collective-permute-start(f32[6,64,128]{2,1,0:T(8,128)S(1)} %get-tuple-element.69.vector.own.v3), channel_id=1, source_target_pairs={{0,252},{4,0},{8,4},{12,8},{16,12},{20,16},{24,20},{28,24},{32,28}... | collective-permute-start | bytes 589832 | tf_op jit(solution)/shard_map/ppermute | solution.py:514
  64.4 2.7 %collective-permute-start.21 = (f32[24,128]{1,0:T(8,128)S(1)}, f32[24,128]{1,0:T(8,128)S(1)}, u32[]{:S(2)}, u32[]{:S(2)}) collective-permute-start(f32[24,128]{1,0:T(8,128)S(1)} %get-tuple-element.71), channel_id=1, source_target_pairs={{0,3},{1,0},{2,1},{3,2},{4,7},{5,4},{6,5},{7,6},{8,11},{9,8},{10,9... | collective-permute-start | bytes 36872 | tf_op jit(solution)/shard_map/ppermute | solution.py:518
  67.0 1.0 %shard_map.87.sums = f32[2,128]{1,0:T(2,128)S(1)} custom-call(f32[6,64,128]{2,1,0:T(8,128)S(1)} %get-tuple-element.59.vector.refs_0_.prior.v2, f32[6,64,128]{2,1,0:T(8,128)S(1)} %get-tuple-element.69.vector.own.v3, f32[6,64,128]{2,1,0:T(8,128)S(1)} %copy-done.4, f32[8,6,64,128]{3,2,1,0:T(8,128)S(1)} %copy-done.1, f32[8,6,64,128]{3,2,1,0:T(8,128)S(1)} %copy-done.2, ...), custom_call_target="tpu_custom_call" | custom-call | flops 2457600 | bytes 3875840 | tf_op jit(solution)/shard_map/pallas_call | solution.py:497
  68.1 0.0 collective-permute-done.20.z_left
  68.1 1.7 %shard_map.88 = f32[256,2,128]{2,1,0:T(2,128)S(1)} custom-call(f32[6,64,128]{2,1,0:T(8,128)S(1)} %get-tuple-element.69.vector.own.v3, f32[6,64,128]{2,1,0:T(8,128)S(1)} %collective-permute-done.18.left, f32[6,64,128]{2,1,0:T(8,128)S(1)} %collective-permute-done.19.right, f32[24,128]{1,0:T(8,128)S(1)} %collective-permute-done.20.z_left, ...), custom_call_target="tpu_custom_call" | custom-call | flops 2949120 | bytes 877568 | tf_op jit(solution)/shard_map/pallas_call | solution.py:497
  69.9 26.9 %all_to_all.5.received = f32[256,2,128]{2,1,0:T(2,128)S(1)} all-to-all(f32[256,2,128]{2,1,0:T(2,128)S(1)} %shard_map.88), channel_id=1, replica_groups=mesh['blk'=64,'gz'=4] {'blk','gz'}, dimensions={0} | all-to-all | bytes 524288 | tf_op jit(solution)/shard_map/all_to_all | solution.py:586
  96.8 1.9 %shard_map.89 = (f32[6,64,128]{2,1,0:T(8,128)}, f32[6,64,128]{2,1,0:T(8,128)}) custom-call(f32[256,2,128]{2,1,0:T(2,128)S(1)} %all_to_all.5.received, f32[6,64,128]{2,1,0:T(8,128)S(1)} %copy-done.4, f32[6,64,128]{2,1,0:T(8,128)S(1)} %copy-done.6, f32[6,64,128]{2,1,0:T(8,128)S(1)} %get-tuple-element.75.grad, ...), custom_call_target="tpu_custom_call" | custom-call | flops 2457600 | bytes 5177344 | tf_op jit(solution)/shard_map/pallas_call | solution.py:497
  (28 shorter events, 0.1 us)
Async XLA Ops:
  0.6 16.2 %collective-permute-start.1 = (f32[6,64,128]{2,1,0:T(8,128)}, f32[6,64,128]{2,1,0:T(8,128)S(1)}, u32[]{:S(2)}, u32[]{:S(2)}) collective-permute-start(f32[6,64,128]{2,1,0:T(8,128)} %hartree.7), channel_id=1, source_target_pairs={{0,252},{4,0},{8,4},{12,8},{16,12},{20,16},{24,20},{28,24},{32,28}... | collective-permute-start | bytes 589832 | tf_op jit(solution)/shard_map/ppermute | solution.py:514
  3.9 12.9 %collective-permute-start = (f32[6,64,128]{2,1,0:T(8,128)}, f32[6,64,128]{2,1,0:T(8,128)S(1)}, u32[]{:S(2)}, u32[]{:S(2)}) collective-permute-start(f32[6,64,128]{2,1,0:T(8,128)} %hartree.7), channel_id=1, source_target_pairs={{0,4},{4,8},{8,12},{12,16},{16,20},{20,24},{24,28},{28,32},{32,36}... | collective-permute-start | bytes 589832 | tf_op jit(solution)/shard_map/ppermute | solution.py:514
  4.0 0.9 copy-start.3
  4.9 0.9 copy-start.5
  6.1 10.7 %collective-permute-start.2 = (f32[48,128]{1,0:T(8,128)S(1)}, f32[48,128]{1,0:T(8,128)S(1)}, u32[]{:S(2)}, u32[]{:S(2)}) collective-permute-start(f32[48,128]{1,0:T(8,128)S(1)} %get-tuple-element.41), channel_id=1, source_target_pairs={{0,1},{1,2},{2,3},{3,0},{4,5},{5,6},{6,7},{7,4},{8,9},{9,10},{10,1... | collective-permute-start | bytes 73736 | tf_op jit(solution)/shard_map/ppermute | solution.py:518
  6.9 9.9 %collective-permute-start.3 = (f32[48,128]{1,0:T(8,128)S(1)}, f32[48,128]{1,0:T(8,128)S(1)}, u32[]{:S(2)}, u32[]{:S(2)}) collective-permute-start(f32[48,128]{1,0:T(8,128)S(1)} %get-tuple-element.42), channel_id=1, source_target_pairs={{0,3},{1,0},{2,1},{3,2},{4,7},{5,4},{6,5},{7,6},{8,11},{9,8},{10,9... | collective-permute-start | bytes 73736 | tf_op jit(solution)/shard_map/ppermute | solution.py:518
  8.8 1.4 %copy-start = (f32[8,6,64,128]{3,2,1,0:T(8,128)S(1)}, f32[8,6,64,128]{3,2,1,0:T(8,128)}, u32[]{:S(2)}) copy-start(f32[8,6,64,128]{3,2,1,0:T(8,128)} %steps.13) | copy-start | bytes 4718596
  10.2 1.4 %copy-start.2 = (f32[8,6,64,128]{3,2,1,0:T(8,128)S(1)}, f32[8,6,64,128]{3,2,1,0:T(8,128)}, u32[]{:S(2)}) copy-start(f32[8,6,64,128]{3,2,1,0:T(8,128)} %changes.13) | copy-start | bytes 4718596
  11.6 5.2 %copy-start.4 = (f32[6,64,128]{2,1,0:T(8,128)S(1)}, f32[6,64,128]{2,1,0:T(8,128)}, u32[]{:S(2)}) copy-start(f32[6,64,128]{2,1,0:T(8,128)} %density.15) | copy-start | bytes 589828
  11.6 5.2 %copy-start.6 = (f32[6,64,128]{2,1,0:T(8,128)S(1)}, f32[6,64,128]{2,1,0:T(8,128)}, u32[]{:S(2)}) copy-start(f32[6,64,128]{2,1,0:T(8,128)} %hartree.7) | copy-start | bytes 589828
  11.6 5.2 %copy-start.8 = (f32[6,64,128]{2,1,0:T(8,128)S(1)}, f32[6,64,128]{2,1,0:T(8,128)}, u32[]{:S(2)}) copy-start(f32[6,64,128]{2,1,0:T(8,128)} %charge.1) | copy-start | bytes 589828
  11.6 15.6 %copy-start.1 = (f32[8,6,64,128]{3,2,1,0:T(8,128)S(1)}, f32[8,6,64,128]{3,2,1,0:T(8,128)}, u32[]{:S(2)}) copy-start(f32[8,6,64,128]{3,2,1,0:T(8,128)} %steps.13) | copy-start | bytes 4718596
  18.2 10.2 %collective-permute-start.5 = (f32[6,64,128]{2,1,0:T(8,128)S(1)}, f32[6,64,128]{2,1,0:T(8,128)S(1)}, u32[]{:S(2)}, u32[]{:S(2)}) collective-permute-start(f32[6,64,128]{2,1,0:T(8,128)S(1)} %get-tuple-element.43.vector.refs_0_.prior.refs_5_.v0), channel_id=1, source_target_pairs={{0,252},{4,0},{8,4},{12,8},{16,12},{20,16},{24,20},{28,24},{32,28}... | collective-permute-start | bytes 589832 | tf_op jit(solution)/shard_map/ppermute | solution.py:514
  24.6 5.6 %collective-permute-start.4 = (f32[6,64,128]{2,1,0:T(8,128)S(1)}, f32[6,64,128]{2,1,0:T(8,128)S(1)}, u32[]{:S(2)}, u32[]{:S(2)}) collective-permute-start(f32[6,64,128]{2,1,0:T(8,128)S(1)} %get-tuple-element.43.vector.refs_0_.prior.refs_5_.v0), channel_id=1, source_target_pairs={{0,4},{4,8},{8,12},{12,16},{16,20},{20,24},{24,28},{28,32},{32,36}... | collective-permute-start | bytes 589832 | tf_op jit(solution)/shard_map/ppermute | solution.py:514
  24.6 3.8 %collective-permute-start.6 = (f32[24,128]{1,0:T(8,128)S(1)}, f32[24,128]{1,0:T(8,128)S(1)}, u32[]{:S(2)}, u32[]{:S(2)}) collective-permute-start(f32[24,128]{1,0:T(8,128)S(1)} %get-tuple-element.44), channel_id=1, source_target_pairs={{0,1},{1,2},{2,3},{3,0},{4,5},{5,6},{6,7},{7,4},{8,9},{9,10},{10,1... | collective-permute-start | bytes 36872 | tf_op jit(solution)/shard_map/ppermute | solution.py:518
  24.7 3.7 %collective-permute-start.7 = (f32[24,128]{1,0:T(8,128)S(1)}, f32[24,128]{1,0:T(8,128)S(1)}, u32[]{:S(2)}, u32[]{:S(2)}) collective-permute-start(f32[24,128]{1,0:T(8,128)S(1)} %get-tuple-element.45), channel_id=1, source_target_pairs={{0,3},{1,0},{2,1},{3,2},{4,7},{5,4},{6,5},{7,6},{8,11},{9,8},{10,9... | collective-permute-start | bytes 36872 | tf_op jit(solution)/shard_map/ppermute | solution.py:518
  31.4 13.0 %collective-permute-start.9 = (f32[6,64,128]{2,1,0:T(8,128)S(1)}, f32[6,64,128]{2,1,0:T(8,128)S(1)}, u32[]{:S(2)}, u32[]{:S(2)}) collective-permute-start(f32[6,64,128]{2,1,0:T(8,128)S(1)} %get-tuple-element.51.vector.refs_0_.prior.refs_5_.v1), channel_id=1, source_target_pairs={{0,252},{4,0},{8,4},{12,8},{16,12},{20,16},{24,20},{28,24},{32,28}... | collective-permute-start | bytes 589832 | tf_op jit(solution)/shard_map/ppermute | solution.py:514
  39.0 5.4 %collective-permute-start.8 = (f32[6,64,128]{2,1,0:T(8,128)S(1)}, f32[6,64,128]{2,1,0:T(8,128)S(1)}, u32[]{:S(2)}, u32[]{:S(2)}) collective-permute-start(f32[6,64,128]{2,1,0:T(8,128)S(1)} %get-tuple-element.51.vector.refs_0_.prior.refs_5_.v1), channel_id=1, source_target_pairs={{0,4},{4,8},{8,12},{12,16},{16,20},{20,24},{24,28},{28,32},{32,36}... | collective-permute-start | bytes 589832 | tf_op jit(solution)/shard_map/ppermute | solution.py:514
  39.0 3.8 %collective-permute-start.10 = (f32[24,128]{1,0:T(8,128)S(1)}, f32[24,128]{1,0:T(8,128)S(1)}, u32[]{:S(2)}, u32[]{:S(2)}) collective-permute-start(f32[24,128]{1,0:T(8,128)S(1)} %get-tuple-element.52), channel_id=1, source_target_pairs={{0,1},{1,2},{2,3},{3,0},{4,5},{5,6},{6,7},{7,4},{8,9},{9,10},{10,1... | collective-permute-start | bytes 36872 | tf_op jit(solution)/shard_map/ppermute | solution.py:518
  39.0 13.2 %copy-start.7 = (f32[6,64,128]{2,1,0:T(8,128)S(1)}, f32[6,64,128]{2,1,0:T(8,128)}, u32[]{:S(2)}) copy-start(f32[6,64,128]{2,1,0:T(8,128)} %potential.1) | copy-start | bytes 589828
  39.0 5.4 %collective-permute-start.11 = (f32[24,128]{1,0:T(8,128)S(1)}, f32[24,128]{1,0:T(8,128)S(1)}, u32[]{:S(2)}, u32[]{:S(2)}) collective-permute-start(f32[24,128]{1,0:T(8,128)S(1)} %get-tuple-element.53), channel_id=1, source_target_pairs={{0,3},{1,0},{2,1},{3,2},{4,7},{5,4},{6,5},{7,6},{8,11},{9,8},{10,9... | collective-permute-start | bytes 36872 | tf_op jit(solution)/shard_map/ppermute | solution.py:518
  41.7 7.9 %collective-permute-start.17 = (f32[6,64,128]{2,1,0:T(8,128)S(1)}, f32[6,64,128]{2,1,0:T(8,128)S(1)}, u32[]{:S(2)}, u32[]{:S(2)}) collective-permute-start(f32[6,64,128]{2,1,0:T(8,128)S(1)} %copy-done.4), channel_id=1, source_target_pairs={{0,252},{4,0},{8,4},{12,8},{16,12},{20,16},{24,20},{28,24},{32,28}... | collective-permute-start | bytes 589832 | tf_op jit(solution)/shard_map/ppermute | solution.py:514
  42.8 9.5 %collective-permute-start.16 = (f32[6,64,128]{2,1,0:T(8,128)S(1)}, f32[6,64,128]{2,1,0:T(8,128)S(1)}, u32[]{:S(2)}, u32[]{:S(2)}) collective-permute-start(f32[6,64,128]{2,1,0:T(8,128)S(1)} %copy-done.4), channel_id=1, source_target_pairs={{0,4},{4,8},{8,12},{12,16},{16,20},{20,24},{24,28},{28,32},{32,36}... | collective-permute-start | bytes 589832 | tf_op jit(solution)/shard_map/ppermute | solution.py:514
  45.7 9.4 %collective-permute-start.13 = (f32[6,64,128]{2,1,0:T(8,128)S(1)}, f32[6,64,128]{2,1,0:T(8,128)S(1)}, u32[]{:S(2)}, u32[]{:S(2)}) collective-permute-start(f32[6,64,128]{2,1,0:T(8,128)S(1)} %get-tuple-element.59.vector.refs_0_.prior.v2), channel_id=1, source_target_pairs={{0,252},{4,0},{8,4},{12,8},{16,12},{20,16},{24,20},{28,24},{32,28}... | collective-permute-start | bytes 589832 | tf_op jit(solution)/shard_map/ppermute | solution.py:514
  49.5 6.0 %collective-permute-start.12 = (f32[6,64,128]{2,1,0:T(8,128)S(1)}, f32[6,64,128]{2,1,0:T(8,128)S(1)}, u32[]{:S(2)}, u32[]{:S(2)}) collective-permute-start(f32[6,64,128]{2,1,0:T(8,128)S(1)} %get-tuple-element.59.vector.refs_0_.prior.v2), channel_id=1, source_target_pairs={{0,4},{4,8},{8,12},{12,16},{16,20},{20,24},{24,28},{28,32},{32,36}... | collective-permute-start | bytes 589832 | tf_op jit(solution)/shard_map/ppermute | solution.py:514
  49.5 5.5 %collective-permute-start.14 = (f32[24,128]{1,0:T(8,128)S(1)}, f32[24,128]{1,0:T(8,128)S(1)}, u32[]{:S(2)}, u32[]{:S(2)}) collective-permute-start(f32[24,128]{1,0:T(8,128)S(1)} %get-tuple-element.60), channel_id=1, source_target_pairs={{0,1},{1,2},{2,3},{3,0},{4,5},{5,6},{6,7},{7,4},{8,9},{9,10},{10,1... | collective-permute-start | bytes 36872 | tf_op jit(solution)/shard_map/ppermute | solution.py:518
  49.6 5.5 %collective-permute-start.15 = (f32[24,128]{1,0:T(8,128)S(1)}, f32[24,128]{1,0:T(8,128)S(1)}, u32[]{:S(2)}, u32[]{:S(2)}) collective-permute-start(f32[24,128]{1,0:T(8,128)S(1)} %get-tuple-element.61), channel_id=1, source_target_pairs={{0,3},{1,0},{2,1},{3,2},{4,7},{5,4},{6,5},{7,6},{8,11},{9,8},{10,9... | collective-permute-start | bytes 36872 | tf_op jit(solution)/shard_map/ppermute | solution.py:518
  56.8 11.3 %collective-permute-start.19 = (f32[6,64,128]{2,1,0:T(8,128)S(1)}, f32[6,64,128]{2,1,0:T(8,128)S(1)}, u32[]{:S(2)}, u32[]{:S(2)}) collective-permute-start(f32[6,64,128]{2,1,0:T(8,128)S(1)} %get-tuple-element.69.vector.own.v3), channel_id=1, source_target_pairs={{0,252},{4,0},{8,4},{12,8},{16,12},{20,16},{24,20},{28,24},{32,28}... | collective-permute-start | bytes 589832 | tf_op jit(solution)/shard_map/ppermute | solution.py:514
  64.4 3.8 %collective-permute-start.18 = (f32[6,64,128]{2,1,0:T(8,128)S(1)}, f32[6,64,128]{2,1,0:T(8,128)S(1)}, u32[]{:S(2)}, u32[]{:S(2)}) collective-permute-start(f32[6,64,128]{2,1,0:T(8,128)S(1)} %get-tuple-element.69.vector.own.v3), channel_id=1, source_target_pairs={{0,4},{4,8},{8,12},{12,16},{16,20},{20,24},{24,28},{28,32},{32,36}... | collective-permute-start | bytes 589832 | tf_op jit(solution)/shard_map/ppermute | solution.py:514
  64.4 3.8 %collective-permute-start.20 = (f32[24,128]{1,0:T(8,128)S(1)}, f32[24,128]{1,0:T(8,128)S(1)}, u32[]{:S(2)}, u32[]{:S(2)}) collective-permute-start(f32[24,128]{1,0:T(8,128)S(1)} %get-tuple-element.70), channel_id=1, source_target_pairs={{0,1},{1,2},{2,3},{3,0},{4,5},{5,6},{6,7},{7,4},{8,9},{9,10},{10,1... | collective-permute-start | bytes 36872 | tf_op jit(solution)/shard_map/ppermute | solution.py:518
  64.4 3.8 %collective-permute-start.21 = (f32[24,128]{1,0:T(8,128)S(1)}, f32[24,128]{1,0:T(8,128)S(1)}, u32[]{:S(2)}, u32[]{:S(2)}) collective-permute-start(f32[24,128]{1,0:T(8,128)S(1)} %get-tuple-element.71), channel_id=1, source_target_pairs={{0,3},{1,0},{2,1},{3,2},{4,7},{5,4},{6,5},{7,6},{8,11},{9,8},{10,9... | collective-permute-start | bytes 36872 | tf_op jit(solution)/shard_map/ppermute | solution.py:518

commit v2 on v1

--- a/solution.py
+++ b/solution.py
@@ -88,35 +88,54 @@
     return lax.broadcasted_iota(jnp.int32, shape, len(shape) - 1)
 
 
-def stencil_plane(i, own, left, right, ext, z_left, z_right):
-    def layer(k):
-        if k < 0:
-            return left[k + REACH]
-        if k >= REACH:
-            return right[k - REACH]
-        return own[k]
-
+def inner_plane(i, own, ext):
     values = own[i]
     rows = values.shape[0]
     lane = lane_ids((rows, LANES))
-    tile_lane = lane_ids((8, LANES))
-    from_right = z_right[8 * (i // 2) : 8 * (i // 2) + 8, :]
-    from_left = z_left[8 * (i // 2) : 8 * (i // 2) + 8, :]
-    wraps = []
-    for b in range(rows // 8):
-        j = 8 * (i % 2) + b
-        upper = pltpu.roll(from_right, (LANES - 8 * j) % LANES, 1)
-        lower = pltpu.roll(from_left, (2 * LANES - 8 * j - 8) % LANES, 1)
-        wraps.append(jnp.where(tile_lane < 64, upper, lower))
-    wrap = jnp.concatenate(wraps, axis=0)
     total = (3.0 * center) * values
     for k, weight in enumerate(coeffs, 1):
-        pair = layer(i + k) + layer(i - k)
-        pair = pair + (ext[i, 8 + k : 8 + k + rows, :] + ext[i, 8 - k : 8 - k + rows, :])
-        up = pltpu.roll(jnp.where(lane < k, wrap, values), LANES - k, 1)
-        down = pltpu.roll(jnp.where(lane >= LANES - k, wrap, values), k, 1)
+        pair = ext[i, 8 + k : 8 + k + rows, :] + ext[i, 8 - k : 8 - k + rows, :]
+        if i + k < REACH:
+            pair = pair + own[i + k]
+        if i - k >= 0:
+            pair = pair + own[i - k]
+        up = pltpu.roll(jnp.where(lane < k, 0.0, values), LANES - k, 1)
+        down = pltpu.roll(jnp.where(lane >= LANES - k, 0.0, values), k, 1)
         total = total + weight * (pair + (up + down))
     return total, values
+
+
+def edge_faces(z_left, z_right):
+    lane = lane_ids((24, LANES)) % 8
+    lower = jnp.zeros((24, LANES), jnp.float32)
+    upper = jnp.zeros((24, LANES), jnp.float32)
+    for k, weight in enumerate(coeffs, 1):
+        lower = lower + jnp.where(lane < k, weight * pltpu.roll(z_left, LANES - 8 + k, 1), 0.0)
+        if z_right is not None:
+            upper = upper + jnp.where(lane >= 8 - k, weight * pltpu.roll(z_right, 8 - k, 1), 0.0)
+    return lower, upper
+
+
+def edge_plane(i, left, right, faces):
+    total = None
+    for k, weight in enumerate(coeffs, 1):
+        terms = []
+        if i - k < 0:
+            terms.append(left[i - k + REACH])
+        if right is not None and i + k >= REACH:
+            terms.append(right[i + k - REACH])
+        for term in terms:
+            total = weight * term if total is None else total + weight * term
+    lane = lane_ids((8, LANES))
+    lower, upper = (face[8 * (i // 2) : 8 * (i // 2) + 8] for face in faces)
+    tiles = []
+    for b in range(total.shape[0] // 8):
+        j = 8 * (i % 2) + b
+        tile = jnp.where(lane < 8, pltpu.roll(lower, (LANES - 8 * j) % LANES, 1), 0.0)
+        if right is not None:
+            tile = jnp.where(lane >= LANES - 8, pltpu.roll(upper, (2 * LANES - 8 - 8 * j) % LANES, 1), tile)
+        tiles.append(tile)
+    return total + jnp.concatenate(tiles, axis=0)
 
 
 def fill_ext(own, ext):
@@ -179,55 +198,62 @@
     return jnp.sum(acc, axis=0, keepdims=True)
 
 
-def pack_kernel(hartree, density, first, last):
-    pack_faces(hartree, first, last, 0)
-    pack_faces(density, first, last, 24)
-
-
-def residual_kernel(hartree, left, right, z_left, z_right, density, charge, out, first, last, ext):
+def pack_kernel(block, first, last):
+    pack_faces(block, first, last, 0)
+
+
+def inner_residual_kernel(hartree, density, charge, out, ext):
     fill_ext(hartree, ext)
     for i in range(REACH):
-        lap, values = stencil_plane(i, hartree, left, right, ext, z_left, z_right)
+        lap, values = inner_plane(i, hartree, ext)
         rho = density[i]
         out[i] = source_scale * (rho * rho - charge[i]) - (screen * values - lap)
-    pack_faces(out, first, last, 0)
-
-
-def basis_kernel(has_prior, *refs):
-    if has_prior:
-        own, left, right, z_left, z_right, prior, out, first, last, ext = refs
-    else:
-        own, left, right, z_left, z_right, out, first, last, ext = refs
+
+
+def inner_basis_kernel(has_prior, *refs):
+    own, prior, out, ext = refs if has_prior else (refs[0], None, *refs[1:])
     fill_ext(own, ext)
     for i in range(REACH):
-        lap, values = stencil_plane(i, own, left, right, ext, z_left, z_right)
+        lap, values = inner_plane(i, own, ext)
         moved = (screen / SHIFT - 1.0) * values - (1.0 / SHIFT) * lap
         out[i] = 2.0 * moved - prior[i] if has_prior else moved
+
+
+def edge_kernel(gain, inner, left, right, z_left, z_right, *rest):
+    *extra, out, first, last = rest
+    for ref, more in zip((first, last), extra):
+        ref[24:48, :] = more[...]
+    faces = edge_faces(z_left[0:24, :], z_right[0:24, :])
+    for i in range(REACH):
+        out[i] = inner[i] + gain * edge_plane(i, left, right, faces)
     pack_faces(out, first, last, 0)
 
 
-def gram_kernel(steps, changes, rows):
+def gram_kernel(work, steps, changes, rows):
     zero = jnp.zeros((8, LANES), jnp.float32)
 
     def run(base, left, right, pairs):
-        def body(n, accs):
-            i, b = n // 8, n % 8
-            at = pl.ds(pl.multiple_of(8 * b, 8), 8)
-            l_need = sorted({p for p, _ in pairs})
-            r_need = sorted({q for _, q in pairs})
-            l_tiles = {p: left[p, i, at, :] for p in l_need}
-            r_tiles = l_tiles if left is right else {}
-            r_tiles = {q: r_tiles[q] if q in r_tiles else right[q, i, at, :] for q in r_need}
-            return tuple(acc + l_tiles[p] * r_tiles[q] for acc, (p, q) in zip(accs, pairs))
-
-        accs = lax.fori_loop(0, 48, body, tuple(zero for _ in pairs))
+        def body(i, accs):
+            for b in range(8):
+                at = pl.ds(8 * b, 8)
+                l_tiles = {p: left[p, i, at, :] for p in sorted({p for p, _ in pairs})}
+                if left is right:
+                    r_tiles = l_tiles
+                else:
+                    r_tiles = {q: right[q, i, at, :] for q in sorted({q for _, q in pairs})}
+                accs = tuple(acc + l_tiles[p] * r_tiles[q] for acc, (p, q) in zip(accs, pairs))
+            return accs
+
+        accs = lax.fori_loop(0, REACH, body, tuple(zero for _ in pairs))
         for n, acc in enumerate(accs):
             rows[base + n : base + n + 1, :] = collapse(acc)
 
-    run(0, steps, steps, PAIRS)
-    run(36, changes, changes, PAIRS)
-    run(72, steps, changes, tuple((i, j) for i in range(4) for j in range(8)))
-    run(104, steps, changes, tuple((i, j) for i in range(4, 8) for j in range(8)))
+    if work == "same":
+        run(0, steps, steps, PAIRS)
+        run(36, changes, changes, PAIRS)
+    else:
+        run(0, steps, changes, tuple((i, j) for i in range(4) for j in range(8)))
+        run(32, steps, changes, tuple((i, j) for i in range(4, 8) for j in range(8)))
 
 
 def field_dots(steps, changes, others):
@@ -262,8 +288,10 @@
 
 def base_kernel(density, left, right, z_left, z_right, hartree, potential, steps, changes, grad, rows, ext):
     fill_ext(density, ext)
+    faces = edge_faces(z_left[24:48, :], z_right[24:48, :])
     for i in range(REACH):
-        lap, rho = stencil_plane(i, density, left, right, ext, z_left.at[24:48], z_right.at[24:48])
+        lap, rho = inner_plane(i, density, ext)
+        lap = lap + edge_plane(i, left, right, faces)
         power = jnp.exp(jnp.log(rho) * (4.0 / 3.0))
         grad[i] = 2.0 * rho * (hartree[i] + potential[i] + tf_scale * power) - lap * (
             1.0 / (spacing * spacing)
@@ -300,11 +328,12 @@
 
 
 def last_dots_kernel(
-    prior, vector, density, steps, changes, gram, base, d0, d1, d2, m0, m1, m2, out, rows, own_rows, moments
+    prior, vector, density, steps, changes, same, cross, base, d0, d1, d2, m0, m1, m2, out, rows, own_rows, moments
 ):
     basis_dots(vector, density, steps, changes, own_rows)
     store_moments([(prior, vector), (vector, vector)], moments)
-    rows[ROW_GRAM : ROW_GRAM + 136, :] = gram[0:136, :]
+    rows[ROW_GRAM : ROW_GRAM + 72, :] = same[...]
+    rows[ROW_GRAM + 72 : ROW_GRAM + 136, :] = cross[...]
     rows[ROW_BASE : ROW_BASE + 34, :] = base[0:34, :]
     for n, d in enumerate((d0, d1, d2, own_rows)):
         rows[ROW_W + 17 * n : ROW_W + 17 * n + 17, :] = d[0:17, :]
@@ -320,17 +349,32 @@
     out[1:2, :] = second
 
 
-def send_kernel(own, left, right, z_left, z_right, sums, out, ext):
+def inner_moment_kernel(own, out, ext):
     fill_ext(own, ext)
     zero = jnp.zeros((8, LANES), jnp.float32)
     accs = [(zero, zero) for _ in range(2)]
     for i in range(REACH):
-        lap, values = stencil_plane(i, own, left, right, ext, z_left, z_right)
+        lap, values = inner_plane(i, own, ext)
         product = values * ((screen / SHIFT - 1.0) * values - (1.0 / SHIFT) * lap)
         for b in range(8):
             accs[b % 2] = add_tile(accs[b % 2], product[8 * b : 8 * b + 8])
     hi, err = two_sum(accs[0][0], accs[1][0])
     hi, lo = exact_total(hi, accs[0][1] + accs[1][1] + err)
+    out[0:1, :] = hi
+    out[1:2, :] = lo
+
+
+def send_kernel(own, left, z_left, inner, sums, out):
+    faces = edge_faces(z_left[...], None)
+    zero = jnp.zeros((8, LANES), jnp.float32)
+    accs = [(zero, zero) for _ in range(2)]
+    for i in range(REACH):
+        product = own[i] * edge_plane(i, left, None, faces)
+        for b in range(8):
+            accs[b % 2] = add_tile(accs[b % 2], product[8 * b : 8 * b + 8])
+    hi, err = two_sum(accs[0][0], accs[1][0])
+    coupling = exact_total(hi, accs[0][1] + accs[1][1] + err)
+    hi, lo = df_add(df_scale(coupling, -2.0 / SHIFT), (inner[0:1, :], inner[1:2, :]))
     lane = lane_ids((1, LANES))
     at = ROW_MOM - 128
     second = jnp.where(lane == at + 7, hi, jnp.where(lane == at + 15, lo, sums[1:2, :]))
@@ -527,62 +571,74 @@
     ext = (block[0], block[1] + 16, block[2])
     face = (24, LANES)
     stencil_flops = 60 * math.prod(block)
+    cells = math.prod(block)
+    history = [hist_steps, hist_changes]
     h_sides = x_halo(hartree_prev)
-    faces = call(pack_kernel, [(48, LANES)] * 2, [hartree_prev, sqrt_density])
-    h_ends = z_halo(*faces)
-    (gram,) = call(gram_kernel, [(136, LANES)], [hist_steps, hist_changes], flops=272 * math.prod(block))
-    h_sides = after(h_sides, gram)
-    v0, first, last = call(
-        residual_kernel,
-        [block, face, face],
-        [hartree_prev, *h_sides, *h_ends, sqrt_density, ion_charge],
-        [ext],
-        stencil_flops,
+    h_ends = z_halo(*call(pack_kernel, [face, face], [hartree_prev]))
+    rho_sides = x_halo(sqrt_density)
+    rho_faces = call(pack_kernel, [face, face], [sqrt_density])
+    (inner,) = call(inner_residual_kernel, [block], [hartree_prev, sqrt_density, ion_charge], [ext], stencil_flops)
+    halo = after((*h_sides, *h_ends), *rho_sides, inner)
+    v0, *faces = call(
+        functools.partial(edge_kernel, 1.0),
+        [block, (48, LANES), (48, LANES)],
+        [inner, *halo, *rho_faces],
+        flops=stencil_flops,
     )
     basis = [v0]
     dots, moments = [], []
     for n in range(3):
-        halo = (*x_halo(basis[n]), *z_halo(first, last))
+        halo = (*x_halo(basis[n]), *z_halo(*faces))
         prior = [basis[n - 1]] if n else []
+        (inner,) = call(
+            functools.partial(inner_basis_kernel, n > 0), [block], [basis[n], *prior], [ext], stencil_flops
+        )
         rows, moment = call(
             dots_kernel if n else first_dots_kernel,
             [(24, LANES), (8, LANES)],
-            [*prior, basis[n], sqrt_density, hist_steps, hist_changes],
-            flops=50 * math.prod(block),
+            [*prior, basis[n], sqrt_density, *history],
+            flops=50 * cells,
         )
         dots.append(rows)
         moments.append(moment)
-        done = [rows]
+        done = [inner, rows]
+        if n == 0:
+            (same,) = call(functools.partial(gram_kernel, "same"), [(72, LANES)], history, flops=144 * cells)
+            done.append(same)
+            rho_ends = halo[2:]
         if n == 1:
-            rho_sides = x_halo(after([sqrt_density], v0)[0])
+            (cross,) = call(functools.partial(gram_kernel, "cross"), [(64, LANES)], history, flops=128 * cells)
+            done.append(cross)
         if n == 2:
             grad, base = call(
                 base_kernel,
                 [block, (40, LANES)],
-                [sqrt_density, *rho_sides, *h_ends, hartree_prev, ion_potential, hist_steps, hist_changes],
+                [sqrt_density, *rho_sides, *rho_ends, hartree_prev, ion_potential, *history],
                 [ext],
                 2 * stencil_flops,
             )
             done.append(base)
         halo = after(halo, *done)
-        fresh, first, last = call(
-            functools.partial(basis_kernel, n > 0),
+        fresh, *faces = call(
+            functools.partial(edge_kernel, -2.0 / SHIFT if n else -1.0 / SHIFT),
             [block, face, face],
-            [basis[n], *halo, *prior],
-            [ext],
-            stencil_flops,
+            [inner, *halo],
+            flops=stencil_flops,
         )
         basis.append(fresh)
-    halo = (*x_halo(basis[3]), *z_halo(first, last))
+    left = lax.ppermute(basis[3], "blk", ring("blk", 1))
+    z_left = lax.ppermute(faces[1], "gz", ring("gz", 1))
+    (inner,) = call(inner_moment_kernel, [(8, LANES)], [basis[3]], [ext], stencil_flops)
     (sums,) = call(
         last_dots_kernel,
         [(2, LANES)],
-        [basis[2], basis[3], sqrt_density, hist_steps, hist_changes, gram, base, *dots, *moments],
+        [basis[2], basis[3], sqrt_density, *history, same, cross, base, *dots, *moments],
         [(256, LANES), (24, LANES), (8, LANES)],
-        50 * math.prod(block),
+        50 * cells,
     )
+    left, z_left = after((left, z_left), inner, sums)
     devices = lax.axis_size("blk") * lax.axis_size("gz")
-    (outgoing,) = call(send_kernel, [(devices, 2, LANES)], [basis[3], *halo, sums], [ext], stencil_flops)
+    (outgoing,) = call(send_kernel, [(devices, 2, LANES)], [basis[3], left, z_left, inner, sums], flops=stencil_flops)
     received = lax.all_to_all(outgoing, ("blk", "gz"), 0, 0, tiled=True)
     return tuple(
         call(

time: 98.9 us -> 96 us (0.971)
  starting transfers between devices: 43.9 us -> 38.3 us
  waiting for transfers between devices: 2.48 us -> 5.8 us
  Pallas kernels: 19.9 us -> 16.7 us
  local copies, waits for them, and re-layouts: 4.69 us -> 6.35 us
    ppermute x0 -> x2, waiting for transfers between devices: none -> 3.23 us  [the longest x1 1.79 us: on_device(): left = lax.ppermute(basis[3], 'blk', ring('blk', 1))]
    pallas_call x13 -> x20, Pallas kernels: 19.9 us -> 16.7 us  [call(): pl.pallas_call(kernel, out_shape=shapes, in_specs=[whole] * len(args), ou...]
    ppermute x5 -> x4, starting transfers between devices: 12.5 us -> 9.48 us  [z_halo(): lax.ppermute(first, 'gz', ring('gz', -1))]
    ppermute x5 -> x4, waiting for transfers between devices: 0.16 us -> 2.53 us  [z_halo(): lax.ppermute(last, 'gz', ring('gz', 1))]
    ppermute x6 -> x5, starting transfers between devices: 29.7 us -> 27.4 us  [x_halo(): lax.ppermute(block, 'blk', ring('blk', -1))]
    ppermute x6 -> x5, waiting for transfers between devices: 2.28 us -> 0.01 us  [x_halo(): lax.ppermute(block, 'blk', ring('blk', 1))]
    unnamed x18 -> x22, local copies, waits for them, and re-layouts: 4.69 us -> 6.35 us
  transfers between devices with their start and end apart: 22 -> 20, of which waited for: 3 -> 3; matrix products, arithmetic and copies ran while one was open for 0% -> 0% of each run, Pallas kernels for 13% -> 13%
where the time goes in v2:
time: 96 us; the launch traced here: 95.7 us
  starting transfers between devices  38.3 us (40%)
  blocking collectives  27.6 us (29%)
  Pallas kernels  16.7 us (17%)
  local copies, waits for them, and re-layouts  6.35 us (7%)
  waiting for transfers between devices  5.8 us (6%)
    all_to_all x1, blocking collectives, on_device(): received = lax.all_to_all(outgoing, ('blk', 'gz'), 0, 0, tiled=True)  27.6 us
    ppermute x5, starting transfers between devices, x_halo(): lax.ppermute(block, 'blk', ring('blk', -1))  27.4 us
    pallas_call x20, Pallas kernels, call(): pl.pallas_call(kernel, out_shape=shapes, in_specs=[whole] * len(args), ou...  16.7 us
    ppermute x4, starting transfers between devices, z_halo(): lax.ppermute(first, 'gz', ring('gz', -1))  9.48 us
    unnamed x22, local copies, waits for them, and re-layouts  6.35 us
    ppermute x4, waiting for transfers between devices, z_halo(): lax.ppermute(last, 'gz', ring('gz', 1))  2.53 us
  transfers between devices with their start and end apart: 20, of which 3 were waited for; matrix products, arithmetic and copies ran while one was open for 0% of the time, Pallas kernels for 13%

profile of v2, /device:TPU:1, one launch (start us, length us, event | category | flops | bytes accessed | tf_op | source)
XLA Modules:
  0.0 95.7 jit_solution(4372224710492230738)
XLA Ops:
  0.6 3.3 %collective-permute-start.1 = (f32[6,64,128]{2,1,0:T(8,128)}, f32[6,64,128]{2,1,0:T(8,128)S(1)}, u32[]{:S(2)}, u32[]{:S(2)}) collective-permute-start(f32[6,64,128]{2,1,0:T(8,128)} %hartree.5), channel_id=1, source_target_pairs={{0,252},{4,0},{8,4},{12,8},{16,12},{20,16},{24,20},{28,24},{32,28}... | collective-permute-start | bytes 589832 | tf_op jit(solution)/shard_map/ppermute | solution.py:558
  4.0 5.8 %collective-permute-start.5 = (f32[6,64,128]{2,1,0:T(8,128)}, f32[6,64,128]{2,1,0:T(8,128)S(1)}, u32[]{:S(2)}, u32[]{:S(2)}) collective-permute-start(f32[6,64,128]{2,1,0:T(8,128)} %density.13), channel_id=1, source_target_pairs={{0,252},{4,0},{8,4},{12,8},{16,12},{20,16},{24,20},{28,24},{32,28}... | collective-permute-start | bytes 589832 | tf_op jit(solution)/shard_map/ppermute | solution.py:558
  9.7 0.0 collective-permute-start.4
  9.7 0.9 copy-done.6
  10.6 0.2 shard_map.78
  10.8 1.4 %collective-permute-start.2 = (f32[24,128]{1,0:T(8,128)S(1)}, f32[24,128]{1,0:T(8,128)S(1)}, u32[]{:S(2)}, u32[]{:S(2)}) collective-permute-start(f32[24,128]{1,0:T(8,128)S(1)} %get-tuple-element.43), channel_id=1, source_target_pairs={{0,1},{1,2},{2,3},{3,0},{4,5},{5,6},{6,7},{7,4},{8,9},{9,10},{10,1... | collective-permute-start | bytes 36872 | tf_op jit(solution)/shard_map/ppermute | solution.py:562
  12.2 2.5 %collective-permute-done.2.z_left = f32[24,128]{1,0:T(8,128)S(1)} collective-permute-done((f32[24,128]{1,0:T(8,128)S(1)}, f32[24,128]{1,0:T(8,128)S(1)}, u32[]{:S(2)}, u32[]{:S(2)}) %collective-permute-start.2) | collective-permute-done | bytes 12320 | tf_op jit(solution)/shard_map/ppermute | solution.py:562
  14.7 1.5 %collective-permute-start.3 = (f32[24,128]{1,0:T(8,128)S(1)}, f32[24,128]{1,0:T(8,128)S(1)}, u32[]{:S(2)}, u32[]{:S(2)}) collective-permute-start(f32[24,128]{1,0:T(8,128)S(1)} %get-tuple-element.44), channel_id=1, source_target_pairs={{0,3},{1,0},{2,1},{3,2},{4,7},{5,4},{6,5},{7,6},{8,11},{9,8},{10,9... | collective-permute-start | bytes 36872 | tf_op jit(solution)/shard_map/ppermute | solution.py:562
  16.2 0.9 copy-done.3
  17.1 0.2 shard_map.79
  17.3 0.0 copy-start.4
  17.3 0.9 copy-done.4
  18.2 0.9 copy-done.7
  19.1 0.9 copy-done.10
  20.0 0.7 shard_map.77.inner
  20.8 0.0 collective-permute-done.1.right
  20.8 0.0 collective-permute-done.left
  20.8 0.4 shard_map.80
  21.2 6.6 %collective-permute-start.7 = (f32[6,64,128]{2,1,0:T(8,128)S(1)}, f32[6,64,128]{2,1,0:T(8,128)S(1)}, u32[]{:S(2)}, u32[]{:S(2)}) collective-permute-start(f32[6,64,128]{2,1,0:T(8,128)S(1)} %get-tuple-element.51.refs_0_.vector.refs_1_.prior.v0), channel_id=1, source_target_pairs={{0,252},{4,0},{8,4},{12,8},{16,12},{20,16},{24,20},{28,24},{32,28}... | collective-permute-start | bytes 589832 | tf_op jit(solution)/shard_map/ppermute | solution.py:558
  27.8 2.7 %collective-permute-start.9 = (f32[48,128]{1,0:T(8,128)S(1)}, f32[48,128]{1,0:T(8,128)S(1)}, u32[]{:S(2)}, u32[]{:S(2)}) collective-permute-start(f32[48,128]{1,0:T(8,128)S(1)} %get-tuple-element.53), channel_id=1, source_target_pairs={{0,3},{1,0},{2,1},{3,2},{4,7},{5,4},{6,5},{7,6},{8,11},{9,8},{10,9... | collective-permute-start | bytes 73736 | tf_op jit(solution)/shard_map/ppermute | solution.py:562
  30.4 1.4 %copy-done.1 = f32[8,6,64,128]{3,2,1,0:T(8,128)S(1)} copy-done((f32[8,6,64,128]{3,2,1,0:T(8,128)S(1)}, f32[8,6,64,128]{3,2,1,0:T(8,128)}, u32[]{:S(2)}) %copy-start.1) | copy-done | bytes 1572888
  31.8 1.1 %shard_map.83.same = f32[72,128]{1,0:T(8,128)S(1)} custom-call(f32[8,6,64,128]{3,2,1,0:T(8,128)S(1)} %copy-done, f32[8,6,64,128]{3,2,1,0:T(8,128)S(1)} %copy-done.1), custom_call_target="tpu_custom_call" | custom-call | flops 7077888 | bytes 3182592 | tf_op jit(solution)/shard_map/pallas_call | solution.py:541
  33.0 0.3 copy-done.2
  33.2 1.0 shard_map.82
  34.2 0.7 shard_map.81.inner
  35.0 0.4 shard_map.84
  35.3 4.9 %collective-permute-start.11 = (f32[6,64,128]{2,1,0:T(8,128)S(1)}, f32[6,64,128]{2,1,0:T(8,128)S(1)}, u32[]{:S(2)}, u32[]{:S(2)}) collective-permute-start(f32[6,64,128]{2,1,0:T(8,128)S(1)} %get-tuple-element.59.refs_0_.vector.refs_1_.prior.v1), channel_id=1, source_target_pairs={{0,252},{4,0},{8,4},{12,8},{16,12},{20,16},{24,20},{28,24},{32,28}... | collective-permute-start | bytes 589832 | tf_op jit(solution)/shard_map/ppermute | solution.py:558
  40.2 0.0 collective-permute-start.12
  40.2 2.7 %collective-permute-start.13 = (f32[24,128]{1,0:T(8,128)S(1)}, f32[24,128]{1,0:T(8,128)S(1)}, u32[]{:S(2)}, u32[]{:S(2)}) collective-permute-start(f32[24,128]{1,0:T(8,128)S(1)} %get-tuple-element.61), channel_id=1, source_target_pairs={{0,3},{1,0},{2,1},{3,2},{4,7},{5,4},{6,5},{7,6},{8,11},{9,8},{10,9... | collective-permute-start | bytes 36872 | tf_op jit(solution)/shard_map/ppermute | solution.py:562
  42.9 1.0 %shard_map.87.cross = f32[64,128]{1,0:T(8,128)S(1)} custom-call(f32[8,6,64,128]{3,2,1,0:T(8,128)S(1)} %copy-done, f32[8,6,64,128]{3,2,1,0:T(8,128)S(1)} %copy-done.2), custom_call_target="tpu_custom_call" | custom-call | flops 6291456 | bytes 3178496 | tf_op jit(solution)/shard_map/pallas_call | solution.py:541
  43.9 0.0 copy-start.8
  43.9 0.0 copy-start.9
  44.0 1.0 %shard_map.86 = (f32[24,128]{1,0:T(8,128)S(1)}, f32[8,128]{1,0:T(8,128)S(1)}) custom-call(f32[6,64,128]{2,1,0:T(8,128)S(1)} %get-tuple-element.51.refs_0_.vector.refs_1_.prior.v0, f32[6,64,128]{2,1,0:T(8,128)S(1)} %get-tuple-element.59.refs_0_.vector.refs_1_.prior.v1, f32[6,64,128]{2,1,0:T(8,128)S(1)} %copy-done.5, f32[8,6,64,128]{3,2,1,0:T(8,128)S(1)} %copy-done, ...), custom_call_target="tpu_custom_call" | custom-call | flops 2457600 | bytes 3751936 | tf_op jit(solution)/shard_map/pallas_call | solution.py:541
  45.0 0.7 shard_map.85.inner
  45.7 0.4 shard_map.88
  46.1 6.9 %collective-permute-start.15 = (f32[6,64,128]{2,1,0:T(8,128)S(1)}, f32[6,64,128]{2,1,0:T(8,128)S(1)}, u32[]{:S(2)}, u32[]{:S(2)}) collective-permute-start(f32[6,64,128]{2,1,0:T(8,128)S(1)} %get-tuple-element.67.refs_0_.vector.prior.v2), channel_id=1, source_target_pairs={{0,252},{4,0},{8,4},{12,8},{16,12},{20,16},{24,20},{28,24},{32,28}... | collective-permute-start | bytes 589832 | tf_op jit(solution)/shard_map/ppermute | solution.py:558
  53.0 2.7 %collective-permute-start.17 = (f32[24,128]{1,0:T(8,128)S(1)}, f32[24,128]{1,0:T(8,128)S(1)}, u32[]{:S(2)}, u32[]{:S(2)}) collective-permute-start(f32[24,128]{1,0:T(8,128)S(1)} %get-tuple-element.69), channel_id=1, source_target_pairs={{0,3},{1,0},{2,1},{3,2},{4,7},{5,4},{6,5},{7,6},{8,11},{9,8},{10,9... | collective-permute-start | bytes 36872 | tf_op jit(solution)/shard_map/ppermute | solution.py:562
  55.6 1.5 %shard_map.91 = (f32[6,64,128]{2,1,0:T(8,128)S(1)}, f32[40,128]{1,0:T(8,128)S(1)}) custom-call(f32[6,64,128]{2,1,0:T(8,128)S(1)} %copy-done.5, f32[6,64,128]{2,1,0:T(8,128)S(1)} %collective-permute-done.4.left, f32[6,64,128]{2,1,0:T(8,128)S(1)} %collective-permute-done.5.right, f32[48,128]{1,0:T(8,128)S(1)} %collective-permute-done.8.z_left, ...), custom_call_target="tpu_custom_call" | custom-call | flops 5898240 | bytes 4395008 | tf_op jit(solution)/shard_map/pallas_call | solution.py:541
  57.1 1.0 %shard_map.90 = (f32[24,128]{1,0:T(8,128)S(1)}, f32[8,128]{1,0:T(8,128)S(1)}) custom-call(f32[6,64,128]{2,1,0:T(8,128)S(1)} %get-tuple-element.59.refs_0_.vector.refs_1_.prior.v1, f32[6,64,128]{2,1,0:T(8,128)S(1)} %get-tuple-element.67.refs_0_.vector.prior.v2, f32[6,64,128]{2,1,0:T(8,128)S(1)} %copy-done.5, f32[8,6,64,128]{3,2,1,0:T(8,128)S(1)} %copy-done, ...), custom_call_target="tpu_custom_call" | custom-call | flops 2457600 | bytes 3751936 | tf_op jit(solution)/shard_map/pallas_call | solution.py:541
  58.1 0.7 shard_map.89.inner
  58.9 1.0 %shard_map.92 = (f32[6,64,128]{2,1,0:T(8,128)S(1)}, f32[24,128]{1,0:T(8,128)}, f32[24,128]{1,0:T(8,128)S(1)}) custom-call(f32[6,64,128]{2,1,0:T(8,128)S(1)} %shard_map.89.inner, f32[6,64,128]{2,1,0:T(8,128)S(1)} %collective-permute-done.14.left, f32[6,64,128]{2,1,0:T(8,128)S(1)} %collective-permute-done.15.right, ...), custom_call_target="tpu_custom_call" | custom-call | flops 2949120 | bytes 835584 | tf_op jit(solution)/shard_map/pallas_call | solution.py:541
  59.8 1.0 %shard_map.94.sums = f32[2,128]{1,0:T(2,128)S(1)} custom-call(f32[6,64,128]{2,1,0:T(8,128)S(1)} %get-tuple-element.67.refs_0_.vector.prior.v2, f32[6,64,128]{2,1,0:T(8,128)S(1)} %get-tuple-element.76.own.vector.v3, f32[6,64,128]{2,1,0:T(8,128)S(1)} %copy-done.5, f32[8,6,64,128]{3,2,1,0:T(8,128)S(1)} %copy-done, f32[8,6,64,128]{3,2,1,0:T(8,128)S(1)} %copy-done.2, ...), custom_call_target="tpu_custom_call" | custom-call | flops 2457600 | bytes 3875840 | tf_op jit(solution)/shard_map/pallas_call | solution.py:541
  60.9 1.3 %shard_map.93.inner = f32[8,128]{1,0:T(8,128)S(1)} custom-call(f32[6,64,128]{2,1,0:T(8,128)S(1)} %get-tuple-element.76.own.vector.v3), custom_call_target="tpu_custom_call" | custom-call | flops 2949120 | bytes 200704 | tf_op jit(solution)/shard_map/pallas_call | solution.py:541
  62.2 1.4 %collective-permute-done.19.z_left = f32[24,128]{1,0:T(8,128)S(1)} collective-permute-done((f32[24,128]{1,0:T(8,128)S(1)}, f32[24,128]{1,0:T(8,128)S(1)}, u32[]{:S(2)}, u32[]{:S(2)}) %collective-permute-start.19) | collective-permute-done | bytes 12320 | tf_op jit(solution)/shard_map/ppermute | solution.py:630
  63.6 1.8 %collective-permute-done.18.left = f32[6,64,128]{2,1,0:T(8,128)S(1)} collective-permute-done((f32[6,64,128]{2,1,0:T(8,128)S(1)}, f32[6,64,128]{2,1,0:T(8,128)S(1)}, u32[]{:S(2)}, u32[]{:S(2)}) %collective-permute-start.18) | collective-permute-done | bytes 196640 | tf_op jit(solution)/shard_map/ppermute | solution.py:629
  65.4 0.8 shard_map.95
  66.2 27.6 %all_to_all.5.received = f32[256,2,128]{2,1,0:T(2,128)S(1)} all-to-all(f32[256,2,128]{2,1,0:T(2,128)S(1)} %shard_map.95), channel_id=1, replica_groups=mesh['blk'=64,'gz'=4] {'blk','gz'}, dimensions={0} | all-to-all | bytes 524288 | tf_op jit(solution)/shard_map/all_to_all | solution.py:642
  93.8 1.9 %shard_map.96 = (f32[6,64,128]{2,1,0:T(8,128)}, f32[6,64,128]{2,1,0:T(8,128)}) custom-call(f32[256,2,128]{2,1,0:T(2,128)S(1)} %all_to_all.5.received, f32[6,64,128]{2,1,0:T(8,128)S(1)} %copy-done.5, f32[6,64,128]{2,1,0:T(8,128)S(1)} %copy-done.8, f32[6,64,128]{2,1,0:T(8,128)S(1)} %get-tuple-element.83.grad, ...), custom_call_target="tpu_custom_call" | custom-call | flops 2457600 | bytes 5177344 | tf_op jit(solution)/shard_map/pallas_call | solution.py:541
  (35 shorter events, 0.1 us)
Async XLA Ops:
  0.6 29.8 %copy-start = (f32[8,6,64,128]{3,2,1,0:T(8,128)S(1)}, f32[8,6,64,128]{3,2,1,0:T(8,128)}, u32[]{:S(2)}) copy-start(f32[8,6,64,128]{3,2,1,0:T(8,128)} %steps.15) | copy-start | bytes 4718596
  0.6 20.1 %collective-permute-start.1 = (f32[6,64,128]{2,1,0:T(8,128)}, f32[6,64,128]{2,1,0:T(8,128)S(1)}, u32[]{:S(2)}, u32[]{:S(2)}) collective-permute-start(f32[6,64,128]{2,1,0:T(8,128)} %hartree.5), channel_id=1, source_target_pairs={{0,252},{4,0},{8,4},{12,8},{16,12},{20,16},{24,20},{28,24},{32,28}... | collective-permute-start | bytes 589832 | tf_op jit(solution)/shard_map/ppermute | solution.py:558
  4.0 16.8 %collective-permute-start = (f32[6,64,128]{2,1,0:T(8,128)}, f32[6,64,128]{2,1,0:T(8,128)S(1)}, u32[]{:S(2)}, u32[]{:S(2)}) collective-permute-start(f32[6,64,128]{2,1,0:T(8,128)} %hartree.5), channel_id=1, source_target_pairs={{0,4},{4,8},{8,12},{12,16},{16,20},{20,24},{24,28},{28,32},{32,36}... | collective-permute-start | bytes 589832 | tf_op jit(solution)/shard_map/ppermute | solution.py:558
  4.0 16.8 %collective-permute-start.5 = (f32[6,64,128]{2,1,0:T(8,128)}, f32[6,64,128]{2,1,0:T(8,128)S(1)}, u32[]{:S(2)}, u32[]{:S(2)}) collective-permute-start(f32[6,64,128]{2,1,0:T(8,128)} %density.13), channel_id=1, source_target_pairs={{0,252},{4,0},{8,4},{12,8},{16,12},{20,16},{24,20},{28,24},{32,28}... | collective-permute-start | bytes 589832 | tf_op jit(solution)/shard_map/ppermute | solution.py:558
  9.7 11.1 %collective-permute-start.4 = (f32[6,64,128]{2,1,0:T(8,128)}, f32[6,64,128]{2,1,0:T(8,128)S(1)}, u32[]{:S(2)}, u32[]{:S(2)}) collective-permute-start(f32[6,64,128]{2,1,0:T(8,128)} %density.13), channel_id=1, source_target_pairs={{0,4},{4,8},{8,12},{12,16},{16,20},{20,24},{24,28},{28,32},{32,36}... | collective-permute-start | bytes 589832 | tf_op jit(solution)/shard_map/ppermute | solution.py:558
  9.7 0.9 copy-start.6
  10.8 3.9 %collective-permute-start.2 = (f32[24,128]{1,0:T(8,128)S(1)}, f32[24,128]{1,0:T(8,128)S(1)}, u32[]{:S(2)}, u32[]{:S(2)}) collective-permute-start(f32[24,128]{1,0:T(8,128)S(1)} %get-tuple-element.43), channel_id=1, source_target_pairs={{0,1},{1,2},{2,3},{3,0},{4,5},{5,6},{6,7},{7,4},{8,9},{9,10},{10,1... | collective-permute-start | bytes 36872 | tf_op jit(solution)/shard_map/ppermute | solution.py:562
  14.7 6.1 %collective-permute-start.3 = (f32[24,128]{1,0:T(8,128)S(1)}, f32[24,128]{1,0:T(8,128)S(1)}, u32[]{:S(2)}, u32[]{:S(2)}) collective-permute-start(f32[24,128]{1,0:T(8,128)S(1)} %get-tuple-element.44), channel_id=1, source_target_pairs={{0,3},{1,0},{2,1},{3,2},{4,7},{5,4},{6,5},{7,6},{8,11},{9,8},{10,9... | collective-permute-start | bytes 36872 | tf_op jit(solution)/shard_map/ppermute | solution.py:562
  16.2 0.9 copy-start.3
  17.3 0.9 copy-start.4
  18.2 0.9 copy-start.7
  19.1 0.9 copy-start.10
  21.2 13.8 %collective-permute-start.7 = (f32[6,64,128]{2,1,0:T(8,128)S(1)}, f32[6,64,128]{2,1,0:T(8,128)S(1)}, u32[]{:S(2)}, u32[]{:S(2)}) collective-permute-start(f32[6,64,128]{2,1,0:T(8,128)S(1)} %get-tuple-element.51.refs_0_.vector.refs_1_.prior.v0), channel_id=1, source_target_pairs={{0,252},{4,0},{8,4},{12,8},{16,12},{20,16},{24,20},{28,24},{32,28}... | collective-permute-start | bytes 589832 | tf_op jit(solution)/shard_map/ppermute | solution.py:558
  27.7 7.2 %collective-permute-start.6 = (f32[6,64,128]{2,1,0:T(8,128)S(1)}, f32[6,64,128]{2,1,0:T(8,128)S(1)}, u32[]{:S(2)}, u32[]{:S(2)}) collective-permute-start(f32[6,64,128]{2,1,0:T(8,128)S(1)} %get-tuple-element.51.refs_0_.vector.refs_1_.prior.v0), channel_id=1, source_target_pairs={{0,4},{4,8},{8,12},{12,16},{16,20},{20,24},{24,28},{28,32},{32,36}... | collective-permute-start | bytes 589832 | tf_op jit(solution)/shard_map/ppermute | solution.py:558
  27.7 7.2 %collective-permute-start.8 = (f32[48,128]{1,0:T(8,128)S(1)}, f32[48,128]{1,0:T(8,128)S(1)}, u32[]{:S(2)}, u32[]{:S(2)}) collective-permute-start(f32[48,128]{1,0:T(8,128)S(1)} %get-tuple-element.52), channel_id=1, source_target_pairs={{0,1},{1,2},{2,3},{3,0},{4,5},{5,6},{6,7},{7,4},{8,9},{9,10},{10,1... | collective-permute-start | bytes 73736 | tf_op jit(solution)/shard_map/ppermute | solution.py:562
  27.8 7.2 %collective-permute-start.9 = (f32[48,128]{1,0:T(8,128)S(1)}, f32[48,128]{1,0:T(8,128)S(1)}, u32[]{:S(2)}, u32[]{:S(2)}) collective-permute-start(f32[48,128]{1,0:T(8,128)S(1)} %get-tuple-element.53), channel_id=1, source_target_pairs={{0,3},{1,0},{2,1},{3,2},{4,7},{5,4},{6,5},{7,6},{8,11},{9,8},{10,9... | collective-permute-start | bytes 73736 | tf_op jit(solution)/shard_map/ppermute | solution.py:562
  30.4 1.4 %copy-start.1 = (f32[8,6,64,128]{3,2,1,0:T(8,128)S(1)}, f32[8,6,64,128]{3,2,1,0:T(8,128)}, u32[]{:S(2)}) copy-start(f32[8,6,64,128]{3,2,1,0:T(8,128)} %changes.15) | copy-start | bytes 4718596
  31.8 1.4 %copy-start.2 = (f32[8,6,64,128]{3,2,1,0:T(8,128)S(1)}, f32[8,6,64,128]{3,2,1,0:T(8,128)}, u32[]{:S(2)}) copy-start(f32[8,6,64,128]{3,2,1,0:T(8,128)} %changes.15) | copy-start | bytes 4718596
  31.8 1.4 %copy-start.5 = (f32[6,64,128]{2,1,0:T(8,128)S(1)}, f32[6,64,128]{2,1,0:T(8,128)}, u32[]{:S(2)}) copy-start(f32[6,64,128]{2,1,0:T(8,128)} %density.13) | copy-start | bytes 589828
  35.3 10.4 %collective-permute-start.11 = (f32[6,64,128]{2,1,0:T(8,128)S(1)}, f32[6,64,128]{2,1,0:T(8,128)S(1)}, u32[]{:S(2)}, u32[]{:S(2)}) collective-permute-start(f32[6,64,128]{2,1,0:T(8,128)S(1)} %get-tuple-element.59.refs_0_.vector.refs_1_.prior.v1), channel_id=1, source_target_pairs={{0,252},{4,0},{8,4},{12,8},{16,12},{20,16},{24,20},{28,24},{32,28}... | collective-permute-start | bytes 589832 | tf_op jit(solution)/shard_map/ppermute | solution.py:558
  40.2 5.5 %collective-permute-start.10 = (f32[6,64,128]{2,1,0:T(8,128)S(1)}, f32[6,64,128]{2,1,0:T(8,128)S(1)}, u32[]{:S(2)}, u32[]{:S(2)}) collective-permute-start(f32[6,64,128]{2,1,0:T(8,128)S(1)} %get-tuple-element.59.refs_0_.vector.refs_1_.prior.v1), channel_id=1, source_target_pairs={{0,4},{4,8},{8,12},{12,16},{16,20},{20,24},{24,28},{28,32},{32,36}... | collective-permute-start | bytes 589832 | tf_op jit(solution)/shard_map/ppermute | solution.py:558
  40.2 5.4 %collective-permute-start.12 = (f32[24,128]{1,0:T(8,128)S(1)}, f32[24,128]{1,0:T(8,128)S(1)}, u32[]{:S(2)}, u32[]{:S(2)}) collective-permute-start(f32[24,128]{1,0:T(8,128)S(1)} %get-tuple-element.60), channel_id=1, source_target_pairs={{0,1},{1,2},{2,3},{3,0},{4,5},{5,6},{6,7},{7,4},{8,9},{9,10},{10,1... | collective-permute-start | bytes 36872 | tf_op jit(solution)/shard_map/ppermute | solution.py:562
  40.2 5.4 %collective-permute-start.13 = (f32[24,128]{1,0:T(8,128)S(1)}, f32[24,128]{1,0:T(8,128)S(1)}, u32[]{:S(2)}, u32[]{:S(2)}) collective-permute-start(f32[24,128]{1,0:T(8,128)S(1)} %get-tuple-element.61), channel_id=1, source_target_pairs={{0,3},{1,0},{2,1},{3,2},{4,7},{5,4},{6,5},{7,6},{8,11},{9,8},{10,9... | collective-permute-start | bytes 36872 | tf_op jit(solution)/shard_map/ppermute | solution.py:562
  43.9 11.7 %copy-start.8 = (f32[6,64,128]{2,1,0:T(8,128)S(1)}, f32[6,64,128]{2,1,0:T(8,128)}, u32[]{:S(2)}) copy-start(f32[6,64,128]{2,1,0:T(8,128)} %hartree.5) | copy-start | bytes 589828
  43.9 11.7 %copy-start.9 = (f32[6,64,128]{2,1,0:T(8,128)S(1)}, f32[6,64,128]{2,1,0:T(8,128)}, u32[]{:S(2)}) copy-start(f32[6,64,128]{2,1,0:T(8,128)} %potential.1) | copy-start | bytes 589828
  46.1 12.8 %collective-permute-start.15 = (f32[6,64,128]{2,1,0:T(8,128)S(1)}, f32[6,64,128]{2,1,0:T(8,128)S(1)}, u32[]{:S(2)}, u32[]{:S(2)}) collective-permute-start(f32[6,64,128]{2,1,0:T(8,128)S(1)} %get-tuple-element.67.refs_0_.vector.prior.v2), channel_id=1, source_target_pairs={{0,252},{4,0},{8,4},{12,8},{16,12},{20,16},{24,20},{28,24},{32,28}... | collective-permute-start | bytes 589832 | tf_op jit(solution)/shard_map/ppermute | solution.py:558
  52.9 5.9 %collective-permute-start.14 = (f32[6,64,128]{2,1,0:T(8,128)S(1)}, f32[6,64,128]{2,1,0:T(8,128)S(1)}, u32[]{:S(2)}, u32[]{:S(2)}) collective-permute-start(f32[6,64,128]{2,1,0:T(8,128)S(1)} %get-tuple-element.67.refs_0_.vector.prior.v2), channel_id=1, source_target_pairs={{0,4},{4,8},{8,12},{12,16},{16,20},{20,24},{24,28},{28,32},{32,36}... | collective-permute-start | bytes 589832 | tf_op jit(solution)/shard_map/ppermute | solution.py:558
  53.0 5.9 %collective-permute-start.16 = (f32[24,128]{1,0:T(8,128)S(1)}, f32[24,128]{1,0:T(8,128)S(1)}, u32[]{:S(2)}, u32[]{:S(2)}) collective-permute-start(f32[24,128]{1,0:T(8,128)S(1)} %get-tuple-element.68), channel_id=1, source_target_pairs={{0,1},{1,2},{2,3},{3,0},{4,5},{5,6},{6,7},{7,4},{8,9},{9,10},{10,1... | collective-permute-start | bytes 36872 | tf_op jit(solution)/shard_map/ppermute | solution.py:562
  53.0 5.9 %collective-permute-start.17 = (f32[24,128]{1,0:T(8,128)S(1)}, f32[24,128]{1,0:T(8,128)S(1)}, u32[]{:S(2)}, u32[]{:S(2)}) collective-permute-start(f32[24,128]{1,0:T(8,128)S(1)} %get-tuple-element.69), channel_id=1, source_target_pairs={{0,3},{1,0},{2,1},{3,2},{4,7},{5,4},{6,5},{7,6},{8,11},{9,8},{10,9... | collective-permute-start | bytes 36872 | tf_op jit(solution)/shard_map/ppermute | solution.py:562
  59.8 5.6 %collective-permute-start.18 = (f32[6,64,128]{2,1,0:T(8,128)S(1)}, f32[6,64,128]{2,1,0:T(8,128)S(1)}, u32[]{:S(2)}, u32[]{:S(2)}) collective-permute-start(f32[6,64,128]{2,1,0:T(8,128)S(1)} %get-tuple-element.76.own.vector.v3), channel_id=1, source_target_pairs={{0,4},{4,8},{8,12},{12,16},{16,20},{20,24},{24,28},{28,32},{32,36}... | collective-permute-start | bytes 589832 | tf_op jit(solution)/shard_map/ppermute | solution.py:629
  59.8 3.8 %collective-permute-start.19 = (f32[24,128]{1,0:T(8,128)S(1)}, f32[24,128]{1,0:T(8,128)S(1)}, u32[]{:S(2)}, u32[]{:S(2)}) collective-permute-start(f32[24,128]{1,0:T(8,128)S(1)} %get-tuple-element.77), channel_id=1, source_target_pairs={{0,1},{1,2},{2,3},{3,0},{4,5},{5,6},{6,7},{7,4},{8,9},{9,10},{10,1... | collective-permute-start | bytes 36872 | tf_op jit(solution)/shard_map/ppermute | solution.py:630

commit v3 on v2

--- a/solution.py
+++ b/solution.py
@@ -145,19 +145,47 @@
     ext[:, 8 + rows : 16 + rows, :] = own[:, 0:8, :]
 
 
-def pack_faces(src, first_ref, last_ref, base):
+def pack_faces(src, layers):
     lane = lane_ids((8, LANES))
+    firsts, lasts = [], []
     for m in range(3):
         first = jnp.zeros((8, LANES), jnp.float32)
         last = jnp.zeros((8, LANES), jnp.float32)
         for j in range(16):
             n = 16 * m + j
-            tile = src[n // 8, 8 * (n % 8) : 8 * (n % 8) + 8, :]
+            tile = src[layers + n // 8, 8 * (n % 8) : 8 * (n % 8) + 8, :]
             here = (lane >= 8 * j) & (lane < 8 * j + 8)
             first = jnp.where(here, pltpu.roll(tile, 8 * j, 1) if j else tile, first)
             last = jnp.where(here, pltpu.roll(tile, (8 * j + 8) % LANES, 1) if j < 15 else tile, last)
-        first_ref[base + 8 * m : base + 8 * m + 8, :] = first
-        last_ref[base + 8 * m : base + 8 * m + 8, :] = last
+        firsts.append(first)
+        lasts.append(last)
+    return jnp.concatenate(firsts, axis=0), jnp.concatenate(lasts, axis=0)
+
+
+def is_odd(axis):
+    return lax.rem(lax.axis_index(axis), 2) == 1
+
+
+def by_partner(lower, upper):
+    odd = is_odd("gz")
+    return jnp.where(odd, lower, upper), jnp.where(odd, upper, lower)
+
+
+def by_side(first, second):
+    odd = is_odd("gz")
+    return jnp.where(odd, first, second), jnp.where(odd, second, first)
+
+
+def with_sides(near, far, body):
+    odd = is_odd("blk")
+
+    @pl.when(odd)
+    def _():
+        body(near, far)
+
+    @pl.when(jnp.logical_not(odd))
+    def _():
+        body(far, near)
 
 
 def exact_total(hi, lo):
@@ -198,15 +226,25 @@
     return jnp.sum(acc, axis=0, keepdims=True)
 
 
-def pack_kernel(block, first, last):
-    pack_faces(block, first, last, 0)
-
-
-def inner_residual_kernel(hartree, density, charge, out, ext):
+def launch_kernel(hartree, density, both, face_a, face_b, sems):
+    copies = [
+        pltpu.make_async_copy(src, both.at[pl.ds(REACH * n, REACH)], sems.at[n])
+        for n, src in enumerate((hartree, density))
+    ]
+    for copy in copies:
+        copy.start()
+    for n, copy in enumerate(copies):
+        copy.wait()
+        rows = slice(24 * n, 24 * n + 24)
+        face_a[rows, :], face_b[rows, :] = by_partner(*pack_faces(both, REACH * n))
+
+
+def inner_residual_kernel(both, charge, out, ext):
+    hartree = both.at[pl.ds(0, REACH)]
     fill_ext(hartree, ext)
     for i in range(REACH):
         lap, values = inner_plane(i, hartree, ext)
-        rho = density[i]
+        rho = both[REACH + i]
         out[i] = source_scale * (rho * rho - charge[i]) - (screen * values - lap)
 
 
@@ -219,14 +257,16 @@
         out[i] = 2.0 * moved - prior[i] if has_prior else moved
 
 
-def edge_kernel(gain, inner, left, right, z_left, z_right, *rest):
-    *extra, out, first, last = rest
-    for ref, more in zip((first, last), extra):
-        ref[24:48, :] = more[...]
-    faces = edge_faces(z_left[0:24, :], z_right[0:24, :])
-    for i in range(REACH):
-        out[i] = inner[i] + gain * edge_plane(i, left, right, faces)
-    pack_faces(out, first, last, 0)
+def edge_kernel(gain, last, inner, near, far, z_first, z_second, out, face_a, face_b):
+    faces = edge_faces(*by_side(z_first[0:24, :], z_second[0:24, :]))
+
+    def body(left, right):
+        for i in range(REACH):
+            out[i] = inner[i] + gain * edge_plane(i, left, right, faces)
+
+    with_sides(near, far, body)
+    packed = pack_faces(out, 0)
+    face_a[...], face_b[...] = packed if last else by_partner(*packed)
 
 
 def gram_kernel(work, steps, changes, rows):
@@ -286,14 +326,21 @@
     return [collapse(acc) for acc in lax.fori_loop(0, REACH, body, tuple(zero for _ in pairs))]
 
 
-def base_kernel(density, left, right, z_left, z_right, hartree, potential, steps, changes, grad, rows, ext):
+def base_kernel(both, near, far, z_first, z_second, potential, steps, changes, grad, rows, ext):
+    hartree = both.at[pl.ds(0, REACH)]
+    density = both.at[pl.ds(REACH, REACH)]
     fill_ext(density, ext)
-    faces = edge_faces(z_left[24:48, :], z_right[24:48, :])
+    faces = edge_faces(*by_side(z_first[24:48, :], z_second[24:48, :]))
+
+    def body(left, right):
+        for i in range(REACH):
+            grad[i] = edge_plane(i, left, right, faces)
+
+    with_sides(near.at[pl.ds(REACH, REACH)], far.at[pl.ds(REACH, REACH)], body)
     for i in range(REACH):
         lap, rho = inner_plane(i, density, ext)
-        lap = lap + edge_plane(i, left, right, faces)
         power = jnp.exp(jnp.log(rho) * (4.0 / 3.0))
-        grad[i] = 2.0 * rho * (hartree[i] + potential[i] + tf_scale * power) - lap * (
+        grad[i] = 2.0 * rho * (hartree[i] + potential[i] + tf_scale * power) - (lap + grad[i]) * (
             1.0 / (spacing * spacing)
         )
     g_tile = lambda i, b: tile_of(grad, i, b)
@@ -534,16 +581,16 @@
             new_density[i, at, :] = parts[0] + (parts[1] + (parts[2] + parts[3]))
 
 
-def call(kernel, outs, args, scratch=(), flops=0):
+def call(kernel, outs, args, scratch=(), flops=0, place=pltpu.VMEM):
     whole = pl.BlockSpec(memory_space=pltpu.VMEM)
     shapes = [jax.ShapeDtypeStruct(shape, jnp.float32) for shape in outs]
     size = sum(4 * math.prod(a.shape) for a in (*args, *shapes))
     return pl.pallas_call(
         kernel,
         out_shape=shapes,
-        in_specs=[whole] * len(args),
+        in_specs=[pl.BlockSpec(memory_space=place)] * len(args),
         out_specs=[whole] * len(outs),
-        scratch_shapes=[pltpu.VMEM(shape, jnp.float32) for shape in scratch],
+        scratch_shapes=[pltpu.VMEM(s, jnp.float32) if isinstance(s, tuple) else s for s in scratch],
         cost_estimate=pl.CostEstimate(flops=flops, bytes_accessed=size, transcendentals=0),
         compiler_params=pltpu.CompilerParams(vmem_limit_bytes=VMEM_LIMIT),
     )(*args)
@@ -554,12 +601,18 @@
     return [(i, (i + step) % size) for i in range(size)]
 
 
+def swap(axis, odd_up):
+    size = lax.axis_size(axis)
+    return [(i, (i + (1 if i % 2 == odd_up else -1)) % size) for i in range(size)]
+
+
 def x_halo(block):
-    return (lax.ppermute(block, "blk", ring("blk", 1)), lax.ppermute(block, "blk", ring("blk", -1)))
-
-
-def z_halo(first, last):
-    return (lax.ppermute(last, "gz", ring("gz", 1)), lax.ppermute(first, "gz", ring("gz", -1)))
+    far = lax.ppermute(block, "blk", swap("blk", 1))
+    return (lax.ppermute(block, "blk", swap("blk", 0)), far)
+
+
+def z_halo(face_a, face_b):
+    return (lax.ppermute(face_a, "gz", swap("gz", 0)), lax.ppermute(face_b, "gz", swap("gz", 1)))
 
 
 def after(values, *earlier):
@@ -573,17 +626,18 @@
     stencil_flops = 60 * math.prod(block)
     cells = math.prod(block)
     history = [hist_steps, hist_changes]
-    h_sides = x_halo(hartree_prev)
-    h_ends = z_halo(*call(pack_kernel, [face, face], [hartree_prev]))
-    rho_sides = x_halo(sqrt_density)
-    rho_faces = call(pack_kernel, [face, face], [sqrt_density])
-    (inner,) = call(inner_residual_kernel, [block], [hartree_prev, sqrt_density, ion_charge], [ext], stencil_flops)
-    halo = after((*h_sides, *h_ends), *rho_sides, inner)
+    both, *faces = call(
+        launch_kernel,
+        [(2 * REACH, *block[1:]), (48, LANES), (48, LANES)],
+        [pltpu.with_memory_space_constraint(x, pltpu.HBM) for x in (hartree_prev, sqrt_density)],
+        [pltpu.SemaphoreType.DMA((2,))],
+        place=pltpu.HBM,
+    )
+    start = (*x_halo(both), *z_halo(*faces))
+    (inner,) = call(inner_residual_kernel, [block], [both, ion_charge], [ext], stencil_flops)
+    halo = after(start, inner)
     v0, *faces = call(
-        functools.partial(edge_kernel, 1.0),
-        [block, (48, LANES), (48, LANES)],
-        [inner, *halo, *rho_faces],
-        flops=stencil_flops,
+        functools.partial(edge_kernel, 1.0, False), [block, face, face], [inner, *halo], flops=stencil_flops
     )
     basis = [v0]
     dots, moments = [], []
@@ -605,7 +659,6 @@
         if n == 0:
             (same,) = call(functools.partial(gram_kernel, "same"), [(72, LANES)], history, flops=144 * cells)
             done.append(same)
-            rho_ends = halo[2:]
         if n == 1:
             (cross,) = call(functools.partial(gram_kernel, "cross"), [(64, LANES)], history, flops=128 * cells)
             done.append(cross)
@@ -613,14 +666,14 @@
             grad, base = call(
                 base_kernel,
                 [block, (40, LANES)],
-                [sqrt_density, *rho_sides, *rho_ends, hartree_prev, ion_potential, *history],
+                [both, *start, ion_potential, *history],
                 [ext],
                 2 * stencil_flops,
             )
             done.append(base)
         halo = after(halo, *done)
         fresh, *faces = call(
-            functools.partial(edge_kernel, -2.0 / SHIFT if n else -1.0 / SHIFT),
+            functools.partial(edge_kernel, -2.0 / SHIFT if n else -1.0 / SHIFT, n == 2),
             [block, face, face],
             [inner, *halo],
             flops=stencil_flops,

time: 96 us -> 80.9 us (0.84)
  starting transfers between devices: 38.3 us -> 30.9 us
  waiting for transfers between devices: 5.8 us -> 1.46 us
  local copies, waits for them, and re-layouts: 6.35 us -> 2.64 us
  Pallas kernels: 16.7 us -> 18.4 us
  blocking collectives: 27.6 us -> 26.5 us
    ppermute x18 -> x16, starting transfers between devices: 38.3 us -> 30.5 us  [the longest x4 14.8 us: x_halo(): return (lax.ppermute(block, 'blk', swap('blk', 0)), far)]
    unnamed x22 -> x14, local copies, waits for them, and re-layouts: 6.35 us -> 2.64 us
    ppermute x18 -> x16, waiting for transfers between devices: 2.57 us -> 0.37 us  [the longest x4 0.34 us: z_halo(): lax.ppermute(face_b, 'gz', swap('gz', 1))]
    ppermute x1, waiting for transfers between devices: 1.79 us -> 0.01 us  [on_device(): left = lax.ppermute(basis[3], 'blk', ring('blk', 1))]
    pallas_call x20 -> x19, Pallas kernels: 16.7 us -> 18.4 us  [call(): pl.pallas_call(kernel, out_shape=shapes, in_specs=[pl.BlockSpec(memory_sp...]
    all_to_all x1, blocking collectives: 27.6 us -> 26.5 us  [on_device(): received = lax.all_to_all(outgoing, ('blk', 'gz'), 0, 0, tiled=True)]
  transfers between devices with their start and end apart: 20 -> 18, of which waited for: 3 -> 2; matrix products, arithmetic and copies ran while one was open for 0% -> 0% of each run, Pallas kernels for 13% -> 15%
where the time goes in v3:
time: 80.9 us; the launch traced here: 80.7 us
  starting transfers between devices  30.9 us (38%)
  blocking collectives  26.5 us (33%)
  Pallas kernels  18.4 us (23%)
  local copies, waits for them, and re-layouts  2.64 us (3%)
  waiting for transfers between devices  1.46 us (2%)
  between operations  0.88 us (1%)
    all_to_all x1, blocking collectives, on_device(): received = lax.all_to_all(outgoing, ('blk', 'gz'), 0, 0, tiled=True)  26.5 us
    pallas_call x19, Pallas kernels, call(): pl.pallas_call(kernel, out_shape=shapes, in_specs=[pl.BlockSpec(memory_sp...  18.4 us
    ppermute x4, starting transfers between devices, x_halo(): return (lax.ppermute(block, 'blk', swap('blk', 0)), far)  14.8 us
    ppermute x4, starting transfers between devices, z_halo(): lax.ppermute(face_b, 'gz', swap('gz', 1))  7.6 us
    ppermute x4, starting transfers between devices, z_halo(): lax.ppermute(face_a, 'gz', swap('gz', 0))  4.48 us
    ppermute x4, starting transfers between devices, x_halo(): far = lax.ppermute(block, 'blk', swap('blk', 1))  3.6 us
    unnamed x14, local copies, waits for them, and re-layouts  2.64 us
  transfers between devices with their start and end apart: 18, of which 2 were waited for; matrix products, arithmetic and copies ran while one was open for 0% of the time, Pallas kernels for 15%

profile of v3, /device:TPU:1, one launch (start us, length us, event | category | flops | bytes accessed | tf_op | source)
XLA Modules:
  0.0 80.7 jit_solution(10545939620751353143)
XLA Ops:
  0.6 1.4 %shard_map.77 = (f32[12,64,128]{2,1,0:T(8,128)S(1)}, f32[48,128]{1,0:T(8,128)S(1)}, f32[48,128]{1,0:T(8,128)S(1)}) custom-call(f32[6,64,128]{2,1,0:T(8,128)} %hartree.3, f32[6,64,128]{2,1,0:T(8,128)} %density.11), custom_call_target="tpu_custom_call" | custom-call | bytes 835584 | tf_op jit(solution)/shard_map/pallas_call | solution.py:588
  2.0 2.7 %collective-permute-start.1 = (f32[12,64,128]{2,1,0:T(8,128)S(1)}, f32[12,64,128]{2,1,0:T(8,128)S(1)}, u32[]{:S(2)}, u32[]{:S(2)}) collective-permute-start(f32[12,64,128]{2,1,0:T(8,128)S(1)} %get-tuple-element.42.both), channel_id=1, source_target_pairs={{0,252},{4,8},{8,4},{12,16},{16,12},{20,24},{24,20},{28,32},{32,28... | collective-permute-start | bytes 1179656 | tf_op jit(solution)/shard_map/ppermute | solution.py:610
  4.7 6.4 %collective-permute-start = (f32[12,64,128]{2,1,0:T(8,128)S(1)}, f32[12,64,128]{2,1,0:T(8,128)S(1)}, u32[]{:S(2)}, u32[]{:S(2)}) collective-permute-start(f32[12,64,128]{2,1,0:T(8,128)S(1)} %get-tuple-element.42.both), channel_id=1, source_target_pairs={{0,4},{4,0},{8,12},{12,8},{16,20},{20,16},{24,28},{28,24},{32,36},... | collective-permute-start | bytes 1179656 | tf_op jit(solution)/shard_map/ppermute | solution.py:611
  11.1 1.3 %collective-permute-start.2 = (f32[48,128]{1,0:T(8,128)S(1)}, f32[48,128]{1,0:T(8,128)S(1)}, u32[]{:S(2)}, u32[]{:S(2)}) collective-permute-start(f32[48,128]{1,0:T(8,128)S(1)} %get-tuple-element.43), channel_id=1, source_target_pairs={{0,1},{1,0},{2,3},{3,2},{4,5},{5,4},{6,7},{7,6},{8,9},{9,8},{10,11... | collective-permute-start | bytes 73736 | tf_op jit(solution)/shard_map/ppermute | solution.py:615
  12.4 1.9 %collective-permute-start.3 = (f32[48,128]{1,0:T(8,128)S(1)}, f32[48,128]{1,0:T(8,128)S(1)}, u32[]{:S(2)}, u32[]{:S(2)}) collective-permute-start(f32[48,128]{1,0:T(8,128)S(1)} %get-tuple-element.44), channel_id=1, source_target_pairs={{0,3},{1,2},{2,1},{3,0},{4,7},{5,6},{6,5},{7,4},{8,11},{9,10},{10,... | collective-permute-start | bytes 73736 | tf_op jit(solution)/shard_map/ppermute | solution.py:615
  14.3 0.9 %copy-done.6 = f32[6,64,128]{2,1,0:T(8,128)S(1)} copy-done((f32[6,64,128]{2,1,0:T(8,128)S(1)}, f32[6,64,128]{2,1,0:T(8,128)}, u32[]{:S(2)}) %copy-start.6) | copy-done | bytes 196632
  15.2 0.7 shard_map.78.inner
  16.0 0.0 collective-permute-done.2.z_first
  16.0 0.3 collective-permute-done.3.z_second
  16.3 0.4 shard_map.79
  16.8 0.1 collective-permute-start.5
  16.9 5.3 %collective-permute-start.4 = (f32[6,64,128]{2,1,0:T(8,128)S(1)}, f32[6,64,128]{2,1,0:T(8,128)S(1)}, u32[]{:S(2)}, u32[]{:S(2)}) collective-permute-start(f32[6,64,128]{2,1,0:T(8,128)S(1)} %get-tuple-element.49.refs_0_.vector.refs_1_.prior.v0), channel_id=1, source_target_pairs={{0,4},{4,0},{8,12},{12,8},{16,20},{20,16},{24,28},{28,24},{32,36},... | collective-permute-start | bytes 589832 | tf_op jit(solution)/shard_map/ppermute | solution.py:611
  22.2 1.3 %collective-permute-start.6 = (f32[24,128]{1,0:T(8,128)S(1)}, f32[24,128]{1,0:T(8,128)S(1)}, u32[]{:S(2)}, u32[]{:S(2)}) collective-permute-start(f32[24,128]{1,0:T(8,128)S(1)} %get-tuple-element.50), channel_id=1, source_target_pairs={{0,1},{1,0},{2,3},{3,2},{4,5},{5,4},{6,7},{7,6},{8,9},{9,8},{10,11... | collective-permute-start | bytes 36872 | tf_op jit(solution)/shard_map/ppermute | solution.py:615
  23.5 1.9 %collective-permute-start.7 = (f32[24,128]{1,0:T(8,128)S(1)}, f32[24,128]{1,0:T(8,128)S(1)}, u32[]{:S(2)}, u32[]{:S(2)}) collective-permute-start(f32[24,128]{1,0:T(8,128)S(1)} %get-tuple-element.51), channel_id=1, source_target_pairs={{0,3},{1,2},{2,1},{3,0},{4,7},{5,6},{6,5},{7,4},{8,11},{9,10},{10,... | collective-permute-start | bytes 36872 | tf_op jit(solution)/shard_map/ppermute | solution.py:615
  25.4 1.4 %copy-done.1 = f32[8,6,64,128]{3,2,1,0:T(8,128)S(1)} copy-done((f32[8,6,64,128]{3,2,1,0:T(8,128)S(1)}, f32[8,6,64,128]{3,2,1,0:T(8,128)}, u32[]{:S(2)}) %copy-start.1) | copy-done | bytes 1572888
  26.8 1.1 %shard_map.82.same = f32[72,128]{1,0:T(8,128)S(1)} custom-call(f32[8,6,64,128]{3,2,1,0:T(8,128)S(1)} %copy-done, f32[8,6,64,128]{3,2,1,0:T(8,128)S(1)} %copy-done.1), custom_call_target="tpu_custom_call" | custom-call | flops 7077888 | bytes 3182592 | tf_op jit(solution)/shard_map/pallas_call | solution.py:588
  27.9 0.3 copy-done.2
  28.2 1.0 %shard_map.81 = (f32[24,128]{1,0:T(8,128)S(1)}, f32[8,128]{1,0:T(8,128)S(1)}) custom-call(f32[6,64,128]{2,1,0:T(8,128)S(1)} %get-tuple-element.49.refs_0_.vector.refs_1_.prior.v0, f32[6,64,128]{2,1,0:T(8,128)S(1)} %copy-done.3, f32[8,6,64,128]{3,2,1,0:T(8,128)S(1)} %copy-done, f32[8,6,64,128]{3,2,1,0:T(8,128)S(1)} %copy-done.2), custom_call_target="tpu_custom_call" | custom-call | flops 2457600 | bytes 3555328 | tf_op jit(solution)/shard_map/pallas_call | solution.py:588
  29.2 0.7 shard_map.80.inner
  29.9 0.0 collective-permute-done.6.z_first
  29.9 0.0 collective-permute-done.7.z_second
  29.9 0.5 shard_map.83
  30.4 0.1 collective-permute-start.9
  30.5 0.7 collective-permute-start.8
  31.1 1.3 %collective-permute-start.10 = (f32[24,128]{1,0:T(8,128)S(1)}, f32[24,128]{1,0:T(8,128)S(1)}, u32[]{:S(2)}, u32[]{:S(2)}) collective-permute-start(f32[24,128]{1,0:T(8,128)S(1)} %get-tuple-element.58), channel_id=1, source_target_pairs={{0,1},{1,0},{2,3},{3,2},{4,5},{5,4},{6,7},{7,6},{8,9},{9,8},{10,11... | collective-permute-start | bytes 36872 | tf_op jit(solution)/shard_map/ppermute | solution.py:615
  32.4 1.9 %collective-permute-start.11 = (f32[24,128]{1,0:T(8,128)S(1)}, f32[24,128]{1,0:T(8,128)S(1)}, u32[]{:S(2)}, u32[]{:S(2)}) collective-permute-start(f32[24,128]{1,0:T(8,128)S(1)} %get-tuple-element.59), channel_id=1, source_target_pairs={{0,3},{1,2},{2,1},{3,0},{4,7},{5,6},{6,5},{7,4},{8,11},{9,10},{10,... | collective-permute-start | bytes 36872 | tf_op jit(solution)/shard_map/ppermute | solution.py:615
  34.3 1.0 %shard_map.86.cross = f32[64,128]{1,0:T(8,128)S(1)} custom-call(f32[8,6,64,128]{3,2,1,0:T(8,128)S(1)} %copy-done, f32[8,6,64,128]{3,2,1,0:T(8,128)S(1)} %copy-done.2), custom_call_target="tpu_custom_call" | custom-call | flops 6291456 | bytes 3178496 | tf_op jit(solution)/shard_map/pallas_call | solution.py:588
  35.3 0.0 copy-start.5
  35.4 1.0 %shard_map.85 = (f32[24,128]{1,0:T(8,128)S(1)}, f32[8,128]{1,0:T(8,128)S(1)}) custom-call(f32[6,64,128]{2,1,0:T(8,128)S(1)} %get-tuple-element.49.refs_0_.vector.refs_1_.prior.v0, f32[6,64,128]{2,1,0:T(8,128)S(1)} %get-tuple-element.57.refs_0_.vector.refs_1_.prior.v1, f32[6,64,128]{2,1,0:T(8,128)S(1)} %copy-done.3, f32[8,6,64,128]{3,2,1,0:T(8,128)S(1)} %copy-done, ...), custom_call_target="tpu_custom_call" | custom-call | flops 2457600 | bytes 3751936 | tf_op jit(solution)/shard_map/pallas_call | solution.py:588
  36.4 0.7 shard_map.84.inner
  37.1 0.0 collective-permute-done.10.z_first
  37.1 0.0 collective-permute-done.11.z_second
  37.2 0.4 shard_map.87
  37.6 0.7 collective-permute-start.13
  38.3 2.4 %collective-permute-start.12 = (f32[6,64,128]{2,1,0:T(8,128)S(1)}, f32[6,64,128]{2,1,0:T(8,128)S(1)}, u32[]{:S(2)}, u32[]{:S(2)}) collective-permute-start(f32[6,64,128]{2,1,0:T(8,128)S(1)} %get-tuple-element.65.refs_0_.vector.prior.v2), channel_id=1, source_target_pairs={{0,4},{4,0},{8,12},{12,8},{16,20},{20,16},{24,28},{28,24},{32,36},... | collective-permute-start | bytes 589832 | tf_op jit(solution)/shard_map/ppermute | solution.py:611
  40.8 0.6 collective-permute-start.14
  41.4 1.9 %collective-permute-start.15 = (f32[24,128]{1,0:T(8,128)S(1)}, f32[24,128]{1,0:T(8,128)S(1)}, u32[]{:S(2)}, u32[]{:S(2)}) collective-permute-start(f32[24,128]{1,0:T(8,128)S(1)} %get-tuple-element.67), channel_id=1, source_target_pairs={{0,3},{1,2},{2,1},{3,0},{4,7},{5,6},{6,5},{7,4},{8,11},{9,10},{10,... | collective-permute-start | bytes 36872 | tf_op jit(solution)/shard_map/ppermute | solution.py:615
  43.3 1.6 %shard_map.90 = (f32[6,64,128]{2,1,0:T(8,128)S(1)}, f32[40,128]{1,0:T(8,128)S(1)}) custom-call(f32[12,64,128]{2,1,0:T(8,128)S(1)} %get-tuple-element.42.both, f32[12,64,128]{2,1,0:T(8,128)S(1)} %collective-permute-done.near, f32[12,64,128]{2,1,0:T(8,128)S(1)} %collective-permute-done.1.far, f32[48,128]{1,0:T(8,128)S(1)} %collective-permute-done.2.z_first, ...), custom_call_target="tpu_custom_call" | custom-call | flops 5898240 | bytes 4788224 | tf_op jit(solution)/shard_map/pallas_call | solution.py:588
  44.9 1.0 %shard_map.89 = (f32[24,128]{1,0:T(8,128)S(1)}, f32[8,128]{1,0:T(8,128)S(1)}) custom-call(f32[6,64,128]{2,1,0:T(8,128)S(1)} %get-tuple-element.57.refs_0_.vector.refs_1_.prior.v1, f32[6,64,128]{2,1,0:T(8,128)S(1)} %get-tuple-element.65.refs_0_.vector.prior.v2, f32[6,64,128]{2,1,0:T(8,128)S(1)} %copy-done.3, f32[8,6,64,128]{3,2,1,0:T(8,128)S(1)} %copy-done, ...), custom_call_target="tpu_custom_call" | custom-call | flops 2457600 | bytes 3751936 | tf_op jit(solution)/shard_map/pallas_call | solution.py:588
  45.9 0.7 shard_map.88.inner
  46.7 1.1 %shard_map.91 = (f32[6,64,128]{2,1,0:T(8,128)S(1)}, f32[24,128]{1,0:T(8,128)}, f32[24,128]{1,0:T(8,128)S(1)}) custom-call(f32[6,64,128]{2,1,0:T(8,128)S(1)} %shard_map.88.inner, f32[6,64,128]{2,1,0:T(8,128)S(1)} %collective-permute-done.12.near, f32[6,64,128]{2,1,0:T(8,128)S(1)} %collective-permute-done.13.far, ...), custom_call_target="tpu_custom_call" | custom-call | flops 2949120 | bytes 835584 | tf_op jit(solution)/shard_map/pallas_call | solution.py:588
  47.7 0.4 collective-permute-start.17
  48.1 1.0 %shard_map.93.sums = f32[2,128]{1,0:T(2,128)S(1)} custom-call(f32[6,64,128]{2,1,0:T(8,128)S(1)} %get-tuple-element.65.refs_0_.vector.prior.v2, f32[6,64,128]{2,1,0:T(8,128)S(1)} %get-tuple-element.74.own.vector.v3, f32[6,64,128]{2,1,0:T(8,128)S(1)} %copy-done.3, f32[8,6,64,128]{3,2,1,0:T(8,128)S(1)} %copy-done, f32[8,6,64,128]{3,2,1,0:T(8,128)S(1)} %copy-done.2, ...), custom_call_target="tpu_custom_call" | custom-call | flops 2457600 | bytes 3875840 | tf_op jit(solution)/shard_map/pallas_call | solution.py:588
  49.2 1.2 %shard_map.92.inner = f32[8,128]{1,0:T(8,128)S(1)} custom-call(f32[6,64,128]{2,1,0:T(8,128)S(1)} %get-tuple-element.74.own.vector.v3), custom_call_target="tpu_custom_call" | custom-call | flops 2949120 | bytes 200704 | tf_op jit(solution)/shard_map/pallas_call | solution.py:588
  50.4 1.1 %collective-permute-done.17.z_left = f32[24,128]{1,0:T(8,128)S(1)} collective-permute-done((f32[24,128]{1,0:T(8,128)S(1)}, f32[24,128]{1,0:T(8,128)S(1)}, u32[]{:S(2)}, u32[]{:S(2)}) %collective-permute-start.17) | collective-permute-done | bytes 12320 | tf_op jit(solution)/shard_map/ppermute | solution.py:683
  51.5 0.8 shard_map.94
  52.3 26.5 %all_to_all.5.received = f32[256,2,128]{2,1,0:T(2,128)S(1)} all-to-all(f32[256,2,128]{2,1,0:T(2,128)S(1)} %shard_map.94), channel_id=1, replica_groups=mesh['blk'=64,'gz'=4] {'blk','gz'}, dimensions={0} | all-to-all | bytes 524288 | tf_op jit(solution)/shard_map/all_to_all | solution.py:695
  78.8 1.9 %shard_map.95 = (f32[6,64,128]{2,1,0:T(8,128)}, f32[6,64,128]{2,1,0:T(8,128)}) custom-call(f32[256,2,128]{2,1,0:T(2,128)S(1)} %all_to_all.5.received, f32[6,64,128]{2,1,0:T(8,128)S(1)} %copy-done.3, f32[6,64,128]{2,1,0:T(8,128)S(1)} %copy-done.4, f32[6,64,128]{2,1,0:T(8,128)S(1)} %get-tuple-element.81.grad, ...), custom_call_target="tpu_custom_call" | custom-call | flops 2457600 | bytes 5177344 | tf_op jit(solution)/shard_map/pallas_call | solution.py:588
  (22 shorter events, 0.0 us)
Async XLA Ops:
  0.6 24.7 %copy-start = (f32[8,6,64,128]{3,2,1,0:T(8,128)S(1)}, f32[8,6,64,128]{3,2,1,0:T(8,128)}, u32[]{:S(2)}) copy-start(f32[8,6,64,128]{3,2,1,0:T(8,128)} %steps.15) | copy-start | bytes 4718596
  2.0 14.3 %collective-permute-start.1 = (f32[12,64,128]{2,1,0:T(8,128)S(1)}, f32[12,64,128]{2,1,0:T(8,128)S(1)}, u32[]{:S(2)}, u32[]{:S(2)}) collective-permute-start(f32[12,64,128]{2,1,0:T(8,128)S(1)} %get-tuple-element.42.both), channel_id=1, source_target_pairs={{0,252},{4,8},{8,4},{12,16},{16,12},{20,24},{24,20},{28,32},{32,28... | collective-permute-start | bytes 1179656 | tf_op jit(solution)/shard_map/ppermute | solution.py:610
  4.7 11.6 %collective-permute-start = (f32[12,64,128]{2,1,0:T(8,128)S(1)}, f32[12,64,128]{2,1,0:T(8,128)S(1)}, u32[]{:S(2)}, u32[]{:S(2)}) collective-permute-start(f32[12,64,128]{2,1,0:T(8,128)S(1)} %get-tuple-element.42.both), channel_id=1, source_target_pairs={{0,4},{4,0},{8,12},{12,8},{16,20},{20,16},{24,28},{28,24},{32,36},... | collective-permute-start | bytes 1179656 | tf_op jit(solution)/shard_map/ppermute | solution.py:611
  11.1 4.8 %collective-permute-start.2 = (f32[48,128]{1,0:T(8,128)S(1)}, f32[48,128]{1,0:T(8,128)S(1)}, u32[]{:S(2)}, u32[]{:S(2)}) collective-permute-start(f32[48,128]{1,0:T(8,128)S(1)} %get-tuple-element.43), channel_id=1, source_target_pairs={{0,1},{1,0},{2,3},{3,2},{4,5},{5,4},{6,7},{7,6},{8,9},{9,8},{10,11... | collective-permute-start | bytes 73736 | tf_op jit(solution)/shard_map/ppermute | solution.py:615
  12.4 3.9 %collective-permute-start.3 = (f32[48,128]{1,0:T(8,128)S(1)}, f32[48,128]{1,0:T(8,128)S(1)}, u32[]{:S(2)}, u32[]{:S(2)}) collective-permute-start(f32[48,128]{1,0:T(8,128)S(1)} %get-tuple-element.44), channel_id=1, source_target_pairs={{0,3},{1,2},{2,1},{3,0},{4,7},{5,6},{6,5},{7,4},{8,11},{9,10},{10,... | collective-permute-start | bytes 73736 | tf_op jit(solution)/shard_map/ppermute | solution.py:615
  14.3 0.9 %copy-start.6 = (f32[6,64,128]{2,1,0:T(8,128)S(1)}, f32[6,64,128]{2,1,0:T(8,128)}, u32[]{:S(2)}) copy-start(f32[6,64,128]{2,1,0:T(8,128)} %charge.1) | copy-start | bytes 589828
  16.8 13.1 %collective-permute-start.5 = (f32[6,64,128]{2,1,0:T(8,128)S(1)}, f32[6,64,128]{2,1,0:T(8,128)S(1)}, u32[]{:S(2)}, u32[]{:S(2)}) collective-permute-start(f32[6,64,128]{2,1,0:T(8,128)S(1)} %get-tuple-element.49.refs_0_.vector.refs_1_.prior.v0), channel_id=1, source_target_pairs={{0,252},{4,8},{8,4},{12,16},{16,12},{20,24},{24,20},{28,32},{32,28... | collective-permute-start | bytes 589832 | tf_op jit(solution)/shard_map/ppermute | solution.py:610
  16.9 13.0 %collective-permute-start.4 = (f32[6,64,128]{2,1,0:T(8,128)S(1)}, f32[6,64,128]{2,1,0:T(8,128)S(1)}, u32[]{:S(2)}, u32[]{:S(2)}) collective-permute-start(f32[6,64,128]{2,1,0:T(8,128)S(1)} %get-tuple-element.49.refs_0_.vector.refs_1_.prior.v0), channel_id=1, source_target_pairs={{0,4},{4,0},{8,12},{12,8},{16,20},{20,16},{24,28},{28,24},{32,36},... | collective-permute-start | bytes 589832 | tf_op jit(solution)/shard_map/ppermute | solution.py:611
  22.2 7.7 %collective-permute-start.6 = (f32[24,128]{1,0:T(8,128)S(1)}, f32[24,128]{1,0:T(8,128)S(1)}, u32[]{:S(2)}, u32[]{:S(2)}) collective-permute-start(f32[24,128]{1,0:T(8,128)S(1)} %get-tuple-element.50), channel_id=1, source_target_pairs={{0,1},{1,0},{2,3},{3,2},{4,5},{5,4},{6,7},{7,6},{8,9},{9,8},{10,11... | collective-permute-start | bytes 36872 | tf_op jit(solution)/shard_map/ppermute | solution.py:615
  23.5 6.4 %collective-permute-start.7 = (f32[24,128]{1,0:T(8,128)S(1)}, f32[24,128]{1,0:T(8,128)S(1)}, u32[]{:S(2)}, u32[]{:S(2)}) collective-permute-start(f32[24,128]{1,0:T(8,128)S(1)} %get-tuple-element.51), channel_id=1, source_target_pairs={{0,3},{1,2},{2,1},{3,0},{4,7},{5,6},{6,5},{7,4},{8,11},{9,10},{10,... | collective-permute-start | bytes 36872 | tf_op jit(solution)/shard_map/ppermute | solution.py:615
  25.4 1.4 %copy-start.1 = (f32[8,6,64,128]{3,2,1,0:T(8,128)S(1)}, f32[8,6,64,128]{3,2,1,0:T(8,128)}, u32[]{:S(2)}) copy-start(f32[8,6,64,128]{3,2,1,0:T(8,128)} %changes.15) | copy-start | bytes 4718596
  26.8 1.4 %copy-start.2 = (f32[8,6,64,128]{3,2,1,0:T(8,128)S(1)}, f32[8,6,64,128]{3,2,1,0:T(8,128)}, u32[]{:S(2)}) copy-start(f32[8,6,64,128]{3,2,1,0:T(8,128)} %changes.15) | copy-start | bytes 4718596
  26.8 1.4 %copy-start.3 = (f32[6,64,128]{2,1,0:T(8,128)S(1)}, f32[6,64,128]{2,1,0:T(8,128)}, u32[]{:S(2)}) copy-start(f32[6,64,128]{2,1,0:T(8,128)} %density.11) | copy-start | bytes 589828
  30.4 6.8 %collective-permute-start.9 = (f32[6,64,128]{2,1,0:T(8,128)S(1)}, f32[6,64,128]{2,1,0:T(8,128)S(1)}, u32[]{:S(2)}, u32[]{:S(2)}) collective-permute-start(f32[6,64,128]{2,1,0:T(8,128)S(1)} %get-tuple-element.57.refs_0_.vector.refs_1_.prior.v1), channel_id=1, source_target_pairs={{0,252},{4,8},{8,4},{12,16},{16,12},{20,24},{24,20},{28,32},{32,28... | collective-permute-start | bytes 589832 | tf_op jit(solution)/shard_map/ppermute | solution.py:610
  30.5 6.7 %collective-permute-start.8 = (f32[6,64,128]{2,1,0:T(8,128)S(1)}, f32[6,64,128]{2,1,0:T(8,128)S(1)}, u32[]{:S(2)}, u32[]{:S(2)}) collective-permute-start(f32[6,64,128]{2,1,0:T(8,128)S(1)} %get-tuple-element.57.refs_0_.vector.refs_1_.prior.v1), channel_id=1, source_target_pairs={{0,4},{4,0},{8,12},{12,8},{16,20},{20,16},{24,28},{28,24},{32,36},... | collective-permute-start | bytes 589832 | tf_op jit(solution)/shard_map/ppermute | solution.py:611
  31.1 6.0 %collective-permute-start.10 = (f32[24,128]{1,0:T(8,128)S(1)}, f32[24,128]{1,0:T(8,128)S(1)}, u32[]{:S(2)}, u32[]{:S(2)}) collective-permute-start(f32[24,128]{1,0:T(8,128)S(1)} %get-tuple-element.58), channel_id=1, source_target_pairs={{0,1},{1,0},{2,3},{3,2},{4,5},{5,4},{6,7},{7,6},{8,9},{9,8},{10,11... | collective-permute-start | bytes 36872 | tf_op jit(solution)/shard_map/ppermute | solution.py:615
  32.4 4.7 %collective-permute-start.11 = (f32[24,128]{1,0:T(8,128)S(1)}, f32[24,128]{1,0:T(8,128)S(1)}, u32[]{:S(2)}, u32[]{:S(2)}) collective-permute-start(f32[24,128]{1,0:T(8,128)S(1)} %get-tuple-element.59), channel_id=1, source_target_pairs={{0,3},{1,2},{2,1},{3,0},{4,7},{5,6},{6,5},{7,4},{8,11},{9,10},{10,... | collective-permute-start | bytes 36872 | tf_op jit(solution)/shard_map/ppermute | solution.py:615
  35.3 7.9 %copy-start.5 = (f32[6,64,128]{2,1,0:T(8,128)S(1)}, f32[6,64,128]{2,1,0:T(8,128)}, u32[]{:S(2)}) copy-start(f32[6,64,128]{2,1,0:T(8,128)} %potential.1) | copy-start | bytes 589828
  37.6 9.1 %collective-permute-start.13 = (f32[6,64,128]{2,1,0:T(8,128)S(1)}, f32[6,64,128]{2,1,0:T(8,128)S(1)}, u32[]{:S(2)}, u32[]{:S(2)}) collective-permute-start(f32[6,64,128]{2,1,0:T(8,128)S(1)} %get-tuple-element.65.refs_0_.vector.prior.v2), channel_id=1, source_target_pairs={{0,252},{4,8},{8,4},{12,16},{16,12},{20,24},{24,20},{28,32},{32,28... | collective-permute-start | bytes 589832 | tf_op jit(solution)/shard_map/ppermute | solution.py:610
  38.3 8.3 %collective-permute-start.12 = (f32[6,64,128]{2,1,0:T(8,128)S(1)}, f32[6,64,128]{2,1,0:T(8,128)S(1)}, u32[]{:S(2)}, u32[]{:S(2)}) collective-permute-start(f32[6,64,128]{2,1,0:T(8,128)S(1)} %get-tuple-element.65.refs_0_.vector.prior.v2), channel_id=1, source_target_pairs={{0,4},{4,0},{8,12},{12,8},{16,20},{20,16},{24,28},{28,24},{32,36},... | collective-permute-start | bytes 589832 | tf_op jit(solution)/shard_map/ppermute | solution.py:611
  40.8 5.9 %collective-permute-start.14 = (f32[24,128]{1,0:T(8,128)S(1)}, f32[24,128]{1,0:T(8,128)S(1)}, u32[]{:S(2)}, u32[]{:S(2)}) collective-permute-start(f32[24,128]{1,0:T(8,128)S(1)} %get-tuple-element.66), channel_id=1, source_target_pairs={{0,1},{1,0},{2,3},{3,2},{4,5},{5,4},{6,7},{7,6},{8,9},{9,8},{10,11... | collective-permute-start | bytes 36872 | tf_op jit(solution)/shard_map/ppermute | solution.py:615
  41.4 5.3 %collective-permute-start.15 = (f32[24,128]{1,0:T(8,128)S(1)}, f32[24,128]{1,0:T(8,128)S(1)}, u32[]{:S(2)}, u32[]{:S(2)}) collective-permute-start(f32[24,128]{1,0:T(8,128)S(1)} %get-tuple-element.67), channel_id=1, source_target_pairs={{0,3},{1,2},{2,1},{3,0},{4,7},{5,6},{6,5},{7,4},{8,11},{9,10},{10,... | collective-permute-start | bytes 36872 | tf_op jit(solution)/shard_map/ppermute | solution.py:615
  47.7 3.8 %collective-permute-start.16 = (f32[6,64,128]{2,1,0:T(8,128)S(1)}, f32[6,64,128]{2,1,0:T(8,128)S(1)}, u32[]{:S(2)}, u32[]{:S(2)}) collective-permute-start(f32[6,64,128]{2,1,0:T(8,128)S(1)} %get-tuple-element.74.own.vector.v3), channel_id=1, source_target_pairs={{0,4},{4,8},{8,12},{12,16},{16,20},{20,24},{24,28},{28,32},{32,36}... | collective-permute-start | bytes 589832 | tf_op jit(solution)/shard_map/ppermute | solution.py:682
  47.7 3.8 %collective-permute-start.17 = (f32[24,128]{1,0:T(8,128)S(1)}, f32[24,128]{1,0:T(8,128)S(1)}, u32[]{:S(2)}, u32[]{:S(2)}) collective-permute-start(f32[24,128]{1,0:T(8,128)S(1)} %get-tuple-element.75), channel_id=1, source_target_pairs={{0,1},{1,2},{2,3},{3,0},{4,5},{5,6},{6,7},{7,4},{8,9},{9,10},{10,1... | collective-permute-start | bytes 36872 | tf_op jit(solution)/shard_map/ppermute | solution.py:683
  48.1 30.6 %copy-start.4 = (f32[6,64,128]{2,1,0:T(8,128)S(1)}, f32[6,64,128]{2,1,0:T(8,128)}, u32[]{:S(2)}) copy-start(f32[6,64,128]{2,1,0:T(8,128)} %hartree.3) | copy-start | bytes 589828

commit v4 on v3

--- a/solution.py
+++ b/solution.py
@@ -27,6 +27,14 @@
 ROW_BASE = 136
 ROW_W = 170
 ROW_MOM = 238
+HALF = 126
+
+
+def place(n):
+    return n if n < HALF else n + LANES - HALF
+
+
+MOM_LANE = place(ROW_MOM) - LANES
 PAIRS = tuple((i, j) for i in range(HIST) for j in range(i, HIST))
 PAIR_ROW = {pair: row for row, pair in enumerate(PAIRS)}
 
@@ -188,15 +196,20 @@
         body(far, near)
 
 
-def exact_total(hi, lo):
-    for step in (4, 2, 1):
-        hi, err = two_sum(hi, pltpu.roll(hi, step, 0))
-        lo = lo + pltpu.roll(lo, step, 0) + err
-    hi, lo = hi[0:1], lo[0:1]
-    for step in (64, 32, 16, 8, 4, 2, 1):
-        hi, err = two_sum(hi, pltpu.roll(hi, step, 1))
-        lo = lo + pltpu.roll(lo, step, 1) + err
-    return quick_sum(hi, lo)
+def fold(hi, lo, axis, steps):
+    for step in steps:
+        hi, err = two_sum(hi, pltpu.roll(hi, step, axis))
+        lo = lo + pltpu.roll(lo, step, axis) + err
+    return hi, lo
+
+
+def fold_rows(acc):
+    hi, lo = fold(*acc, 0, (4, 2, 1))
+    return hi[0:1], lo[0:1]
+
+
+def fold_lanes(hi, lo):
+    return quick_sum(*fold(hi, lo, 1, (64, 32, 16, 8, 4, 2, 1)))
 
 
 def add_tile(acc, product):
@@ -205,10 +218,10 @@
 
 
 def tile_of(ref, i, b):
-    return ref[i, pl.ds(pl.multiple_of(8 * b, 8), 8), :]
-
-
-def exact_dots(pairs):
+    return ref[i, 8 * b : 8 * b + 8, :]
+
+
+def store_moments(pairs, moments):
     zero = jnp.zeros((8, LANES), jnp.float32)
 
     def body(i, accs):
@@ -219,27 +232,30 @@
         return accs
 
     accs = lax.fori_loop(0, REACH, body, tuple((zero, zero) for _ in pairs))
-    return [exact_total(*acc) for acc in accs]
+    for n, acc in enumerate(accs):
+        moments[2 * n : 2 * n + 1, :], moments[2 * n + 1 : 2 * n + 2, :] = fold_rows(acc)
 
 
 def collapse(acc):
     return jnp.sum(acc, axis=0, keepdims=True)
 
 
-def launch_kernel(hartree, density, both, face_a, face_b, sems):
+def launch_kernel(hartree, density, charge, both, charge_here, face_a, face_b, sems):
+    places = (both.at[pl.ds(0, REACH)], both.at[pl.ds(REACH, REACH)], charge_here)
     copies = [
-        pltpu.make_async_copy(src, both.at[pl.ds(REACH * n, REACH)], sems.at[n])
-        for n, src in enumerate((hartree, density))
+        pltpu.make_async_copy(src, dst, sems.at[n])
+        for n, (src, dst) in enumerate(zip((hartree, density, charge), places))
     ]
     for copy in copies:
         copy.start()
-    for n, copy in enumerate(copies):
-        copy.wait()
+    for n in range(2):
+        copies[n].wait()
         rows = slice(24 * n, 24 * n + 24)
         face_a[rows, :], face_b[rows, :] = by_partner(*pack_faces(both, REACH * n))
-
-
-def inner_residual_kernel(both, charge, out, ext):
+    copies[2].wait()
+
+
+def inner_residual(both, charge, out, ext):
     hartree = both.at[pl.ds(0, REACH)]
     fill_ext(hartree, ext)
     for i in range(REACH):
@@ -248,16 +264,15 @@
         out[i] = source_scale * (rho * rho - charge[i]) - (screen * values - lap)
 
 
-def inner_basis_kernel(has_prior, *refs):
-    own, prior, out, ext = refs if has_prior else (refs[0], None, *refs[1:])
+def inner_basis(own, prior, out, ext):
     fill_ext(own, ext)
     for i in range(REACH):
         lap, values = inner_plane(i, own, ext)
         moved = (screen / SHIFT - 1.0) * values - (1.0 / SHIFT) * lap
-        out[i] = 2.0 * moved - prior[i] if has_prior else moved
-
-
-def edge_kernel(gain, last, inner, near, far, z_first, z_second, out, face_a, face_b):
+        out[i] = moved if prior is None else 2.0 * moved - prior[i]
+
+
+def edge_kernel(gain, last, inner, near, far, z_first, z_second, out, *sent):
     faces = edge_faces(*by_side(z_first[0:24, :], z_second[0:24, :]))
 
     def body(left, right):
@@ -266,37 +281,39 @@
 
     with_sides(near, far, body)
     packed = pack_faces(out, 0)
-    face_a[...], face_b[...] = packed if last else by_partner(*packed)
-
-
-def gram_kernel(work, steps, changes, rows):
+    if last:
+        sent[0][...] = packed[1]
+    else:
+        sent[0][...], sent[1][...] = by_partner(*packed)
+
+
+def store(rows, base, values):
+    for n, value in enumerate(values):
+        rows[base + n : base + n + 1, :] = value
+
+
+def gram_dots(left, right, pairs):
     zero = jnp.zeros((8, LANES), jnp.float32)
 
-    def run(base, left, right, pairs):
-        def body(i, accs):
-            for b in range(8):
-                at = pl.ds(8 * b, 8)
-                l_tiles = {p: left[p, i, at, :] for p in sorted({p for p, _ in pairs})}
-                if left is right:
-                    r_tiles = l_tiles
-                else:
-                    r_tiles = {q: right[q, i, at, :] for q in sorted({q for _, q in pairs})}
-                accs = tuple(acc + l_tiles[p] * r_tiles[q] for acc, (p, q) in zip(accs, pairs))
-            return accs
-
-        accs = lax.fori_loop(0, REACH, body, tuple(zero for _ in pairs))
-        for n, acc in enumerate(accs):
-            rows[base + n : base + n + 1, :] = collapse(acc)
-
-    if work == "same":
-        run(0, steps, steps, PAIRS)
-        run(36, changes, changes, PAIRS)
-    else:
-        run(0, steps, changes, tuple((i, j) for i in range(4) for j in range(8)))
-        run(32, steps, changes, tuple((i, j) for i in range(4, 8) for j in range(8)))
-
-
-def field_dots(steps, changes, others):
+    def body(i, accs):
+        for b in range(8):
+            at = pl.ds(8 * b, 8)
+            l_tiles = {p: left[p, i, at, :] for p in sorted({p for p, _ in pairs})}
+            if left is right:
+                r_tiles = l_tiles
+            else:
+                r_tiles = {q: right[q, i, at, :] for q in sorted({q for _, q in pairs})}
+            accs = tuple(acc + l_tiles[p] * r_tiles[q] for acc, (p, q) in zip(accs, pairs))
+        return accs
+
+    accs = lax.fori_loop(0, REACH, body, tuple(zero for _ in pairs))
+    return [collapse(acc) for acc in accs]
+
+
+CROSS_PAIRS = tuple((i, j) for i in range(HIST) for j in range(HIST))
+
+
+def field_dots(steps, changes, others, plain=()):
     zero = jnp.zeros((8, LANES), jnp.float32)
     count = 2 * HIST
 
@@ -309,24 +326,15 @@
                 field = steps[f, i, at, :] if f < HIST else changes[f - HIST, i, at, :]
                 for o, tile in enumerate(tiles):
                     accs[o * count + f] = accs[o * count + f] + field * tile
+            for n, (one, two) in enumerate(plain, len(others) * count):
+                accs[n] = accs[n] + one(i, b) * two(i, b)
         return tuple(accs)
 
-    accs = lax.fori_loop(0, REACH, body, tuple(zero for _ in range(count * len(others))))
-    return [collapse(acc) for acc in accs]
-
-
-def plain_dots(pairs):
-    zero = jnp.zeros((8, LANES), jnp.float32)
-
-    def body(i, accs):
-        for b in range(8):
-            accs = tuple(acc + a(i, b) * c(i, b) for acc, (a, c) in zip(accs, pairs))
-        return accs
-
-    return [collapse(acc) for acc in lax.fori_loop(0, REACH, body, tuple(zero for _ in pairs))]
-
-
-def base_kernel(both, near, far, z_first, z_second, potential, steps, changes, grad, rows, ext):
+    total = count * len(others) + len(plain)
+    return [collapse(acc) for acc in lax.fori_loop(0, REACH, body, (zero,) * total)]
+
+
+def base_gradient(both, near, far, z_first, z_second, potential, grad, ext):
     hartree = both.at[pl.ds(0, REACH)]
     density = both.at[pl.ds(REACH, REACH)]
     fill_ext(density, ext)
@@ -343,75 +351,104 @@
         grad[i] = 2.0 * rho * (hartree[i] + potential[i] + tf_scale * power) - (lap + grad[i]) * (
             1.0 / (spacing * spacing)
         )
-    g_tile = lambda i, b: tile_of(grad, i, b)
-    r_tile = lambda i, b: tile_of(density, i, b)
-    dots = field_dots(steps, changes, [g_tile, r_tile]) + plain_dots([(r_tile, g_tile), (r_tile, r_tile)])
-    for n, row in enumerate(dots):
-        rows[n : n + 1, :] = row
-
-
-def basis_dots(vector, density, steps, changes, rows):
-    w_tile = lambda i, b: 2.0 * tile_of(density, i, b) * tile_of(vector, i, b)
-    r_tile = lambda i, b: tile_of(density, i, b)
-    dots = field_dots(steps, changes, [w_tile]) + plain_dots([(r_tile, w_tile)])
-    for n, row in enumerate(dots):
-        rows[n : n + 1, :] = row
-
-
-def store_moments(pairs, moments):
-    for n, (hi, lo) in enumerate(exact_dots(pairs)):
-        moments[2 * n : 2 * n + 1, :] = hi
-        moments[2 * n + 1 : 2 * n + 2, :] = lo
-
-
-def first_dots_kernel(vector, density, steps, changes, rows, moments):
-    basis_dots(vector, density, steps, changes, rows)
+
+
+def density_tile(both):
+    return lambda i, b: tile_of(both, REACH + i, b)
+
+
+def lifted_tile(both, vector):
+    return lambda i, b: 2.0 * tile_of(both, REACH + i, b) * tile_of(vector, i, b)
+
+
+def side_one(both, charge, steps, inner, rows, ext):
+    inner_residual(both, charge, inner, ext)
+    store(rows, 0, gram_dots(steps, steps, PAIRS))
+
+
+def side_two(vector, both, steps, changes, inner, rows, moments, ext):
+    inner_basis(vector, None, inner, ext)
+    lifted, rho = lifted_tile(both, vector), density_tile(both)
+    store(rows, 0, field_dots(steps, changes, [lifted], [(rho, lifted)]))
+    store(rows, 17, gram_dots(changes, changes, PAIRS))
+    store(rows, 53, gram_dots(steps, changes, CROSS_PAIRS[:32]))
     store_moments([(vector, vector)], moments)
 
 
-def dots_kernel(prior, vector, density, steps, changes, rows, moments):
-    basis_dots(vector, density, steps, changes, rows)
+def side_three(prior, vector, both, near, far, z_first, z_second, potential, steps, changes, *outs):
+    inner, grad, rows, moments, ext = outs
+    inner_basis(vector, prior, inner, ext)
+    lifted, rho = lifted_tile(both, vector), density_tile(both)
+    values = field_dots(steps, changes, [lifted, rho], [(rho, lifted)])
+    store(rows, 0, values[:16] + values[32:] + values[16:32])
+    store(rows, 33, gram_dots(steps, changes, CROSS_PAIRS[32:]))
     store_moments([(prior, vector), (vector, vector)], moments)
-
-
-def last_dots_kernel(
-    prior, vector, density, steps, changes, same, cross, base, d0, d1, d2, m0, m1, m2, out, rows, own_rows, moments
-):
-    basis_dots(vector, density, steps, changes, own_rows)
+    base_gradient(both, near, far, z_first, z_second, potential, grad, ext)
+
+
+def side_four(prior, vector, both, grad, steps, changes, inner, rows, moments, ext):
+    inner_basis(vector, prior, inner, ext)
+    lifted, rho = lifted_tile(both, vector), density_tile(both)
+    slope = lambda i, b: tile_of(grad, i, b)
+    values = field_dots(steps, changes, [lifted, slope], [(rho, lifted), (rho, slope), (rho, rho)])
+    store(rows, 0, values[:16] + values[32:33] + values[16:32] + values[33:])
     store_moments([(prior, vector), (vector, vector)], moments)
-    rows[ROW_GRAM : ROW_GRAM + 72, :] = same[...]
-    rows[ROW_GRAM + 72 : ROW_GRAM + 136, :] = cross[...]
-    rows[ROW_BASE : ROW_BASE + 34, :] = base[0:34, :]
-    for n, d in enumerate((d0, d1, d2, own_rows)):
-        rows[ROW_W + 17 * n : ROW_W + 17 * n + 17, :] = d[0:17, :]
-    rows[ROW_MOM:256, :] = jnp.zeros((256 - ROW_MOM, LANES), jnp.float32)
+
+
+def side_five(prior, vector, both, steps, changes, r1, r2, r3, r4, m2, m3, m4, kept, given, inner, table, m5, ext):
+    lifted, rho = lifted_tile(both, vector), density_tile(both)
+    own = field_dots(steps, changes, [lifted], [(rho, lifted)])
+    store_moments([(prior, vector), (vector, vector)], m5)
+    table[...] = jnp.zeros_like(table)
+
+    def put(base, ref, start, count):
+        before = max(0, min(count, HALF - base))
+        if before:
+            table[base : base + before, :] = ref[start : start + before, :]
+        if before < count:
+            at = place(base + before)
+            table[at : at + count - before, :] = ref[start + before : start + count, :]
+
+    put(ROW_GRAM, r1, 0, 36)
+    put(ROW_GRAM + 36, r2, 17, 36)
+    put(ROW_GRAM + 72, r2, 53, 32)
+    put(ROW_GRAM + 104, r3, 33, 32)
+    put(ROW_BASE, r3, 17, 16)
+    put(ROW_BASE + 16, r4, 17, 18)
+    for n, rows in enumerate((r2, r3, r4)):
+        put(ROW_W + 17 * n, rows, 0, 17)
+    store(table, place(ROW_W + 51), own)
+
+    order = [(m2, 0), (m3, 0), (m3, 1), (m4, 0), (m4, 1), (m5, 0), (m5, 1)]
+    zero = jnp.zeros((1, LANES), jnp.float32)
+    parts = [
+        jnp.concatenate([ref[2 * which + low : 2 * which + low + 1, :] for ref, which in order] + [zero], axis=0)
+        for low in range(2)
+    ]
+    hi, lo = fold_lanes(*parts)
     lane = lane_ids((1, LANES))
-    out[0:1, :] = jnp.sum(jnp.transpose(rows[0:128, :]), axis=0, keepdims=True)
-    second = jnp.sum(jnp.transpose(rows[128:256, :]), axis=0, keepdims=True)
-    at = ROW_MOM - 128
-    order = [(m0, 0), (m1, 0), (m1, 1), (m2, 0), (m2, 1), (moments, 0), (moments, 1)]
-    for n, (ref, which) in enumerate(order):
-        second = jnp.where(lane == at + n, ref[2 * which : 2 * which + 1, :], second)
-        second = jnp.where(lane == at + 8 + n, ref[2 * which + 1 : 2 * which + 2, :], second)
-    out[1:2, :] = second
-
-
-def inner_moment_kernel(own, out, ext):
-    fill_ext(own, ext)
+    first = jnp.sum(jnp.transpose(table[0:LANES, :]), axis=0, keepdims=True)
+    second = jnp.sum(jnp.transpose(table[LANES : 2 * LANES, :]), axis=0, keepdims=True)
+    for n in range(7):
+        second = jnp.where(lane == MOM_LANE + n, hi[n : n + 1], second)
+        second = jnp.where(lane == MOM_LANE + 7 + n, lo[n : n + 1], second)
+    odd = is_odd("blk")
+    kept[...] = jnp.where(odd, second, first)
+    given[...] = jnp.where(odd, first, second)
+
+    fill_ext(vector, ext)
     zero = jnp.zeros((8, LANES), jnp.float32)
     accs = [(zero, zero) for _ in range(2)]
     for i in range(REACH):
-        lap, values = inner_plane(i, own, ext)
+        lap, values = inner_plane(i, vector, ext)
         product = values * ((screen / SHIFT - 1.0) * values - (1.0 / SHIFT) * lap)
         for b in range(8):
             accs[b % 2] = add_tile(accs[b % 2], product[8 * b : 8 * b + 8])
     hi, err = two_sum(accs[0][0], accs[1][0])
-    hi, lo = exact_total(hi, accs[0][1] + accs[1][1] + err)
-    out[0:1, :] = hi
-    out[1:2, :] = lo
-
-
-def send_kernel(own, left, z_left, inner, sums, out):
+    inner[0:1, :], inner[1:2, :] = fold_rows((hi, accs[0][1] + accs[1][1] + err))
+
+
+def send_kernel(own, left, z_left, inner, kept, taken, out):
     faces = edge_faces(z_left[...], None)
     zero = jnp.zeros((8, LANES), jnp.float32)
     accs = [(zero, zero) for _ in range(2)]
@@ -420,13 +457,14 @@
         for b in range(8):
             accs[b % 2] = add_tile(accs[b % 2], product[8 * b : 8 * b + 8])
     hi, err = two_sum(accs[0][0], accs[1][0])
-    coupling = exact_total(hi, accs[0][1] + accs[1][1] + err)
-    hi, lo = df_add(df_scale(coupling, -2.0 / SHIFT), (inner[0:1, :], inner[1:2, :]))
+    coupling = fold_rows((hi, accs[0][1] + accs[1][1] + err))
+    hi, lo = fold_lanes(*df_add(df_scale(coupling, -2.0 / SHIFT), (inner[0:1, :], inner[1:2, :])))
     lane = lane_ids((1, LANES))
-    at = ROW_MOM - 128
-    second = jnp.where(lane == at + 7, hi, jnp.where(lane == at + 15, lo, sums[1:2, :]))
-    both = jnp.concatenate([sums[0:1, :], second], axis=0)
-    out[...] = jnp.broadcast_to(both[None], out.shape)
+    row, err = two_sum(kept[...], taken[...])
+    low_lane = (lane >= MOM_LANE + 7) & (lane < MOM_LANE + 14) & is_odd("blk")
+    row = jnp.where(low_lane, row + pltpu.roll(err, 7, 1), row)
+    row = jnp.where(lane == HALF, hi, jnp.where(lane == HALF + 1, lo, row))
+    out[...] = jnp.broadcast_to(row, out.shape)
 
 
 def solve_krylov(moment):
@@ -469,11 +507,10 @@
     return [hi + lo for hi, lo in sol]
 
 
-def final_kernel(received, density, hartree, grad, v0, v1, v2, v3, steps, changes, new_density, new_hartree, spread):
-    chains = 8
-    parts = [(received[n], jnp.zeros((2, LANES), jnp.float32)) for n in range(chains)]
-    for n in range(chains, received.shape[0]):
-        parts[n % chains] = add_tile(parts[n % chains], received[n])
+def final_kernel(received, both, grad, v0, v1, v2, v3, steps, changes, new_density, new_hartree, spread):
+    parts = [(received[8 * n : 8 * n + 8, :], jnp.zeros((8, LANES), jnp.float32)) for n in range(4)]
+    for n in range(4, received.shape[0] // 8):
+        parts[n % 4] = add_tile(parts[n % 4], received[8 * n : 8 * n + 8, :])
     while len(parts) > 1:
         half = len(parts) // 2
         merged = []
@@ -481,18 +518,23 @@
             hi, err = two_sum(a[0], b[0])
             merged.append((hi, a[1] + b[1] + err))
         parts = merged
-    hi, lo = quick_sum(*parts[0])
-    spread[0:128, :] = jnp.transpose(jnp.broadcast_to(hi[0:1], (LANES, LANES)))
-    spread[128:256, :] = jnp.transpose(jnp.broadcast_to(hi[1:2], (LANES, LANES)))
-    spread[256:384, :] = jnp.transpose(jnp.broadcast_to(lo[1:2], (LANES, LANES)))
+    hi, lo = fold(*parts[0], 0, (1, 2))
+    lane = lane_ids((1, LANES))
+    last, err = two_sum(hi[3:4], hi[7:8])
+    err = err + (lo[3:4] + lo[7:8])
+    first = hi[3:4]
+    second = jnp.where(lane >= HALF, last, hi[7:8])
+    low = jnp.where(lane >= HALF, err, lo[7:8])
+    low = low + jnp.where(lane == HALF, pltpu.roll(second, LANES - 1, 1), pltpu.roll(second, LANES - 7, 1))
+    for n, value in enumerate((first, second, low)):
+        spread[LANES * n : LANES * n + LANES, :] = jnp.transpose(jnp.broadcast_to(value, (LANES, LANES)))
 
     def row(n):
-        return spread[n : n + 1, :]
+        return spread[place(n) : place(n) + 1, :]
 
     def moment(n):
-        low = 128 + ROW_MOM
-        a = df_add((row(ROW_MOM + n), row(low + n)), (row(ROW_MOM + 8 + n), row(low + 8 + n)))
-        return a
+        at = LANES + (MOM_LANE + n if n < 7 else HALF)
+        return quick_sum(spread[at : at + 1, :], spread[LANES + at : LANES + at + 1, :])
 
     mix = solve_krylov([moment(n) for n in range(8)])
 
@@ -525,7 +567,7 @@
     scaling = s_bar(last, last) / bar_bar(last, last)
 
     def energy(n):
-        value = row(ROW_BASE + n) if n < 16 else row(ROW_BASE + 32)
+        value = row(ROW_BASE + 16 + n)
         for j in range(4):
             value = value + mix[j] * row(ROW_W + 17 * j + n)
         return value
@@ -533,7 +575,7 @@
     chem = energy(16) / row(ROW_BASE + 33)
 
     def gradient(n):
-        return energy(n) - chem * row(ROW_BASE + 16 + n)
+        return energy(n) - chem * row(ROW_BASE + n)
 
     s_grad = [gradient(i) for i in pairs]
     bar_grad = [theta[i] * gradient(HIST + i) + rest[i] * s_grad[i] for i in pairs]
@@ -568,11 +610,11 @@
     def _(i):
         for b in range(8):
             at = pl.ds(8 * b, 8)
-            rho = density[i, at, :]
+            rho = both[REACH + i, at, :]
             lift = mix[0] * v0[i, at, :]
             for j in range(1, 4):
                 lift = lift + mix[j] * basis[j][i, at, :]
-            new_hartree[i, at, :] = hartree[i, at, :] + lift
+            new_hartree[i, at, :] = both[i, at, :] + lift
             slope = grad[i, at, :] + 2.0 * rho * lift - chem * rho
             parts = [rho, gain * slope, step_mix[0] * steps[0, i, at, :], change_mix[0] * changes[0, i, at, :]]
             for f in range(1, HIST):
@@ -623,83 +665,76 @@
     block = sqrt_density.shape
     ext = (block[0], block[1] + 16, block[2])
     face = (24, LANES)
-    stencil_flops = 60 * math.prod(block)
     cells = math.prod(block)
     history = [hist_steps, hist_changes]
-    both, *faces = call(
+    cells = math.prod(block)
+    history = [hist_steps, hist_changes]
+    work = 300 * cells
+    inputs = (hartree_prev, sqrt_density, ion_charge)
+    both, charge, *faces = call(
         launch_kernel,
-        [(2 * REACH, *block[1:]), (48, LANES), (48, LANES)],
-        [pltpu.with_memory_space_constraint(x, pltpu.HBM) for x in (hartree_prev, sqrt_density)],
-        [pltpu.SemaphoreType.DMA((2,))],
+        [(2 * REACH, *block[1:]), block, (48, LANES), (48, LANES)],
+        [pltpu.with_memory_space_constraint(x, pltpu.HBM) for x in inputs],
+        [pltpu.SemaphoreType.DMA((3,))],
         place=pltpu.HBM,
     )
     start = (*x_halo(both), *z_halo(*faces))
-    (inner,) = call(inner_residual_kernel, [block], [both, ion_charge], [ext], stencil_flops)
-    halo = after(start, inner)
+    inner, r1 = call(side_one, [block, (40, LANES)], [both, charge, hist_steps], [ext], work)
     v0, *faces = call(
-        functools.partial(edge_kernel, 1.0, False), [block, face, face], [inner, *halo], flops=stencil_flops
-    )
-    basis = [v0]
-    dots, moments = [], []
-    for n in range(3):
-        halo = (*x_halo(basis[n]), *z_halo(*faces))
-        prior = [basis[n - 1]] if n else []
-        (inner,) = call(
-            functools.partial(inner_basis_kernel, n > 0), [block], [basis[n], *prior], [ext], stencil_flops
-        )
-        rows, moment = call(
-            dots_kernel if n else first_dots_kernel,
-            [(24, LANES), (8, LANES)],
-            [*prior, basis[n], sqrt_density, *history],
-            flops=50 * cells,
-        )
-        dots.append(rows)
-        moments.append(moment)
-        done = [inner, rows]
-        if n == 0:
-            (same,) = call(functools.partial(gram_kernel, "same"), [(72, LANES)], history, flops=144 * cells)
-            done.append(same)
-        if n == 1:
-            (cross,) = call(functools.partial(gram_kernel, "cross"), [(64, LANES)], history, flops=128 * cells)
-            done.append(cross)
-        if n == 2:
-            grad, base = call(
-                base_kernel,
-                [block, (40, LANES)],
-                [both, *start, ion_potential, *history],
-                [ext],
-                2 * stencil_flops,
-            )
-            done.append(base)
-        halo = after(halo, *done)
-        fresh, *faces = call(
-            functools.partial(edge_kernel, -2.0 / SHIFT if n else -1.0 / SHIFT, n == 2),
-            [block, face, face],
-            [inner, *halo],
-            flops=stencil_flops,
-        )
-        basis.append(fresh)
-    left = lax.ppermute(basis[3], "blk", ring("blk", 1))
-    z_left = lax.ppermute(faces[1], "gz", ring("gz", 1))
-    (inner,) = call(inner_moment_kernel, [(8, LANES)], [basis[3]], [ext], stencil_flops)
-    (sums,) = call(
-        last_dots_kernel,
-        [(2, LANES)],
-        [basis[2], basis[3], sqrt_density, *history, same, cross, base, *dots, *moments],
-        [(256, LANES), (24, LANES), (8, LANES)],
-        50 * cells,
-    )
-    left, z_left = after((left, z_left), inner, sums)
+        functools.partial(edge_kernel, 1.0, False), [block, face, face], [inner, *after(start, inner)], flops=work
+    )
+    halo = (*x_halo(v0), *z_halo(*faces))
+    inner, r2, m2 = call(
+        side_two, [block, (88, LANES), (8, LANES)], [v0, both, *history], [ext], work
+    )
+    v1, *faces = call(
+        functools.partial(edge_kernel, -1.0 / SHIFT, False),
+        [block, face, face],
+        [inner, *after(halo, inner)],
+        flops=work,
+    )
+    halo = (*x_halo(v1), *z_halo(*faces))
+    inner, grad, r3, m3 = call(
+        side_three,
+        [block, block, (72, LANES), (8, LANES)],
+        [v0, v1, both, *start, ion_potential, *history],
+        [ext],
+        work,
+    )
+    v2, *faces = call(
+        functools.partial(edge_kernel, -2.0 / SHIFT, False),
+        [block, face, face],
+        [inner, *after(halo, inner)],
+        flops=work,
+    )
+    halo = (*x_halo(v2), *z_halo(*faces))
+    inner, r4, m4 = call(
+        side_four, [block, (40, LANES), (8, LANES)], [v1, v2, both, grad, *history], [ext], work
+    )
+    v3, upper = call(
+        functools.partial(edge_kernel, -2.0 / SHIFT, True), [block, face], [inner, *after(halo, inner)], flops=work
+    )
+    left = lax.ppermute(v3, "blk", ring("blk", 1))
+    z_left = lax.ppermute(upper, "gz", ring("gz", 1))
+    kept, given, inner = call(
+        side_five,
+        [(1, LANES), (1, LANES), (8, LANES)],
+        [v2, v3, both, *history, r1, r2, r3, r4, m2, m3, m4],
+        [(2 * LANES, LANES), (8, LANES), ext],
+        work,
+    )
+    taken = lax.ppermute(given, "blk", swap("blk", 0))
+    left, z_left = after((left, z_left), inner, taken)
     devices = lax.axis_size("blk") * lax.axis_size("gz")
-    (outgoing,) = call(send_kernel, [(devices, 2, LANES)], [basis[3], left, z_left, inner, sums], flops=stencil_flops)
-    received = lax.all_to_all(outgoing, ("blk", "gz"), 0, 0, tiled=True)
+    (outgoing,) = call(send_kernel, [(devices, LANES)], [v3, left, z_left, inner, kept, taken], flops=work)
+    received = lax.all_to_all(outgoing.reshape(devices, 1, LANES), ("blk", "gz"), 0, 0, tiled=True)
     return tuple(
         call(
             final_kernel,
             [block, block],
-            [received, sqrt_density, hartree_prev, grad, *basis, hist_steps, hist_changes],
-            [(384, LANES)],
-            50 * math.prod(block),
+            [received.reshape(devices, LANES), both, grad, v0, v1, v2, v3, *history],
+            [(3 * LANES, LANES)],
+            work,
         )
     )
 

time: 80.9 us -> 76.8 us (0.949)
  Pallas kernels: 18.4 us -> 14.6 us
  starting transfers between devices: 30.9 us -> 34.4 us
  blocking collectives: 26.5 us -> 23.8 us
  local copies, waits for them, and re-layouts: 2.64 us -> 1.42 us
    pallas_call x19 -> x12, Pallas kernels: 18.4 us -> 14.6 us  [call(): pl.pallas_call(kernel, out_shape=shapes, in_specs=[pl.BlockSpec(memory_sp...]
    all_to_all x1, blocking collectives: 26.5 us -> 23.8 us  [on_device(): lax.all_to_all(outgoing.reshape(devices, 1, LANES), ('blk', 'gz'), 0, 0,...]
    ppermute x2 -> x3, starting transfers between devices: 0.4 us -> 2.26 us  [the longest x1 2.1 us: on_device(): taken = lax.ppermute(given, 'blk', swap('blk', 0))]
    ppermute x4, starting transfers between devices: 14.8 us -> 16.2 us  [x_halo(): return (lax.ppermute(block, 'blk', swap('blk', 0)), far)]
    unnamed x14 -> x8, local copies, waits for them, and re-layouts: 2.64 us -> 1.42 us
  transfers between devices with their start and end apart: 18 -> 19, of which waited for: 2 -> 2; matrix products, arithmetic and copies ran while one was open for 0% -> 0% of each run, Pallas kernels for 15% -> 12%
where the time goes in v4:
time: 76.8 us; the launch traced here: 76.7 us
  starting transfers between devices  34.4 us (45%)
  blocking collectives  23.8 us (31%)
  Pallas kernels  14.6 us (19%)
  waiting for transfers between devices  1.59 us (2%)
  local copies, waits for them, and re-layouts  1.42 us (2%)
  between operations  0.86 us (1%)
    all_to_all x1, blocking collectives, on_device(): lax.all_to_all(outgoing.reshape(devices, 1, LANES), ('blk', 'gz'), 0, 0,...  23.8 us
    ppermute x4, starting transfers between devices, x_halo(): return (lax.ppermute(block, 'blk', swap('blk', 0)), far)  16.2 us
    pallas_call x12, Pallas kernels, call(): pl.pallas_call(kernel, out_shape=shapes, in_specs=[pl.BlockSpec(memory_sp...  14.6 us
    ppermute x4, starting transfers between devices, z_halo(): lax.ppermute(face_b, 'gz', swap('gz', 1))  7.6 us
    ppermute x4, starting transfers between devices, z_halo(): lax.ppermute(face_a, 'gz', swap('gz', 0))  5.19 us
    ppermute x4, starting transfers between devices, x_halo(): far = lax.ppermute(block, 'blk', swap('blk', 1))  3.15 us
    ppermute x1, starting transfers between devices, on_device(): taken = lax.ppermute(given, 'blk', swap('blk', 0))  2.1 us
  transfers between devices with their start and end apart: 19, of which 2 were waited for; matrix products, arithmetic and copies ran while one was open for 0% of the time, Pallas kernels for 12%

profile of v4, /device:TPU:1, one launch (start us, length us, event | category | flops | bytes accessed | tf_op | source)
XLA Modules:
  0.0 76.7 jit_solution(14347407179753617298)
XLA Ops:
  0.6 1.3 %shard_map.77 = (f32[12,64,128]{2,1,0:T(8,128)S(1)}, f32[6,64,128]{2,1,0:T(8,128)S(1)}, f32[48,128]{1,0:T(8,128)S(1)}, f32[48,128]{1,0:T(8,128)S(1)}) custom-call(f32[6,64,128]{2,1,0:T(8,128)} %hartree.1, f32[6,64,128]{2,1,0:T(8,128)} %density.1, f32[6,64,128]{2,1,0:T(8,128)} %charge.1), custom_call_target="tpu_custom_call" | custom-call | bytes 1228800 | tf_op jit(solution)/shard_map/pallas_call | solution.py:630
  1.9 2.7 %collective-permute-start.1 = (f32[12,64,128]{2,1,0:T(8,128)S(1)}, f32[12,64,128]{2,1,0:T(8,128)S(1)}, u32[]{:S(2)}, u32[]{:S(2)}) collective-permute-start(f32[12,64,128]{2,1,0:T(8,128)S(1)} %get-tuple-element.50.both), channel_id=1, source_target_pairs={{0,252},{4,8},{8,4},{12,16},{16,12},{20,24},{24,20},{28,32},{32,28... | collective-permute-start | bytes 1179656 | tf_op jit(solution)/shard_map/ppermute | solution.py:652
  4.6 6.4 %collective-permute-start = (f32[12,64,128]{2,1,0:T(8,128)S(1)}, f32[12,64,128]{2,1,0:T(8,128)S(1)}, u32[]{:S(2)}, u32[]{:S(2)}) collective-permute-start(f32[12,64,128]{2,1,0:T(8,128)S(1)} %get-tuple-element.50.both), channel_id=1, source_target_pairs={{0,4},{4,0},{8,12},{12,8},{16,20},{20,16},{24,28},{28,24},{32,36},... | collective-permute-start | bytes 1179656 | tf_op jit(solution)/shard_map/ppermute | solution.py:653
  11.0 1.3 %collective-permute-start.2 = (f32[48,128]{1,0:T(8,128)S(1)}, f32[48,128]{1,0:T(8,128)S(1)}, u32[]{:S(2)}, u32[]{:S(2)}) collective-permute-start(f32[48,128]{1,0:T(8,128)S(1)} %get-tuple-element.53), channel_id=1, source_target_pairs={{0,1},{1,0},{2,3},{3,2},{4,5},{5,4},{6,7},{7,6},{8,9},{9,8},{10,11... | collective-permute-start | bytes 73736 | tf_op jit(solution)/shard_map/ppermute | solution.py:657
  12.3 1.9 %collective-permute-start.3 = (f32[48,128]{1,0:T(8,128)S(1)}, f32[48,128]{1,0:T(8,128)S(1)}, u32[]{:S(2)}, u32[]{:S(2)}) collective-permute-start(f32[48,128]{1,0:T(8,128)S(1)} %get-tuple-element.54), channel_id=1, source_target_pairs={{0,3},{1,2},{2,1},{3,0},{4,7},{5,6},{6,5},{7,4},{8,11},{9,10},{10,... | collective-permute-start | bytes 73736 | tf_op jit(solution)/shard_map/ppermute | solution.py:657
  14.2 1.4 %copy-done = f32[8,6,64,128]{3,2,1,0:T(8,128)S(1)} copy-done((f32[8,6,64,128]{3,2,1,0:T(8,128)S(1)}, f32[8,6,64,128]{3,2,1,0:T(8,128)}, u32[]{:S(2)}) %copy-start) | copy-done | bytes 1572888
  15.6 1.3 %shard_map.78 = (f32[6,64,128]{2,1,0:T(8,128)S(1)}, f32[40,128]{1,0:T(8,128)S(1)}) custom-call(f32[12,64,128]{2,1,0:T(8,128)S(1)} %get-tuple-element.50.both, f32[6,64,128]{2,1,0:T(8,128)S(1)} %get-tuple-element.51.charge, f32[8,6,64,128]{3,2,1,0:T(8,128)S(1)} %copy-done), custom_call_target="tpu_custom_call" | custom-call | flops 14745600 | bytes 2379776 | tf_op jit(solution)/shard_map/pallas_call | solution.py:630
  16.9 0.0 collective-permute-done.2.z_first
  16.9 0.0 collective-permute-done.3.z_second
  16.9 0.0 collective-permute-done.1.far
  16.9 0.0 collective-permute-done.near
  16.9 0.4 shard_map.79
  17.4 0.1 collective-permute-start.5
  17.5 4.6 %collective-permute-start.4 = (f32[6,64,128]{2,1,0:T(8,128)S(1)}, f32[6,64,128]{2,1,0:T(8,128)S(1)}, u32[]{:S(2)}, u32[]{:S(2)}) collective-permute-start(f32[6,64,128]{2,1,0:T(8,128)S(1)} %get-tuple-element.59.vector.prior.v0), channel_id=1, source_target_pairs={{0,4},{4,0},{8,12},{12,8},{16,20},{20,16},{24,28},{28,24},{32,36},... | collective-permute-start | bytes 589832 | tf_op jit(solution)/shard_map/ppermute | solution.py:653
  22.1 1.3 %collective-permute-start.6 = (f32[24,128]{1,0:T(8,128)S(1)}, f32[24,128]{1,0:T(8,128)S(1)}, u32[]{:S(2)}, u32[]{:S(2)}) collective-permute-start(f32[24,128]{1,0:T(8,128)S(1)} %get-tuple-element.61), channel_id=1, source_target_pairs={{0,1},{1,0},{2,3},{3,2},{4,5},{5,4},{6,7},{7,6},{8,9},{9,8},{10,11... | collective-permute-start | bytes 36872 | tf_op jit(solution)/shard_map/ppermute | solution.py:657
  23.4 1.9 %collective-permute-start.7 = (f32[24,128]{1,0:T(8,128)S(1)}, f32[24,128]{1,0:T(8,128)S(1)}, u32[]{:S(2)}, u32[]{:S(2)}) collective-permute-start(f32[24,128]{1,0:T(8,128)S(1)} %get-tuple-element.62), channel_id=1, source_target_pairs={{0,3},{1,2},{2,1},{3,0},{4,7},{5,6},{6,5},{7,4},{8,11},{9,10},{10,... | collective-permute-start | bytes 36872 | tf_op jit(solution)/shard_map/ppermute | solution.py:657
  25.3 2.2 %shard_map.80 = (f32[6,64,128]{2,1,0:T(8,128)S(1)}, f32[88,128]{1,0:T(8,128)S(1)}, f32[8,128]{1,0:T(8,128)S(1)}) custom-call(f32[6,64,128]{2,1,0:T(8,128)S(1)} %get-tuple-element.59.vector.prior.v0, f32[12,64,128]{2,1,0:T(8,128)S(1)} %get-tuple-element.50.both, f32[8,6,64,128]{3,2,1,0:T(8,128)S(1)} %copy-done.1, f32[8,6,64,128]{3,2,1,0:T(8,128)S(1)} %copy-done.2), custom_call_target="tpu_custom_call" | custom-call | flops 14745600 | bytes 3981312 | tf_op jit(solution)/shard_map/pallas_call | solution.py:630
  27.4 0.0 collective-permute-done.6.z_first
  27.4 0.0 collective-permute-done.7.z_second
  27.5 0.0 collective-permute-done.5.far
  27.5 0.0 collective-permute-done.4.near
  27.5 0.4 shard_map.81
  27.9 0.1 collective-permute-start.9
  28.0 3.0 %collective-permute-start.8 = (f32[6,64,128]{2,1,0:T(8,128)S(1)}, f32[6,64,128]{2,1,0:T(8,128)S(1)}, u32[]{:S(2)}, u32[]{:S(2)}) collective-permute-start(f32[6,64,128]{2,1,0:T(8,128)S(1)} %get-tuple-element.67.vector.prior.v1), channel_id=1, source_target_pairs={{0,4},{4,0},{8,12},{12,8},{16,20},{20,16},{24,28},{28,24},{32,36},... | collective-permute-start | bytes 589832 | tf_op jit(solution)/shard_map/ppermute | solution.py:653
  31.0 1.3 %collective-permute-start.10 = (f32[24,128]{1,0:T(8,128)S(1)}, f32[24,128]{1,0:T(8,128)S(1)}, u32[]{:S(2)}, u32[]{:S(2)}) collective-permute-start(f32[24,128]{1,0:T(8,128)S(1)} %get-tuple-element.69), channel_id=1, source_target_pairs={{0,1},{1,0},{2,3},{3,2},{4,5},{5,4},{6,7},{7,6},{8,9},{9,8},{10,11... | collective-permute-start | bytes 36872 | tf_op jit(solution)/shard_map/ppermute | solution.py:657
  32.3 1.9 %collective-permute-start.11 = (f32[24,128]{1,0:T(8,128)S(1)}, f32[24,128]{1,0:T(8,128)S(1)}, u32[]{:S(2)}, u32[]{:S(2)}) collective-permute-start(f32[24,128]{1,0:T(8,128)S(1)} %get-tuple-element.70), channel_id=1, source_target_pairs={{0,3},{1,2},{2,1},{3,0},{4,7},{5,6},{6,5},{7,4},{8,11},{9,10},{10,... | collective-permute-start | bytes 36872 | tf_op jit(solution)/shard_map/ppermute | solution.py:657
  34.2 2.9 %shard_map.82 = (f32[6,64,128]{2,1,0:T(8,128)S(1)}, f32[6,64,128]{2,1,0:T(8,128)S(1)}, f32[72,128]{1,0:T(8,128)S(1)}, f32[8,128]{1,0:T(8,128)S(1)}) custom-call(f32[6,64,128]{2,1,0:T(8,128)S(1)} %get-tuple-element.59.vector.prior.v0, f32[6,64,128]{2,1,0:T(8,128)S(1)} %get-tuple-element.67.vector.prior.v1, f32[12,64,128]{2,1,0:T(8,128)S(1)} %get-tuple-element.50.both, ...), custom_call_target="tpu_custom_call" | custom-call | flops 14745600 | bytes 5398528 | tf_op jit(solution)/shard_map/pallas_call | solution.py:630
  37.1 0.0 collective-permute-done.10.z_first
  37.1 0.0 collective-permute-done.9.far
  37.1 0.0 collective-permute-done.8.near
  37.1 0.4 shard_map.83
  37.6 0.3 collective-permute-start.13
  37.9 2.3 %collective-permute-start.12 = (f32[6,64,128]{2,1,0:T(8,128)S(1)}, f32[6,64,128]{2,1,0:T(8,128)S(1)}, u32[]{:S(2)}, u32[]{:S(2)}) collective-permute-start(f32[6,64,128]{2,1,0:T(8,128)S(1)} %get-tuple-element.75.vector.prior.v2), channel_id=1, source_target_pairs={{0,4},{4,0},{8,12},{12,8},{16,20},{20,16},{24,28},{28,24},{32,36},... | collective-permute-start | bytes 589832 | tf_op jit(solution)/shard_map/ppermute | solution.py:653
  40.1 1.3 %collective-permute-start.14 = (f32[24,128]{1,0:T(8,128)S(1)}, f32[24,128]{1,0:T(8,128)S(1)}, u32[]{:S(2)}, u32[]{:S(2)}) collective-permute-start(f32[24,128]{1,0:T(8,128)S(1)} %get-tuple-element.78), channel_id=1, source_target_pairs={{0,1},{1,0},{2,3},{3,2},{4,5},{5,4},{6,7},{7,6},{8,9},{9,8},{10,11... | collective-permute-start | bytes 36872 | tf_op jit(solution)/shard_map/ppermute | solution.py:657
  41.4 1.9 %collective-permute-start.15 = (f32[24,128]{1,0:T(8,128)S(1)}, f32[24,128]{1,0:T(8,128)S(1)}, u32[]{:S(2)}, u32[]{:S(2)}) collective-permute-start(f32[24,128]{1,0:T(8,128)S(1)} %get-tuple-element.79), channel_id=1, source_target_pairs={{0,3},{1,2},{2,1},{3,0},{4,7},{5,6},{6,5},{7,4},{8,11},{9,10},{10,... | collective-permute-start | bytes 36872 | tf_op jit(solution)/shard_map/ppermute | solution.py:657
  43.3 1.4 %shard_map.84 = (f32[6,64,128]{2,1,0:T(8,128)S(1)}, f32[40,128]{1,0:T(8,128)S(1)}, f32[8,128]{1,0:T(8,128)S(1)}) custom-call(f32[6,64,128]{2,1,0:T(8,128)S(1)} %get-tuple-element.67.vector.prior.v1, f32[6,64,128]{2,1,0:T(8,128)S(1)} %get-tuple-element.75.vector.prior.v2, f32[12,64,128]{2,1,0:T(8,128)S(1)} %get-tuple-element.50.both, ...), custom_call_target="tpu_custom_call" | custom-call | flops 14745600 | bytes 4349952 | tf_op jit(solution)/shard_map/pallas_call | solution.py:630
  44.8 0.7 collective-permute-done.15.z_second
  45.5 0.0 collective-permute-done.13.far
  45.5 0.0 collective-permute-done.12.near
  45.5 0.4 shard_map.85
  45.9 0.1 collective-permute-start.16
  46.0 0.1 collective-permute-start.17
  46.1 1.4 %shard_map.86 = (f32[1,128]{1,0:T(1,128)S(1)}, f32[1,128]{1,0:T(1,128)S(1)}, f32[8,128]{1,0:T(8,128)S(1)}) custom-call(f32[6,64,128]{2,1,0:T(8,128)S(1)} %get-tuple-element.75.vector.prior.v2, f32[6,64,128]{2,1,0:T(8,128)S(1)} %get-tuple-element.84.vector.own.v3, f32[12,64,128]{2,1,0:T(8,128)S(1)} %get-tuple-element.50.both, ...), custom_call_target="tpu_custom_call" | custom-call | flops 14745600 | bytes 4072448 | tf_op jit(solution)/shard_map/pallas_call | solution.py:630
  47.4 2.1 %collective-permute-start.18 = (f32[1,128]{1,0:T(1,128)S(1)}, f32[1,128]{1,0:T(1,128)S(1)}, u32[]{:S(2)}, u32[]{:S(2)}) collective-permute-start(f32[1,128]{1,0:T(1,128)S(1)} %get-tuple-element.94), channel_id=1, source_target_pairs={{0,4},{4,0},{8,12},{12,8},{16,20},{20,16},{24,28},{28,24},{32,36},... | collective-permute-start | bytes 1544 | tf_op jit(solution)/shard_map/ppermute | solution.py:726
  49.5 0.8 %collective-permute-done.18.taken = f32[1,128]{1,0:T(1,128)S(1)} collective-permute-done((f32[1,128]{1,0:T(1,128)S(1)}, f32[1,128]{1,0:T(1,128)S(1)}, u32[]{:S(2)}, u32[]{:S(2)}) %collective-permute-start.18) | collective-permute-done | bytes 544 | tf_op jit(solution)/shard_map/ppermute | solution.py:726
  50.3 0.7 shard_map.87
  51.1 23.8 %all_to_all.5 = f32[256,1,128]{2,1,0:T(1,128)S(1)} all-to-all(f32[256,1,128]{2,1,0:T(1,128)S(1)} %bitcast.5), channel_id=1, replica_groups=mesh['blk'=64,'gz'=4] {'blk','gz'}, dimensions={0} | all-to-all | bytes 262144 | tf_op jit(solution)/shard_map/all_to_all | solution.py:730
  74.9 1.7 %shard_map.88 = (f32[6,64,128]{2,1,0:T(8,128)}, f32[6,64,128]{2,1,0:T(8,128)}) custom-call(f32[256,128]{1,0:T(8,128)S(1)} %bitcast.4, f32[12,64,128]{2,1,0:T(8,128)S(1)} %get-tuple-element.50.both, f32[6,64,128]{2,1,0:T(8,128)S(1)} %get-tuple-element.76.grad, f32[6,64,128]{2,1,0:T(8,128)S(1)} %get-tuple-element.59.vector.prior.v0, ...), custom_call_target="tpu_custom_call" | custom-call | flops 14745600 | bytes 5046272 | tf_op jit(solution)/shard_map/pallas_call | solution.py:630
  (11 shorter events, 0.0 us)
Async XLA Ops:
  1.9 15.0 %collective-permute-start.1 = (f32[12,64,128]{2,1,0:T(8,128)S(1)}, f32[12,64,128]{2,1,0:T(8,128)S(1)}, u32[]{:S(2)}, u32[]{:S(2)}) collective-permute-start(f32[12,64,128]{2,1,0:T(8,128)S(1)} %get-tuple-element.50.both), channel_id=1, source_target_pairs={{0,252},{4,8},{8,4},{12,16},{16,12},{20,24},{24,20},{28,32},{32,28... | collective-permute-start | bytes 1179656 | tf_op jit(solution)/shard_map/ppermute | solution.py:652
  4.6 12.3 %collective-permute-start = (f32[12,64,128]{2,1,0:T(8,128)S(1)}, f32[12,64,128]{2,1,0:T(8,128)S(1)}, u32[]{:S(2)}, u32[]{:S(2)}) collective-permute-start(f32[12,64,128]{2,1,0:T(8,128)S(1)} %get-tuple-element.50.both), channel_id=1, source_target_pairs={{0,4},{4,0},{8,12},{12,8},{16,20},{20,16},{24,28},{28,24},{32,36},... | collective-permute-start | bytes 1179656 | tf_op jit(solution)/shard_map/ppermute | solution.py:653
  11.0 5.9 %collective-permute-start.2 = (f32[48,128]{1,0:T(8,128)S(1)}, f32[48,128]{1,0:T(8,128)S(1)}, u32[]{:S(2)}, u32[]{:S(2)}) collective-permute-start(f32[48,128]{1,0:T(8,128)S(1)} %get-tuple-element.53), channel_id=1, source_target_pairs={{0,1},{1,0},{2,3},{3,2},{4,5},{5,4},{6,7},{7,6},{8,9},{9,8},{10,11... | collective-permute-start | bytes 73736 | tf_op jit(solution)/shard_map/ppermute | solution.py:657
  12.3 4.6 %collective-permute-start.3 = (f32[48,128]{1,0:T(8,128)S(1)}, f32[48,128]{1,0:T(8,128)S(1)}, u32[]{:S(2)}, u32[]{:S(2)}) collective-permute-start(f32[48,128]{1,0:T(8,128)S(1)} %get-tuple-element.54), channel_id=1, source_target_pairs={{0,3},{1,2},{2,1},{3,0},{4,7},{5,6},{6,5},{7,4},{8,11},{9,10},{10,... | collective-permute-start | bytes 73736 | tf_op jit(solution)/shard_map/ppermute | solution.py:657
  14.2 1.4 %copy-start = (f32[8,6,64,128]{3,2,1,0:T(8,128)S(1)}, f32[8,6,64,128]{3,2,1,0:T(8,128)}, u32[]{:S(2)}) copy-start(f32[8,6,64,128]{3,2,1,0:T(8,128)} %steps.11) | copy-start | bytes 4718596
  15.6 9.6 %copy-start.1 = (f32[8,6,64,128]{3,2,1,0:T(8,128)S(1)}, f32[8,6,64,128]{3,2,1,0:T(8,128)}, u32[]{:S(2)}) copy-start(f32[8,6,64,128]{3,2,1,0:T(8,128)} %steps.11) | copy-start | bytes 4718596
  15.6 9.6 %copy-start.2 = (f32[8,6,64,128]{3,2,1,0:T(8,128)S(1)}, f32[8,6,64,128]{3,2,1,0:T(8,128)}, u32[]{:S(2)}) copy-start(f32[8,6,64,128]{3,2,1,0:T(8,128)} %changes.9) | copy-start | bytes 4718596
  17.4 10.1 %collective-permute-start.5 = (f32[6,64,128]{2,1,0:T(8,128)S(1)}, f32[6,64,128]{2,1,0:T(8,128)S(1)}, u32[]{:S(2)}, u32[]{:S(2)}) collective-permute-start(f32[6,64,128]{2,1,0:T(8,128)S(1)} %get-tuple-element.59.vector.prior.v0), channel_id=1, source_target_pairs={{0,252},{4,8},{8,4},{12,16},{16,12},{20,24},{24,20},{28,32},{32,28... | collective-permute-start | bytes 589832 | tf_op jit(solution)/shard_map/ppermute | solution.py:652
  17.5 10.0 %collective-permute-start.4 = (f32[6,64,128]{2,1,0:T(8,128)S(1)}, f32[6,64,128]{2,1,0:T(8,128)S(1)}, u32[]{:S(2)}, u32[]{:S(2)}) collective-permute-start(f32[6,64,128]{2,1,0:T(8,128)S(1)} %get-tuple-element.59.vector.prior.v0), channel_id=1, source_target_pairs={{0,4},{4,0},{8,12},{12,8},{16,20},{20,16},{24,28},{28,24},{32,36},... | collective-permute-start | bytes 589832 | tf_op jit(solution)/shard_map/ppermute | solution.py:653
  22.1 5.4 %collective-permute-start.6 = (f32[24,128]{1,0:T(8,128)S(1)}, f32[24,128]{1,0:T(8,128)S(1)}, u32[]{:S(2)}, u32[]{:S(2)}) collective-permute-start(f32[24,128]{1,0:T(8,128)S(1)} %get-tuple-element.61), channel_id=1, source_target_pairs={{0,1},{1,0},{2,3},{3,2},{4,5},{5,4},{6,7},{7,6},{8,9},{9,8},{10,11... | collective-permute-start | bytes 36872 | tf_op jit(solution)/shard_map/ppermute | solution.py:657
  23.4 10.9 %copy-start.3 = (f32[6,64,128]{2,1,0:T(8,128)S(1)}, f32[6,64,128]{2,1,0:T(8,128)}, u32[]{:S(2)}) copy-start(f32[6,64,128]{2,1,0:T(8,128)} %potential.1) | copy-start | bytes 589828
  23.4 4.1 %collective-permute-start.7 = (f32[24,128]{1,0:T(8,128)S(1)}, f32[24,128]{1,0:T(8,128)S(1)}, u32[]{:S(2)}, u32[]{:S(2)}) collective-permute-start(f32[24,128]{1,0:T(8,128)S(1)} %get-tuple-element.62), channel_id=1, source_target_pairs={{0,3},{1,2},{2,1},{3,0},{4,7},{5,6},{6,5},{7,4},{8,11},{9,10},{10,... | collective-permute-start | bytes 36872 | tf_op jit(solution)/shard_map/ppermute | solution.py:657
  27.9 9.2 %collective-permute-start.9 = (f32[6,64,128]{2,1,0:T(8,128)S(1)}, f32[6,64,128]{2,1,0:T(8,128)S(1)}, u32[]{:S(2)}, u32[]{:S(2)}) collective-permute-start(f32[6,64,128]{2,1,0:T(8,128)S(1)} %get-tuple-element.67.vector.prior.v1), channel_id=1, source_target_pairs={{0,252},{4,8},{8,4},{12,16},{16,12},{20,24},{24,20},{28,32},{32,28... | collective-permute-start | bytes 589832 | tf_op jit(solution)/shard_map/ppermute | solution.py:652
  28.0 9.1 %collective-permute-start.8 = (f32[6,64,128]{2,1,0:T(8,128)S(1)}, f32[6,64,128]{2,1,0:T(8,128)S(1)}, u32[]{:S(2)}, u32[]{:S(2)}) collective-permute-start(f32[6,64,128]{2,1,0:T(8,128)S(1)} %get-tuple-element.67.vector.prior.v1), channel_id=1, source_target_pairs={{0,4},{4,0},{8,12},{12,8},{16,20},{20,16},{24,28},{28,24},{32,36},... | collective-permute-start | bytes 589832 | tf_op jit(solution)/shard_map/ppermute | solution.py:653
  31.0 6.1 %collective-permute-start.10 = (f32[24,128]{1,0:T(8,128)S(1)}, f32[24,128]{1,0:T(8,128)S(1)}, u32[]{:S(2)}, u32[]{:S(2)}) collective-permute-start(f32[24,128]{1,0:T(8,128)S(1)} %get-tuple-element.69), channel_id=1, source_target_pairs={{0,1},{1,0},{2,3},{3,2},{4,5},{5,4},{6,7},{7,6},{8,9},{9,8},{10,11... | collective-permute-start | bytes 36872 | tf_op jit(solution)/shard_map/ppermute | solution.py:657
  32.3 4.8 %collective-permute-start.11 = (f32[24,128]{1,0:T(8,128)S(1)}, f32[24,128]{1,0:T(8,128)S(1)}, u32[]{:S(2)}, u32[]{:S(2)}) collective-permute-start(f32[24,128]{1,0:T(8,128)S(1)} %get-tuple-element.70), channel_id=1, source_target_pairs={{0,3},{1,2},{2,1},{3,0},{4,7},{5,6},{6,5},{7,4},{8,11},{9,10},{10,... | collective-permute-start | bytes 36872 | tf_op jit(solution)/shard_map/ppermute | solution.py:657
  37.6 7.9 %collective-permute-start.13 = (f32[6,64,128]{2,1,0:T(8,128)S(1)}, f32[6,64,128]{2,1,0:T(8,128)S(1)}, u32[]{:S(2)}, u32[]{:S(2)}) collective-permute-start(f32[6,64,128]{2,1,0:T(8,128)S(1)} %get-tuple-element.75.vector.prior.v2), channel_id=1, source_target_pairs={{0,252},{4,8},{8,4},{12,16},{16,12},{20,24},{24,20},{28,32},{32,28... | collective-permute-start | bytes 589832 | tf_op jit(solution)/shard_map/ppermute | solution.py:652
  37.9 7.6 %collective-permute-start.12 = (f32[6,64,128]{2,1,0:T(8,128)S(1)}, f32[6,64,128]{2,1,0:T(8,128)S(1)}, u32[]{:S(2)}, u32[]{:S(2)}) collective-permute-start(f32[6,64,128]{2,1,0:T(8,128)S(1)} %get-tuple-element.75.vector.prior.v2), channel_id=1, source_target_pairs={{0,4},{4,0},{8,12},{12,8},{16,20},{20,16},{24,28},{28,24},{32,36},... | collective-permute-start | bytes 589832 | tf_op jit(solution)/shard_map/ppermute | solution.py:653
  40.1 4.6 %collective-permute-start.14 = (f32[24,128]{1,0:T(8,128)S(1)}, f32[24,128]{1,0:T(8,128)S(1)}, u32[]{:S(2)}, u32[]{:S(2)}) collective-permute-start(f32[24,128]{1,0:T(8,128)S(1)} %get-tuple-element.78), channel_id=1, source_target_pairs={{0,1},{1,0},{2,3},{3,2},{4,5},{5,4},{6,7},{7,6},{8,9},{9,8},{10,11... | collective-permute-start | bytes 36872 | tf_op jit(solution)/shard_map/ppermute | solution.py:657
  41.4 4.1 %collective-permute-start.15 = (f32[24,128]{1,0:T(8,128)S(1)}, f32[24,128]{1,0:T(8,128)S(1)}, u32[]{:S(2)}, u32[]{:S(2)}) collective-permute-start(f32[24,128]{1,0:T(8,128)S(1)} %get-tuple-element.79), channel_id=1, source_target_pairs={{0,3},{1,2},{2,1},{3,0},{4,7},{5,6},{6,5},{7,4},{8,11},{9,10},{10,... | collective-permute-start | bytes 36872 | tf_op jit(solution)/shard_map/ppermute | solution.py:657
  45.9 4.5 %collective-permute-start.16 = (f32[6,64,128]{2,1,0:T(8,128)S(1)}, f32[6,64,128]{2,1,0:T(8,128)S(1)}, u32[]{:S(2)}, u32[]{:S(2)}) collective-permute-start(f32[6,64,128]{2,1,0:T(8,128)S(1)} %get-tuple-element.84.vector.own.v3), channel_id=1, source_target_pairs={{0,4},{4,8},{8,12},{12,16},{16,20},{20,24},{24,28},{28,32},{32,36}... | collective-permute-start | bytes 589832 | tf_op jit(solution)/shard_map/ppermute | solution.py:717
  46.0 4.4 %collective-permute-start.17 = (f32[24,128]{1,0:T(8,128)S(1)}, f32[24,128]{1,0:T(8,128)S(1)}, u32[]{:S(2)}, u32[]{:S(2)}) collective-permute-start(f32[24,128]{1,0:T(8,128)S(1)} %get-tuple-element.85), channel_id=1, source_target_pairs={{0,1},{1,2},{2,3},{3,0},{4,5},{5,6},{6,7},{7,4},{8,9},{9,10},{10,1... | collective-permute-start | bytes 36872 | tf_op jit(solution)/shard_map/ppermute | solution.py:718
  47.4 2.9 %collective-permute-start.18 = (f32[1,128]{1,0:T(1,128)S(1)}, f32[1,128]{1,0:T(1,128)S(1)}, u32[]{:S(2)}, u32[]{:S(2)}) collective-permute-start(f32[1,128]{1,0:T(1,128)S(1)} %get-tuple-element.94), channel_id=1, source_target_pairs={{0,4},{4,0},{8,12},{12,8},{16,20},{20,16},{24,28},{28,24},{32,36},... | collective-permute-start | bytes 1544 | tf_op jit(solution)/shard_map/ppermute | solution.py:726

commit v5 on v4

--- a/solution.py
+++ b/solution.py
@@ -124,26 +124,26 @@
     return lower, upper
 
 
-def edge_plane(i, left, right, faces):
+def side_plane(i, block, below, rows=slice(None)):
     total = None
     for k, weight in enumerate(coeffs, 1):
-        terms = []
-        if i - k < 0:
-            terms.append(left[i - k + REACH])
-        if right is not None and i + k >= REACH:
-            terms.append(right[i + k - REACH])
-        for term in terms:
-            total = weight * term if total is None else total + weight * term
+        layer = i - k + REACH if below else i + k - REACH
+        if 0 <= layer < REACH:
+            term = weight * block[layer, rows, :]
+            total = term if total is None else total + term
+    return total
+
+
+def z_plane(i, faces, tiles=8):
     lane = lane_ids((8, LANES))
     lower, upper = (face[8 * (i // 2) : 8 * (i // 2) + 8] for face in faces)
-    tiles = []
-    for b in range(total.shape[0] // 8):
+    out = []
+    for b in range(tiles):
         j = 8 * (i % 2) + b
         tile = jnp.where(lane < 8, pltpu.roll(lower, (LANES - 8 * j) % LANES, 1), 0.0)
-        if right is not None:
-            tile = jnp.where(lane >= LANES - 8, pltpu.roll(upper, (2 * LANES - 8 - 8 * j) % LANES, 1), tile)
-        tiles.append(tile)
-    return total + jnp.concatenate(tiles, axis=0)
+        tile = jnp.where(lane >= LANES - 8, pltpu.roll(upper, (2 * LANES - 8 - 8 * j) % LANES, 1), tile)
+        out.append(tile)
+    return jnp.concatenate(out, axis=0)
 
 
 def fill_ext(own, ext):
@@ -184,16 +184,16 @@
     return jnp.where(odd, first, second), jnp.where(odd, second, first)
 
 
-def with_sides(near, far, body):
+def with_sides(body):
     odd = is_odd("blk")
 
     @pl.when(odd)
     def _():
-        body(near, far)
+        body(True, False)
 
     @pl.when(jnp.logical_not(odd))
     def _():
-        body(far, near)
+        body(False, True)
 
 
 def fold(hi, lo, axis, steps):
@@ -272,19 +272,43 @@
         out[i] = moved if prior is None else 2.0 * moved - prior[i]
 
 
-def edge_kernel(gain, last, inner, near, far, z_first, z_second, out, *sent):
+def near_kernel(gain, inner, near, z_first, z_second, out):
     faces = edge_faces(*by_side(z_first[0:24, :], z_second[0:24, :]))
 
-    def body(left, right):
+    def body(near_below, far_below):
         for i in range(REACH):
-            out[i] = inner[i] + gain * edge_plane(i, left, right, faces)
-
-    with_sides(near, far, body)
-    packed = pack_faces(out, 0)
-    if last:
-        sent[0][...] = packed[1]
-    else:
-        sent[0][...], sent[1][...] = by_partner(*packed)
+            out[i] = inner[i] + gain * (side_plane(i, near, near_below) + z_plane(i, faces))
+
+    with_sides(body)
+
+
+def far_kernel(gain, inner, far, out):
+    def body(near_below, far_below):
+        for i in range(REACH):
+            out[i] = inner[i] + gain * side_plane(i, far, far_below)
+
+    with_sides(body)
+
+
+def last_far_kernel(gain, inner, far, out, to_near, to_far):
+    half = out.shape[1] // 2
+
+    def body(near_below, far_below):
+        for i in range(REACH):
+            plane = inner[i] + gain * side_plane(i, far, far_below)
+            out[i] = plane
+            for ref, below in ((to_near, near_below), (to_far, far_below)):
+                ref[i] = plane[:half] if below else plane[half:]
+
+    with_sides(body)
+
+
+def pack_kernel(block, face_a, face_b):
+    face_a[...], face_b[...] = by_partner(*pack_faces(block, 0))
+
+
+def pack_upper_kernel(block, face):
+    face[...] = pack_faces(block, 0)[1]
 
 
 def store(rows, base, values):
@@ -340,11 +364,11 @@
     fill_ext(density, ext)
     faces = edge_faces(*by_side(z_first[24:48, :], z_second[24:48, :]))
 
-    def body(left, right):
+    def body(near_below, far_below):
         for i in range(REACH):
-            grad[i] = edge_plane(i, left, right, faces)
-
-    with_sides(near.at[pl.ds(REACH, REACH)], far.at[pl.ds(REACH, REACH)], body)
+            grad[i] = side_plane(i, near, near_below) + side_plane(i, far, far_below) + z_plane(i, faces)
+
+    with_sides(body)
     for i in range(REACH):
         lap, rho = inner_plane(i, density, ext)
         power = jnp.exp(jnp.log(rho) * (4.0 / 3.0))
@@ -448,23 +472,47 @@
     inner[0:1, :], inner[1:2, :] = fold_rows((hi, accs[0][1] + accs[1][1] + err))
 
 
-def send_kernel(own, left, z_left, inner, kept, taken, out):
+def couple(own, block, below, acc):
+    half = own.shape[1] // 2
+    for i in range(REACH):
+        product = own[i, half:, :] * side_plane(i, block, True) if below else own[i, :half, :] * side_plane(i, block, False)
+        for b in range(half // 8):
+            acc = add_tile(acc, product[8 * b : 8 * b + 8])
+    return acc
+
+
+def couple_kernel(own, near, z_left, inner, kept, taken, row, part):
+    zero = jnp.zeros((8, LANES), jnp.float32)
     faces = edge_faces(z_left[...], None)
+    acc = (zero, zero)
+    for i in range(REACH):
+        product = own[i] * z_plane(i, faces)
+        for b in range(8):
+            acc = add_tile(acc, product[8 * b : 8 * b + 8])
+    z_rows = fold_rows(acc)
+
+    def body(near_below, far_below):
+        sides = df_add(fold_rows(couple(own, near, near_below, (zero, zero))), z_rows)
+        part[0:1, :], part[1:2, :] = df_add(df_scale(sides, -2.0 / SHIFT), (inner[0:1, :], inner[1:2, :]))
+
+    with_sides(body)
+    lane = lane_ids((1, LANES))
+    total, err = two_sum(kept[...], taken[...])
+    low_lane = (lane >= MOM_LANE + 7) & (lane < MOM_LANE + 14) & is_odd("blk")
+    row[...] = jnp.where(low_lane, total + pltpu.roll(err, 7, 1), total)
+
+
+def send_kernel(own, far, part, row, out):
     zero = jnp.zeros((8, LANES), jnp.float32)
-    accs = [(zero, zero) for _ in range(2)]
-    for i in range(REACH):
-        product = own[i] * edge_plane(i, left, None, faces)
-        for b in range(8):
-            accs[b % 2] = add_tile(accs[b % 2], product[8 * b : 8 * b + 8])
-    hi, err = two_sum(accs[0][0], accs[1][0])
-    coupling = fold_rows((hi, accs[0][1] + accs[1][1] + err))
-    hi, lo = fold_lanes(*df_add(df_scale(coupling, -2.0 / SHIFT), (inner[0:1, :], inner[1:2, :])))
-    lane = lane_ids((1, LANES))
-    row, err = two_sum(kept[...], taken[...])
-    low_lane = (lane >= MOM_LANE + 7) & (lane < MOM_LANE + 14) & is_odd("blk")
-    row = jnp.where(low_lane, row + pltpu.roll(err, 7, 1), row)
-    row = jnp.where(lane == HALF, hi, jnp.where(lane == HALF + 1, lo, row))
-    out[...] = jnp.broadcast_to(row, out.shape)
+
+    def body(near_below, far_below):
+        side = fold_rows(couple(own, far, far_below, (zero, zero)))
+        hi, lo = fold_lanes(*df_add(df_scale(side, -2.0 / SHIFT), (part[0:1, :], part[1:2, :])))
+        lane = lane_ids((1, LANES))
+        value = jnp.where(lane == HALF, hi, jnp.where(lane == HALF + 1, lo, row[...]))
+        out[...] = jnp.broadcast_to(value, out.shape)
+
+    with_sides(body)
 
 
 def solve_krylov(moment):
@@ -648,17 +696,20 @@
     return [(i, (i + (1 if i % 2 == odd_up else -1)) % size) for i in range(size)]
 
 
-def x_halo(block):
-    far = lax.ppermute(block, "blk", swap("blk", 1))
-    return (lax.ppermute(block, "blk", swap("blk", 0)), far)
+def after(values, *earlier):
+    return lax.optimization_barrier((tuple(values), earlier))[0]
+
+
+def from_far(block):
+    return lax.ppermute(block, "blk", swap("blk", 1))
+
+
+def from_near(block, *earlier):
+    return lax.ppermute(after((block,), *earlier)[0] if earlier else block, "blk", swap("blk", 0))
 
 
 def z_halo(face_a, face_b):
     return (lax.ppermute(face_a, "gz", swap("gz", 0)), lax.ppermute(face_b, "gz", swap("gz", 1)))
-
-
-def after(values, *earlier):
-    return lax.optimization_barrier((tuple(values), earlier))[0]
 
 
 def on_device(sqrt_density, ion_charge, ion_potential, hartree_prev, hist_steps, hist_changes):
@@ -671,6 +722,7 @@
     history = [hist_steps, hist_changes]
     work = 300 * cells
     inputs = (hartree_prev, sqrt_density, ion_charge)
+    far = from_far(hartree_prev)
     both, charge, *faces = call(
         launch_kernel,
         [(2 * REACH, *block[1:]), block, (48, LANES), (48, LANES)],
@@ -678,43 +730,52 @@
         [pltpu.SemaphoreType.DMA((3,))],
         place=pltpu.HBM,
     )
-    start = (*x_halo(both), *z_halo(*faces))
+    halo = (from_near(hartree_prev, *faces), far)
+    ends = z_halo(*faces)
+    density_ends = ends
+
+    def advance(gain, inner, halo, ends, last=False):
+        near, far = halo
+        (mid,) = call(
+            functools.partial(near_kernel, gain), [block], [*after((inner,), *ends), near, *ends], flops=work
+        )
+        half = (REACH, block[1] // 2, LANES)
+        return mid, call(
+            functools.partial(last_far_kernel if last else far_kernel, gain),
+            [block, half, half] if last else [block],
+            [mid, far],
+            flops=work,
+        )
+
+    def exchange(block_now):
+        far = from_far(block_now)
+        faces = call(pack_kernel, [face, face], [block_now], flops=work)
+        return (from_near(block_now, *faces), far), z_halo(*faces)
+
     inner, r1 = call(side_one, [block, (40, LANES)], [both, charge, hist_steps], [ext], work)
-    v0, *faces = call(
-        functools.partial(edge_kernel, 1.0, False), [block, face, face], [inner, *after(start, inner)], flops=work
-    )
-    halo = (*x_halo(v0), *z_halo(*faces))
-    inner, r2, m2 = call(
-        side_two, [block, (88, LANES), (8, LANES)], [v0, both, *history], [ext], work
-    )
-    v1, *faces = call(
-        functools.partial(edge_kernel, -1.0 / SHIFT, False),
-        [block, face, face],
-        [inner, *after(halo, inner)],
-        flops=work,
-    )
-    halo = (*x_halo(v1), *z_halo(*faces))
+    _, (v0,) = advance(1.0, inner, halo, ends)
+    halo, ends = exchange(v0)
+    inner, r2, m2 = call(side_two, [block, (88, LANES), (8, LANES)], [v0, both, *history], [ext], work)
+    mid, (v1,) = advance(-1.0 / SHIFT, inner, halo, ends)
+    late_density = after((sqrt_density,), mid)[0]
+    density_halo = (from_near(late_density), from_far(late_density))
+    halo, ends = exchange(v1)
     inner, grad, r3, m3 = call(
         side_three,
         [block, block, (72, LANES), (8, LANES)],
-        [v0, v1, both, *start, ion_potential, *history],
+        [v0, v1, both, *density_halo, *density_ends, ion_potential, *history],
         [ext],
         work,
     )
-    v2, *faces = call(
-        functools.partial(edge_kernel, -2.0 / SHIFT, False),
-        [block, face, face],
-        [inner, *after(halo, inner)],
-        flops=work,
-    )
-    halo = (*x_halo(v2), *z_halo(*faces))
+    _, (v2,) = advance(-2.0 / SHIFT, inner, halo, ends)
+    halo, ends = exchange(v2)
     inner, r4, m4 = call(
         side_four, [block, (40, LANES), (8, LANES)], [v1, v2, both, grad, *history], [ext], work
     )
-    v3, upper = call(
-        functools.partial(edge_kernel, -2.0 / SHIFT, True), [block, face], [inner, *after(halo, inner)], flops=work
-    )
-    left = lax.ppermute(v3, "blk", ring("blk", 1))
+    _, (v3, to_near, to_far) = advance(-2.0 / SHIFT, inner, halo, ends, last=True)
+    far = from_far(to_far)
+    (upper,) = call(pack_upper_kernel, [face], [v3], flops=work)
+    near = from_near(to_near, upper)
     z_left = lax.ppermute(upper, "gz", ring("gz", 1))
     kept, given, inner = call(
         side_five,
@@ -723,10 +784,12 @@
         [(2 * LANES, LANES), (8, LANES), ext],
         work,
     )
-    taken = lax.ppermute(given, "blk", swap("blk", 0))
-    left, z_left = after((left, z_left), inner, taken)
+    taken = from_near(given)
+    row, part = call(
+        couple_kernel, [(1, LANES), (8, LANES)], [v3, near, z_left, inner, kept, taken], flops=work
+    )
     devices = lax.axis_size("blk") * lax.axis_size("gz")
-    (outgoing,) = call(send_kernel, [(devices, LANES)], [v3, left, z_left, inner, kept, taken], flops=work)
+    (outgoing,) = call(send_kernel, [(devices, LANES)], [v3, far, part, row], flops=work)
     received = lax.all_to_all(outgoing.reshape(devices, 1, LANES), ("blk", "gz"), 0, 0, tiled=True)
     return tuple(
         call(

time: 76.8 us -> 76.7 us (level)
  blocking collectives: 23.8 us -> 20.5 us
  waiting for transfers between devices: 1.59 us -> 3.62 us
  Pallas kernels: 14.6 us -> 15.5 us
    ppermute x10 -> x13, starting transfers between devices: 21.5 us -> 25.8 us  [the longest x7 25.1 us: from_near(): lax.ppermute(after((block,), *earlier)[0] if earlier else block, 'blk', s...]
    ppermute x4, starting transfers between devices: 5.19 us -> 1.64 us  [z_halo(): lax.ppermute(face_a, 'gz', swap('gz', 0))]
    all_to_all x1, blocking collectives: 23.8 us -> 20.5 us  [on_device(): lax.all_to_all(outgoing.reshape(devices, 1, LANES), ('blk', 'gz'), 0, 0,...]
    ppermute x10 -> x13, waiting for transfers between devices: 0.84 us -> 2.79 us  [the longest x6 1.96 us: from_far(): return lax.ppermute(block, 'blk', swap('blk', 1))]
    pallas_call x12 -> x21, Pallas kernels: 14.6 us -> 15.5 us  [call(): pl.pallas_call(kernel, out_shape=shapes, in_specs=[pl.BlockSpec(memory_sp...]
    ppermute x4, starting transfers between devices: 7.6 us -> 6.73 us  [z_halo(): lax.ppermute(face_b, 'gz', swap('gz', 1))]
  transfers between devices with their start and end apart: 19 -> 22, of which waited for: 2 -> 4; matrix products, arithmetic and copies ran while one was open for 0% -> 0% of each run, Pallas kernels for 12% -> 15%
where the time goes in v5:
time: 76.7 us; the launch traced here: 76.6 us
  starting transfers between devices  34.6 us (45%)
  blocking collectives  20.5 us (27%)
  Pallas kernels  15.5 us (20%)
  waiting for transfers between devices  3.62 us (5%)
  local copies, waits for them, and re-layouts  1.43 us (2%)
  between operations  0.91 us (1%)
    ppermute x7, starting transfers between devices, from_near(): lax.ppermute(after((block,), *earlier)[0] if earlier else block, 'blk', s...  25.1 us
    all_to_all x1, blocking collectives, on_device(): lax.all_to_all(outgoing.reshape(devices, 1, LANES), ('blk', 'gz'), 0, 0,...  20.5 us
    pallas_call x21, Pallas kernels, call(): pl.pallas_call(kernel, out_shape=shapes, in_specs=[pl.BlockSpec(memory_sp...  15.5 us
    ppermute x4, starting transfers between devices, z_halo(): lax.ppermute(face_b, 'gz', swap('gz', 1))  6.73 us
    ppermute x6, waiting for transfers between devices, from_far(): return lax.ppermute(block, 'blk', swap('blk', 1))  1.96 us
    ppermute x4, starting transfers between devices, z_halo(): lax.ppermute(face_a, 'gz', swap('gz', 0))  1.64 us
  transfers between devices with their start and end apart: 22, of which 4 were waited for; matrix products, arithmetic and copies ran while one was open for 0% of the time, Pallas kernels for 15%

profile of v5, /device:TPU:1, one launch (start us, length us, event | category | flops | bytes accessed | tf_op | source)
XLA Modules:
  0.0 76.6 jit_solution(2755892666090166555)
XLA Ops:
  0.6 1.3 %shard_map.77 = (f32[12,64,128]{2,1,0:T(8,128)S(1)}, f32[6,64,128]{2,1,0:T(8,128)S(1)}, f32[48,128]{1,0:T(8,128)S(1)}, f32[48,128]{1,0:T(8,128)S(1)}) custom-call(f32[6,64,128]{2,1,0:T(8,128)} %hartree.1, f32[6,64,128]{2,1,0:T(8,128)} %density.1, f32[6,64,128]{2,1,0:T(8,128)} %charge.1), custom_call_target="tpu_custom_call" | custom-call | bytes 1228800 | tf_op jit(solution)/shard_map/pallas_call | solution.py:678
  1.9 3.3 %collective-permute-start.2 = (f32[6,64,128]{2,1,0:T(8,128)}, f32[6,64,128]{2,1,0:T(8,128)S(1)}, u32[]{:S(2)}, u32[]{:S(2)}) collective-permute-start(f32[6,64,128]{2,1,0:T(8,128)} %hartree.1), channel_id=1, source_target_pairs={{0,4},{4,0},{8,12},{12,8},{16,20},{20,16},{24,28},{28,24},{32,36},... | collective-permute-start | bytes 589832 | tf_op jit(solution)/shard_map/ppermute | solution.py:708
  5.2 0.0 collective-permute-start.3
  5.3 0.8 collective-permute-start
  6.0 1.9 %collective-permute-start.1 = (f32[48,128]{1,0:T(8,128)S(1)}, f32[48,128]{1,0:T(8,128)S(1)}, u32[]{:S(2)}, u32[]{:S(2)}) collective-permute-start(f32[48,128]{1,0:T(8,128)S(1)} %get-tuple-element.46), channel_id=1, source_target_pairs={{0,3},{1,2},{2,1},{3,0},{4,7},{5,6},{6,5},{7,4},{8,11},{9,10},{10,... | collective-permute-start | bytes 73736 | tf_op jit(solution)/shard_map/ppermute | solution.py:712
  7.9 1.4 %copy-done = f32[8,6,64,128]{3,2,1,0:T(8,128)S(1)} copy-done((f32[8,6,64,128]{3,2,1,0:T(8,128)S(1)}, f32[8,6,64,128]{3,2,1,0:T(8,128)}, u32[]{:S(2)}) %copy-start) | copy-done | bytes 1572888
  9.3 1.3 %shard_map.78 = (f32[6,64,128]{2,1,0:T(8,128)S(1)}, f32[40,128]{1,0:T(8,128)S(1)}) custom-call(f32[12,64,128]{2,1,0:T(8,128)S(1)} %get-tuple-element.42.both, f32[6,64,128]{2,1,0:T(8,128)S(1)} %get-tuple-element.43.charge, f32[8,6,64,128]{3,2,1,0:T(8,128)S(1)} %copy-done), custom_call_target="tpu_custom_call" | custom-call | flops 14745600 | bytes 2379776 | tf_op jit(solution)/shard_map/pallas_call | solution.py:678
  10.7 0.0 collective-permute-done.z_first
  10.7 0.3 shard_map.79.inner
  11.0 0.1 shard_map.80.vector.block.prior.v0
  11.1 0.2 shard_map.82
  11.2 0.0 copy-start.4
  11.2 0.0 copy-start.3
  11.3 7.7 %collective-permute-start.6 = (f32[6,64,128]{2,1,0:T(8,128)S(1)}, f32[6,64,128]{2,1,0:T(8,128)S(1)}, u32[]{:S(2)}, u32[]{:S(2)}) collective-permute-start(f32[6,64,128]{2,1,0:T(8,128)S(1)} %shard_map.80.vector.block.prior.v0), channel_id=1, source_target_pairs={{0,4},{4,0},{8,12},{12,8},{16,20},{20,16},{24,28},{28,24},{32,36},... | collective-permute-start | bytes 589832 | tf_op jit(solution)/shard_map/ppermute | solution.py:708
  18.9 0.3 collective-permute-start.4
  19.3 1.6 %collective-permute-start.5 = (f32[24,128]{1,0:T(8,128)S(1)}, f32[24,128]{1,0:T(8,128)S(1)}, u32[]{:S(2)}, u32[]{:S(2)}) collective-permute-start(f32[24,128]{1,0:T(8,128)S(1)} %get-tuple-element.51), channel_id=1, source_target_pairs={{0,3},{1,2},{2,1},{3,0},{4,7},{5,6},{6,5},{7,4},{8,11},{9,10},{10,... | collective-permute-start | bytes 36872 | tf_op jit(solution)/shard_map/ppermute | solution.py:712
  20.9 2.2 %shard_map.81 = (f32[6,64,128]{2,1,0:T(8,128)S(1)}, f32[88,128]{1,0:T(8,128)S(1)}, f32[8,128]{1,0:T(8,128)S(1)}) custom-call(f32[6,64,128]{2,1,0:T(8,128)S(1)} %shard_map.80.vector.block.prior.v0, f32[12,64,128]{2,1,0:T(8,128)S(1)} %get-tuple-element.42.both, f32[8,6,64,128]{3,2,1,0:T(8,128)S(1)} %copy-done.1, f32[8,6,64,128]{3,2,1,0:T(8,128)S(1)} %copy-done.2), custom_call_target="tpu_custom_call" | custom-call | flops 14745600 | bytes 3981312 | tf_op jit(solution)/shard_map/pallas_call | solution.py:678
  23.1 0.3 shard_map.83.inner
  23.4 4.2 %collective-permute-start.8 = (f32[6,64,128]{2,1,0:T(8,128)S(1)}, f32[6,64,128]{2,1,0:T(8,128)S(1)}, u32[]{:S(2)}, u32[]{:S(2)}) collective-permute-start(f32[6,64,128]{2,1,0:T(8,128)S(1)} %copy-done.4), channel_id=1, source_target_pairs={{0,4},{4,0},{8,12},{12,8},{16,20},{20,16},{24,28},{28,24},{32,36},... | collective-permute-start | bytes 589832 | tf_op jit(solution)/shard_map/ppermute | solution.py:708
  27.6 0.1 shard_map.84.vector.block.prior.v1
  27.7 0.2 shard_map.86
  27.9 1.2 %collective-permute-start.12 = (f32[6,64,128]{2,1,0:T(8,128)S(1)}, f32[6,64,128]{2,1,0:T(8,128)S(1)}, u32[]{:S(2)}, u32[]{:S(2)}) collective-permute-start(f32[6,64,128]{2,1,0:T(8,128)S(1)} %shard_map.84.vector.block.prior.v1), channel_id=1, source_target_pairs={{0,4},{4,0},{8,12},{12,8},{16,20},{20,16},{24,28},{28,24},{32,36},... | collective-permute-start | bytes 589832 | tf_op jit(solution)/shard_map/ppermute | solution.py:708
  29.1 0.7 collective-permute-start.13
  29.8 0.2 collective-permute-start.10
  29.9 1.7 %collective-permute-start.11 = (f32[24,128]{1,0:T(8,128)S(1)}, f32[24,128]{1,0:T(8,128)S(1)}, u32[]{:S(2)}, u32[]{:S(2)}) collective-permute-start(f32[24,128]{1,0:T(8,128)S(1)} %get-tuple-element.57), channel_id=1, source_target_pairs={{0,3},{1,2},{2,1},{3,0},{4,7},{5,6},{6,5},{7,4},{8,11},{9,10},{10,... | collective-permute-start | bytes 36872 | tf_op jit(solution)/shard_map/ppermute | solution.py:712
  31.7 1.0 %collective-permute-done.9.far = f32[6,64,128]{2,1,0:T(8,128)S(1)} collective-permute-done((f32[6,64,128]{2,1,0:T(8,128)S(1)}, f32[6,64,128]{2,1,0:T(8,128)S(1)}, u32[]{:S(2)}, u32[]{:S(2)}) %collective-permute-start.9) | collective-permute-done | bytes 196640 | tf_op jit(solution)/shard_map/ppermute | solution.py:704
  32.7 3.1 %shard_map.85 = (f32[6,64,128]{2,1,0:T(8,128)S(1)}, f32[6,64,128]{2,1,0:T(8,128)S(1)}, f32[72,128]{1,0:T(8,128)S(1)}, f32[8,128]{1,0:T(8,128)S(1)}) custom-call(f32[6,64,128]{2,1,0:T(8,128)S(1)} %shard_map.80.vector.block.prior.v0, f32[6,64,128]{2,1,0:T(8,128)S(1)} %shard_map.84.vector.block.prior.v1, f32[12,64,128]{2,1,0:T(8,128)S(1)} %get-tuple-element.42.both, ...), custom_call_target="tpu_custom_call" | custom-call | flops 14745600 | bytes 5005312 | tf_op jit(solution)/shard_map/pallas_call | solution.py:678
  35.9 0.3 shard_map.87.inner
  36.2 0.1 shard_map.88.vector.block.prior.v2
  36.3 0.2 shard_map.90
  36.4 3.5 %collective-permute-start.16 = (f32[6,64,128]{2,1,0:T(8,128)S(1)}, f32[6,64,128]{2,1,0:T(8,128)S(1)}, u32[]{:S(2)}, u32[]{:S(2)}) collective-permute-start(f32[6,64,128]{2,1,0:T(8,128)S(1)} %shard_map.88.vector.block.prior.v2), channel_id=1, source_target_pairs={{0,4},{4,0},{8,12},{12,8},{16,20},{20,16},{24,28},{28,24},{32,36},... | collective-permute-start | bytes 589832 | tf_op jit(solution)/shard_map/ppermute | solution.py:708
  40.0 0.4 collective-permute-start.14
  40.4 1.5 %collective-permute-start.15 = (f32[24,128]{1,0:T(8,128)S(1)}, f32[24,128]{1,0:T(8,128)S(1)}, u32[]{:S(2)}, u32[]{:S(2)}) collective-permute-start(f32[24,128]{1,0:T(8,128)S(1)} %get-tuple-element.63), channel_id=1, source_target_pairs={{0,3},{1,2},{2,1},{3,0},{4,7},{5,6},{6,5},{7,4},{8,11},{9,10},{10,... | collective-permute-start | bytes 36872 | tf_op jit(solution)/shard_map/ppermute | solution.py:712
  41.9 1.4 %shard_map.89 = (f32[6,64,128]{2,1,0:T(8,128)S(1)}, f32[40,128]{1,0:T(8,128)S(1)}, f32[8,128]{1,0:T(8,128)S(1)}) custom-call(f32[6,64,128]{2,1,0:T(8,128)S(1)} %shard_map.84.vector.block.prior.v1, f32[6,64,128]{2,1,0:T(8,128)S(1)} %shard_map.88.vector.block.prior.v2, f32[12,64,128]{2,1,0:T(8,128)S(1)} %get-tuple-element.42.both, ...), custom_call_target="tpu_custom_call" | custom-call | flops 14745600 | bytes 4349952 | tf_op jit(solution)/shard_map/pallas_call | solution.py:678
  43.3 0.8 %collective-permute-done.15.z_second = f32[24,128]{1,0:T(8,128)S(1)} collective-permute-done((f32[24,128]{1,0:T(8,128)S(1)}, f32[24,128]{1,0:T(8,128)S(1)}, u32[]{:S(2)}, u32[]{:S(2)}) %collective-permute-start.15) | collective-permute-done | bytes 12320 | tf_op jit(solution)/shard_map/ppermute | solution.py:712
  44.1 0.3 shard_map.91.inner
  44.4 0.9 %collective-permute-done.17.far = f32[6,64,128]{2,1,0:T(8,128)S(1)} collective-permute-done((f32[6,64,128]{2,1,0:T(8,128)S(1)}, f32[6,64,128]{2,1,0:T(8,128)S(1)}, u32[]{:S(2)}, u32[]{:S(2)}) %collective-permute-start.17) | collective-permute-done | bytes 196640 | tf_op jit(solution)/shard_map/ppermute | solution.py:704
  45.3 0.1 shard_map.92
  45.4 0.1 shard_map.93
  45.5 3.2 %collective-permute-start.19 = (f32[6,32,128]{2,1,0:T(8,128)S(1)}, f32[6,32,128]{2,1,0:T(8,128)S(1)}, u32[]{:S(2)}, u32[]{:S(2)}) collective-permute-start(f32[6,32,128]{2,1,0:T(8,128)S(1)} %get-tuple-element.69), channel_id=1, source_target_pairs={{0,4},{4,0},{8,12},{12,8},{16,20},{20,16},{24,28},{28,24},{32,36},... | collective-permute-start | bytes 294920 | tf_op jit(solution)/shard_map/ppermute | solution.py:708
  48.7 0.4 collective-permute-start.20
  49.1 1.4 %shard_map.94 = (f32[1,128]{1,0:T(1,128)S(1)}, f32[1,128]{1,0:T(1,128)S(1)}, f32[8,128]{1,0:T(8,128)S(1)}) custom-call(f32[6,64,128]{2,1,0:T(8,128)S(1)} %shard_map.88.vector.block.prior.v2, f32[6,64,128]{2,1,0:T(8,128)S(1)} %get-tuple-element.66.block.vector.own.v3, f32[12,64,128]{2,1,0:T(8,128)S(1)} %get-tuple-element.42.both, ...), custom_call_target="tpu_custom_call" | custom-call | flops 14745600 | bytes 4072448 | tf_op jit(solution)/shard_map/pallas_call | solution.py:678
  50.5 2.0 %collective-permute-start.21 = (f32[1,128]{1,0:T(1,128)S(1)}, f32[1,128]{1,0:T(1,128)S(1)}, u32[]{:S(2)}, u32[]{:S(2)}) collective-permute-start(f32[1,128]{1,0:T(1,128)S(1)} %get-tuple-element.79), channel_id=1, source_target_pairs={{0,4},{4,0},{8,12},{12,8},{16,20},{20,16},{24,28},{28,24},{32,36},... | collective-permute-start | bytes 1544 | tf_op jit(solution)/shard_map/ppermute | solution.py:708
  52.5 0.8 %collective-permute-done.21.taken = f32[1,128]{1,0:T(1,128)S(1)} collective-permute-done((f32[1,128]{1,0:T(1,128)S(1)}, f32[1,128]{1,0:T(1,128)S(1)}, u32[]{:S(2)}, u32[]{:S(2)}) %collective-permute-start.21) | collective-permute-done | bytes 544 | tf_op jit(solution)/shard_map/ppermute | solution.py:708
  53.3 0.4 shard_map.95
  53.7 0.6 shard_map.96
  54.3 20.5 %all_to_all.5 = f32[256,1,128]{2,1,0:T(1,128)S(1)} all-to-all(f32[256,1,128]{2,1,0:T(1,128)S(1)} %bitcast.5), channel_id=1, replica_groups=mesh['blk'=64,'gz'=4] {'blk','gz'}, dimensions={0} | all-to-all | bytes 262144 | tf_op jit(solution)/shard_map/all_to_all | solution.py:793
  74.8 1.8 %shard_map.97 = (f32[6,64,128]{2,1,0:T(8,128)}, f32[6,64,128]{2,1,0:T(8,128)}) custom-call(f32[256,128]{1,0:T(8,128)S(1)} %bitcast.4, f32[12,64,128]{2,1,0:T(8,128)S(1)} %get-tuple-element.42.both, f32[6,64,128]{2,1,0:T(8,128)S(1)} %get-tuple-element.60.grad, f32[6,64,128]{2,1,0:T(8,128)S(1)} %shard_map.80.vector.block.prior.v0, ...), custom_call_target="tpu_custom_call" | custom-call | flops 14745600 | bytes 5046272 | tf_op jit(solution)/shard_map/pallas_call | solution.py:678
  (28 shorter events, 0.1 us)
Async XLA Ops:
  1.9 8.8 %collective-permute-start.2 = (f32[6,64,128]{2,1,0:T(8,128)}, f32[6,64,128]{2,1,0:T(8,128)S(1)}, u32[]{:S(2)}, u32[]{:S(2)}) collective-permute-start(f32[6,64,128]{2,1,0:T(8,128)} %hartree.1), channel_id=1, source_target_pairs={{0,4},{4,0},{8,12},{12,8},{16,20},{20,16},{24,28},{28,24},{32,36},... | collective-permute-start | bytes 589832 | tf_op jit(solution)/shard_map/ppermute | solution.py:708
  5.2 5.7 %collective-permute-start.3 = (f32[6,64,128]{2,1,0:T(8,128)}, f32[6,64,128]{2,1,0:T(8,128)S(1)}, u32[]{:S(2)}, u32[]{:S(2)}) collective-permute-start(f32[6,64,128]{2,1,0:T(8,128)} %hartree.1), channel_id=1, source_target_pairs={{0,252},{4,8},{8,4},{12,16},{16,12},{20,24},{24,20},{28,32},{32,28... | collective-permute-start | bytes 589832 | tf_op jit(solution)/shard_map/ppermute | solution.py:704
  5.3 5.4 %collective-permute-start = (f32[48,128]{1,0:T(8,128)S(1)}, f32[48,128]{1,0:T(8,128)S(1)}, u32[]{:S(2)}, u32[]{:S(2)}) collective-permute-start(f32[48,128]{1,0:T(8,128)S(1)} %get-tuple-element.45), channel_id=1, source_target_pairs={{0,1},{1,0},{2,3},{3,2},{4,5},{5,4},{6,7},{7,6},{8,9},{9,8},{10,11... | collective-permute-start | bytes 73736 | tf_op jit(solution)/shard_map/ppermute | solution.py:712
  6.0 4.7 %collective-permute-start.1 = (f32[48,128]{1,0:T(8,128)S(1)}, f32[48,128]{1,0:T(8,128)S(1)}, u32[]{:S(2)}, u32[]{:S(2)}) collective-permute-start(f32[48,128]{1,0:T(8,128)S(1)} %get-tuple-element.46), channel_id=1, source_target_pairs={{0,3},{1,2},{2,1},{3,0},{4,7},{5,6},{6,5},{7,4},{8,11},{9,10},{10,... | collective-permute-start | bytes 73736 | tf_op jit(solution)/shard_map/ppermute | solution.py:712
  7.9 1.4 %copy-start = (f32[8,6,64,128]{3,2,1,0:T(8,128)S(1)}, f32[8,6,64,128]{3,2,1,0:T(8,128)}, u32[]{:S(2)}) copy-start(f32[8,6,64,128]{3,2,1,0:T(8,128)} %steps.11) | copy-start | bytes 4718596
  9.3 11.5 %copy-start.1 = (f32[8,6,64,128]{3,2,1,0:T(8,128)S(1)}, f32[8,6,64,128]{3,2,1,0:T(8,128)}, u32[]{:S(2)}) copy-start(f32[8,6,64,128]{3,2,1,0:T(8,128)} %steps.11) | copy-start | bytes 4718596
  9.3 11.5 %copy-start.2 = (f32[8,6,64,128]{3,2,1,0:T(8,128)S(1)}, f32[8,6,64,128]{3,2,1,0:T(8,128)}, u32[]{:S(2)}) copy-start(f32[8,6,64,128]{3,2,1,0:T(8,128)} %changes.9) | copy-start | bytes 4718596
  11.2 12.2 %copy-start.4 = (f32[6,64,128]{2,1,0:T(8,128)S(1)}, f32[6,64,128]{2,1,0:T(8,128)}, u32[]{:S(2)}) copy-start(f32[6,64,128]{2,1,0:T(8,128)} %density.1) | copy-start | bytes 589828
  11.2 21.5 %copy-start.3 = (f32[6,64,128]{2,1,0:T(8,128)S(1)}, f32[6,64,128]{2,1,0:T(8,128)}, u32[]{:S(2)}) copy-start(f32[6,64,128]{2,1,0:T(8,128)} %potential.1) | copy-start | bytes 589828
  11.3 11.8 %collective-permute-start.6 = (f32[6,64,128]{2,1,0:T(8,128)S(1)}, f32[6,64,128]{2,1,0:T(8,128)S(1)}, u32[]{:S(2)}, u32[]{:S(2)}) collective-permute-start(f32[6,64,128]{2,1,0:T(8,128)S(1)} %shard_map.80.vector.block.prior.v0), channel_id=1, source_target_pairs={{0,4},{4,0},{8,12},{12,8},{16,20},{20,16},{24,28},{28,24},{32,36},... | collective-permute-start | bytes 589832 | tf_op jit(solution)/shard_map/ppermute | solution.py:708
  18.9 8.7 %collective-permute-start.7 = (f32[6,64,128]{2,1,0:T(8,128)S(1)}, f32[6,64,128]{2,1,0:T(8,128)S(1)}, u32[]{:S(2)}, u32[]{:S(2)}) collective-permute-start(f32[6,64,128]{2,1,0:T(8,128)S(1)} %shard_map.80.vector.block.prior.v0), channel_id=1, source_target_pairs={{0,252},{4,8},{8,4},{12,16},{16,12},{20,24},{24,20},{28,32},{32,28... | collective-permute-start | bytes 589832 | tf_op jit(solution)/shard_map/ppermute | solution.py:704
  18.9 4.1 %collective-permute-start.4 = (f32[24,128]{1,0:T(8,128)S(1)}, f32[24,128]{1,0:T(8,128)S(1)}, u32[]{:S(2)}, u32[]{:S(2)}) collective-permute-start(f32[24,128]{1,0:T(8,128)S(1)} %get-tuple-element.50), channel_id=1, source_target_pairs={{0,1},{1,0},{2,3},{3,2},{4,5},{5,4},{6,7},{7,6},{8,9},{9,8},{10,11... | collective-permute-start | bytes 36872 | tf_op jit(solution)/shard_map/ppermute | solution.py:712
  19.3 3.8 %collective-permute-start.5 = (f32[24,128]{1,0:T(8,128)S(1)}, f32[24,128]{1,0:T(8,128)S(1)}, u32[]{:S(2)}, u32[]{:S(2)}) collective-permute-start(f32[24,128]{1,0:T(8,128)S(1)} %get-tuple-element.51), channel_id=1, source_target_pairs={{0,3},{1,2},{2,1},{3,0},{4,7},{5,6},{6,5},{7,4},{8,11},{9,10},{10,... | collective-permute-start | bytes 36872 | tf_op jit(solution)/shard_map/ppermute | solution.py:712
  23.4 6.5 %collective-permute-start.8 = (f32[6,64,128]{2,1,0:T(8,128)S(1)}, f32[6,64,128]{2,1,0:T(8,128)S(1)}, u32[]{:S(2)}, u32[]{:S(2)}) collective-permute-start(f32[6,64,128]{2,1,0:T(8,128)S(1)} %copy-done.4), channel_id=1, source_target_pairs={{0,4},{4,0},{8,12},{12,8},{16,20},{20,16},{24,28},{28,24},{32,36},... | collective-permute-start | bytes 589832 | tf_op jit(solution)/shard_map/ppermute | solution.py:708
  27.6 5.1 %collective-permute-start.9 = (f32[6,64,128]{2,1,0:T(8,128)S(1)}, f32[6,64,128]{2,1,0:T(8,128)S(1)}, u32[]{:S(2)}, u32[]{:S(2)}) collective-permute-start(f32[6,64,128]{2,1,0:T(8,128)S(1)} %copy-done.4), channel_id=1, source_target_pairs={{0,252},{4,8},{8,4},{12,16},{16,12},{20,24},{24,20},{28,32},{32,28... | collective-permute-start | bytes 589832 | tf_op jit(solution)/shard_map/ppermute | solution.py:704
  27.9 8.0 %collective-permute-start.12 = (f32[6,64,128]{2,1,0:T(8,128)S(1)}, f32[6,64,128]{2,1,0:T(8,128)S(1)}, u32[]{:S(2)}, u32[]{:S(2)}) collective-permute-start(f32[6,64,128]{2,1,0:T(8,128)S(1)} %shard_map.84.vector.block.prior.v1), channel_id=1, source_target_pairs={{0,4},{4,0},{8,12},{12,8},{16,20},{20,16},{24,28},{28,24},{32,36},... | collective-permute-start | bytes 589832 | tf_op jit(solution)/shard_map/ppermute | solution.py:708
  29.1 7.1 %collective-permute-start.13 = (f32[6,64,128]{2,1,0:T(8,128)S(1)}, f32[6,64,128]{2,1,0:T(8,128)S(1)}, u32[]{:S(2)}, u32[]{:S(2)}) collective-permute-start(f32[6,64,128]{2,1,0:T(8,128)S(1)} %shard_map.84.vector.block.prior.v1), channel_id=1, source_target_pairs={{0,252},{4,8},{8,4},{12,16},{16,12},{20,24},{24,20},{28,32},{32,28... | collective-permute-start | bytes 589832 | tf_op jit(solution)/shard_map/ppermute | solution.py:704
  29.8 6.1 %collective-permute-start.10 = (f32[24,128]{1,0:T(8,128)S(1)}, f32[24,128]{1,0:T(8,128)S(1)}, u32[]{:S(2)}, u32[]{:S(2)}) collective-permute-start(f32[24,128]{1,0:T(8,128)S(1)} %get-tuple-element.56), channel_id=1, source_target_pairs={{0,1},{1,0},{2,3},{3,2},{4,5},{5,4},{6,7},{7,6},{8,9},{9,8},{10,11... | collective-permute-start | bytes 36872 | tf_op jit(solution)/shard_map/ppermute | solution.py:712
  29.9 5.9 %collective-permute-start.11 = (f32[24,128]{1,0:T(8,128)S(1)}, f32[24,128]{1,0:T(8,128)S(1)}, u32[]{:S(2)}, u32[]{:S(2)}) collective-permute-start(f32[24,128]{1,0:T(8,128)S(1)} %get-tuple-element.57), channel_id=1, source_target_pairs={{0,3},{1,2},{2,1},{3,0},{4,7},{5,6},{6,5},{7,4},{8,11},{9,10},{10,... | collective-permute-start | bytes 36872 | tf_op jit(solution)/shard_map/ppermute | solution.py:712
  36.4 7.7 %collective-permute-start.16 = (f32[6,64,128]{2,1,0:T(8,128)S(1)}, f32[6,64,128]{2,1,0:T(8,128)S(1)}, u32[]{:S(2)}, u32[]{:S(2)}) collective-permute-start(f32[6,64,128]{2,1,0:T(8,128)S(1)} %shard_map.88.vector.block.prior.v2), channel_id=1, source_target_pairs={{0,4},{4,0},{8,12},{12,8},{16,20},{20,16},{24,28},{28,24},{32,36},... | collective-permute-start | bytes 589832 | tf_op jit(solution)/shard_map/ppermute | solution.py:708
  40.0 5.4 %collective-permute-start.17 = (f32[6,64,128]{2,1,0:T(8,128)S(1)}, f32[6,64,128]{2,1,0:T(8,128)S(1)}, u32[]{:S(2)}, u32[]{:S(2)}) collective-permute-start(f32[6,64,128]{2,1,0:T(8,128)S(1)} %shard_map.88.vector.block.prior.v2), channel_id=1, source_target_pairs={{0,252},{4,8},{8,4},{12,16},{16,12},{20,24},{24,20},{28,32},{32,28... | collective-permute-start | bytes 589832 | tf_op jit(solution)/shard_map/ppermute | solution.py:704
  40.0 3.3 %collective-permute-start.14 = (f32[24,128]{1,0:T(8,128)S(1)}, f32[24,128]{1,0:T(8,128)S(1)}, u32[]{:S(2)}, u32[]{:S(2)}) collective-permute-start(f32[24,128]{1,0:T(8,128)S(1)} %get-tuple-element.62), channel_id=1, source_target_pairs={{0,1},{1,0},{2,3},{3,2},{4,5},{5,4},{6,7},{7,6},{8,9},{9,8},{10,11... | collective-permute-start | bytes 36872 | tf_op jit(solution)/shard_map/ppermute | solution.py:712
  40.4 3.8 %collective-permute-start.15 = (f32[24,128]{1,0:T(8,128)S(1)}, f32[24,128]{1,0:T(8,128)S(1)}, u32[]{:S(2)}, u32[]{:S(2)}) collective-permute-start(f32[24,128]{1,0:T(8,128)S(1)} %get-tuple-element.63), channel_id=1, source_target_pairs={{0,3},{1,2},{2,1},{3,0},{4,7},{5,6},{6,5},{7,4},{8,11},{9,10},{10,... | collective-permute-start | bytes 36872 | tf_op jit(solution)/shard_map/ppermute | solution.py:712
  45.5 7.8 %collective-permute-start.19 = (f32[6,32,128]{2,1,0:T(8,128)S(1)}, f32[6,32,128]{2,1,0:T(8,128)S(1)}, u32[]{:S(2)}, u32[]{:S(2)}) collective-permute-start(f32[6,32,128]{2,1,0:T(8,128)S(1)} %get-tuple-element.69), channel_id=1, source_target_pairs={{0,4},{4,0},{8,12},{12,8},{16,20},{20,16},{24,28},{28,24},{32,36},... | collective-permute-start | bytes 294920 | tf_op jit(solution)/shard_map/ppermute | solution.py:708
  48.7 4.9 %collective-permute-start.18 = (f32[6,32,128]{2,1,0:T(8,128)S(1)}, f32[6,32,128]{2,1,0:T(8,128)S(1)}, u32[]{:S(2)}, u32[]{:S(2)}) collective-permute-start(f32[6,32,128]{2,1,0:T(8,128)S(1)} %get-tuple-element.67), channel_id=1, source_target_pairs={{0,252},{4,8},{8,4},{12,16},{16,12},{20,24},{24,20},{28,32},{32,28... | collective-permute-start | bytes 294920 | tf_op jit(solution)/shard_map/ppermute | solution.py:704
  48.7 4.6 %collective-permute-start.20 = (f32[24,128]{1,0:T(8,128)S(1)}, f32[24,128]{1,0:T(8,128)S(1)}, u32[]{:S(2)}, u32[]{:S(2)}) collective-permute-start(f32[24,128]{1,0:T(8,128)S(1)} %shard_map.93), channel_id=1, source_target_pairs={{0,1},{1,2},{2,3},{3,0},{4,5},{5,6},{6,7},{7,4},{8,9},{9,10},{10,1... | collective-permute-start | bytes 36872 | tf_op jit(solution)/shard_map/ppermute | solution.py:779
  50.5 2.8 %collective-permute-start.21 = (f32[1,128]{1,0:T(1,128)S(1)}, f32[1,128]{1,0:T(1,128)S(1)}, u32[]{:S(2)}, u32[]{:S(2)}) collective-permute-start(f32[1,128]{1,0:T(1,128)S(1)} %get-tuple-element.79), channel_id=1, source_target_pairs={{0,4},{4,0},{8,12},{12,8},{16,20},{20,16},{24,28},{28,24},{32,36},... | collective-permute-start | bytes 1544 | tf_op jit(solution)/shard_map/ppermute | solution.py:708

commit v6 on v5

--- a/solution.py
+++ b/solution.py
@@ -272,30 +272,26 @@
         out[i] = moved if prior is None else 2.0 * moved - prior[i]
 
 
-def near_kernel(gain, inner, near, z_first, z_second, out):
+def z_kernel(gain, inner, z_first, z_second, out):
     faces = edge_faces(*by_side(z_first[0:24, :], z_second[0:24, :]))
-
+    for i in range(REACH):
+        out[i] = inner[i] + gain * z_plane(i, faces)
+
+
+def x_kernel(gain, inner, near, far, out):
     def body(near_below, far_below):
         for i in range(REACH):
-            out[i] = inner[i] + gain * (side_plane(i, near, near_below) + z_plane(i, faces))
+            out[i] = inner[i] + gain * (side_plane(i, near, near_below) + side_plane(i, far, far_below))
 
     with_sides(body)
 
 
-def far_kernel(gain, inner, far, out):
+def last_x_kernel(gain, inner, near, far, out, to_near, to_far):
+    half = out.shape[1] // 2
+
     def body(near_below, far_below):
         for i in range(REACH):
-            out[i] = inner[i] + gain * side_plane(i, far, far_below)
-
-    with_sides(body)
-
-
-def last_far_kernel(gain, inner, far, out, to_near, to_far):
-    half = out.shape[1] // 2
-
-    def body(near_below, far_below):
-        for i in range(REACH):
-            plane = inner[i] + gain * side_plane(i, far, far_below)
+            plane = inner[i] + gain * (side_plane(i, near, near_below) + side_plane(i, far, far_below))
             out[i] = plane
             for ref, below in ((to_near, near_below), (to_far, far_below)):
                 ref[i] = plane[:half] if below else plane[half:]
@@ -385,17 +381,14 @@
     return lambda i, b: 2.0 * tile_of(both, REACH + i, b) * tile_of(vector, i, b)
 
 
-def side_one(both, charge, steps, inner, rows, ext):
+def side_one(both, charge, inner, ext):
     inner_residual(both, charge, inner, ext)
-    store(rows, 0, gram_dots(steps, steps, PAIRS))
 
 
 def side_two(vector, both, steps, changes, inner, rows, moments, ext):
     inner_basis(vector, None, inner, ext)
     lifted, rho = lifted_tile(both, vector), density_tile(both)
     store(rows, 0, field_dots(steps, changes, [lifted], [(rho, lifted)]))
-    store(rows, 17, gram_dots(changes, changes, PAIRS))
-    store(rows, 53, gram_dots(steps, changes, CROSS_PAIRS[:32]))
     store_moments([(vector, vector)], moments)
 
 
@@ -416,10 +409,13 @@
     slope = lambda i, b: tile_of(grad, i, b)
     values = field_dots(steps, changes, [lifted, slope], [(rho, lifted), (rho, slope), (rho, rho)])
     store(rows, 0, values[:16] + values[32:33] + values[16:32] + values[33:])
+    store(rows, 35, gram_dots(steps, steps, PAIRS))
+    store(rows, 71, gram_dots(changes, changes, PAIRS))
+    store(rows, 107, gram_dots(steps, changes, CROSS_PAIRS[:32]))
     store_moments([(prior, vector), (vector, vector)], moments)
 
 
-def side_five(prior, vector, both, steps, changes, r1, r2, r3, r4, m2, m3, m4, kept, given, inner, table, m5, ext):
+def side_five(prior, vector, both, steps, changes, r2, r3, r4, m2, m3, m4, kept, given, inner, table, m5, ext):
     lifted, rho = lifted_tile(both, vector), density_tile(both)
     own = field_dots(steps, changes, [lifted], [(rho, lifted)])
     store_moments([(prior, vector), (vector, vector)], m5)
@@ -433,9 +429,7 @@
             at = place(base + before)
             table[at : at + count - before, :] = ref[start + before : start + count, :]
 
-    put(ROW_GRAM, r1, 0, 36)
-    put(ROW_GRAM + 36, r2, 17, 36)
-    put(ROW_GRAM + 72, r2, 53, 32)
+    put(ROW_GRAM, r4, 35, 104)
     put(ROW_GRAM + 104, r3, 33, 32)
     put(ROW_BASE, r3, 17, 16)
     put(ROW_BASE + 16, r4, 17, 18)
@@ -481,7 +475,7 @@
     return acc
 
 
-def couple_kernel(own, near, z_left, inner, kept, taken, row, part):
+def couple_kernel(own, z_left, inner, kept, taken, row, part):
     zero = jnp.zeros((8, LANES), jnp.float32)
     faces = edge_faces(z_left[...], None)
     acc = (zero, zero)
@@ -489,25 +483,20 @@
         product = own[i] * z_plane(i, faces)
         for b in range(8):
             acc = add_tile(acc, product[8 * b : 8 * b + 8])
-    z_rows = fold_rows(acc)
-
-    def body(near_below, far_below):
-        sides = df_add(fold_rows(couple(own, near, near_below, (zero, zero))), z_rows)
-        part[0:1, :], part[1:2, :] = df_add(df_scale(sides, -2.0 / SHIFT), (inner[0:1, :], inner[1:2, :]))
-
-    with_sides(body)
+    sides = df_scale(fold_rows(acc), -2.0 / SHIFT)
+    part[0:1, :], part[1:2, :] = df_add(sides, (inner[0:1, :], inner[1:2, :]))
     lane = lane_ids((1, LANES))
     total, err = two_sum(kept[...], taken[...])
     low_lane = (lane >= MOM_LANE + 7) & (lane < MOM_LANE + 14) & is_odd("blk")
     row[...] = jnp.where(low_lane, total + pltpu.roll(err, 7, 1), total)
 
 
-def send_kernel(own, far, part, row, out):
+def send_kernel(own, far, near, part, row, out):
     zero = jnp.zeros((8, LANES), jnp.float32)
 
     def body(near_below, far_below):
-        side = fold_rows(couple(own, far, far_below, (zero, zero)))
-        hi, lo = fold_lanes(*df_add(df_scale(side, -2.0 / SHIFT), (part[0:1, :], part[1:2, :])))
+        acc = couple(own, far, far_below, couple(own, near, near_below, (zero, zero)))
+        hi, lo = fold_lanes(*df_add(df_scale(fold_rows(acc), -2.0 / SHIFT), (part[0:1, :], part[1:2, :])))
         lane = lane_ids((1, LANES))
         value = jnp.where(lane == HALF, hi, jnp.where(lane == HALF + 1, lo, row[...]))
         out[...] = jnp.broadcast_to(value, out.shape)
@@ -700,12 +689,9 @@
     return lax.optimization_barrier((tuple(values), earlier))[0]
 
 
-def from_far(block):
-    return lax.ppermute(block, "blk", swap("blk", 1))
-
-
-def from_near(block, *earlier):
-    return lax.ppermute(after((block,), *earlier)[0] if earlier else block, "blk", swap("blk", 0))
+def x_halo(block):
+    far = lax.ppermute(block, "blk", swap("blk", 1))
+    return (lax.ppermute(block, "blk", swap("blk", 0)), far)
 
 
 def z_halo(face_a, face_b):
@@ -722,7 +708,7 @@
     history = [hist_steps, hist_changes]
     work = 300 * cells
     inputs = (hartree_prev, sqrt_density, ion_charge)
-    far = from_far(hartree_prev)
+    halo = x_halo(hartree_prev)
     both, charge, *faces = call(
         launch_kernel,
         [(2 * REACH, *block[1:]), block, (48, LANES), (48, LANES)],
@@ -730,35 +716,29 @@
         [pltpu.SemaphoreType.DMA((3,))],
         place=pltpu.HBM,
     )
-    halo = (from_near(hartree_prev, *faces), far)
     ends = z_halo(*faces)
     density_ends = ends
+    half = (REACH, block[1] // 2, LANES)
 
     def advance(gain, inner, halo, ends, last=False):
-        near, far = halo
-        (mid,) = call(
-            functools.partial(near_kernel, gain), [block], [*after((inner,), *ends), near, *ends], flops=work
-        )
-        half = (REACH, block[1] // 2, LANES)
-        return mid, call(
-            functools.partial(last_far_kernel if last else far_kernel, gain),
+        (mid,) = call(functools.partial(z_kernel, gain), [block], [inner, *ends], flops=work)
+        return call(
+            functools.partial(last_x_kernel if last else x_kernel, gain),
             [block, half, half] if last else [block],
-            [mid, far],
+            [mid, *halo],
             flops=work,
         )
 
     def exchange(block_now):
-        far = from_far(block_now)
-        faces = call(pack_kernel, [face, face], [block_now], flops=work)
-        return (from_near(block_now, *faces), far), z_halo(*faces)
-
-    inner, r1 = call(side_one, [block, (40, LANES)], [both, charge, hist_steps], [ext], work)
-    _, (v0,) = advance(1.0, inner, halo, ends)
+        halo = x_halo(block_now)
+        return halo, z_halo(*call(pack_kernel, [face, face], [block_now], flops=work))
+
+    (inner,) = call(side_one, [block], [both, charge], [ext], work)
+    (v0,) = advance(1.0, inner, halo, ends)
     halo, ends = exchange(v0)
-    inner, r2, m2 = call(side_two, [block, (88, LANES), (8, LANES)], [v0, both, *history], [ext], work)
-    mid, (v1,) = advance(-1.0 / SHIFT, inner, halo, ends)
-    late_density = after((sqrt_density,), mid)[0]
-    density_halo = (from_near(late_density), from_far(late_density))
+    density_halo = x_halo(after((sqrt_density,), v0)[0])
+    inner, r2, m2 = call(side_two, [block, (24, LANES), (8, LANES)], [v0, both, *history], [ext], work)
+    (v1,) = advance(-1.0 / SHIFT, inner, halo, ends)
     halo, ends = exchange(v1)
     inner, grad, r3, m3 = call(
         side_three,
@@ -767,29 +747,29 @@
         [ext],
         work,
     )
-    _, (v2,) = advance(-2.0 / SHIFT, inner, halo, ends)
+    (v2,) = advance(-2.0 / SHIFT, inner, halo, ends)
     halo, ends = exchange(v2)
     inner, r4, m4 = call(
-        side_four, [block, (40, LANES), (8, LANES)], [v1, v2, both, grad, *history], [ext], work
+        side_four, [block, (144, LANES), (8, LANES)], [v1, v2, both, grad, *history], [ext], work
     )
-    _, (v3, to_near, to_far) = advance(-2.0 / SHIFT, inner, halo, ends, last=True)
-    far = from_far(to_far)
+    v3, to_near, to_far = advance(-2.0 / SHIFT, inner, halo, ends, last=True)
+    far = lax.ppermute(to_far, "blk", swap("blk", 1))
+    near = lax.ppermute(to_near, "blk", swap("blk", 0))
     (upper,) = call(pack_upper_kernel, [face], [v3], flops=work)
-    near = from_near(to_near, upper)
     z_left = lax.ppermute(upper, "gz", ring("gz", 1))
     kept, given, inner = call(
         side_five,
         [(1, LANES), (1, LANES), (8, LANES)],
-        [v2, v3, both, *history, r1, r2, r3, r4, m2, m3, m4],
+        [v2, v3, both, *history, r2, r3, r4, m2, m3, m4],
         [(2 * LANES, LANES), (8, LANES), ext],
         work,
     )
-    taken = from_near(given)
+    taken = lax.ppermute(given, "blk", swap("blk", 0))
     row, part = call(
-        couple_kernel, [(1, LANES), (8, LANES)], [v3, near, z_left, inner, kept, taken], flops=work
+        couple_kernel, [(1, LANES), (8, LANES)], [v3, z_left, inner, kept, taken], flops=work
     )
     devices = lax.axis_size("blk") * lax.axis_size("gz")
-    (outgoing,) = call(send_kernel, [(devices, LANES)], [v3, far, part, row], flops=work)
+    (outgoing,) = call(send_kernel, [(devices, LANES)], [v3, far, near, part, row], flops=work)
     received = lax.all_to_all(outgoing.reshape(devices, 1, LANES), ("blk", "gz"), 0, 0, tiled=True)
     return tuple(
         call(

time: 76.7 us -> 74.1 us (0.966)
  blocking collectives: 20.5 us -> 18.9 us
  starting transfers between devices: 34.6 us -> 33.6 us
    ppermute x13, starting transfers between devices: 25.8 us -> 23.7 us  [the longest x5 16.1 us: x_halo(): return (lax.ppermute(block, 'blk', swap('blk', 0)), far)]
    ppermute x4, starting transfers between devices: 1.64 us -> 3.74 us  [z_halo(): lax.ppermute(face_a, 'gz', swap('gz', 0))]
    ppermute x13, waiting for transfers between devices: 2.79 us -> 0.87 us  [the longest x1 0.84 us: on_device(): taken = lax.ppermute(given, 'blk', swap('blk', 0))]
    all_to_all x1, blocking collectives: 20.5 us -> 18.9 us  [on_device(): lax.all_to_all(outgoing.reshape(devices, 1, LANES), ('blk', 'gz'), 0, 0,...]
    ppermute x1, waiting for transfers between devices: 0.01 us -> 1.15 us  [on_device(): z_left = lax.ppermute(upper, 'gz', ring('gz', 1))]
    ppermute x4, starting transfers between devices: 6.73 us -> 5.7 us  [z_halo(): lax.ppermute(face_b, 'gz', swap('gz', 1))]
    ppermute x4, waiting for transfers between devices: 0.82 us -> 1.75 us  [z_halo(): lax.ppermute(face_b, 'gz', swap('gz', 1))]
  transfers between devices with their start and end apart: 22 -> 22, of which waited for: 4 -> 4; matrix products, arithmetic and copies ran while one was open for 0% -> 0% of each run, Pallas kernels for 15% -> 17%
where the time goes in v6:
time: 74.1 us; the launch traced here: 73.9 us
  starting transfers between devices  33.6 us (45%)
  blocking collectives  18.9 us (26%)
  Pallas kernels  15.2 us (21%)
  waiting for transfers between devices  3.78 us (5%)
  local copies, waits for them, and re-layouts  1.42 us (2%)
  between operations  0.94 us (1%)
    all_to_all x1, blocking collectives, on_device(): lax.all_to_all(outgoing.reshape(devices, 1, LANES), ('blk', 'gz'), 0, 0,...  18.9 us
    ppermute x5, starting transfers between devices, x_halo(): return (lax.ppermute(block, 'blk', swap('blk', 0)), far)  16.1 us
    pallas_call x21, Pallas kernels, call(): pl.pallas_call(kernel, out_shape=shapes, in_specs=[pl.BlockSpec(memory_sp...  15.2 us
    ppermute x4, starting transfers between devices, z_halo(): lax.ppermute(face_b, 'gz', swap('gz', 1))  5.7 us
    ppermute x5, starting transfers between devices, x_halo(): far = lax.ppermute(block, 'blk', swap('blk', 1))  4.13 us
    ppermute x4, starting transfers between devices, z_halo(): lax.ppermute(face_a, 'gz', swap('gz', 0))  3.74 us
    ppermute x1, starting transfers between devices, on_device(): near = lax.ppermute(to_near, 'blk', swap('blk', 0))  2.98 us
    ppermute x4, waiting for transfers between devices, z_halo(): lax.ppermute(face_b, 'gz', swap('gz', 1))  1.75 us
  transfers between devices with their start and end apart: 22, of which 4 were waited for; matrix products, arithmetic and copies ran while one was open for 0% of the time, Pallas kernels for 17%

profile of v6, /device:TPU:1, one launch (start us, length us, event | category | flops | bytes accessed | tf_op | source)
XLA Modules:
  0.0 73.9 jit_solution(16373408509983872842)
XLA Ops:
  0.7 2.7 %collective-permute-start.3 = (f32[6,64,128]{2,1,0:T(8,128)}, f32[6,64,128]{2,1,0:T(8,128)S(1)}, u32[]{:S(2)}, u32[]{:S(2)}) collective-permute-start(f32[6,64,128]{2,1,0:T(8,128)} %hartree.1), channel_id=1, source_target_pairs={{0,252},{4,8},{8,4},{12,16},{16,12},{20,24},{24,20},{28,32},{32,28... | collective-permute-start | bytes 589832 | tf_op jit(solution)/shard_map/ppermute | solution.py:693
  3.3 6.4 %collective-permute-start.2 = (f32[6,64,128]{2,1,0:T(8,128)}, f32[6,64,128]{2,1,0:T(8,128)S(1)}, u32[]{:S(2)}, u32[]{:S(2)}) collective-permute-start(f32[6,64,128]{2,1,0:T(8,128)} %hartree.1), channel_id=1, source_target_pairs={{0,4},{4,0},{8,12},{12,8},{16,20},{20,16},{24,28},{28,24},{32,36},... | collective-permute-start | bytes 589832 | tf_op jit(solution)/shard_map/ppermute | solution.py:694
  9.7 1.3 %shard_map.77 = (f32[12,64,128]{2,1,0:T(8,128)S(1)}, f32[6,64,128]{2,1,0:T(8,128)S(1)}, f32[48,128]{1,0:T(8,128)S(1)}, f32[48,128]{1,0:T(8,128)S(1)}) custom-call(f32[6,64,128]{2,1,0:T(8,128)} %hartree.1, f32[6,64,128]{2,1,0:T(8,128)} %density.1, f32[6,64,128]{2,1,0:T(8,128)} %charge.1), custom_call_target="tpu_custom_call" | custom-call | bytes 1228800 | tf_op jit(solution)/shard_map/pallas_call | solution.py:667
  11.0 1.4 %collective-permute-start = (f32[48,128]{1,0:T(8,128)S(1)}, f32[48,128]{1,0:T(8,128)S(1)}, u32[]{:S(2)}, u32[]{:S(2)}) collective-permute-start(f32[48,128]{1,0:T(8,128)S(1)} %get-tuple-element.33), channel_id=1, source_target_pairs={{0,1},{1,0},{2,3},{3,2},{4,5},{5,4},{6,7},{7,6},{8,9},{9,8},{10,11... | collective-permute-start | bytes 73736 | tf_op jit(solution)/shard_map/ppermute | solution.py:698
  12.4 1.9 %collective-permute-start.1 = (f32[48,128]{1,0:T(8,128)S(1)}, f32[48,128]{1,0:T(8,128)S(1)}, u32[]{:S(2)}, u32[]{:S(2)}) collective-permute-start(f32[48,128]{1,0:T(8,128)S(1)} %get-tuple-element.34), channel_id=1, source_target_pairs={{0,3},{1,2},{2,1},{3,0},{4,7},{5,6},{6,5},{7,4},{8,11},{9,10},{10,... | collective-permute-start | bytes 73736 | tf_op jit(solution)/shard_map/ppermute | solution.py:698
  14.3 0.7 shard_map.78.inner
  15.0 1.3 %collective-permute-done.1.z_second = f32[48,128]{1,0:T(8,128)S(1)} collective-permute-done((f32[48,128]{1,0:T(8,128)S(1)}, f32[48,128]{1,0:T(8,128)S(1)}, u32[]{:S(2)}, u32[]{:S(2)}) %collective-permute-start.1) | collective-permute-done | bytes 24608 | tf_op jit(solution)/shard_map/ppermute | solution.py:698
  16.3 0.3 shard_map.79.inner
  16.6 0.1 shard_map.80.vector.block.prior.v0
  16.7 0.1 collective-permute-start.7
  16.8 1.7 %collective-permute-start.6 = (f32[6,64,128]{2,1,0:T(8,128)S(1)}, f32[6,64,128]{2,1,0:T(8,128)S(1)}, u32[]{:S(2)}, u32[]{:S(2)}) collective-permute-start(f32[6,64,128]{2,1,0:T(8,128)S(1)} %shard_map.80.vector.block.prior.v0), channel_id=1, source_target_pairs={{0,4},{4,0},{8,12},{12,8},{16,20},{20,16},{24,28},{28,24},{32,36},... | collective-permute-start | bytes 589832 | tf_op jit(solution)/shard_map/ppermute | solution.py:694
  18.6 0.2 shard_map.82
  18.7 1.4 %collective-permute-start.4 = (f32[24,128]{1,0:T(8,128)S(1)}, f32[24,128]{1,0:T(8,128)S(1)}, u32[]{:S(2)}, u32[]{:S(2)}) collective-permute-start(f32[24,128]{1,0:T(8,128)S(1)} %get-tuple-element.36), channel_id=1, source_target_pairs={{0,1},{1,0},{2,3},{3,2},{4,5},{5,4},{6,7},{7,6},{8,9},{9,8},{10,11... | collective-permute-start | bytes 36872 | tf_op jit(solution)/shard_map/ppermute | solution.py:698
  20.1 1.9 %collective-permute-start.5 = (f32[24,128]{1,0:T(8,128)S(1)}, f32[24,128]{1,0:T(8,128)S(1)}, u32[]{:S(2)}, u32[]{:S(2)}) collective-permute-start(f32[24,128]{1,0:T(8,128)S(1)} %get-tuple-element.37), channel_id=1, source_target_pairs={{0,3},{1,2},{2,1},{3,0},{4,7},{5,6},{6,5},{7,4},{8,11},{9,10},{10,... | collective-permute-start | bytes 36872 | tf_op jit(solution)/shard_map/ppermute | solution.py:698
  22.0 1.4 %copy-done.1 = f32[8,6,64,128]{3,2,1,0:T(8,128)S(1)} copy-done((f32[8,6,64,128]{3,2,1,0:T(8,128)S(1)}, f32[8,6,64,128]{3,2,1,0:T(8,128)}, u32[]{:S(2)}) %copy-start.1) | copy-done | bytes 1572888
  23.4 1.1 %shard_map.81 = (f32[6,64,128]{2,1,0:T(8,128)S(1)}, f32[24,128]{1,0:T(8,128)S(1)}, f32[8,128]{1,0:T(8,128)S(1)}) custom-call(f32[6,64,128]{2,1,0:T(8,128)S(1)} %shard_map.80.vector.block.prior.v0, f32[12,64,128]{2,1,0:T(8,128)S(1)} %get-tuple-element.31.both, f32[8,6,64,128]{3,2,1,0:T(8,128)S(1)} %copy-done, f32[8,6,64,128]{3,2,1,0:T(8,128)S(1)} %copy-done.1), custom_call_target="tpu_custom_call" | custom-call | flops 14745600 | bytes 3948544 | tf_op jit(solution)/shard_map/pallas_call | solution.py:667
  24.6 3.7 %collective-permute-start.8 = (f32[6,64,128]{2,1,0:T(8,128)S(1)}, f32[6,64,128]{2,1,0:T(8,128)S(1)}, u32[]{:S(2)}, u32[]{:S(2)}) collective-permute-start(f32[6,64,128]{2,1,0:T(8,128)S(1)} %copy-done.4), channel_id=1, source_target_pairs={{0,4},{4,0},{8,12},{12,8},{16,20},{20,16},{24,28},{28,24},{32,36},... | collective-permute-start | bytes 589832 | tf_op jit(solution)/shard_map/ppermute | solution.py:694
  28.2 0.3 shard_map.83.inner
  28.5 0.1 shard_map.84.vector.block.prior.v1
  28.7 0.1 collective-permute-start.13
  28.8 2.1 %collective-permute-start.12 = (f32[6,64,128]{2,1,0:T(8,128)S(1)}, f32[6,64,128]{2,1,0:T(8,128)S(1)}, u32[]{:S(2)}, u32[]{:S(2)}) collective-permute-start(f32[6,64,128]{2,1,0:T(8,128)S(1)} %shard_map.84.vector.block.prior.v1), channel_id=1, source_target_pairs={{0,4},{4,0},{8,12},{12,8},{16,20},{20,16},{24,28},{28,24},{32,36},... | collective-permute-start | bytes 589832 | tf_op jit(solution)/shard_map/ppermute | solution.py:694
  30.8 0.2 shard_map.86
  31.0 0.5 collective-permute-start.10
  31.5 0.5 collective-permute-start.11
  32.0 3.1 %shard_map.85 = (f32[6,64,128]{2,1,0:T(8,128)S(1)}, f32[6,64,128]{2,1,0:T(8,128)S(1)}, f32[72,128]{1,0:T(8,128)S(1)}, f32[8,128]{1,0:T(8,128)S(1)}) custom-call(f32[6,64,128]{2,1,0:T(8,128)S(1)} %shard_map.80.vector.block.prior.v0, f32[6,64,128]{2,1,0:T(8,128)S(1)} %shard_map.84.vector.block.prior.v1, f32[12,64,128]{2,1,0:T(8,128)S(1)} %get-tuple-element.31.both, ...), custom_call_target="tpu_custom_call" | custom-call | flops 14745600 | bytes 5005312 | tf_op jit(solution)/shard_map/pallas_call | solution.py:667
  35.0 0.5 collective-permute-done.11.z_second
  35.5 0.3 shard_map.87.inner
  35.8 0.1 shard_map.88.vector.block.prior.v2
  36.0 1.3 %collective-permute-start.17 = (f32[6,64,128]{2,1,0:T(8,128)S(1)}, f32[6,64,128]{2,1,0:T(8,128)S(1)}, u32[]{:S(2)}, u32[]{:S(2)}) collective-permute-start(f32[6,64,128]{2,1,0:T(8,128)S(1)} %shard_map.88.vector.block.prior.v2), channel_id=1, source_target_pairs={{0,252},{4,8},{8,4},{12,16},{16,12},{20,24},{24,20},{28,32},{32,28... | collective-permute-start | bytes 589832 | tf_op jit(solution)/shard_map/ppermute | solution.py:693
  37.2 2.2 %collective-permute-start.16 = (f32[6,64,128]{2,1,0:T(8,128)S(1)}, f32[6,64,128]{2,1,0:T(8,128)S(1)}, u32[]{:S(2)}, u32[]{:S(2)}) collective-permute-start(f32[6,64,128]{2,1,0:T(8,128)S(1)} %shard_map.88.vector.block.prior.v2), channel_id=1, source_target_pairs={{0,4},{4,0},{8,12},{12,8},{16,20},{20,16},{24,28},{28,24},{32,36},... | collective-permute-start | bytes 589832 | tf_op jit(solution)/shard_map/ppermute | solution.py:694
  39.4 0.2 shard_map.90
  39.6 0.5 collective-permute-start.14
  40.1 1.4 %collective-permute-start.15 = (f32[24,128]{1,0:T(8,128)S(1)}, f32[24,128]{1,0:T(8,128)S(1)}, u32[]{:S(2)}, u32[]{:S(2)}) collective-permute-start(f32[24,128]{1,0:T(8,128)S(1)} %get-tuple-element.45), channel_id=1, source_target_pairs={{0,3},{1,2},{2,1},{3,0},{4,7},{5,6},{6,5},{7,4},{8,11},{9,10},{10,... | collective-permute-start | bytes 36872 | tf_op jit(solution)/shard_map/ppermute | solution.py:698
  41.5 3.0 %shard_map.89 = (f32[6,64,128]{2,1,0:T(8,128)S(1)}, f32[144,128]{1,0:T(8,128)S(1)}, f32[8,128]{1,0:T(8,128)S(1)}) custom-call(f32[6,64,128]{2,1,0:T(8,128)S(1)} %shard_map.84.vector.block.prior.v1, f32[6,64,128]{2,1,0:T(8,128)S(1)} %shard_map.88.vector.block.prior.v2, f32[12,64,128]{2,1,0:T(8,128)S(1)} %get-tuple-element.31.both, ...), custom_call_target="tpu_custom_call" | custom-call | flops 14745600 | bytes 4403200 | tf_op jit(solution)/shard_map/pallas_call | solution.py:667
  44.6 0.3 shard_map.91.inner
  44.9 0.1 shard_map.92
  45.0 0.1 collective-permute-start.18
  45.1 3.0 %collective-permute-start.19 = (f32[6,32,128]{2,1,0:T(8,128)S(1)}, f32[6,32,128]{2,1,0:T(8,128)S(1)}, u32[]{:S(2)}, u32[]{:S(2)}) collective-permute-start(f32[6,32,128]{2,1,0:T(8,128)S(1)} %get-tuple-element.48), channel_id=1, source_target_pairs={{0,4},{4,0},{8,12},{12,8},{16,20},{20,16},{24,28},{28,24},{32,36},... | collective-permute-start | bytes 294920 | tf_op jit(solution)/shard_map/ppermute | solution.py:757
  48.1 0.1 shard_map.93
  48.2 0.5 collective-permute-start.20
  48.7 1.3 %shard_map.94 = (f32[1,128]{1,0:T(1,128)S(1)}, f32[1,128]{1,0:T(1,128)S(1)}, f32[8,128]{1,0:T(8,128)S(1)}) custom-call(f32[6,64,128]{2,1,0:T(8,128)S(1)} %shard_map.88.vector.block.prior.v2, f32[6,64,128]{2,1,0:T(8,128)S(1)} %get-tuple-element.46.block.vector.own.v3, f32[12,64,128]{2,1,0:T(8,128)S(1)} %get-tuple-element.31.both, ...), custom_call_target="tpu_custom_call" | custom-call | flops 14745600 | bytes 4072448 | tf_op jit(solution)/shard_map/pallas_call | solution.py:667
  50.0 0.4 collective-permute-start.21
  50.3 0.8 %collective-permute-done.21.taken = f32[1,128]{1,0:T(1,128)S(1)} collective-permute-done((f32[1,128]{1,0:T(1,128)S(1)}, f32[1,128]{1,0:T(1,128)S(1)}, u32[]{:S(2)}, u32[]{:S(2)}) %collective-permute-start.21) | collective-permute-done | bytes 544 | tf_op jit(solution)/shard_map/ppermute | solution.py:767
  51.2 1.1 %collective-permute-done.20.z_left = f32[24,128]{1,0:T(8,128)S(1)} collective-permute-done((f32[24,128]{1,0:T(8,128)S(1)}, f32[24,128]{1,0:T(8,128)S(1)}, u32[]{:S(2)}, u32[]{:S(2)}) %collective-permute-start.20) | collective-permute-done | bytes 12320 | tf_op jit(solution)/shard_map/ppermute | solution.py:759
  52.3 0.2 shard_map.95
  52.6 0.6 shard_map.96
  53.2 18.9 %all_to_all.5 = f32[256,1,128]{2,1,0:T(1,128)S(1)} all-to-all(f32[256,1,128]{2,1,0:T(1,128)S(1)} %bitcast.5), channel_id=1, replica_groups=mesh['blk'=64,'gz'=4] {'blk','gz'}, dimensions={0} | all-to-all | bytes 262144 | tf_op jit(solution)/shard_map/all_to_all | solution.py:773
  72.2 1.7 %shard_map.97 = (f32[6,64,128]{2,1,0:T(8,128)}, f32[6,64,128]{2,1,0:T(8,128)}) custom-call(f32[256,128]{1,0:T(8,128)S(1)} %bitcast.4, f32[12,64,128]{2,1,0:T(8,128)S(1)} %get-tuple-element.31.both, f32[6,64,128]{2,1,0:T(8,128)S(1)} %get-tuple-element.42.grad, f32[6,64,128]{2,1,0:T(8,128)S(1)} %shard_map.80.vector.block.prior.v0, ...), custom_call_target="tpu_custom_call" | custom-call | flops 14745600 | bytes 5046272 | tf_op jit(solution)/shard_map/pallas_call | solution.py:667
  (28 shorter events, 0.1 us)
Async XLA Ops:
  0.6 21.4 %copy-start.4 = (f32[6,64,128]{2,1,0:T(8,128)S(1)}, f32[6,64,128]{2,1,0:T(8,128)}, u32[]{:S(2)}) copy-start(f32[6,64,128]{2,1,0:T(8,128)} %density.1) | copy-start | bytes 589828
  0.6 21.4 %copy-start = (f32[8,6,64,128]{3,2,1,0:T(8,128)S(1)}, f32[8,6,64,128]{3,2,1,0:T(8,128)}, u32[]{:S(2)}) copy-start(f32[8,6,64,128]{3,2,1,0:T(8,128)} %steps.9) | copy-start | bytes 4718596
  0.7 15.9 %collective-permute-start.3 = (f32[6,64,128]{2,1,0:T(8,128)}, f32[6,64,128]{2,1,0:T(8,128)S(1)}, u32[]{:S(2)}, u32[]{:S(2)}) collective-permute-start(f32[6,64,128]{2,1,0:T(8,128)} %hartree.1), channel_id=1, source_target_pairs={{0,252},{4,8},{8,4},{12,16},{16,12},{20,24},{24,20},{28,32},{32,28... | collective-permute-start | bytes 589832 | tf_op jit(solution)/shard_map/ppermute | solution.py:693
  3.3 13.2 %collective-permute-start.2 = (f32[6,64,128]{2,1,0:T(8,128)}, f32[6,64,128]{2,1,0:T(8,128)S(1)}, u32[]{:S(2)}, u32[]{:S(2)}) collective-permute-start(f32[6,64,128]{2,1,0:T(8,128)} %hartree.1), channel_id=1, source_target_pairs={{0,4},{4,0},{8,12},{12,8},{16,20},{20,16},{24,28},{28,24},{32,36},... | collective-permute-start | bytes 589832 | tf_op jit(solution)/shard_map/ppermute | solution.py:694
  11.0 4.0 %collective-permute-start = (f32[48,128]{1,0:T(8,128)S(1)}, f32[48,128]{1,0:T(8,128)S(1)}, u32[]{:S(2)}, u32[]{:S(2)}) collective-permute-start(f32[48,128]{1,0:T(8,128)S(1)} %get-tuple-element.33), channel_id=1, source_target_pairs={{0,1},{1,0},{2,3},{3,2},{4,5},{5,4},{6,7},{7,6},{8,9},{9,8},{10,11... | collective-permute-start | bytes 73736 | tf_op jit(solution)/shard_map/ppermute | solution.py:698
  12.4 3.9 %collective-permute-start.1 = (f32[48,128]{1,0:T(8,128)S(1)}, f32[48,128]{1,0:T(8,128)S(1)}, u32[]{:S(2)}, u32[]{:S(2)}) collective-permute-start(f32[48,128]{1,0:T(8,128)S(1)} %get-tuple-element.34), channel_id=1, source_target_pairs={{0,3},{1,2},{2,1},{3,0},{4,7},{5,6},{6,5},{7,4},{8,11},{9,10},{10,... | collective-permute-start | bytes 73736 | tf_op jit(solution)/shard_map/ppermute | solution.py:698
  16.7 11.8 %collective-permute-start.7 = (f32[6,64,128]{2,1,0:T(8,128)S(1)}, f32[6,64,128]{2,1,0:T(8,128)S(1)}, u32[]{:S(2)}, u32[]{:S(2)}) collective-permute-start(f32[6,64,128]{2,1,0:T(8,128)S(1)} %shard_map.80.vector.block.prior.v0), channel_id=1, source_target_pairs={{0,252},{4,8},{8,4},{12,16},{16,12},{20,24},{24,20},{28,32},{32,28... | collective-permute-start | bytes 589832 | tf_op jit(solution)/shard_map/ppermute | solution.py:693
  16.8 11.7 %collective-permute-start.6 = (f32[6,64,128]{2,1,0:T(8,128)S(1)}, f32[6,64,128]{2,1,0:T(8,128)S(1)}, u32[]{:S(2)}, u32[]{:S(2)}) collective-permute-start(f32[6,64,128]{2,1,0:T(8,128)S(1)} %shard_map.80.vector.block.prior.v0), channel_id=1, source_target_pairs={{0,4},{4,0},{8,12},{12,8},{16,20},{20,16},{24,28},{28,24},{32,36},... | collective-permute-start | bytes 589832 | tf_op jit(solution)/shard_map/ppermute | solution.py:694
  18.7 5.8 %collective-permute-start.4 = (f32[24,128]{1,0:T(8,128)S(1)}, f32[24,128]{1,0:T(8,128)S(1)}, u32[]{:S(2)}, u32[]{:S(2)}) collective-permute-start(f32[24,128]{1,0:T(8,128)S(1)} %get-tuple-element.36), channel_id=1, source_target_pairs={{0,1},{1,0},{2,3},{3,2},{4,5},{5,4},{6,7},{7,6},{8,9},{9,8},{10,11... | collective-permute-start | bytes 36872 | tf_op jit(solution)/shard_map/ppermute | solution.py:698
  20.1 8.1 %collective-permute-start.5 = (f32[24,128]{1,0:T(8,128)S(1)}, f32[24,128]{1,0:T(8,128)S(1)}, u32[]{:S(2)}, u32[]{:S(2)}) collective-permute-start(f32[24,128]{1,0:T(8,128)S(1)} %get-tuple-element.37), channel_id=1, source_target_pairs={{0,3},{1,2},{2,1},{3,0},{4,7},{5,6},{6,5},{7,4},{8,11},{9,10},{10,... | collective-permute-start | bytes 36872 | tf_op jit(solution)/shard_map/ppermute | solution.py:698
  22.0 9.5 %collective-permute-start.9 = (f32[6,64,128]{2,1,0:T(8,128)S(1)}, f32[6,64,128]{2,1,0:T(8,128)S(1)}, u32[]{:S(2)}, u32[]{:S(2)}) collective-permute-start(f32[6,64,128]{2,1,0:T(8,128)S(1)} %copy-done.4), channel_id=1, source_target_pairs={{0,252},{4,8},{8,4},{12,16},{16,12},{20,24},{24,20},{28,32},{32,28... | collective-permute-start | bytes 589832 | tf_op jit(solution)/shard_map/ppermute | solution.py:693
  22.0 1.4 %copy-start.1 = (f32[8,6,64,128]{3,2,1,0:T(8,128)S(1)}, f32[8,6,64,128]{3,2,1,0:T(8,128)}, u32[]{:S(2)}) copy-start(f32[8,6,64,128]{3,2,1,0:T(8,128)} %changes.9) | copy-start | bytes 4718596
  23.4 8.5 %copy-start.2 = (f32[8,6,64,128]{3,2,1,0:T(8,128)S(1)}, f32[8,6,64,128]{3,2,1,0:T(8,128)}, u32[]{:S(2)}) copy-start(f32[8,6,64,128]{3,2,1,0:T(8,128)} %changes.9) | copy-start | bytes 4718596
  23.4 8.5 %copy-start.3 = (f32[6,64,128]{2,1,0:T(8,128)S(1)}, f32[6,64,128]{2,1,0:T(8,128)}, u32[]{:S(2)}) copy-start(f32[6,64,128]{2,1,0:T(8,128)} %potential.1) | copy-start | bytes 589828
  24.6 7.4 %collective-permute-start.8 = (f32[6,64,128]{2,1,0:T(8,128)S(1)}, f32[6,64,128]{2,1,0:T(8,128)S(1)}, u32[]{:S(2)}, u32[]{:S(2)}) collective-permute-start(f32[6,64,128]{2,1,0:T(8,128)S(1)} %copy-done.4), channel_id=1, source_target_pairs={{0,4},{4,0},{8,12},{12,8},{16,20},{20,16},{24,28},{28,24},{32,36},... | collective-permute-start | bytes 589832 | tf_op jit(solution)/shard_map/ppermute | solution.py:694
  28.7 7.1 %collective-permute-start.13 = (f32[6,64,128]{2,1,0:T(8,128)S(1)}, f32[6,64,128]{2,1,0:T(8,128)S(1)}, u32[]{:S(2)}, u32[]{:S(2)}) collective-permute-start(f32[6,64,128]{2,1,0:T(8,128)S(1)} %shard_map.84.vector.block.prior.v1), channel_id=1, source_target_pairs={{0,252},{4,8},{8,4},{12,16},{16,12},{20,24},{24,20},{28,32},{32,28... | collective-permute-start | bytes 589832 | tf_op jit(solution)/shard_map/ppermute | solution.py:693
  28.8 7.1 %collective-permute-start.12 = (f32[6,64,128]{2,1,0:T(8,128)S(1)}, f32[6,64,128]{2,1,0:T(8,128)S(1)}, u32[]{:S(2)}, u32[]{:S(2)}) collective-permute-start(f32[6,64,128]{2,1,0:T(8,128)S(1)} %shard_map.84.vector.block.prior.v1), channel_id=1, source_target_pairs={{0,4},{4,0},{8,12},{12,8},{16,20},{20,16},{24,28},{28,24},{32,36},... | collective-permute-start | bytes 589832 | tf_op jit(solution)/shard_map/ppermute | solution.py:694
  31.0 4.1 %collective-permute-start.10 = (f32[24,128]{1,0:T(8,128)S(1)}, f32[24,128]{1,0:T(8,128)S(1)}, u32[]{:S(2)}, u32[]{:S(2)}) collective-permute-start(f32[24,128]{1,0:T(8,128)S(1)} %get-tuple-element.40), channel_id=1, source_target_pairs={{0,1},{1,0},{2,3},{3,2},{4,5},{5,4},{6,7},{7,6},{8,9},{9,8},{10,11... | collective-permute-start | bytes 36872 | tf_op jit(solution)/shard_map/ppermute | solution.py:698
  31.5 4.1 %collective-permute-start.11 = (f32[24,128]{1,0:T(8,128)S(1)}, f32[24,128]{1,0:T(8,128)S(1)}, u32[]{:S(2)}, u32[]{:S(2)}) collective-permute-start(f32[24,128]{1,0:T(8,128)S(1)} %get-tuple-element.41), channel_id=1, source_target_pairs={{0,3},{1,2},{2,1},{3,0},{4,7},{5,6},{6,5},{7,4},{8,11},{9,10},{10,... | collective-permute-start | bytes 36872 | tf_op jit(solution)/shard_map/ppermute | solution.py:698
  36.0 8.9 %collective-permute-start.17 = (f32[6,64,128]{2,1,0:T(8,128)S(1)}, f32[6,64,128]{2,1,0:T(8,128)S(1)}, u32[]{:S(2)}, u32[]{:S(2)}) collective-permute-start(f32[6,64,128]{2,1,0:T(8,128)S(1)} %shard_map.88.vector.block.prior.v2), channel_id=1, source_target_pairs={{0,252},{4,8},{8,4},{12,16},{16,12},{20,24},{24,20},{28,32},{32,28... | collective-permute-start | bytes 589832 | tf_op jit(solution)/shard_map/ppermute | solution.py:693
  37.2 7.6 %collective-permute-start.16 = (f32[6,64,128]{2,1,0:T(8,128)S(1)}, f32[6,64,128]{2,1,0:T(8,128)S(1)}, u32[]{:S(2)}, u32[]{:S(2)}) collective-permute-start(f32[6,64,128]{2,1,0:T(8,128)S(1)} %shard_map.88.vector.block.prior.v2), channel_id=1, source_target_pairs={{0,4},{4,0},{8,12},{12,8},{16,20},{20,16},{24,28},{28,24},{32,36},... | collective-permute-start | bytes 589832 | tf_op jit(solution)/shard_map/ppermute | solution.py:694
  39.6 4.9 %collective-permute-start.14 = (f32[24,128]{1,0:T(8,128)S(1)}, f32[24,128]{1,0:T(8,128)S(1)}, u32[]{:S(2)}, u32[]{:S(2)}) collective-permute-start(f32[24,128]{1,0:T(8,128)S(1)} %get-tuple-element.44), channel_id=1, source_target_pairs={{0,1},{1,0},{2,3},{3,2},{4,5},{5,4},{6,7},{7,6},{8,9},{9,8},{10,11... | collective-permute-start | bytes 36872 | tf_op jit(solution)/shard_map/ppermute | solution.py:698
  40.1 4.5 %collective-permute-start.15 = (f32[24,128]{1,0:T(8,128)S(1)}, f32[24,128]{1,0:T(8,128)S(1)}, u32[]{:S(2)}, u32[]{:S(2)}) collective-permute-start(f32[24,128]{1,0:T(8,128)S(1)} %get-tuple-element.45), channel_id=1, source_target_pairs={{0,3},{1,2},{2,1},{3,0},{4,7},{5,6},{6,5},{7,4},{8,11},{9,10},{10,... | collective-permute-start | bytes 36872 | tf_op jit(solution)/shard_map/ppermute | solution.py:698
  45.0 7.6 %collective-permute-start.18 = (f32[6,32,128]{2,1,0:T(8,128)S(1)}, f32[6,32,128]{2,1,0:T(8,128)S(1)}, u32[]{:S(2)}, u32[]{:S(2)}) collective-permute-start(f32[6,32,128]{2,1,0:T(8,128)S(1)} %get-tuple-element.47), channel_id=1, source_target_pairs={{0,252},{4,8},{8,4},{12,16},{16,12},{20,24},{24,20},{28,32},{32,28... | collective-permute-start | bytes 294920 | tf_op jit(solution)/shard_map/ppermute | solution.py:756
  45.1 7.5 %collective-permute-start.19 = (f32[6,32,128]{2,1,0:T(8,128)S(1)}, f32[6,32,128]{2,1,0:T(8,128)S(1)}, u32[]{:S(2)}, u32[]{:S(2)}) collective-permute-start(f32[6,32,128]{2,1,0:T(8,128)S(1)} %get-tuple-element.48), channel_id=1, source_target_pairs={{0,4},{4,0},{8,12},{12,8},{16,20},{20,16},{24,28},{28,24},{32,36},... | collective-permute-start | bytes 294920 | tf_op jit(solution)/shard_map/ppermute | solution.py:757
  48.2 4.1 %collective-permute-start.20 = (f32[24,128]{1,0:T(8,128)S(1)}, f32[24,128]{1,0:T(8,128)S(1)}, u32[]{:S(2)}, u32[]{:S(2)}) collective-permute-start(f32[24,128]{1,0:T(8,128)S(1)} %shard_map.93), channel_id=1, source_target_pairs={{0,1},{1,2},{2,3},{3,0},{4,5},{5,6},{6,7},{7,4},{8,9},{9,10},{10,1... | collective-permute-start | bytes 36872 | tf_op jit(solution)/shard_map/ppermute | solution.py:759
  50.0 1.2 %collective-permute-start.21 = (f32[1,128]{1,0:T(1,128)S(1)}, f32[1,128]{1,0:T(1,128)S(1)}, u32[]{:S(2)}, u32[]{:S(2)}) collective-permute-start(f32[1,128]{1,0:T(1,128)S(1)} %get-tuple-element.57), channel_id=1, source_target_pairs={{0,4},{4,0},{8,12},{12,8},{16,20},{20,16},{24,28},{28,24},{32,36},... | collective-permute-start | bytes 1544 | tf_op jit(solution)/shard_map/ppermute | solution.py:767

commit v7 on v6

--- a/solution.py
+++ b/solution.py
@@ -85,11 +85,11 @@
     return quick_sum(p, e + (a[0] * b[1] + a[1] * b[0]))
 
 
-def df_div(a, b):
-    q1 = a[0] / b[0]
-    r = df_sub(a, df_mul(b, (q1, jnp.zeros_like(q1))))
-    q2 = r[0] / b[0]
-    return quick_sum(q1, q2)
+def df_over(a, b, inverse):
+    q = a[0] * inverse
+    p, e = two_prod(q, b[0])
+    rest = ((a[0] - p) - e) + (a[1] - q * b[1])
+    return quick_sum(q, rest * inverse)
 
 
 def lane_ids(shape):
@@ -381,14 +381,28 @@
     return lambda i, b: 2.0 * tile_of(both, REACH + i, b) * tile_of(vector, i, b)
 
 
-def side_one(both, charge, inner, ext):
+FETCHES = 4
+
+
+def side_one(both, charge, steps, changes, inner, steps_here, changes_here, ext, sems):
+    each = HIST // FETCHES
+    copies = [
+        pltpu.make_async_copy(src.at[pl.ds(each * n, each)], dst.at[pl.ds(each * n, each)], sems.at[FETCHES * m + n])
+        for m, (src, dst) in enumerate(((steps, steps_here), (changes, changes_here)))
+        for n in range(FETCHES)
+    ]
+    for copy in copies:
+        copy.start()
     inner_residual(both, charge, inner, ext)
+    for copy in copies:
+        copy.wait()
 
 
 def side_two(vector, both, steps, changes, inner, rows, moments, ext):
     inner_basis(vector, None, inner, ext)
     lifted, rho = lifted_tile(both, vector), density_tile(both)
-    store(rows, 0, field_dots(steps, changes, [lifted], [(rho, lifted)]))
+    values = field_dots(steps, changes, [lifted, rho], [(rho, lifted)])
+    store(rows, 0, values[:16] + values[32:] + values[16:32])
     store_moments([(vector, vector)], moments)
 
 
@@ -396,9 +410,8 @@
     inner, grad, rows, moments, ext = outs
     inner_basis(vector, prior, inner, ext)
     lifted, rho = lifted_tile(both, vector), density_tile(both)
-    values = field_dots(steps, changes, [lifted, rho], [(rho, lifted)])
-    store(rows, 0, values[:16] + values[32:] + values[16:32])
-    store(rows, 33, gram_dots(steps, changes, CROSS_PAIRS[32:]))
+    store(rows, 0, field_dots(steps, changes, [lifted], [(rho, lifted)]))
+    store(rows, 17, gram_dots(steps, changes, CROSS_PAIRS[32:]))
     store_moments([(prior, vector), (vector, vector)], moments)
     base_gradient(both, near, far, z_first, z_second, potential, grad, ext)
 
@@ -411,7 +424,6 @@
     store(rows, 0, values[:16] + values[32:33] + values[16:32] + values[33:])
     store(rows, 35, gram_dots(steps, steps, PAIRS))
     store(rows, 71, gram_dots(changes, changes, PAIRS))
-    store(rows, 107, gram_dots(steps, changes, CROSS_PAIRS[:32]))
     store_moments([(prior, vector), (vector, vector)], moments)
 
 
@@ -429,9 +441,10 @@
             at = place(base + before)
             table[at : at + count - before, :] = ref[start + before : start + count, :]
 
-    put(ROW_GRAM, r4, 35, 104)
-    put(ROW_GRAM + 104, r3, 33, 32)
-    put(ROW_BASE, r3, 17, 16)
+    put(ROW_GRAM, r4, 35, 72)
+    store(table, ROW_GRAM + 72, gram_dots(steps, changes, CROSS_PAIRS[:32]))
+    put(ROW_GRAM + 104, r3, 17, 32)
+    put(ROW_BASE, r2, 17, 16)
     put(ROW_BASE + 16, r4, 17, 18)
     for n, rows in enumerate((r2, r3, r4)):
         put(ROW_W + 17 * n, rows, 0, 17)
@@ -527,24 +540,25 @@
 
     mat = {(i, j): df_add(moved(i, j), gram(i, j)) for i in range(4) for j in range(i + 1)}
     rhs = [df_scale(gram(i, 0), 1.0 / SHIFT) for i in range(4)]
-    low = {}
+    low, inverse = {}, []
     for k in range(4):
+        inverse.append(1.0 / mat[k, k][0])
         for i in range(k + 1, 4):
-            low[i, k] = df_div(mat[i, k], mat[k, k])
+            low[i, k] = df_over(mat[i, k], mat[k, k], inverse[k])
         for i in range(k + 1, 4):
             for j in range(k + 1, i + 1):
                 mat[i, j] = df_sub(mat[i, j], df_mul(low[i, k], mat[j, k]))
             rhs[i] = df_sub(rhs[i], df_mul(low[i, k], rhs[k]))
     sol = [None] * 4
     for k in reversed(range(4)):
-        value = df_div(rhs[k], mat[k, k])
+        value = df_over(rhs[k], mat[k, k], inverse[k])
         for i in range(k + 1, 4):
             value = df_sub(value, df_mul(low[i, k], sol[i]))
         sol[k] = value
     return [hi + lo for hi, lo in sol]
 
 
-def final_kernel(received, both, grad, v0, v1, v2, v3, steps, changes, new_density, new_hartree, spread):
+def final_kernel(received, both, grad, v0, v1, v2, v3, steps, changes, new_density, new_hartree, spread, density_here, hartree_here, sems):
     parts = [(received[8 * n : 8 * n + 8, :], jnp.zeros((8, LANES), jnp.float32)) for n in range(4)]
     for n in range(4, received.shape[0] // 8):
         parts[n % 4] = add_tile(parts[n % 4], received[8 * n : 8 * n + 8, :])
@@ -643,32 +657,42 @@
     change_mix = [wide(value) for value in change_mix]
     basis = (v0, v1, v2, v3)
 
-    @pl.loop(0, REACH)
-    def _(i):
+    def leave(i):
+        return [
+            pltpu.make_async_copy(here.at[i], out.at[i], sems.at[n, i])
+            for n, (here, out) in enumerate(((density_here, new_density), (hartree_here, new_hartree)))
+        ]
+
+    for i in range(REACH):
         for b in range(8):
             at = pl.ds(8 * b, 8)
             rho = both[REACH + i, at, :]
             lift = mix[0] * v0[i, at, :]
             for j in range(1, 4):
                 lift = lift + mix[j] * basis[j][i, at, :]
-            new_hartree[i, at, :] = both[i, at, :] + lift
+            hartree_here[i, at, :] = both[i, at, :] + lift
             slope = grad[i, at, :] + 2.0 * rho * lift - chem * rho
             parts = [rho, gain * slope, step_mix[0] * steps[0, i, at, :], change_mix[0] * changes[0, i, at, :]]
             for f in range(1, HIST):
                 parts[2] = parts[2] + step_mix[f] * steps[f, i, at, :]
                 parts[3] = parts[3] + change_mix[f] * changes[f, i, at, :]
-            new_density[i, at, :] = parts[0] + (parts[1] + (parts[2] + parts[3]))
-
-
-def call(kernel, outs, args, scratch=(), flops=0, place=pltpu.VMEM):
-    whole = pl.BlockSpec(memory_space=pltpu.VMEM)
+            density_here[i, at, :] = parts[0] + (parts[1] + (parts[2] + parts[3]))
+        for copy in leave(i):
+            copy.start()
+    for i in range(REACH):
+        for copy in leave(i):
+            copy.wait()
+
+
+def call(kernel, outs, args, scratch=(), flops=0, in_hbm=(), out_hbm=False):
+    args = [pltpu.with_memory_space_constraint(x, pltpu.HBM) if n in in_hbm else x for n, x in enumerate(args)]
     shapes = [jax.ShapeDtypeStruct(shape, jnp.float32) for shape in outs]
     size = sum(4 * math.prod(a.shape) for a in (*args, *shapes))
     return pl.pallas_call(
         kernel,
         out_shape=shapes,
-        in_specs=[pl.BlockSpec(memory_space=place)] * len(args),
-        out_specs=[whole] * len(outs),
+        in_specs=[pl.BlockSpec(memory_space=pltpu.HBM if n in in_hbm else pltpu.VMEM) for n in range(len(args))],
+        out_specs=[pl.BlockSpec(memory_space=pltpu.HBM if out_hbm else pltpu.VMEM)] * len(outs),
         scratch_shapes=[pltpu.VMEM(s, jnp.float32) if isinstance(s, tuple) else s for s in scratch],
         cost_estimate=pl.CostEstimate(flops=flops, bytes_accessed=size, transcendentals=0),
         compiler_params=pltpu.CompilerParams(vmem_limit_bytes=VMEM_LIMIT),
@@ -703,18 +727,16 @@
     ext = (block[0], block[1] + 16, block[2])
     face = (24, LANES)
     cells = math.prod(block)
-    history = [hist_steps, hist_changes]
     cells = math.prod(block)
-    history = [hist_steps, hist_changes]
     work = 300 * cells
     inputs = (hartree_prev, sqrt_density, ion_charge)
     halo = x_halo(hartree_prev)
     both, charge, *faces = call(
         launch_kernel,
         [(2 * REACH, *block[1:]), block, (48, LANES), (48, LANES)],
-        [pltpu.with_memory_space_constraint(x, pltpu.HBM) for x in inputs],
+        inputs,
         [pltpu.SemaphoreType.DMA((3,))],
-        place=pltpu.HBM,
+        in_hbm=(0, 1, 2),
     )
     ends = z_halo(*faces)
     density_ends = ends
@@ -733,16 +755,24 @@
         halo = x_halo(block_now)
         return halo, z_halo(*call(pack_kernel, [face, face], [block_now], flops=work))
 
-    (inner,) = call(side_one, [block], [both, charge], [ext], work)
+    stored = hist_steps.shape
+    inner, *history = call(
+        side_one,
+        [block, stored, stored],
+        [both, charge, hist_steps, hist_changes],
+        [ext, pltpu.SemaphoreType.DMA((2 * FETCHES,))],
+        work,
+        in_hbm=(2, 3),
+    )
     (v0,) = advance(1.0, inner, halo, ends)
     halo, ends = exchange(v0)
     density_halo = x_halo(after((sqrt_density,), v0)[0])
-    inner, r2, m2 = call(side_two, [block, (24, LANES), (8, LANES)], [v0, both, *history], [ext], work)
+    inner, r2, m2 = call(side_two, [block, (40, LANES), (8, LANES)], [v0, both, *history], [ext], work)
     (v1,) = advance(-1.0 / SHIFT, inner, halo, ends)
     halo, ends = exchange(v1)
     inner, grad, r3, m3 = call(
         side_three,
-        [block, block, (72, LANES), (8, LANES)],
+        [block, block, (56, LANES), (8, LANES)],
         [v0, v1, both, *density_halo, *density_ends, ion_potential, *history],
         [ext],
         work,
@@ -750,7 +780,7 @@
     (v2,) = advance(-2.0 / SHIFT, inner, halo, ends)
     halo, ends = exchange(v2)
     inner, r4, m4 = call(
-        side_four, [block, (144, LANES), (8, LANES)], [v1, v2, both, grad, *history], [ext], work
+        side_four, [block, (112, LANES), (8, LANES)], [v1, v2, both, grad, *history], [ext], work
     )
     v3, to_near, to_far = advance(-2.0 / SHIFT, inner, halo, ends, last=True)
     far = lax.ppermute(to_far, "blk", swap("blk", 1))
@@ -776,8 +806,9 @@
             final_kernel,
             [block, block],
             [received.reshape(devices, LANES), both, grad, v0, v1, v2, v3, *history],
-            [(3 * LANES, LANES)],
+            [(3 * LANES, LANES), block, block, pltpu.SemaphoreType.DMA((2, REACH))],
             work,
+            out_hbm=True,
         )
     )
 

time: 74.1 us -> 73.6 us (level)
  Pallas kernels: 15.2 us -> 16.9 us
  waiting for transfers between devices: 3.78 us -> 2.29 us
  local copies, waits for them, and re-layouts: 1.42 us -> 0.01 us
    pallas_call x21, Pallas kernels: 15.2 us -> 16.9 us  [call(): pl.pallas_call(kernel, out_shape=shapes, in_specs=[pl.BlockSpec(memory_sp...]
    unnamed x10 -> x4, local copies, waits for them, and re-layouts: 1.42 us -> 0.01 us
    ppermute x4, waiting for transfers between devices: 1.75 us -> 0.74 us  [z_halo(): lax.ppermute(face_b, 'gz', swap('gz', 1))]
  transfers between devices with their start and end apart: 22 -> 22, of which waited for: 4 -> 3; matrix products, arithmetic and copies ran while one was open for 0% -> 0% of each run, Pallas kernels for 17% -> 19%
where the time goes in v7:
time: 73.6 us; the launch traced here: 73.4 us
  starting transfers between devices  33.5 us (46%)
  blocking collectives  19.6 us (27%)
  Pallas kernels  16.9 us (23%)
  waiting for transfers between devices  2.29 us (3%)
  between operations  1.08 us (1%)
    all_to_all x1, blocking collectives, on_device(): lax.all_to_all(outgoing.reshape(devices, 1, LANES), ('blk', 'gz'), 0, 0,...  19.6 us
    pallas_call x21, Pallas kernels, call(): pl.pallas_call(kernel, out_shape=shapes, in_specs=[pl.BlockSpec(memory_sp...  16.9 us
    ppermute x5, starting transfers between devices, x_halo(): return (lax.ppermute(block, 'blk', swap('blk', 0)), far)  15.5 us
    ppermute x4, starting transfers between devices, z_halo(): lax.ppermute(face_b, 'gz', swap('gz', 1))  5.83 us
    ppermute x5, starting transfers between devices, x_halo(): far = lax.ppermute(block, 'blk', swap('blk', 1))  4.13 us
    ppermute x4, starting transfers between devices, z_halo(): lax.ppermute(face_a, 'gz', swap('gz', 0))  3.72 us
    ppermute x1, starting transfers between devices, on_device(): near = lax.ppermute(to_near, 'blk', swap('blk', 0))  3.37 us
  transfers between devices with their start and end apart: 22, of which 3 were waited for; matrix products, arithmetic and copies ran while one was open for 0% of the time, Pallas kernels for 19%

profile of v7, /device:TPU:1, one launch (start us, length us, event | category | flops | bytes accessed | tf_op | source)
XLA Modules:
  0.0 73.4 jit_solution(10125799823637399529)
XLA Ops:
  0.6 2.7 %collective-permute-start.3 = (f32[6,64,128]{2,1,0:T(8,128)}, f32[6,64,128]{2,1,0:T(8,128)S(1)}, u32[]{:S(2)}, u32[]{:S(2)}) collective-permute-start(f32[6,64,128]{2,1,0:T(8,128)} %hartree.1), channel_id=1, source_target_pairs={{0,252},{4,8},{8,4},{12,16},{16,12},{20,24},{24,20},{28,32},{32,28... | collective-permute-start | bytes 589832 | tf_op jit(solution)/shard_map/ppermute | solution.py:717
  3.3 6.4 %collective-permute-start.2 = (f32[6,64,128]{2,1,0:T(8,128)}, f32[6,64,128]{2,1,0:T(8,128)S(1)}, u32[]{:S(2)}, u32[]{:S(2)}) collective-permute-start(f32[6,64,128]{2,1,0:T(8,128)} %hartree.1), channel_id=1, source_target_pairs={{0,4},{4,0},{8,12},{12,8},{16,20},{20,16},{24,28},{28,24},{32,36},... | collective-permute-start | bytes 589832 | tf_op jit(solution)/shard_map/ppermute | solution.py:718
  9.7 1.3 %shard_map.77 = (f32[12,64,128]{2,1,0:T(8,128)S(1)}, f32[6,64,128]{2,1,0:T(8,128)S(1)}, f32[48,128]{1,0:T(8,128)S(1)}, f32[48,128]{1,0:T(8,128)S(1)}) custom-call(f32[6,64,128]{2,1,0:T(8,128)} %hartree.1, f32[6,64,128]{2,1,0:T(8,128)} %density.1, f32[6,64,128]{2,1,0:T(8,128)} %charge.1), custom_call_target="tpu_custom_call" | custom-call | bytes 1228800 | tf_op jit(solution)/shard_map/pallas_call | solution.py:691
  11.0 1.4 %collective-permute-start = (f32[48,128]{1,0:T(8,128)S(1)}, f32[48,128]{1,0:T(8,128)S(1)}, u32[]{:S(2)}, u32[]{:S(2)}) collective-permute-start(f32[48,128]{1,0:T(8,128)S(1)} %get-tuple-element.37), channel_id=1, source_target_pairs={{0,1},{1,0},{2,3},{3,2},{4,5},{5,4},{6,7},{7,6},{8,9},{9,8},{10,11... | collective-permute-start | bytes 73736 | tf_op jit(solution)/shard_map/ppermute | solution.py:722
  12.4 1.9 %collective-permute-start.1 = (f32[48,128]{1,0:T(8,128)S(1)}, f32[48,128]{1,0:T(8,128)S(1)}, u32[]{:S(2)}, u32[]{:S(2)}) collective-permute-start(f32[48,128]{1,0:T(8,128)S(1)} %get-tuple-element.38), channel_id=1, source_target_pairs={{0,3},{1,2},{2,1},{3,0},{4,7},{5,6},{6,5},{7,4},{8,11},{9,10},{10,... | collective-permute-start | bytes 73736 | tf_op jit(solution)/shard_map/ppermute | solution.py:722
  14.3 2.5 %shard_map.78 = (f32[6,64,128]{2,1,0:T(8,128)S(1)}, f32[8,6,64,128]{3,2,1,0:T(8,128)S(1)}, f32[8,6,64,128]{3,2,1,0:T(8,128)S(1)}) custom-call(f32[12,64,128]{2,1,0:T(8,128)S(1)} %get-tuple-element.34.both, f32[6,64,128]{2,1,0:T(8,128)S(1)} %get-tuple-element.35.charge, f32[8,6,64,128]{3,2,1,0:T(8,128)} %steps.1, f32[8,6,64,128]{3,2,1,0:T(8,128)} %changes.1), custom_call_target="tpu_custom_call" | custom-call | flops 14745600 | bytes 7077888 | tf_op jit(solution)/shard_map/pallas_call | solution.py:691
  16.8 0.0 collective-permute-done.1.z_second
  16.8 0.3 shard_map.79.inner
  17.1 0.0 collective-permute-done.3.far
  17.1 0.1 shard_map.80.vector.block.prior.v0
  17.3 0.1 collective-permute-start.7
  17.4 1.2 %collective-permute-start.6 = (f32[6,64,128]{2,1,0:T(8,128)S(1)}, f32[6,64,128]{2,1,0:T(8,128)S(1)}, u32[]{:S(2)}, u32[]{:S(2)}) collective-permute-start(f32[6,64,128]{2,1,0:T(8,128)S(1)} %shard_map.80.vector.block.prior.v0), channel_id=1, source_target_pairs={{0,4},{4,0},{8,12},{12,8},{16,20},{20,16},{24,28},{28,24},{32,36},... | collective-permute-start | bytes 589832 | tf_op jit(solution)/shard_map/ppermute | solution.py:718
  18.5 0.2 shard_map.82
  18.7 1.4 %collective-permute-start.4 = (f32[24,128]{1,0:T(8,128)S(1)}, f32[24,128]{1,0:T(8,128)S(1)}, u32[]{:S(2)}, u32[]{:S(2)}) collective-permute-start(f32[24,128]{1,0:T(8,128)S(1)} %get-tuple-element.42), channel_id=1, source_target_pairs={{0,1},{1,0},{2,3},{3,2},{4,5},{5,4},{6,7},{7,6},{8,9},{9,8},{10,11... | collective-permute-start | bytes 36872 | tf_op jit(solution)/shard_map/ppermute | solution.py:722
  20.1 1.9 %collective-permute-start.5 = (f32[24,128]{1,0:T(8,128)S(1)}, f32[24,128]{1,0:T(8,128)S(1)}, u32[]{:S(2)}, u32[]{:S(2)}) collective-permute-start(f32[24,128]{1,0:T(8,128)S(1)} %get-tuple-element.43), channel_id=1, source_target_pairs={{0,3},{1,2},{2,1},{3,0},{4,7},{5,6},{6,5},{7,4},{8,11},{9,10},{10,... | collective-permute-start | bytes 36872 | tf_op jit(solution)/shard_map/ppermute | solution.py:722
  22.0 1.3 %shard_map.81 = (f32[6,64,128]{2,1,0:T(8,128)S(1)}, f32[40,128]{1,0:T(8,128)S(1)}, f32[8,128]{1,0:T(8,128)S(1)}) custom-call(f32[6,64,128]{2,1,0:T(8,128)S(1)} %shard_map.80.vector.block.prior.v0, f32[12,64,128]{2,1,0:T(8,128)S(1)} %get-tuple-element.34.both, f32[8,6,64,128]{3,2,1,0:T(8,128)S(1)} %get-tuple-element.39.steps, ...), custom_call_target="tpu_custom_call" | custom-call | flops 14745600 | bytes 3956736 | tf_op jit(solution)/shard_map/pallas_call | solution.py:691
  23.4 3.7 %collective-permute-start.8 = (f32[6,64,128]{2,1,0:T(8,128)S(1)}, f32[6,64,128]{2,1,0:T(8,128)S(1)}, u32[]{:S(2)}, u32[]{:S(2)}) collective-permute-start(f32[6,64,128]{2,1,0:T(8,128)S(1)} %copy-done.1), channel_id=1, source_target_pairs={{0,4},{4,0},{8,12},{12,8},{16,20},{20,16},{24,28},{28,24},{32,36},... | collective-permute-start | bytes 589832 | tf_op jit(solution)/shard_map/ppermute | solution.py:718
  27.0 0.3 shard_map.83.inner
  27.3 0.1 shard_map.84.vector.block.prior.v1
  27.5 0.1 collective-permute-start.13
  27.6 2.1 %collective-permute-start.12 = (f32[6,64,128]{2,1,0:T(8,128)S(1)}, f32[6,64,128]{2,1,0:T(8,128)S(1)}, u32[]{:S(2)}, u32[]{:S(2)}) collective-permute-start(f32[6,64,128]{2,1,0:T(8,128)S(1)} %shard_map.84.vector.block.prior.v1), channel_id=1, source_target_pairs={{0,4},{4,0},{8,12},{12,8},{16,20},{20,16},{24,28},{28,24},{32,36},... | collective-permute-start | bytes 589832 | tf_op jit(solution)/shard_map/ppermute | solution.py:718
  29.6 0.2 shard_map.86
  29.8 0.5 collective-permute-start.10
  30.3 0.5 collective-permute-start.11
  30.8 2.8 %shard_map.85 = (f32[6,64,128]{2,1,0:T(8,128)S(1)}, f32[6,64,128]{2,1,0:T(8,128)S(1)}, f32[56,128]{1,0:T(8,128)S(1)}, f32[8,128]{1,0:T(8,128)S(1)}) custom-call(f32[6,64,128]{2,1,0:T(8,128)S(1)} %shard_map.80.vector.block.prior.v0, f32[6,64,128]{2,1,0:T(8,128)S(1)} %shard_map.84.vector.block.prior.v1, f32[12,64,128]{2,1,0:T(8,128)S(1)} %get-tuple-element.34.both, ...), custom_call_target="tpu_custom_call" | custom-call | flops 14745600 | bytes 4997120 | tf_op jit(solution)/shard_map/pallas_call | solution.py:691
  33.6 0.7 collective-permute-done.11.z_second
  34.3 0.3 shard_map.87.inner
  34.6 0.1 shard_map.88.vector.block.prior.v2
  34.7 1.3 %collective-permute-start.17 = (f32[6,64,128]{2,1,0:T(8,128)S(1)}, f32[6,64,128]{2,1,0:T(8,128)S(1)}, u32[]{:S(2)}, u32[]{:S(2)}) collective-permute-start(f32[6,64,128]{2,1,0:T(8,128)S(1)} %shard_map.88.vector.block.prior.v2), channel_id=1, source_target_pairs={{0,252},{4,8},{8,4},{12,16},{16,12},{20,24},{24,20},{28,32},{32,28... | collective-permute-start | bytes 589832 | tf_op jit(solution)/shard_map/ppermute | solution.py:717
  36.0 2.3 %collective-permute-start.16 = (f32[6,64,128]{2,1,0:T(8,128)S(1)}, f32[6,64,128]{2,1,0:T(8,128)S(1)}, u32[]{:S(2)}, u32[]{:S(2)}) collective-permute-start(f32[6,64,128]{2,1,0:T(8,128)S(1)} %shard_map.88.vector.block.prior.v2), channel_id=1, source_target_pairs={{0,4},{4,0},{8,12},{12,8},{16,20},{20,16},{24,28},{28,24},{32,36},... | collective-permute-start | bytes 589832 | tf_op jit(solution)/shard_map/ppermute | solution.py:718
  38.3 0.2 shard_map.90
  38.4 0.5 collective-permute-start.14
  38.9 1.5 %collective-permute-start.15 = (f32[24,128]{1,0:T(8,128)S(1)}, f32[24,128]{1,0:T(8,128)S(1)}, u32[]{:S(2)}, u32[]{:S(2)}) collective-permute-start(f32[24,128]{1,0:T(8,128)S(1)} %get-tuple-element.51), channel_id=1, source_target_pairs={{0,3},{1,2},{2,1},{3,0},{4,7},{5,6},{6,5},{7,4},{8,11},{9,10},{10,... | collective-permute-start | bytes 36872 | tf_op jit(solution)/shard_map/ppermute | solution.py:722
  40.4 2.5 %shard_map.89 = (f32[6,64,128]{2,1,0:T(8,128)S(1)}, f32[112,128]{1,0:T(8,128)S(1)}, f32[8,128]{1,0:T(8,128)S(1)}) custom-call(f32[6,64,128]{2,1,0:T(8,128)S(1)} %shard_map.84.vector.block.prior.v1, f32[6,64,128]{2,1,0:T(8,128)S(1)} %shard_map.88.vector.block.prior.v2, f32[12,64,128]{2,1,0:T(8,128)S(1)} %get-tuple-element.34.both, ...), custom_call_target="tpu_custom_call" | custom-call | flops 14745600 | bytes 4386816 | tf_op jit(solution)/shard_map/pallas_call | solution.py:691
  43.0 0.3 shard_map.91.inner
  43.3 0.1 shard_map.92
  43.4 0.1 collective-permute-start.18
  43.5 3.4 %collective-permute-start.19 = (f32[6,32,128]{2,1,0:T(8,128)S(1)}, f32[6,32,128]{2,1,0:T(8,128)S(1)}, u32[]{:S(2)}, u32[]{:S(2)}) collective-permute-start(f32[6,32,128]{2,1,0:T(8,128)S(1)} %get-tuple-element.54), channel_id=1, source_target_pairs={{0,4},{4,0},{8,12},{12,8},{16,20},{20,16},{24,28},{28,24},{32,36},... | collective-permute-start | bytes 294920 | tf_op jit(solution)/shard_map/ppermute | solution.py:787
  46.9 0.1 shard_map.93
  47.0 0.5 collective-permute-start.20
  47.5 1.8 %shard_map.94 = (f32[1,128]{1,0:T(1,128)S(1)}, f32[1,128]{1,0:T(1,128)S(1)}, f32[8,128]{1,0:T(8,128)S(1)}) custom-call(f32[6,64,128]{2,1,0:T(8,128)S(1)} %shard_map.88.vector.block.prior.v2, f32[6,64,128]{2,1,0:T(8,128)S(1)} %get-tuple-element.52.block.vector.own.v3, f32[12,64,128]{2,1,0:T(8,128)S(1)} %get-tuple-element.34.both, ...), custom_call_target="tpu_custom_call" | custom-call | flops 14745600 | bytes 4056064 | tf_op jit(solution)/shard_map/pallas_call | solution.py:691
  49.3 0.4 collective-permute-start.21
  49.6 0.8 %collective-permute-done.21.taken = f32[1,128]{1,0:T(1,128)S(1)} collective-permute-done((f32[1,128]{1,0:T(1,128)S(1)}, f32[1,128]{1,0:T(1,128)S(1)}, u32[]{:S(2)}, u32[]{:S(2)}) %collective-permute-start.21) | collective-permute-done | bytes 544 | tf_op jit(solution)/shard_map/ppermute | solution.py:797
  50.5 0.7 collective-permute-done.20.z_left
  51.1 0.2 shard_map.95
  51.4 0.6 shard_map.96
  52.0 19.6 %all_to_all.5 = f32[256,1,128]{2,1,0:T(1,128)S(1)} all-to-all(f32[256,1,128]{2,1,0:T(1,128)S(1)} %bitcast.5), channel_id=1, replica_groups=mesh['blk'=64,'gz'=4] {'blk','gz'}, dimensions={0} | all-to-all | bytes 262144 | tf_op jit(solution)/shard_map/all_to_all | solution.py:803
  71.7 1.6 %shard_map.97 = (f32[6,64,128]{2,1,0:T(8,128)}, f32[6,64,128]{2,1,0:T(8,128)}) custom-call(f32[256,128]{1,0:T(8,128)S(1)} %bitcast.4, f32[12,64,128]{2,1,0:T(8,128)S(1)} %get-tuple-element.34.both, f32[6,64,128]{2,1,0:T(8,128)S(1)} %get-tuple-element.48.grad, f32[6,64,128]{2,1,0:T(8,128)S(1)} %shard_map.80.vector.block.prior.v0, ...), custom_call_target="tpu_custom_call" | custom-call | flops 14745600 | bytes 5046272 | tf_op jit(solution)/shard_map/pallas_call | solution.py:691
  (22 shorter events, 0.1 us)
Async XLA Ops:
  0.6 16.5 %collective-permute-start.3 = (f32[6,64,128]{2,1,0:T(8,128)}, f32[6,64,128]{2,1,0:T(8,128)S(1)}, u32[]{:S(2)}, u32[]{:S(2)}) collective-permute-start(f32[6,64,128]{2,1,0:T(8,128)} %hartree.1), channel_id=1, source_target_pairs={{0,252},{4,8},{8,4},{12,16},{16,12},{20,24},{24,20},{28,32},{32,28... | collective-permute-start | bytes 589832 | tf_op jit(solution)/shard_map/ppermute | solution.py:717
  3.3 13.8 %collective-permute-start.2 = (f32[6,64,128]{2,1,0:T(8,128)}, f32[6,64,128]{2,1,0:T(8,128)S(1)}, u32[]{:S(2)}, u32[]{:S(2)}) collective-permute-start(f32[6,64,128]{2,1,0:T(8,128)} %hartree.1), channel_id=1, source_target_pairs={{0,4},{4,0},{8,12},{12,8},{16,20},{20,16},{24,28},{28,24},{32,36},... | collective-permute-start | bytes 589832 | tf_op jit(solution)/shard_map/ppermute | solution.py:718
  11.0 5.8 %collective-permute-start = (f32[48,128]{1,0:T(8,128)S(1)}, f32[48,128]{1,0:T(8,128)S(1)}, u32[]{:S(2)}, u32[]{:S(2)}) collective-permute-start(f32[48,128]{1,0:T(8,128)S(1)} %get-tuple-element.37), channel_id=1, source_target_pairs={{0,1},{1,0},{2,3},{3,2},{4,5},{5,4},{6,7},{7,6},{8,9},{9,8},{10,11... | collective-permute-start | bytes 73736 | tf_op jit(solution)/shard_map/ppermute | solution.py:722
  12.4 4.5 %collective-permute-start.1 = (f32[48,128]{1,0:T(8,128)S(1)}, f32[48,128]{1,0:T(8,128)S(1)}, u32[]{:S(2)}, u32[]{:S(2)}) collective-permute-start(f32[48,128]{1,0:T(8,128)S(1)} %get-tuple-element.38), channel_id=1, source_target_pairs={{0,3},{1,2},{2,1},{3,0},{4,7},{5,6},{6,5},{7,4},{8,11},{9,10},{10,... | collective-permute-start | bytes 73736 | tf_op jit(solution)/shard_map/ppermute | solution.py:722
  14.3 7.7 %copy-start.1 = (f32[6,64,128]{2,1,0:T(8,128)S(1)}, f32[6,64,128]{2,1,0:T(8,128)}, u32[]{:S(2)}) copy-start(f32[6,64,128]{2,1,0:T(8,128)} %density.1) | copy-start | bytes 589828
  17.3 10.0 %collective-permute-start.7 = (f32[6,64,128]{2,1,0:T(8,128)S(1)}, f32[6,64,128]{2,1,0:T(8,128)S(1)}, u32[]{:S(2)}, u32[]{:S(2)}) collective-permute-start(f32[6,64,128]{2,1,0:T(8,128)S(1)} %shard_map.80.vector.block.prior.v0), channel_id=1, source_target_pairs={{0,252},{4,8},{8,4},{12,16},{16,12},{20,24},{24,20},{28,32},{32,28... | collective-permute-start | bytes 589832 | tf_op jit(solution)/shard_map/ppermute | solution.py:717
  17.4 9.9 %collective-permute-start.6 = (f32[6,64,128]{2,1,0:T(8,128)S(1)}, f32[6,64,128]{2,1,0:T(8,128)S(1)}, u32[]{:S(2)}, u32[]{:S(2)}) collective-permute-start(f32[6,64,128]{2,1,0:T(8,128)S(1)} %shard_map.80.vector.block.prior.v0), channel_id=1, source_target_pairs={{0,4},{4,0},{8,12},{12,8},{16,20},{20,16},{24,28},{28,24},{32,36},... | collective-permute-start | bytes 589832 | tf_op jit(solution)/shard_map/ppermute | solution.py:718
  18.7 4.6 %collective-permute-start.4 = (f32[24,128]{1,0:T(8,128)S(1)}, f32[24,128]{1,0:T(8,128)S(1)}, u32[]{:S(2)}, u32[]{:S(2)}) collective-permute-start(f32[24,128]{1,0:T(8,128)S(1)} %get-tuple-element.42), channel_id=1, source_target_pairs={{0,1},{1,0},{2,3},{3,2},{4,5},{5,4},{6,7},{7,6},{8,9},{9,8},{10,11... | collective-permute-start | bytes 36872 | tf_op jit(solution)/shard_map/ppermute | solution.py:722
  20.1 6.9 %collective-permute-start.5 = (f32[24,128]{1,0:T(8,128)S(1)}, f32[24,128]{1,0:T(8,128)S(1)}, u32[]{:S(2)}, u32[]{:S(2)}) collective-permute-start(f32[24,128]{1,0:T(8,128)S(1)} %get-tuple-element.43), channel_id=1, source_target_pairs={{0,3},{1,2},{2,1},{3,0},{4,7},{5,6},{6,5},{7,4},{8,11},{9,10},{10,... | collective-permute-start | bytes 36872 | tf_op jit(solution)/shard_map/ppermute | solution.py:722
  22.0 8.3 %collective-permute-start.9 = (f32[6,64,128]{2,1,0:T(8,128)S(1)}, f32[6,64,128]{2,1,0:T(8,128)S(1)}, u32[]{:S(2)}, u32[]{:S(2)}) collective-permute-start(f32[6,64,128]{2,1,0:T(8,128)S(1)} %copy-done.1), channel_id=1, source_target_pairs={{0,252},{4,8},{8,4},{12,16},{16,12},{20,24},{24,20},{28,32},{32,28... | collective-permute-start | bytes 589832 | tf_op jit(solution)/shard_map/ppermute | solution.py:717
  22.0 8.8 %copy-start = (f32[6,64,128]{2,1,0:T(8,128)S(1)}, f32[6,64,128]{2,1,0:T(8,128)}, u32[]{:S(2)}) copy-start(f32[6,64,128]{2,1,0:T(8,128)} %potential.1) | copy-start | bytes 589828
  23.4 7.4 %collective-permute-start.8 = (f32[6,64,128]{2,1,0:T(8,128)S(1)}, f32[6,64,128]{2,1,0:T(8,128)S(1)}, u32[]{:S(2)}, u32[]{:S(2)}) collective-permute-start(f32[6,64,128]{2,1,0:T(8,128)S(1)} %copy-done.1), channel_id=1, source_target_pairs={{0,4},{4,0},{8,12},{12,8},{16,20},{20,16},{24,28},{28,24},{32,36},... | collective-permute-start | bytes 589832 | tf_op jit(solution)/shard_map/ppermute | solution.py:718
  27.5 7.1 %collective-permute-start.13 = (f32[6,64,128]{2,1,0:T(8,128)S(1)}, f32[6,64,128]{2,1,0:T(8,128)S(1)}, u32[]{:S(2)}, u32[]{:S(2)}) collective-permute-start(f32[6,64,128]{2,1,0:T(8,128)S(1)} %shard_map.84.vector.block.prior.v1), channel_id=1, source_target_pairs={{0,252},{4,8},{8,4},{12,16},{16,12},{20,24},{24,20},{28,32},{32,28... | collective-permute-start | bytes 589832 | tf_op jit(solution)/shard_map/ppermute | solution.py:717
  27.6 7.1 %collective-permute-start.12 = (f32[6,64,128]{2,1,0:T(8,128)S(1)}, f32[6,64,128]{2,1,0:T(8,128)S(1)}, u32[]{:S(2)}, u32[]{:S(2)}) collective-permute-start(f32[6,64,128]{2,1,0:T(8,128)S(1)} %shard_map.84.vector.block.prior.v1), channel_id=1, source_target_pairs={{0,4},{4,0},{8,12},{12,8},{16,20},{20,16},{24,28},{28,24},{32,36},... | collective-permute-start | bytes 589832 | tf_op jit(solution)/shard_map/ppermute | solution.py:718
  29.8 3.8 %collective-permute-start.10 = (f32[24,128]{1,0:T(8,128)S(1)}, f32[24,128]{1,0:T(8,128)S(1)}, u32[]{:S(2)}, u32[]{:S(2)}) collective-permute-start(f32[24,128]{1,0:T(8,128)S(1)} %get-tuple-element.46), channel_id=1, source_target_pairs={{0,1},{1,0},{2,3},{3,2},{4,5},{5,4},{6,7},{7,6},{8,9},{9,8},{10,11... | collective-permute-start | bytes 36872 | tf_op jit(solution)/shard_map/ppermute | solution.py:722
  30.3 4.1 %collective-permute-start.11 = (f32[24,128]{1,0:T(8,128)S(1)}, f32[24,128]{1,0:T(8,128)S(1)}, u32[]{:S(2)}, u32[]{:S(2)}) collective-permute-start(f32[24,128]{1,0:T(8,128)S(1)} %get-tuple-element.47), channel_id=1, source_target_pairs={{0,3},{1,2},{2,1},{3,0},{4,7},{5,6},{6,5},{7,4},{8,11},{9,10},{10,... | collective-permute-start | bytes 36872 | tf_op jit(solution)/shard_map/ppermute | solution.py:722
  34.7 8.5 %collective-permute-start.17 = (f32[6,64,128]{2,1,0:T(8,128)S(1)}, f32[6,64,128]{2,1,0:T(8,128)S(1)}, u32[]{:S(2)}, u32[]{:S(2)}) collective-permute-start(f32[6,64,128]{2,1,0:T(8,128)S(1)} %shard_map.88.vector.block.prior.v2), channel_id=1, source_target_pairs={{0,252},{4,8},{8,4},{12,16},{16,12},{20,24},{24,20},{28,32},{32,28... | collective-permute-start | bytes 589832 | tf_op jit(solution)/shard_map/ppermute | solution.py:717
  36.0 7.3 %collective-permute-start.16 = (f32[6,64,128]{2,1,0:T(8,128)S(1)}, f32[6,64,128]{2,1,0:T(8,128)S(1)}, u32[]{:S(2)}, u32[]{:S(2)}) collective-permute-start(f32[6,64,128]{2,1,0:T(8,128)S(1)} %shard_map.88.vector.block.prior.v2), channel_id=1, source_target_pairs={{0,4},{4,0},{8,12},{12,8},{16,20},{20,16},{24,28},{28,24},{32,36},... | collective-permute-start | bytes 589832 | tf_op jit(solution)/shard_map/ppermute | solution.py:718
  38.4 4.5 %collective-permute-start.14 = (f32[24,128]{1,0:T(8,128)S(1)}, f32[24,128]{1,0:T(8,128)S(1)}, u32[]{:S(2)}, u32[]{:S(2)}) collective-permute-start(f32[24,128]{1,0:T(8,128)S(1)} %get-tuple-element.50), channel_id=1, source_target_pairs={{0,1},{1,0},{2,3},{3,2},{4,5},{5,4},{6,7},{7,6},{8,9},{9,8},{10,11... | collective-permute-start | bytes 36872 | tf_op jit(solution)/shard_map/ppermute | solution.py:722
  38.9 4.1 %collective-permute-start.15 = (f32[24,128]{1,0:T(8,128)S(1)}, f32[24,128]{1,0:T(8,128)S(1)}, u32[]{:S(2)}, u32[]{:S(2)}) collective-permute-start(f32[24,128]{1,0:T(8,128)S(1)} %get-tuple-element.51), channel_id=1, source_target_pairs={{0,3},{1,2},{2,1},{3,0},{4,7},{5,6},{6,5},{7,4},{8,11},{9,10},{10,... | collective-permute-start | bytes 36872 | tf_op jit(solution)/shard_map/ppermute | solution.py:722
  43.4 7.9 %collective-permute-start.18 = (f32[6,32,128]{2,1,0:T(8,128)S(1)}, f32[6,32,128]{2,1,0:T(8,128)S(1)}, u32[]{:S(2)}, u32[]{:S(2)}) collective-permute-start(f32[6,32,128]{2,1,0:T(8,128)S(1)} %get-tuple-element.53), channel_id=1, source_target_pairs={{0,252},{4,8},{8,4},{12,16},{16,12},{20,24},{24,20},{28,32},{32,28... | collective-permute-start | bytes 294920 | tf_op jit(solution)/shard_map/ppermute | solution.py:786
  43.5 7.9 %collective-permute-start.19 = (f32[6,32,128]{2,1,0:T(8,128)S(1)}, f32[6,32,128]{2,1,0:T(8,128)S(1)}, u32[]{:S(2)}, u32[]{:S(2)}) collective-permute-start(f32[6,32,128]{2,1,0:T(8,128)S(1)} %get-tuple-element.54), channel_id=1, source_target_pairs={{0,4},{4,0},{8,12},{12,8},{16,20},{20,16},{24,28},{28,24},{32,36},... | collective-permute-start | bytes 294920 | tf_op jit(solution)/shard_map/ppermute | solution.py:787
  47.0 4.1 %collective-permute-start.20 = (f32[24,128]{1,0:T(8,128)S(1)}, f32[24,128]{1,0:T(8,128)S(1)}, u32[]{:S(2)}, u32[]{:S(2)}) collective-permute-start(f32[24,128]{1,0:T(8,128)S(1)} %shard_map.93), channel_id=1, source_target_pairs={{0,1},{1,2},{2,3},{3,0},{4,5},{5,6},{6,7},{7,4},{8,9},{9,10},{10,1... | collective-permute-start | bytes 36872 | tf_op jit(solution)/shard_map/ppermute | solution.py:789
  49.3 1.2 %collective-permute-start.21 = (f32[1,128]{1,0:T(1,128)S(1)}, f32[1,128]{1,0:T(1,128)S(1)}, u32[]{:S(2)}, u32[]{:S(2)}) collective-permute-start(f32[1,128]{1,0:T(1,128)S(1)} %get-tuple-element.63), channel_id=1, source_target_pairs={{0,4},{4,0},{8,12},{12,8},{16,20},{20,16},{24,28},{28,24},{32,36},... | collective-permute-start | bytes 1544 | tf_op jit(solution)/shard_map/ppermute | solution.py:797

commit v8 on v7

--- a/solution.py
+++ b/solution.py
@@ -333,17 +333,18 @@
 CROSS_PAIRS = tuple((i, j) for i in range(HIST) for j in range(HIST))
 
 
-def field_dots(steps, changes, others, plain=()):
+def field_dots(groups, others, plain=()):
     zero = jnp.zeros((8, LANES), jnp.float32)
-    count = 2 * HIST
+    fields = [(group, f) for group in groups for f in range(HIST)]
+    count = len(fields)
 
     def body(i, accs):
         accs = list(accs)
         for b in range(8):
             at = pl.ds(8 * b, 8)
             tiles = [other(i, b) for other in others]
-            for f in range(count):
-                field = steps[f, i, at, :] if f < HIST else changes[f - HIST, i, at, :]
+            for f, (group, which) in enumerate(fields):
+                field = group[which, i, at, :]
                 for o, tile in enumerate(tiles):
                     accs[o * count + f] = accs[o * count + f] + field * tile
             for n, (one, two) in enumerate(plain, len(others) * count):
@@ -384,7 +385,7 @@
 FETCHES = 4
 
 
-def side_one(both, charge, steps, changes, inner, steps_here, changes_here, ext, sems):
+def side_one(both, charge, steps, changes, inner, steps_here, changes_here, rows, ext, sems):
     each = HIST // FETCHES
     copies = [
         pltpu.make_async_copy(src.at[pl.ds(each * n, each)], dst.at[pl.ds(each * n, each)], sems.at[FETCHES * m + n])
@@ -394,15 +395,21 @@
     for copy in copies:
         copy.start()
     inner_residual(both, charge, inner, ext)
-    for copy in copies:
+    for copy in copies[:FETCHES]:
         copy.wait()
+    store(rows, 0, gram_dots(steps_here, steps_here, PAIRS))
+    store(rows, 36, field_dots((steps_here,), [density_tile(both)]))
+    for copy in copies[FETCHES:]:
+        copy.wait()
+    store(rows, 44, gram_dots(steps_here, changes_here, CROSS_PAIRS[:32]))
 
 
 def side_two(vector, both, steps, changes, inner, rows, moments, ext):
     inner_basis(vector, None, inner, ext)
     lifted, rho = lifted_tile(both, vector), density_tile(both)
-    values = field_dots(steps, changes, [lifted, rho], [(rho, lifted)])
-    store(rows, 0, values[:16] + values[32:] + values[16:32])
+    by_step = field_dots((steps,), [lifted], [(rho, lifted)])
+    by_change = field_dots((changes,), [lifted, rho])
+    store(rows, 0, by_step[:8] + by_change[:8] + by_step[8:] + by_change[8:])
     store_moments([(vector, vector)], moments)
 
 
@@ -410,8 +417,7 @@
     inner, grad, rows, moments, ext = outs
     inner_basis(vector, prior, inner, ext)
     lifted, rho = lifted_tile(both, vector), density_tile(both)
-    store(rows, 0, field_dots(steps, changes, [lifted], [(rho, lifted)]))
-    store(rows, 17, gram_dots(steps, changes, CROSS_PAIRS[32:]))
+    store(rows, 0, field_dots((steps, changes), [lifted], [(rho, lifted)]))
     store_moments([(prior, vector), (vector, vector)], moments)
     base_gradient(both, near, far, z_first, z_second, potential, grad, ext)
 
@@ -420,16 +426,16 @@
     inner_basis(vector, prior, inner, ext)
     lifted, rho = lifted_tile(both, vector), density_tile(both)
     slope = lambda i, b: tile_of(grad, i, b)
-    values = field_dots(steps, changes, [lifted, slope], [(rho, lifted), (rho, slope), (rho, rho)])
+    values = field_dots((steps, changes), [lifted, slope], [(rho, lifted), (rho, slope), (rho, rho)])
     store(rows, 0, values[:16] + values[32:33] + values[16:32] + values[33:])
-    store(rows, 35, gram_dots(steps, steps, PAIRS))
-    store(rows, 71, gram_dots(changes, changes, PAIRS))
+    store(rows, 35, gram_dots(changes, changes, PAIRS))
+    store(rows, 71, gram_dots(steps, changes, CROSS_PAIRS[32:]))
     store_moments([(prior, vector), (vector, vector)], moments)
 
 
-def side_five(prior, vector, both, steps, changes, r2, r3, r4, m2, m3, m4, kept, given, inner, table, m5, ext):
+def side_five(prior, vector, both, steps, changes, r1, r2, r3, r4, m2, m3, m4, kept, given, table, m5):
     lifted, rho = lifted_tile(both, vector), density_tile(both)
-    own = field_dots(steps, changes, [lifted], [(rho, lifted)])
+    own = field_dots((steps, changes), [lifted], [(rho, lifted)])
     store_moments([(prior, vector), (vector, vector)], m5)
     table[...] = jnp.zeros_like(table)
 
@@ -441,10 +447,12 @@
             at = place(base + before)
             table[at : at + count - before, :] = ref[start + before : start + count, :]
 
-    put(ROW_GRAM, r4, 35, 72)
-    store(table, ROW_GRAM + 72, gram_dots(steps, changes, CROSS_PAIRS[:32]))
-    put(ROW_GRAM + 104, r3, 17, 32)
-    put(ROW_BASE, r2, 17, 16)
+    put(ROW_GRAM, r1, 0, 36)
+    put(ROW_GRAM + 36, r4, 35, 36)
+    put(ROW_GRAM + 72, r1, 44, 32)
+    put(ROW_GRAM + 104, r4, 71, 32)
+    put(ROW_BASE, r1, 36, 8)
+    put(ROW_BASE + 8, r2, 17, 8)
     put(ROW_BASE + 16, r4, 17, 18)
     for n, rows in enumerate((r2, r3, r4)):
         put(ROW_W + 17 * n, rows, 0, 17)
@@ -467,6 +475,8 @@
     kept[...] = jnp.where(odd, second, first)
     given[...] = jnp.where(odd, first, second)
 
+
+def inner_moment_kernel(vector, inner, ext):
     fill_ext(vector, ext)
     zero = jnp.zeros((8, LANES), jnp.float32)
     accs = [(zero, zero) for _ in range(2)]
@@ -756,9 +766,9 @@
         return halo, z_halo(*call(pack_kernel, [face, face], [block_now], flops=work))
 
     stored = hist_steps.shape
-    inner, *history = call(
+    inner, *history, r1 = call(
         side_one,
-        [block, stored, stored],
+        [block, stored, stored, (80, LANES)],
         [both, charge, hist_steps, hist_changes],
         [ext, pltpu.SemaphoreType.DMA((2 * FETCHES,))],
         work,
@@ -772,7 +782,7 @@
     halo, ends = exchange(v1)
     inner, grad, r3, m3 = call(
         side_three,
-        [block, block, (56, LANES), (8, LANES)],
+        [block, block, (24, LANES), (8, LANES)],
         [v0, v1, both, *density_halo, *density_ends, ion_potential, *history],
         [ext],
         work,
@@ -787,17 +797,16 @@
     near = lax.ppermute(to_near, "blk", swap("blk", 0))
     (upper,) = call(pack_upper_kernel, [face], [v3], flops=work)
     z_left = lax.ppermute(upper, "gz", ring("gz", 1))
-    kept, given, inner = call(
+    kept, given = call(
         side_five,
-        [(1, LANES), (1, LANES), (8, LANES)],
-        [v2, v3, both, *history, r2, r3, r4, m2, m3, m4],
-        [(2 * LANES, LANES), (8, LANES), ext],
+        [(1, LANES), (1, LANES)],
+        [v2, v3, both, *history, r1, r2, r3, r4, m2, m3, m4],
+        [(2 * LANES, LANES), (8, LANES)],
         work,
     )
     taken = lax.ppermute(given, "blk", swap("blk", 0))
-    row, part = call(
-        couple_kernel, [(1, LANES), (8, LANES)], [v3, z_left, inner, kept, taken], flops=work
-    )
+    (inner,) = call(inner_moment_kernel, [(8, LANES)], [after((v3,), given)[0]], [ext], work)
+    row, part = call(couple_kernel, [(1, LANES), (8, LANES)], [v3, z_left, inner, kept, taken], flops=work)
     devices = lax.axis_size("blk") * lax.axis_size("gz")
     (outgoing,) = call(send_kernel, [(devices, LANES)], [v3, far, near, part, row], flops=work)
     received = lax.all_to_all(outgoing.reshape(devices, 1, LANES), ("blk", "gz"), 0, 0, tiled=True)

time: 73.6 us -> 73.3 us (level)
  waiting for transfers between devices: 2.29 us -> 3.19 us
  starting transfers between devices: 33.5 us -> 32.7 us
    ppermute x1, waiting for transfers between devices: 0.67 us -> 1.67 us  [on_device(): z_left = lax.ppermute(upper, 'gz', ring('gz', 1))]
    ppermute x1, waiting for transfers between devices: 0.84 us -> 0.1 us  [on_device(): taken = lax.ppermute(given, 'blk', swap('blk', 0))]
    pallas_call x21 -> x22, Pallas kernels: 16.9 us -> 16.9 us  [call(): pl.pallas_call(kernel, out_shape=shapes, in_specs=[pl.BlockSpec(memory_sp...]
  transfers between devices with their start and end apart: 22 -> 22, of which waited for: 3 -> 4; matrix products, arithmetic and copies ran while one was open for 0% -> 0% of each run, Pallas kernels for 19% -> 20%
where the time goes in v8:
time: 73.3 us; the launch traced here: 73.1 us
  starting transfers between devices  32.7 us (45%)
  blocking collectives  19.2 us (26%)
  Pallas kernels  16.9 us (23%)
  waiting for transfers between devices  3.19 us (4%)
  between operations  1.07 us (1%)
    all_to_all x1, blocking collectives, on_device(): lax.all_to_all(outgoing.reshape(devices, 1, LANES), ('blk', 'gz'), 0, 0,...  19.2 us
    pallas_call x22, Pallas kernels, call(): pl.pallas_call(kernel, out_shape=shapes, in_specs=[pl.BlockSpec(memory_sp...  16.9 us
    ppermute x5, starting transfers between devices, x_halo(): return (lax.ppermute(block, 'blk', swap('blk', 0)), far)  15.5 us
    ppermute x4, starting transfers between devices, z_halo(): lax.ppermute(face_b, 'gz', swap('gz', 1))  5.72 us
    ppermute x5, starting transfers between devices, x_halo(): far = lax.ppermute(block, 'blk', swap('blk', 1))  4.13 us
    ppermute x1, starting transfers between devices, on_device(): near = lax.ppermute(to_near, 'blk', swap('blk', 0))  3.61 us
    ppermute x4, starting transfers between devices, z_halo(): lax.ppermute(face_a, 'gz', swap('gz', 0))  3.03 us
    ppermute x1, waiting for transfers between devices, on_device(): z_left = lax.ppermute(upper, 'gz', ring('gz', 1))  1.67 us
  transfers between devices with their start and end apart: 22, of which 4 were waited for; matrix products, arithmetic and copies ran while one was open for 0% of the time, Pallas kernels for 20%

profile of v8, /device:TPU:1, one launch (start us, length us, event | category | flops | bytes accessed | tf_op | source)
XLA Modules:
  0.0 73.1 jit_solution(8395546356678015750)
XLA Ops:
  0.6 2.7 %collective-permute-start.3 = (f32[6,64,128]{2,1,0:T(8,128)}, f32[6,64,128]{2,1,0:T(8,128)S(1)}, u32[]{:S(2)}, u32[]{:S(2)}) collective-permute-start(f32[6,64,128]{2,1,0:T(8,128)} %hartree.1), channel_id=1, source_target_pairs={{0,252},{4,8},{8,4},{12,16},{16,12},{20,24},{24,20},{28,32},{32,28... | collective-permute-start | bytes 589832 | tf_op jit(solution)/shard_map/ppermute | solution.py:727
  3.3 6.4 %collective-permute-start.2 = (f32[6,64,128]{2,1,0:T(8,128)}, f32[6,64,128]{2,1,0:T(8,128)S(1)}, u32[]{:S(2)}, u32[]{:S(2)}) collective-permute-start(f32[6,64,128]{2,1,0:T(8,128)} %hartree.1), channel_id=1, source_target_pairs={{0,4},{4,0},{8,12},{12,8},{16,20},{20,16},{24,28},{28,24},{32,36},... | collective-permute-start | bytes 589832 | tf_op jit(solution)/shard_map/ppermute | solution.py:728
  9.7 1.3 %shard_map.77 = (f32[12,64,128]{2,1,0:T(8,128)S(1)}, f32[6,64,128]{2,1,0:T(8,128)S(1)}, f32[48,128]{1,0:T(8,128)S(1)}, f32[48,128]{1,0:T(8,128)S(1)}) custom-call(f32[6,64,128]{2,1,0:T(8,128)} %hartree.1, f32[6,64,128]{2,1,0:T(8,128)} %density.1, f32[6,64,128]{2,1,0:T(8,128)} %charge.1), custom_call_target="tpu_custom_call" | custom-call | bytes 1228800 | tf_op jit(solution)/shard_map/pallas_call | solution.py:701
  11.0 1.4 %collective-permute-start = (f32[48,128]{1,0:T(8,128)S(1)}, f32[48,128]{1,0:T(8,128)S(1)}, u32[]{:S(2)}, u32[]{:S(2)}) collective-permute-start(f32[48,128]{1,0:T(8,128)S(1)} %get-tuple-element.38), channel_id=1, source_target_pairs={{0,1},{1,0},{2,3},{3,2},{4,5},{5,4},{6,7},{7,6},{8,9},{9,8},{10,11... | collective-permute-start | bytes 73736 | tf_op jit(solution)/shard_map/ppermute | solution.py:732
  12.4 1.9 %collective-permute-start.1 = (f32[48,128]{1,0:T(8,128)S(1)}, f32[48,128]{1,0:T(8,128)S(1)}, u32[]{:S(2)}, u32[]{:S(2)}) collective-permute-start(f32[48,128]{1,0:T(8,128)S(1)} %get-tuple-element.39), channel_id=1, source_target_pairs={{0,3},{1,2},{2,1},{3,0},{4,7},{5,6},{6,5},{7,4},{8,11},{9,10},{10,... | collective-permute-start | bytes 73736 | tf_op jit(solution)/shard_map/ppermute | solution.py:732
  14.3 3.3 %shard_map.78 = (f32[6,64,128]{2,1,0:T(8,128)S(1)}, f32[8,6,64,128]{3,2,1,0:T(8,128)S(1)}, f32[8,6,64,128]{3,2,1,0:T(8,128)S(1)}, f32[80,128]{1,0:T(8,128)S(1)}) custom-call(f32[12,64,128]{2,1,0:T(8,128)S(1)} %get-tuple-element.35.both, f32[6,64,128]{2,1,0:T(8,128)S(1)} %get-tuple-element.36.charge, f32[8,6,64,128]{3,2,1,0:T(8,128)} %steps.1, ...), custom_call_target="tpu_custom_call" | custom-call | flops 14745600 | bytes 7118848 | tf_op jit(solution)/shard_map/pallas_call | solution.py:701
  17.6 0.3 shard_map.79.inner
  17.9 0.1 shard_map.80.vector.block.prior.v0
  18.0 0.1 collective-permute-start.7
  18.1 0.9 %collective-permute-start.6 = (f32[6,64,128]{2,1,0:T(8,128)S(1)}, f32[6,64,128]{2,1,0:T(8,128)S(1)}, u32[]{:S(2)}, u32[]{:S(2)}) collective-permute-start(f32[6,64,128]{2,1,0:T(8,128)S(1)} %shard_map.80.vector.block.prior.v0), channel_id=1, source_target_pairs={{0,4},{4,0},{8,12},{12,8},{16,20},{20,16},{24,28},{28,24},{32,36},... | collective-permute-start | bytes 589832 | tf_op jit(solution)/shard_map/ppermute | solution.py:728
  19.0 0.2 shard_map.82
  19.2 0.9 %collective-permute-start.4 = (f32[24,128]{1,0:T(8,128)S(1)}, f32[24,128]{1,0:T(8,128)S(1)}, u32[]{:S(2)}, u32[]{:S(2)}) collective-permute-start(f32[24,128]{1,0:T(8,128)S(1)} %get-tuple-element.43), channel_id=1, source_target_pairs={{0,1},{1,0},{2,3},{3,2},{4,5},{5,4},{6,7},{7,6},{8,9},{9,8},{10,11... | collective-permute-start | bytes 36872 | tf_op jit(solution)/shard_map/ppermute | solution.py:732
  20.1 1.9 %collective-permute-start.5 = (f32[24,128]{1,0:T(8,128)S(1)}, f32[24,128]{1,0:T(8,128)S(1)}, u32[]{:S(2)}, u32[]{:S(2)}) collective-permute-start(f32[24,128]{1,0:T(8,128)S(1)} %get-tuple-element.44), channel_id=1, source_target_pairs={{0,3},{1,2},{2,1},{3,0},{4,7},{5,6},{6,5},{7,4},{8,11},{9,10},{10,... | collective-permute-start | bytes 36872 | tf_op jit(solution)/shard_map/ppermute | solution.py:732
  22.0 1.3 %shard_map.81 = (f32[6,64,128]{2,1,0:T(8,128)S(1)}, f32[40,128]{1,0:T(8,128)S(1)}, f32[8,128]{1,0:T(8,128)S(1)}) custom-call(f32[6,64,128]{2,1,0:T(8,128)S(1)} %shard_map.80.vector.block.prior.v0, f32[12,64,128]{2,1,0:T(8,128)S(1)} %get-tuple-element.35.both, f32[8,6,64,128]{3,2,1,0:T(8,128)S(1)} %get-tuple-element.40.steps, ...), custom_call_target="tpu_custom_call" | custom-call | flops 14745600 | bytes 3956736 | tf_op jit(solution)/shard_map/pallas_call | solution.py:701
  23.3 3.7 %collective-permute-start.8 = (f32[6,64,128]{2,1,0:T(8,128)S(1)}, f32[6,64,128]{2,1,0:T(8,128)S(1)}, u32[]{:S(2)}, u32[]{:S(2)}) collective-permute-start(f32[6,64,128]{2,1,0:T(8,128)S(1)} %copy-done.1), channel_id=1, source_target_pairs={{0,4},{4,0},{8,12},{12,8},{16,20},{20,16},{24,28},{28,24},{32,36},... | collective-permute-start | bytes 589832 | tf_op jit(solution)/shard_map/ppermute | solution.py:728
  26.9 0.3 shard_map.83.inner
  27.2 0.1 shard_map.84.vector.block.prior.v1
  27.4 0.1 collective-permute-start.13
  27.5 2.1 %collective-permute-start.12 = (f32[6,64,128]{2,1,0:T(8,128)S(1)}, f32[6,64,128]{2,1,0:T(8,128)S(1)}, u32[]{:S(2)}, u32[]{:S(2)}) collective-permute-start(f32[6,64,128]{2,1,0:T(8,128)S(1)} %shard_map.84.vector.block.prior.v1), channel_id=1, source_target_pairs={{0,4},{4,0},{8,12},{12,8},{16,20},{20,16},{24,28},{28,24},{32,36},... | collective-permute-start | bytes 589832 | tf_op jit(solution)/shard_map/ppermute | solution.py:728
  29.5 0.2 shard_map.86
  29.7 0.5 collective-permute-start.10
  30.2 0.6 collective-permute-start.11
  30.8 2.3 %shard_map.85 = (f32[6,64,128]{2,1,0:T(8,128)S(1)}, f32[6,64,128]{2,1,0:T(8,128)S(1)}, f32[24,128]{1,0:T(8,128)S(1)}, f32[8,128]{1,0:T(8,128)S(1)}) custom-call(f32[6,64,128]{2,1,0:T(8,128)S(1)} %shard_map.80.vector.block.prior.v0, f32[6,64,128]{2,1,0:T(8,128)S(1)} %shard_map.84.vector.block.prior.v1, f32[12,64,128]{2,1,0:T(8,128)S(1)} %get-tuple-element.35.both, ...), custom_call_target="tpu_custom_call" | custom-call | flops 14745600 | bytes 4980736 | tf_op jit(solution)/shard_map/pallas_call | solution.py:701
  33.1 1.2 %collective-permute-done.11.z_second = f32[24,128]{1,0:T(8,128)S(1)} collective-permute-done((f32[24,128]{1,0:T(8,128)S(1)}, f32[24,128]{1,0:T(8,128)S(1)}, u32[]{:S(2)}, u32[]{:S(2)}) %collective-permute-start.11) | collective-permute-done | bytes 12320 | tf_op jit(solution)/shard_map/ppermute | solution.py:732
  34.2 0.3 shard_map.87.inner
  34.5 0.1 shard_map.88.vector.block.prior.v2
  34.7 1.3 %collective-permute-start.17 = (f32[6,64,128]{2,1,0:T(8,128)S(1)}, f32[6,64,128]{2,1,0:T(8,128)S(1)}, u32[]{:S(2)}, u32[]{:S(2)}) collective-permute-start(f32[6,64,128]{2,1,0:T(8,128)S(1)} %shard_map.88.vector.block.prior.v2), channel_id=1, source_target_pairs={{0,252},{4,8},{8,4},{12,16},{16,12},{20,24},{24,20},{28,32},{32,28... | collective-permute-start | bytes 589832 | tf_op jit(solution)/shard_map/ppermute | solution.py:727
  35.9 2.4 %collective-permute-start.16 = (f32[6,64,128]{2,1,0:T(8,128)S(1)}, f32[6,64,128]{2,1,0:T(8,128)S(1)}, u32[]{:S(2)}, u32[]{:S(2)}) collective-permute-start(f32[6,64,128]{2,1,0:T(8,128)S(1)} %shard_map.88.vector.block.prior.v2), channel_id=1, source_target_pairs={{0,4},{4,0},{8,12},{12,8},{16,20},{20,16},{24,28},{28,24},{32,36},... | collective-permute-start | bytes 589832 | tf_op jit(solution)/shard_map/ppermute | solution.py:728
  38.4 0.2 shard_map.90
  38.5 0.3 collective-permute-start.14
  38.8 1.3 %collective-permute-start.15 = (f32[24,128]{1,0:T(8,128)S(1)}, f32[24,128]{1,0:T(8,128)S(1)}, u32[]{:S(2)}, u32[]{:S(2)}) collective-permute-start(f32[24,128]{1,0:T(8,128)S(1)} %get-tuple-element.52), channel_id=1, source_target_pairs={{0,3},{1,2},{2,1},{3,0},{4,7},{5,6},{6,5},{7,4},{8,11},{9,10},{10,... | collective-permute-start | bytes 36872 | tf_op jit(solution)/shard_map/ppermute | solution.py:732
  40.1 2.5 %shard_map.89 = (f32[6,64,128]{2,1,0:T(8,128)S(1)}, f32[112,128]{1,0:T(8,128)S(1)}, f32[8,128]{1,0:T(8,128)S(1)}) custom-call(f32[6,64,128]{2,1,0:T(8,128)S(1)} %shard_map.84.vector.block.prior.v1, f32[6,64,128]{2,1,0:T(8,128)S(1)} %shard_map.88.vector.block.prior.v2, f32[12,64,128]{2,1,0:T(8,128)S(1)} %get-tuple-element.35.both, ...), custom_call_target="tpu_custom_call" | custom-call | flops 14745600 | bytes 4386816 | tf_op jit(solution)/shard_map/pallas_call | solution.py:701
  42.6 0.2 collective-permute-done.15.z_second
  42.8 0.3 shard_map.91.inner
  43.1 0.1 shard_map.92
  43.3 0.1 collective-permute-start.18
  43.4 3.6 %collective-permute-start.19 = (f32[6,32,128]{2,1,0:T(8,128)S(1)}, f32[6,32,128]{2,1,0:T(8,128)S(1)}, u32[]{:S(2)}, u32[]{:S(2)}) collective-permute-start(f32[6,32,128]{2,1,0:T(8,128)S(1)} %get-tuple-element.55), channel_id=1, source_target_pairs={{0,4},{4,0},{8,12},{12,8},{16,20},{20,16},{24,28},{28,24},{32,36},... | collective-permute-start | bytes 294920 | tf_op jit(solution)/shard_map/ppermute | solution.py:797
  47.0 0.1 shard_map.93
  47.1 0.3 collective-permute-start.20
  47.4 1.0 %shard_map.94 = (f32[1,128]{1,0:T(1,128)S(1)}, f32[1,128]{1,0:T(1,128)S(1)}) custom-call(f32[6,64,128]{2,1,0:T(8,128)S(1)} %shard_map.88.vector.block.prior.v2, f32[6,64,128]{2,1,0:T(8,128)S(1)} %get-tuple-element.64.block.vector.own.v3, f32[12,64,128]{2,1,0:T(8,128)S(1)} %get-tuple-element.35.both, f32[8,6,64,128]{3,2,1,0:T(8,128)S(1)} %get-tuple-element.40.steps, ...), custom_call_target="tpu_custom_call" | custom-call | flops 14745600 | bytes 4076544 | tf_op jit(solution)/shard_map/pallas_call | solution.py:701
  48.3 0.4 collective-permute-start.21
  48.7 0.7 %shard_map.95.inner = f32[8,128]{1,0:T(8,128)S(1)} custom-call(f32[6,64,128]{2,1,0:T(8,128)S(1)} %get-tuple-element.64.block.vector.own.v3), custom_call_target="tpu_custom_call" | custom-call | flops 14745600 | bytes 200704 | tf_op jit(solution)/shard_map/pallas_call | solution.py:701
  49.5 0.1 collective-permute-done.21.taken
  49.6 1.7 %collective-permute-done.20.z_left = f32[24,128]{1,0:T(8,128)S(1)} collective-permute-done((f32[24,128]{1,0:T(8,128)S(1)}, f32[24,128]{1,0:T(8,128)S(1)}, u32[]{:S(2)}, u32[]{:S(2)}) %collective-permute-start.20) | collective-permute-done | bytes 12320 | tf_op jit(solution)/shard_map/ppermute | solution.py:799
  51.2 0.2 shard_map.96
  51.5 0.6 shard_map.97
  52.1 19.2 %all_to_all.5 = f32[256,1,128]{2,1,0:T(1,128)S(1)} all-to-all(f32[256,1,128]{2,1,0:T(1,128)S(1)} %bitcast.5), channel_id=1, replica_groups=mesh['blk'=64,'gz'=4] {'blk','gz'}, dimensions={0} | all-to-all | bytes 262144 | tf_op jit(solution)/shard_map/all_to_all | solution.py:812
  71.4 1.6 %shard_map.98 = (f32[6,64,128]{2,1,0:T(8,128)}, f32[6,64,128]{2,1,0:T(8,128)}) custom-call(f32[256,128]{1,0:T(8,128)S(1)} %bitcast.4, f32[12,64,128]{2,1,0:T(8,128)S(1)} %get-tuple-element.35.both, f32[6,64,128]{2,1,0:T(8,128)S(1)} %get-tuple-element.49.grad, f32[6,64,128]{2,1,0:T(8,128)S(1)} %shard_map.80.vector.block.prior.v0, ...), custom_call_target="tpu_custom_call" | custom-call | flops 14745600 | bytes 5046272 | tf_op jit(solution)/shard_map/pallas_call | solution.py:701
  (23 shorter events, 0.1 us)
Async XLA Ops:
  0.6 17.2 %collective-permute-start.3 = (f32[6,64,128]{2,1,0:T(8,128)}, f32[6,64,128]{2,1,0:T(8,128)S(1)}, u32[]{:S(2)}, u32[]{:S(2)}) collective-permute-start(f32[6,64,128]{2,1,0:T(8,128)} %hartree.1), channel_id=1, source_target_pairs={{0,252},{4,8},{8,4},{12,16},{16,12},{20,24},{24,20},{28,32},{32,28... | collective-permute-start | bytes 589832 | tf_op jit(solution)/shard_map/ppermute | solution.py:727
  3.3 14.6 %collective-permute-start.2 = (f32[6,64,128]{2,1,0:T(8,128)}, f32[6,64,128]{2,1,0:T(8,128)S(1)}, u32[]{:S(2)}, u32[]{:S(2)}) collective-permute-start(f32[6,64,128]{2,1,0:T(8,128)} %hartree.1), channel_id=1, source_target_pairs={{0,4},{4,0},{8,12},{12,8},{16,20},{20,16},{24,28},{28,24},{32,36},... | collective-permute-start | bytes 589832 | tf_op jit(solution)/shard_map/ppermute | solution.py:728
  11.0 6.6 %collective-permute-start = (f32[48,128]{1,0:T(8,128)S(1)}, f32[48,128]{1,0:T(8,128)S(1)}, u32[]{:S(2)}, u32[]{:S(2)}) collective-permute-start(f32[48,128]{1,0:T(8,128)S(1)} %get-tuple-element.38), channel_id=1, source_target_pairs={{0,1},{1,0},{2,3},{3,2},{4,5},{5,4},{6,7},{7,6},{8,9},{9,8},{10,11... | collective-permute-start | bytes 73736 | tf_op jit(solution)/shard_map/ppermute | solution.py:732
  12.4 5.2 %collective-permute-start.1 = (f32[48,128]{1,0:T(8,128)S(1)}, f32[48,128]{1,0:T(8,128)S(1)}, u32[]{:S(2)}, u32[]{:S(2)}) collective-permute-start(f32[48,128]{1,0:T(8,128)S(1)} %get-tuple-element.39), channel_id=1, source_target_pairs={{0,3},{1,2},{2,1},{3,0},{4,7},{5,6},{6,5},{7,4},{8,11},{9,10},{10,... | collective-permute-start | bytes 73736 | tf_op jit(solution)/shard_map/ppermute | solution.py:732
  14.3 7.7 %copy-start.1 = (f32[6,64,128]{2,1,0:T(8,128)S(1)}, f32[6,64,128]{2,1,0:T(8,128)}, u32[]{:S(2)}) copy-start(f32[6,64,128]{2,1,0:T(8,128)} %density.1) | copy-start | bytes 589828
  18.0 9.2 %collective-permute-start.7 = (f32[6,64,128]{2,1,0:T(8,128)S(1)}, f32[6,64,128]{2,1,0:T(8,128)S(1)}, u32[]{:S(2)}, u32[]{:S(2)}) collective-permute-start(f32[6,64,128]{2,1,0:T(8,128)S(1)} %shard_map.80.vector.block.prior.v0), channel_id=1, source_target_pairs={{0,252},{4,8},{8,4},{12,16},{16,12},{20,24},{24,20},{28,32},{32,28... | collective-permute-start | bytes 589832 | tf_op jit(solution)/shard_map/ppermute | solution.py:727
  18.1 9.1 %collective-permute-start.6 = (f32[6,64,128]{2,1,0:T(8,128)S(1)}, f32[6,64,128]{2,1,0:T(8,128)S(1)}, u32[]{:S(2)}, u32[]{:S(2)}) collective-permute-start(f32[6,64,128]{2,1,0:T(8,128)S(1)} %shard_map.80.vector.block.prior.v0), channel_id=1, source_target_pairs={{0,4},{4,0},{8,12},{12,8},{16,20},{20,16},{24,28},{28,24},{32,36},... | collective-permute-start | bytes 589832 | tf_op jit(solution)/shard_map/ppermute | solution.py:728
  19.2 4.1 %collective-permute-start.4 = (f32[24,128]{1,0:T(8,128)S(1)}, f32[24,128]{1,0:T(8,128)S(1)}, u32[]{:S(2)}, u32[]{:S(2)}) collective-permute-start(f32[24,128]{1,0:T(8,128)S(1)} %get-tuple-element.43), channel_id=1, source_target_pairs={{0,1},{1,0},{2,3},{3,2},{4,5},{5,4},{6,7},{7,6},{8,9},{9,8},{10,11... | collective-permute-start | bytes 36872 | tf_op jit(solution)/shard_map/ppermute | solution.py:732
  20.1 6.8 %collective-permute-start.5 = (f32[24,128]{1,0:T(8,128)S(1)}, f32[24,128]{1,0:T(8,128)S(1)}, u32[]{:S(2)}, u32[]{:S(2)}) collective-permute-start(f32[24,128]{1,0:T(8,128)S(1)} %get-tuple-element.44), channel_id=1, source_target_pairs={{0,3},{1,2},{2,1},{3,0},{4,7},{5,6},{6,5},{7,4},{8,11},{9,10},{10,... | collective-permute-start | bytes 36872 | tf_op jit(solution)/shard_map/ppermute | solution.py:732
  22.0 8.2 %collective-permute-start.9 = (f32[6,64,128]{2,1,0:T(8,128)S(1)}, f32[6,64,128]{2,1,0:T(8,128)S(1)}, u32[]{:S(2)}, u32[]{:S(2)}) collective-permute-start(f32[6,64,128]{2,1,0:T(8,128)S(1)} %copy-done.1), channel_id=1, source_target_pairs={{0,252},{4,8},{8,4},{12,16},{16,12},{20,24},{24,20},{28,32},{32,28... | collective-permute-start | bytes 589832 | tf_op jit(solution)/shard_map/ppermute | solution.py:727
  22.0 8.8 %copy-start = (f32[6,64,128]{2,1,0:T(8,128)S(1)}, f32[6,64,128]{2,1,0:T(8,128)}, u32[]{:S(2)}) copy-start(f32[6,64,128]{2,1,0:T(8,128)} %potential.1) | copy-start | bytes 589828
  23.3 7.5 %collective-permute-start.8 = (f32[6,64,128]{2,1,0:T(8,128)S(1)}, f32[6,64,128]{2,1,0:T(8,128)S(1)}, u32[]{:S(2)}, u32[]{:S(2)}) collective-permute-start(f32[6,64,128]{2,1,0:T(8,128)S(1)} %copy-done.1), channel_id=1, source_target_pairs={{0,4},{4,0},{8,12},{12,8},{16,20},{20,16},{24,28},{28,24},{32,36},... | collective-permute-start | bytes 589832 | tf_op jit(solution)/shard_map/ppermute | solution.py:728
  27.4 7.1 %collective-permute-start.13 = (f32[6,64,128]{2,1,0:T(8,128)S(1)}, f32[6,64,128]{2,1,0:T(8,128)S(1)}, u32[]{:S(2)}, u32[]{:S(2)}) collective-permute-start(f32[6,64,128]{2,1,0:T(8,128)S(1)} %shard_map.84.vector.block.prior.v1), channel_id=1, source_target_pairs={{0,252},{4,8},{8,4},{12,16},{16,12},{20,24},{24,20},{28,32},{32,28... | collective-permute-start | bytes 589832 | tf_op jit(solution)/shard_map/ppermute | solution.py:727
  27.5 7.1 %collective-permute-start.12 = (f32[6,64,128]{2,1,0:T(8,128)S(1)}, f32[6,64,128]{2,1,0:T(8,128)S(1)}, u32[]{:S(2)}, u32[]{:S(2)}) collective-permute-start(f32[6,64,128]{2,1,0:T(8,128)S(1)} %shard_map.84.vector.block.prior.v1), channel_id=1, source_target_pairs={{0,4},{4,0},{8,12},{12,8},{16,20},{20,16},{24,28},{28,24},{32,36},... | collective-permute-start | bytes 589832 | tf_op jit(solution)/shard_map/ppermute | solution.py:728
  29.7 3.4 %collective-permute-start.10 = (f32[24,128]{1,0:T(8,128)S(1)}, f32[24,128]{1,0:T(8,128)S(1)}, u32[]{:S(2)}, u32[]{:S(2)}) collective-permute-start(f32[24,128]{1,0:T(8,128)S(1)} %get-tuple-element.47), channel_id=1, source_target_pairs={{0,1},{1,0},{2,3},{3,2},{4,5},{5,4},{6,7},{7,6},{8,9},{9,8},{10,11... | collective-permute-start | bytes 36872 | tf_op jit(solution)/shard_map/ppermute | solution.py:732
  30.2 4.1 %collective-permute-start.11 = (f32[24,128]{1,0:T(8,128)S(1)}, f32[24,128]{1,0:T(8,128)S(1)}, u32[]{:S(2)}, u32[]{:S(2)}) collective-permute-start(f32[24,128]{1,0:T(8,128)S(1)} %get-tuple-element.48), channel_id=1, source_target_pairs={{0,3},{1,2},{2,1},{3,0},{4,7},{5,6},{6,5},{7,4},{8,11},{9,10},{10,... | collective-permute-start | bytes 36872 | tf_op jit(solution)/shard_map/ppermute | solution.py:732
  34.7 8.5 %collective-permute-start.17 = (f32[6,64,128]{2,1,0:T(8,128)S(1)}, f32[6,64,128]{2,1,0:T(8,128)S(1)}, u32[]{:S(2)}, u32[]{:S(2)}) collective-permute-start(f32[6,64,128]{2,1,0:T(8,128)S(1)} %shard_map.88.vector.block.prior.v2), channel_id=1, source_target_pairs={{0,252},{4,8},{8,4},{12,16},{16,12},{20,24},{24,20},{28,32},{32,28... | collective-permute-start | bytes 589832 | tf_op jit(solution)/shard_map/ppermute | solution.py:727
  35.9 7.2 %collective-permute-start.16 = (f32[6,64,128]{2,1,0:T(8,128)S(1)}, f32[6,64,128]{2,1,0:T(8,128)S(1)}, u32[]{:S(2)}, u32[]{:S(2)}) collective-permute-start(f32[6,64,128]{2,1,0:T(8,128)S(1)} %shard_map.88.vector.block.prior.v2), channel_id=1, source_target_pairs={{0,4},{4,0},{8,12},{12,8},{16,20},{20,16},{24,28},{28,24},{32,36},... | collective-permute-start | bytes 589832 | tf_op jit(solution)/shard_map/ppermute | solution.py:728
  38.5 4.1 %collective-permute-start.14 = (f32[24,128]{1,0:T(8,128)S(1)}, f32[24,128]{1,0:T(8,128)S(1)}, u32[]{:S(2)}, u32[]{:S(2)}) collective-permute-start(f32[24,128]{1,0:T(8,128)S(1)} %get-tuple-element.51), channel_id=1, source_target_pairs={{0,1},{1,0},{2,3},{3,2},{4,5},{5,4},{6,7},{7,6},{8,9},{9,8},{10,11... | collective-permute-start | bytes 36872 | tf_op jit(solution)/shard_map/ppermute | solution.py:732
  38.8 4.1 %collective-permute-start.15 = (f32[24,128]{1,0:T(8,128)S(1)}, f32[24,128]{1,0:T(8,128)S(1)}, u32[]{:S(2)}, u32[]{:S(2)}) collective-permute-start(f32[24,128]{1,0:T(8,128)S(1)} %get-tuple-element.52), channel_id=1, source_target_pairs={{0,3},{1,2},{2,1},{3,0},{4,7},{5,6},{6,5},{7,4},{8,11},{9,10},{10,... | collective-permute-start | bytes 36872 | tf_op jit(solution)/shard_map/ppermute | solution.py:732
  43.3 8.2 %collective-permute-start.18 = (f32[6,32,128]{2,1,0:T(8,128)S(1)}, f32[6,32,128]{2,1,0:T(8,128)S(1)}, u32[]{:S(2)}, u32[]{:S(2)}) collective-permute-start(f32[6,32,128]{2,1,0:T(8,128)S(1)} %get-tuple-element.54), channel_id=1, source_target_pairs={{0,252},{4,8},{8,4},{12,16},{16,12},{20,24},{24,20},{28,32},{32,28... | collective-permute-start | bytes 294920 | tf_op jit(solution)/shard_map/ppermute | solution.py:796
  43.4 8.1 %collective-permute-start.19 = (f32[6,32,128]{2,1,0:T(8,128)S(1)}, f32[6,32,128]{2,1,0:T(8,128)S(1)}, u32[]{:S(2)}, u32[]{:S(2)}) collective-permute-start(f32[6,32,128]{2,1,0:T(8,128)S(1)} %get-tuple-element.55), channel_id=1, source_target_pairs={{0,4},{4,0},{8,12},{12,8},{16,20},{20,16},{24,28},{28,24},{32,36},... | collective-permute-start | bytes 294920 | tf_op jit(solution)/shard_map/ppermute | solution.py:797
  47.1 4.1 %collective-permute-start.20 = (f32[24,128]{1,0:T(8,128)S(1)}, f32[24,128]{1,0:T(8,128)S(1)}, u32[]{:S(2)}, u32[]{:S(2)}) collective-permute-start(f32[24,128]{1,0:T(8,128)S(1)} %shard_map.93), channel_id=1, source_target_pairs={{0,1},{1,2},{2,3},{3,0},{4,5},{5,6},{6,7},{7,4},{8,9},{9,10},{10,1... | collective-permute-start | bytes 36872 | tf_op jit(solution)/shard_map/ppermute | solution.py:799
  48.3 1.2 %collective-permute-start.21 = (f32[1,128]{1,0:T(1,128)S(1)}, f32[1,128]{1,0:T(1,128)S(1)}, u32[]{:S(2)}, u32[]{:S(2)}) collective-permute-start(f32[1,128]{1,0:T(1,128)S(1)} %get-tuple-element.63), channel_id=1, source_target_pairs={{0,4},{4,0},{8,12},{12,8},{16,20},{20,16},{24,28},{28,24},{32,36},... | collective-permute-start | bytes 1544 | tf_op jit(solution)/shard_map/ppermute | solution.py:807

commit v9 on v8

--- a/solution.py
+++ b/solution.py
@@ -385,41 +385,46 @@
 FETCHES = 4
 
 
-def side_one(both, charge, steps, changes, inner, steps_here, changes_here, rows, ext, sems):
+def fetch(src, dst, sems):
     each = HIST // FETCHES
-    copies = [
-        pltpu.make_async_copy(src.at[pl.ds(each * n, each)], dst.at[pl.ds(each * n, each)], sems.at[FETCHES * m + n])
-        for m, (src, dst) in enumerate(((steps, steps_here), (changes, changes_here)))
+    return [
+        pltpu.make_async_copy(src.at[pl.ds(each * n, each)], dst.at[pl.ds(each * n, each)], sems.at[n])
         for n in range(FETCHES)
     ]
+
+
+def side_one(both, charge, steps, inner, steps_here, ext, sems):
+    copies = fetch(steps, steps_here, sems)
     for copy in copies:
         copy.start()
     inner_residual(both, charge, inner, ext)
-    for copy in copies[:FETCHES]:
+    for copy in copies:
         copy.wait()
-    store(rows, 0, gram_dots(steps_here, steps_here, PAIRS))
-    store(rows, 36, field_dots((steps_here,), [density_tile(both)]))
-    for copy in copies[FETCHES:]:
-        copy.wait()
-    store(rows, 44, gram_dots(steps_here, changes_here, CROSS_PAIRS[:32]))
-
-
-def side_two(vector, both, steps, changes, inner, rows, moments, ext):
+
+
+def side_two(vector, both, near, far, z_first, z_second, potential, steps, changes, *outs):
+    inner, grad, changes_here, rows, moments, ext, sems = outs
+    copies = fetch(changes, changes_here, sems)
+    for copy in copies:
+        copy.start()
     inner_basis(vector, None, inner, ext)
     lifted, rho = lifted_tile(both, vector), density_tile(both)
-    by_step = field_dots((steps,), [lifted], [(rho, lifted)])
-    by_change = field_dots((changes,), [lifted, rho])
-    store(rows, 0, by_step[:8] + by_change[:8] + by_step[8:] + by_change[8:])
+    by_step = field_dots((steps,), [lifted, rho], [(rho, lifted)])
     store_moments([(vector, vector)], moments)
-
-
-def side_three(prior, vector, both, near, far, z_first, z_second, potential, steps, changes, *outs):
-    inner, grad, rows, moments, ext = outs
+    base_gradient(both, near, far, z_first, z_second, potential, grad, ext)
+    for copy in copies:
+        copy.wait()
+    by_change = field_dots((changes_here,), [lifted, rho])
+    store(rows, 0, by_step[:8] + by_change[:8] + by_step[16:] + by_step[8:16] + by_change[8:])
+
+
+def side_three(prior, vector, both, steps, changes, inner, rows, moments, ext):
     inner_basis(vector, prior, inner, ext)
     lifted, rho = lifted_tile(both, vector), density_tile(both)
     store(rows, 0, field_dots((steps, changes), [lifted], [(rho, lifted)]))
+    store(rows, 17, gram_dots(steps, changes, CROSS_PAIRS[:32]))
+    store(rows, 49, gram_dots(steps, steps, PAIRS))
     store_moments([(prior, vector), (vector, vector)], moments)
-    base_gradient(both, near, far, z_first, z_second, potential, grad, ext)
 
 
 def side_four(prior, vector, both, grad, steps, changes, inner, rows, moments, ext):
@@ -433,7 +438,7 @@
     store_moments([(prior, vector), (vector, vector)], moments)
 
 
-def side_five(prior, vector, both, steps, changes, r1, r2, r3, r4, m2, m3, m4, kept, given, table, m5):
+def side_five(prior, vector, both, steps, changes, r2, r3, r4, m2, m3, m4, kept, given, table, m5):
     lifted, rho = lifted_tile(both, vector), density_tile(both)
     own = field_dots((steps, changes), [lifted], [(rho, lifted)])
     store_moments([(prior, vector), (vector, vector)], m5)
@@ -447,12 +452,11 @@
             at = place(base + before)
             table[at : at + count - before, :] = ref[start + before : start + count, :]
 
-    put(ROW_GRAM, r1, 0, 36)
+    put(ROW_GRAM, r3, 49, 36)
     put(ROW_GRAM + 36, r4, 35, 36)
-    put(ROW_GRAM + 72, r1, 44, 32)
+    put(ROW_GRAM + 72, r3, 17, 32)
     put(ROW_GRAM + 104, r4, 71, 32)
-    put(ROW_BASE, r1, 36, 8)
-    put(ROW_BASE + 8, r2, 17, 8)
+    put(ROW_BASE, r2, 17, 16)
     put(ROW_BASE + 16, r4, 17, 18)
     for n, rows in enumerate((r2, r3, r4)):
         put(ROW_W + 17 * n, rows, 0, 17)
@@ -766,26 +770,32 @@
         return halo, z_halo(*call(pack_kernel, [face, face], [block_now], flops=work))
 
     stored = hist_steps.shape
-    inner, *history, r1 = call(
+    inner, steps = call(
         side_one,
-        [block, stored, stored, (80, LANES)],
-        [both, charge, hist_steps, hist_changes],
-        [ext, pltpu.SemaphoreType.DMA((2 * FETCHES,))],
+        [block, stored],
+        [both, charge, hist_steps],
+        [ext, pltpu.SemaphoreType.DMA((FETCHES,))],
         work,
-        in_hbm=(2, 3),
+        in_hbm=(2,),
     )
-    (v0,) = advance(1.0, inner, halo, ends)
+    density_far = lax.ppermute(after((sqrt_density,), *faces)[0], "blk", swap("blk", 1))
+    (mid,) = call(functools.partial(z_kernel, 1.0), [block], [inner, *ends], flops=work)
+    density_near = lax.ppermute(after((sqrt_density,), mid)[0], "blk", swap("blk", 0))
+    (v0,) = call(functools.partial(x_kernel, 1.0), [block], [mid, *halo], flops=work)
     halo, ends = exchange(v0)
-    density_halo = x_halo(after((sqrt_density,), v0)[0])
-    inner, r2, m2 = call(side_two, [block, (40, LANES), (8, LANES)], [v0, both, *history], [ext], work)
+    inner, grad, changes, r2, m2 = call(
+        side_two,
+        [block, block, stored, (40, LANES), (8, LANES)],
+        [v0, both, density_near, density_far, *density_ends, ion_potential, steps, hist_changes],
+        [ext, pltpu.SemaphoreType.DMA((FETCHES,))],
+        work,
+        in_hbm=(8,),
+    )
+    history = (steps, changes)
     (v1,) = advance(-1.0 / SHIFT, inner, halo, ends)
     halo, ends = exchange(v1)
-    inner, grad, r3, m3 = call(
-        side_three,
-        [block, block, (24, LANES), (8, LANES)],
-        [v0, v1, both, *density_halo, *density_ends, ion_potential, *history],
-        [ext],
-        work,
+    inner, r3, m3 = call(
+        side_three, [block, (88, LANES), (8, LANES)], [v0, v1, both, *history], [ext], work
     )
     (v2,) = advance(-2.0 / SHIFT, inner, halo, ends)
     halo, ends = exchange(v2)
@@ -800,7 +810,7 @@
     kept, given = call(
         side_five,
         [(1, LANES), (1, LANES)],
-        [v2, v3, both, *history, r1, r2, r3, r4, m2, m3, m4],
+        [v2, v3, both, *history, r2, r3, r4, m2, m3, m4],
         [(2 * LANES, LANES), (8, LANES)],
         work,
     )

time: 73.3 us -> 74 us (level)
  waiting for transfers between devices: 3.19 us -> 4.68 us
    ppermute x4, starting transfers between devices: 5.72 us -> 3.52 us  [z_halo(): lax.ppermute(face_b, 'gz', swap('gz', 1))]
    ppermute x5 -> x4, starting transfers between devices: 15.5 us -> 17.4 us  [x_halo(): return (lax.ppermute(block, 'blk', swap('blk', 0)), far)]
    ppermute x4, waiting for transfers between devices: 1.38 us -> 3.1 us  [z_halo(): lax.ppermute(face_b, 'gz', swap('gz', 1))]
    ppermute x0 -> x2, starting transfers between devices: none -> 1.52 us  [the longest x1 1.51 us: on_device(): lax.ppermute(after((sqrt_density,), mid)[0], 'blk', swap('blk', 0))]
    ppermute x5 -> x4, starting transfers between devices: 4.13 us -> 3.32 us  [x_halo(): far = lax.ppermute(block, 'blk', swap('blk', 1))]
    all_to_all x1, blocking collectives: 19.2 us -> 18.5 us  [on_device(): lax.all_to_all(outgoing.reshape(devices, 1, LANES), ('blk', 'gz'), 0, 0,...]
  transfers between devices with their start and end apart: 22 -> 22, of which waited for: 4 -> 5; matrix products, arithmetic and copies ran while one was open for 0% -> 0% of each run, Pallas kernels for 20% -> 19%
where the time goes in v9:
time: 74 us; the launch traced here: 73.9 us
  starting transfers between devices  32.9 us (44%)
  blocking collectives  18.5 us (25%)
  Pallas kernels  16.7 us (23%)
  waiting for transfers between devices  4.68 us (6%)
  between operations  1.08 us (1%)
    all_to_all x1, blocking collectives, on_device(): lax.all_to_all(outgoing.reshape(devices, 1, LANES), ('blk', 'gz'), 0, 0,...  18.5 us
    ppermute x4, starting transfers between devices, x_halo(): return (lax.ppermute(block, 'blk', swap('blk', 0)), far)  17.4 us
    pallas_call x22, Pallas kernels, call(): pl.pallas_call(kernel, out_shape=shapes, in_specs=[pl.BlockSpec(memory_sp...  16.7 us
    ppermute x4, starting transfers between devices, z_halo(): lax.ppermute(face_b, 'gz', swap('gz', 1))  3.52 us
    ppermute x1, starting transfers between devices, on_device(): near = lax.ppermute(to_near, 'blk', swap('blk', 0))  3.4 us
    ppermute x4, starting transfers between devices, x_halo(): far = lax.ppermute(block, 'blk', swap('blk', 1))  3.32 us
    ppermute x4, waiting for transfers between devices, z_halo(): lax.ppermute(face_b, 'gz', swap('gz', 1))  3.1 us
    ppermute x4, starting transfers between devices, z_halo(): lax.ppermute(face_a, 'gz', swap('gz', 0))  2.84 us
  transfers between devices with their start and end apart: 22, of which 5 were waited for; matrix products, arithmetic and copies ran while one was open for 0% of the time, Pallas kernels for 19%

profile of v9, /device:TPU:1, one launch (start us, length us, event | category | flops | bytes accessed | tf_op | source)
XLA Modules:
  0.0 73.9 jit_solution(12709644987973289659)
XLA Ops:
  0.6 2.7 %collective-permute-start.3 = (f32[6,64,128]{2,1,0:T(8,128)}, f32[6,64,128]{2,1,0:T(8,128)S(1)}, u32[]{:S(2)}, u32[]{:S(2)}) collective-permute-start(f32[6,64,128]{2,1,0:T(8,128)} %hartree.1), channel_id=1, source_target_pairs={{0,252},{4,8},{8,4},{12,16},{16,12},{20,24},{24,20},{28,32},{32,28... | collective-permute-start | bytes 589832 | tf_op jit(solution)/shard_map/ppermute | solution.py:731
  3.3 6.4 %collective-permute-start.2 = (f32[6,64,128]{2,1,0:T(8,128)}, f32[6,64,128]{2,1,0:T(8,128)S(1)}, u32[]{:S(2)}, u32[]{:S(2)}) collective-permute-start(f32[6,64,128]{2,1,0:T(8,128)} %hartree.1), channel_id=1, source_target_pairs={{0,4},{4,0},{8,12},{12,8},{16,20},{20,16},{24,28},{28,24},{32,36},... | collective-permute-start | bytes 589832 | tf_op jit(solution)/shard_map/ppermute | solution.py:732
  9.7 1.3 %shard_map.77 = (f32[12,64,128]{2,1,0:T(8,128)S(1)}, f32[6,64,128]{2,1,0:T(8,128)S(1)}, f32[48,128]{1,0:T(8,128)S(1)}, f32[48,128]{1,0:T(8,128)S(1)}) custom-call(f32[6,64,128]{2,1,0:T(8,128)} %hartree.1, f32[6,64,128]{2,1,0:T(8,128)} %density.1, f32[6,64,128]{2,1,0:T(8,128)} %charge.1), custom_call_target="tpu_custom_call" | custom-call | bytes 1228800 | tf_op jit(solution)/shard_map/pallas_call | solution.py:705
  11.0 1.4 %collective-permute-start = (f32[48,128]{1,0:T(8,128)S(1)}, f32[48,128]{1,0:T(8,128)S(1)}, u32[]{:S(2)}, u32[]{:S(2)}) collective-permute-start(f32[48,128]{1,0:T(8,128)S(1)} %get-tuple-element.38), channel_id=1, source_target_pairs={{0,1},{1,0},{2,3},{3,2},{4,5},{5,4},{6,7},{7,6},{8,9},{9,8},{10,11... | collective-permute-start | bytes 73736 | tf_op jit(solution)/shard_map/ppermute | solution.py:736
  12.4 1.9 %collective-permute-start.1 = (f32[48,128]{1,0:T(8,128)S(1)}, f32[48,128]{1,0:T(8,128)S(1)}, u32[]{:S(2)}, u32[]{:S(2)}) collective-permute-start(f32[48,128]{1,0:T(8,128)S(1)} %get-tuple-element.39), channel_id=1, source_target_pairs={{0,3},{1,2},{2,1},{3,0},{4,7},{5,6},{6,5},{7,4},{8,11},{9,10},{10,... | collective-permute-start | bytes 73736 | tf_op jit(solution)/shard_map/ppermute | solution.py:736
  14.3 2.0 %shard_map.78 = (f32[6,64,128]{2,1,0:T(8,128)S(1)}, f32[8,6,64,128]{3,2,1,0:T(8,128)S(1)}) custom-call(f32[12,64,128]{2,1,0:T(8,128)S(1)} %get-tuple-element.35.both, f32[6,64,128]{2,1,0:T(8,128)S(1)} %get-tuple-element.36.charge, f32[8,6,64,128]{3,2,1,0:T(8,128)} %steps.1), custom_call_target="tpu_custom_call" | custom-call | flops 14745600 | bytes 3932160 | tf_op jit(solution)/shard_map/pallas_call | solution.py:705
  16.3 0.3 shard_map.79.inner
  16.6 1.5 %collective-permute-start.4 = (f32[6,64,128]{2,1,0:T(8,128)S(1)}, f32[6,64,128]{2,1,0:T(8,128)S(1)}, u32[]{:S(2)}, u32[]{:S(2)}) collective-permute-start(f32[6,64,128]{2,1,0:T(8,128)S(1)} %copy-done.1), channel_id=1, source_target_pairs={{0,4},{4,0},{8,12},{12,8},{16,20},{20,16},{24,28},{28,24},{32,36},... | collective-permute-start | bytes 589832 | tf_op jit(solution)/shard_map/ppermute | solution.py:783
  18.1 0.1 shard_map.80.vector.block.prior.v0
  18.2 0.4 collective-permute-start.9
  18.7 3.9 %collective-permute-start.8 = (f32[6,64,128]{2,1,0:T(8,128)S(1)}, f32[6,64,128]{2,1,0:T(8,128)S(1)}, u32[]{:S(2)}, u32[]{:S(2)}) collective-permute-start(f32[6,64,128]{2,1,0:T(8,128)S(1)} %shard_map.80.vector.block.prior.v0), channel_id=1, source_target_pairs={{0,4},{4,0},{8,12},{12,8},{16,20},{20,16},{24,28},{28,24},{32,36},... | collective-permute-start | bytes 589832 | tf_op jit(solution)/shard_map/ppermute | solution.py:732
  22.6 0.2 shard_map.82
  22.8 0.5 collective-permute-start.6
  23.2 0.5 collective-permute-start.7
  23.7 2.4 %shard_map.81 = (f32[6,64,128]{2,1,0:T(8,128)S(1)}, f32[6,64,128]{2,1,0:T(8,128)S(1)}, f32[8,6,64,128]{3,2,1,0:T(8,128)S(1)}, f32[40,128]{1,0:T(8,128)S(1)}, f32[8,128]{1,0:T(8,128)S(1)}) custom-call(f32[6,64,128]{2,1,0:T(8,128)S(1)} %shard_map.80.vector.block.prior.v0, f32[12,64,128]{2,1,0:T(8,128)S(1)} %get-tuple-element.35.both, ...), custom_call_target="tpu_custom_call" | custom-call | flops 14745600 | bytes 6365184 | tf_op jit(solution)/shard_map/pallas_call | solution.py:705
  26.2 0.8 %collective-permute-done.7.z_second = f32[24,128]{1,0:T(8,128)S(1)} collective-permute-done((f32[24,128]{1,0:T(8,128)S(1)}, f32[24,128]{1,0:T(8,128)S(1)}, u32[]{:S(2)}, u32[]{:S(2)}) %collective-permute-start.7) | collective-permute-done | bytes 12320 | tf_op jit(solution)/shard_map/ppermute | solution.py:736
  27.0 0.3 shard_map.83.inner
  27.3 0.1 shard_map.84.vector.block.prior.v1
  27.4 0.1 collective-permute-start.13
  27.5 3.7 %collective-permute-start.12 = (f32[6,64,128]{2,1,0:T(8,128)S(1)}, f32[6,64,128]{2,1,0:T(8,128)S(1)}, u32[]{:S(2)}, u32[]{:S(2)}) collective-permute-start(f32[6,64,128]{2,1,0:T(8,128)S(1)} %shard_map.84.vector.block.prior.v1), channel_id=1, source_target_pairs={{0,4},{4,0},{8,12},{12,8},{16,20},{20,16},{24,28},{28,24},{32,36},... | collective-permute-start | bytes 589832 | tf_op jit(solution)/shard_map/ppermute | solution.py:732
  31.2 0.2 shard_map.86
  31.4 0.5 collective-permute-start.10
  31.9 0.7 collective-permute-start.11
  32.5 2.2 %shard_map.85 = (f32[6,64,128]{2,1,0:T(8,128)S(1)}, f32[88,128]{1,0:T(8,128)S(1)}, f32[8,128]{1,0:T(8,128)S(1)}) custom-call(f32[6,64,128]{2,1,0:T(8,128)S(1)} %shard_map.80.vector.block.prior.v0, f32[6,64,128]{2,1,0:T(8,128)S(1)} %shard_map.84.vector.block.prior.v1, f32[12,64,128]{2,1,0:T(8,128)S(1)} %get-tuple-element.35.both, ...), custom_call_target="tpu_custom_call" | custom-call | flops 14745600 | bytes 4177920 | tf_op jit(solution)/shard_map/pallas_call | solution.py:705
  34.8 1.2 %collective-permute-done.11.z_second = f32[24,128]{1,0:T(8,128)S(1)} collective-permute-done((f32[24,128]{1,0:T(8,128)S(1)}, f32[24,128]{1,0:T(8,128)S(1)}, u32[]{:S(2)}, u32[]{:S(2)}) %collective-permute-start.11) | collective-permute-done | bytes 12320 | tf_op jit(solution)/shard_map/ppermute | solution.py:736
  35.9 0.3 shard_map.87.inner
  36.2 0.1 shard_map.88.vector.block.prior.v2
  36.4 3.4 %collective-permute-start.16 = (f32[6,64,128]{2,1,0:T(8,128)S(1)}, f32[6,64,128]{2,1,0:T(8,128)S(1)}, u32[]{:S(2)}, u32[]{:S(2)}) collective-permute-start(f32[6,64,128]{2,1,0:T(8,128)S(1)} %shard_map.88.vector.block.prior.v2), channel_id=1, source_target_pairs={{0,4},{4,0},{8,12},{12,8},{16,20},{20,16},{24,28},{28,24},{32,36},... | collective-permute-start | bytes 589832 | tf_op jit(solution)/shard_map/ppermute | solution.py:732
  39.8 0.2 shard_map.90
  40.0 0.5 collective-permute-start.14
  40.5 0.5 collective-permute-start.15
  41.0 2.5 %shard_map.89 = (f32[6,64,128]{2,1,0:T(8,128)S(1)}, f32[112,128]{1,0:T(8,128)S(1)}, f32[8,128]{1,0:T(8,128)S(1)}) custom-call(f32[6,64,128]{2,1,0:T(8,128)S(1)} %shard_map.84.vector.block.prior.v1, f32[6,64,128]{2,1,0:T(8,128)S(1)} %shard_map.88.vector.block.prior.v2, f32[12,64,128]{2,1,0:T(8,128)S(1)} %get-tuple-element.35.both, ...), custom_call_target="tpu_custom_call" | custom-call | flops 14745600 | bytes 4386816 | tf_op jit(solution)/shard_map/pallas_call | solution.py:705
  43.4 1.1 %collective-permute-done.15.z_second = f32[24,128]{1,0:T(8,128)S(1)} collective-permute-done((f32[24,128]{1,0:T(8,128)S(1)}, f32[24,128]{1,0:T(8,128)S(1)}, u32[]{:S(2)}, u32[]{:S(2)}) %collective-permute-start.15) | collective-permute-done | bytes 12320 | tf_op jit(solution)/shard_map/ppermute | solution.py:736
  44.5 0.3 shard_map.91.inner
  44.8 0.1 shard_map.92
  45.0 0.1 collective-permute-start.18
  45.1 3.4 %collective-permute-start.19 = (f32[6,32,128]{2,1,0:T(8,128)S(1)}, f32[6,32,128]{2,1,0:T(8,128)S(1)}, u32[]{:S(2)}, u32[]{:S(2)}) collective-permute-start(f32[6,32,128]{2,1,0:T(8,128)S(1)} %get-tuple-element.56), channel_id=1, source_target_pairs={{0,4},{4,0},{8,12},{12,8},{16,20},{20,16},{24,28},{28,24},{32,36},... | collective-permute-start | bytes 294920 | tf_op jit(solution)/shard_map/ppermute | solution.py:807
  48.5 0.1 shard_map.93
  48.6 0.5 collective-permute-start.20
  49.1 1.0 %shard_map.94 = (f32[1,128]{1,0:T(1,128)S(1)}, f32[1,128]{1,0:T(1,128)S(1)}) custom-call(f32[6,64,128]{2,1,0:T(8,128)S(1)} %shard_map.88.vector.block.prior.v2, f32[6,64,128]{2,1,0:T(8,128)S(1)} %get-tuple-element.64.block.vector.own.v3, f32[12,64,128]{2,1,0:T(8,128)S(1)} %get-tuple-element.35.both, f32[8,6,64,128]{3,2,1,0:T(8,128)S(1)} %get-tuple-element.42.steps, ...), custom_call_target="tpu_custom_call" | custom-call | flops 14745600 | bytes 4068352 | tf_op jit(solution)/shard_map/pallas_call | solution.py:705
  50.0 0.4 collective-permute-start.21
  50.4 0.7 %shard_map.95.inner = f32[8,128]{1,0:T(8,128)S(1)} custom-call(f32[6,64,128]{2,1,0:T(8,128)S(1)} %get-tuple-element.64.block.vector.own.v3), custom_call_target="tpu_custom_call" | custom-call | flops 14745600 | bytes 200704 | tf_op jit(solution)/shard_map/pallas_call | solution.py:705
  51.2 0.1 collective-permute-done.21.taken
  51.3 1.4 %collective-permute-done.20.z_left = f32[24,128]{1,0:T(8,128)S(1)} collective-permute-done((f32[24,128]{1,0:T(8,128)S(1)}, f32[24,128]{1,0:T(8,128)S(1)}, u32[]{:S(2)}, u32[]{:S(2)}) %collective-permute-start.20) | collective-permute-done | bytes 12320 | tf_op jit(solution)/shard_map/ppermute | solution.py:809
  52.7 0.2 shard_map.96
  53.0 0.6 shard_map.97
  53.6 18.5 %all_to_all.5 = f32[256,1,128]{2,1,0:T(1,128)S(1)} all-to-all(f32[256,1,128]{2,1,0:T(1,128)S(1)} %bitcast.5), channel_id=1, replica_groups=mesh['blk'=64,'gz'=4] {'blk','gz'}, dimensions={0} | all-to-all | bytes 262144 | tf_op jit(solution)/shard_map/all_to_all | solution.py:822
  72.1 1.6 %shard_map.98 = (f32[6,64,128]{2,1,0:T(8,128)}, f32[6,64,128]{2,1,0:T(8,128)}) custom-call(f32[256,128]{1,0:T(8,128)S(1)} %bitcast.4, f32[12,64,128]{2,1,0:T(8,128)S(1)} %get-tuple-element.35.both, f32[6,64,128]{2,1,0:T(8,128)S(1)} %get-tuple-element.50.grad, f32[6,64,128]{2,1,0:T(8,128)S(1)} %shard_map.80.vector.block.prior.v0, ...), custom_call_target="tpu_custom_call" | custom-call | flops 14745600 | bytes 5046272 | tf_op jit(solution)/shard_map/pallas_call | solution.py:705
  (23 shorter events, 0.1 us)
Async XLA Ops:
  0.6 16.0 %copy-start.1 = (f32[6,64,128]{2,1,0:T(8,128)S(1)}, f32[6,64,128]{2,1,0:T(8,128)}, u32[]{:S(2)}) copy-start(f32[6,64,128]{2,1,0:T(8,128)} %density.1) | copy-start | bytes 589828
  0.6 17.5 %collective-permute-start.3 = (f32[6,64,128]{2,1,0:T(8,128)}, f32[6,64,128]{2,1,0:T(8,128)S(1)}, u32[]{:S(2)}, u32[]{:S(2)}) collective-permute-start(f32[6,64,128]{2,1,0:T(8,128)} %hartree.1), channel_id=1, source_target_pairs={{0,252},{4,8},{8,4},{12,16},{16,12},{20,24},{24,20},{28,32},{32,28... | collective-permute-start | bytes 589832 | tf_op jit(solution)/shard_map/ppermute | solution.py:731
  3.3 14.8 %collective-permute-start.2 = (f32[6,64,128]{2,1,0:T(8,128)}, f32[6,64,128]{2,1,0:T(8,128)S(1)}, u32[]{:S(2)}, u32[]{:S(2)}) collective-permute-start(f32[6,64,128]{2,1,0:T(8,128)} %hartree.1), channel_id=1, source_target_pairs={{0,4},{4,0},{8,12},{12,8},{16,20},{20,16},{24,28},{28,24},{32,36},... | collective-permute-start | bytes 589832 | tf_op jit(solution)/shard_map/ppermute | solution.py:732
  11.0 5.3 %collective-permute-start = (f32[48,128]{1,0:T(8,128)S(1)}, f32[48,128]{1,0:T(8,128)S(1)}, u32[]{:S(2)}, u32[]{:S(2)}) collective-permute-start(f32[48,128]{1,0:T(8,128)S(1)} %get-tuple-element.38), channel_id=1, source_target_pairs={{0,1},{1,0},{2,3},{3,2},{4,5},{5,4},{6,7},{7,6},{8,9},{9,8},{10,11... | collective-permute-start | bytes 73736 | tf_op jit(solution)/shard_map/ppermute | solution.py:736
  12.4 3.9 %collective-permute-start.1 = (f32[48,128]{1,0:T(8,128)S(1)}, f32[48,128]{1,0:T(8,128)S(1)}, u32[]{:S(2)}, u32[]{:S(2)}) collective-permute-start(f32[48,128]{1,0:T(8,128)S(1)} %get-tuple-element.39), channel_id=1, source_target_pairs={{0,3},{1,2},{2,1},{3,0},{4,7},{5,6},{6,5},{7,4},{8,11},{9,10},{10,... | collective-permute-start | bytes 73736 | tf_op jit(solution)/shard_map/ppermute | solution.py:736
  14.3 8.9 %collective-permute-start.5 = (f32[6,64,128]{2,1,0:T(8,128)}, f32[6,64,128]{2,1,0:T(8,128)S(1)}, u32[]{:S(2)}, u32[]{:S(2)}) collective-permute-start(f32[6,64,128]{2,1,0:T(8,128)} %density.1), channel_id=1, source_target_pairs={{0,252},{4,8},{8,4},{12,16},{16,12},{20,24},{24,20},{28,32},{32,28... | collective-permute-start | bytes 589832 | tf_op jit(solution)/shard_map/ppermute | solution.py:781
  14.3 9.4 %copy-start = (f32[6,64,128]{2,1,0:T(8,128)S(1)}, f32[6,64,128]{2,1,0:T(8,128)}, u32[]{:S(2)}) copy-start(f32[6,64,128]{2,1,0:T(8,128)} %potential.1) | copy-start | bytes 589828
  16.6 7.1 %collective-permute-start.4 = (f32[6,64,128]{2,1,0:T(8,128)S(1)}, f32[6,64,128]{2,1,0:T(8,128)S(1)}, u32[]{:S(2)}, u32[]{:S(2)}) collective-permute-start(f32[6,64,128]{2,1,0:T(8,128)S(1)} %copy-done.1), channel_id=1, source_target_pairs={{0,4},{4,0},{8,12},{12,8},{16,20},{20,16},{24,28},{28,24},{32,36},... | collective-permute-start | bytes 589832 | tf_op jit(solution)/shard_map/ppermute | solution.py:783
  18.2 9.0 %collective-permute-start.9 = (f32[6,64,128]{2,1,0:T(8,128)S(1)}, f32[6,64,128]{2,1,0:T(8,128)S(1)}, u32[]{:S(2)}, u32[]{:S(2)}) collective-permute-start(f32[6,64,128]{2,1,0:T(8,128)S(1)} %shard_map.80.vector.block.prior.v0), channel_id=1, source_target_pairs={{0,252},{4,8},{8,4},{12,16},{16,12},{20,24},{24,20},{28,32},{32,28... | collective-permute-start | bytes 589832 | tf_op jit(solution)/shard_map/ppermute | solution.py:731
  18.7 8.6 %collective-permute-start.8 = (f32[6,64,128]{2,1,0:T(8,128)S(1)}, f32[6,64,128]{2,1,0:T(8,128)S(1)}, u32[]{:S(2)}, u32[]{:S(2)}) collective-permute-start(f32[6,64,128]{2,1,0:T(8,128)S(1)} %shard_map.80.vector.block.prior.v0), channel_id=1, source_target_pairs={{0,4},{4,0},{8,12},{12,8},{16,20},{20,16},{24,28},{28,24},{32,36},... | collective-permute-start | bytes 589832 | tf_op jit(solution)/shard_map/ppermute | solution.py:732
  22.8 3.4 %collective-permute-start.6 = (f32[24,128]{1,0:T(8,128)S(1)}, f32[24,128]{1,0:T(8,128)S(1)}, u32[]{:S(2)}, u32[]{:S(2)}) collective-permute-start(f32[24,128]{1,0:T(8,128)S(1)} %get-tuple-element.44), channel_id=1, source_target_pairs={{0,1},{1,0},{2,3},{3,2},{4,5},{5,4},{6,7},{7,6},{8,9},{9,8},{10,11... | collective-permute-start | bytes 36872 | tf_op jit(solution)/shard_map/ppermute | solution.py:736
  23.2 3.8 %collective-permute-start.7 = (f32[24,128]{1,0:T(8,128)S(1)}, f32[24,128]{1,0:T(8,128)S(1)}, u32[]{:S(2)}, u32[]{:S(2)}) collective-permute-start(f32[24,128]{1,0:T(8,128)S(1)} %get-tuple-element.45), channel_id=1, source_target_pairs={{0,3},{1,2},{2,1},{3,0},{4,7},{5,6},{6,5},{7,4},{8,11},{9,10},{10,... | collective-permute-start | bytes 36872 | tf_op jit(solution)/shard_map/ppermute | solution.py:736
  27.4 8.8 %collective-permute-start.13 = (f32[6,64,128]{2,1,0:T(8,128)S(1)}, f32[6,64,128]{2,1,0:T(8,128)S(1)}, u32[]{:S(2)}, u32[]{:S(2)}) collective-permute-start(f32[6,64,128]{2,1,0:T(8,128)S(1)} %shard_map.84.vector.block.prior.v1), channel_id=1, source_target_pairs={{0,252},{4,8},{8,4},{12,16},{16,12},{20,24},{24,20},{28,32},{32,28... | collective-permute-start | bytes 589832 | tf_op jit(solution)/shard_map/ppermute | solution.py:731
  27.5 8.7 %collective-permute-start.12 = (f32[6,64,128]{2,1,0:T(8,128)S(1)}, f32[6,64,128]{2,1,0:T(8,128)S(1)}, u32[]{:S(2)}, u32[]{:S(2)}) collective-permute-start(f32[6,64,128]{2,1,0:T(8,128)S(1)} %shard_map.84.vector.block.prior.v1), channel_id=1, source_target_pairs={{0,4},{4,0},{8,12},{12,8},{16,20},{20,16},{24,28},{28,24},{32,36},... | collective-permute-start | bytes 589832 | tf_op jit(solution)/shard_map/ppermute | solution.py:732
  31.4 3.4 %collective-permute-start.10 = (f32[24,128]{1,0:T(8,128)S(1)}, f32[24,128]{1,0:T(8,128)S(1)}, u32[]{:S(2)}, u32[]{:S(2)}) collective-permute-start(f32[24,128]{1,0:T(8,128)S(1)} %get-tuple-element.48), channel_id=1, source_target_pairs={{0,1},{1,0},{2,3},{3,2},{4,5},{5,4},{6,7},{7,6},{8,9},{9,8},{10,11... | collective-permute-start | bytes 36872 | tf_op jit(solution)/shard_map/ppermute | solution.py:736
  31.9 4.1 %collective-permute-start.11 = (f32[24,128]{1,0:T(8,128)S(1)}, f32[24,128]{1,0:T(8,128)S(1)}, u32[]{:S(2)}, u32[]{:S(2)}) collective-permute-start(f32[24,128]{1,0:T(8,128)S(1)} %get-tuple-element.49), channel_id=1, source_target_pairs={{0,3},{1,2},{2,1},{3,0},{4,7},{5,6},{6,5},{7,4},{8,11},{9,10},{10,... | collective-permute-start | bytes 36872 | tf_op jit(solution)/shard_map/ppermute | solution.py:736
  36.3 8.5 %collective-permute-start.17 = (f32[6,64,128]{2,1,0:T(8,128)S(1)}, f32[6,64,128]{2,1,0:T(8,128)S(1)}, u32[]{:S(2)}, u32[]{:S(2)}) collective-permute-start(f32[6,64,128]{2,1,0:T(8,128)S(1)} %shard_map.88.vector.block.prior.v2), channel_id=1, source_target_pairs={{0,252},{4,8},{8,4},{12,16},{16,12},{20,24},{24,20},{28,32},{32,28... | collective-permute-start | bytes 589832 | tf_op jit(solution)/shard_map/ppermute | solution.py:731
  36.4 8.4 %collective-permute-start.16 = (f32[6,64,128]{2,1,0:T(8,128)S(1)}, f32[6,64,128]{2,1,0:T(8,128)S(1)}, u32[]{:S(2)}, u32[]{:S(2)}) collective-permute-start(f32[6,64,128]{2,1,0:T(8,128)S(1)} %shard_map.88.vector.block.prior.v2), channel_id=1, source_target_pairs={{0,4},{4,0},{8,12},{12,8},{16,20},{20,16},{24,28},{28,24},{32,36},... | collective-permute-start | bytes 589832 | tf_op jit(solution)/shard_map/ppermute | solution.py:732
  40.0 3.4 %collective-permute-start.14 = (f32[24,128]{1,0:T(8,128)S(1)}, f32[24,128]{1,0:T(8,128)S(1)}, u32[]{:S(2)}, u32[]{:S(2)}) collective-permute-start(f32[24,128]{1,0:T(8,128)S(1)} %get-tuple-element.52), channel_id=1, source_target_pairs={{0,1},{1,0},{2,3},{3,2},{4,5},{5,4},{6,7},{7,6},{8,9},{9,8},{10,11... | collective-permute-start | bytes 36872 | tf_op jit(solution)/shard_map/ppermute | solution.py:736
  40.5 4.1 %collective-permute-start.15 = (f32[24,128]{1,0:T(8,128)S(1)}, f32[24,128]{1,0:T(8,128)S(1)}, u32[]{:S(2)}, u32[]{:S(2)}) collective-permute-start(f32[24,128]{1,0:T(8,128)S(1)} %get-tuple-element.53), channel_id=1, source_target_pairs={{0,3},{1,2},{2,1},{3,0},{4,7},{5,6},{6,5},{7,4},{8,11},{9,10},{10,... | collective-permute-start | bytes 36872 | tf_op jit(solution)/shard_map/ppermute | solution.py:736
  45.0 8.0 %collective-permute-start.18 = (f32[6,32,128]{2,1,0:T(8,128)S(1)}, f32[6,32,128]{2,1,0:T(8,128)S(1)}, u32[]{:S(2)}, u32[]{:S(2)}) collective-permute-start(f32[6,32,128]{2,1,0:T(8,128)S(1)} %get-tuple-element.55), channel_id=1, source_target_pairs={{0,252},{4,8},{8,4},{12,16},{16,12},{20,24},{24,20},{28,32},{32,28... | collective-permute-start | bytes 294920 | tf_op jit(solution)/shard_map/ppermute | solution.py:806
  45.1 7.9 %collective-permute-start.19 = (f32[6,32,128]{2,1,0:T(8,128)S(1)}, f32[6,32,128]{2,1,0:T(8,128)S(1)}, u32[]{:S(2)}, u32[]{:S(2)}) collective-permute-start(f32[6,32,128]{2,1,0:T(8,128)S(1)} %get-tuple-element.56), channel_id=1, source_target_pairs={{0,4},{4,0},{8,12},{12,8},{16,20},{20,16},{24,28},{28,24},{32,36},... | collective-permute-start | bytes 294920 | tf_op jit(solution)/shard_map/ppermute | solution.py:807
  48.6 4.1 %collective-permute-start.20 = (f32[24,128]{1,0:T(8,128)S(1)}, f32[24,128]{1,0:T(8,128)S(1)}, u32[]{:S(2)}, u32[]{:S(2)}) collective-permute-start(f32[24,128]{1,0:T(8,128)S(1)} %shard_map.93), channel_id=1, source_target_pairs={{0,1},{1,2},{2,3},{3,0},{4,5},{5,6},{6,7},{7,4},{8,9},{9,10},{10,1... | collective-permute-start | bytes 36872 | tf_op jit(solution)/shard_map/ppermute | solution.py:809
  50.0 1.2 %collective-permute-start.21 = (f32[1,128]{1,0:T(1,128)S(1)}, f32[1,128]{1,0:T(1,128)S(1)}, u32[]{:S(2)}, u32[]{:S(2)}) collective-permute-start(f32[1,128]{1,0:T(1,128)S(1)} %get-tuple-element.63), channel_id=1, source_target_pairs={{0,4},{4,0},{8,12},{12,8},{16,20},{20,16},{24,28},{28,24},{32,36},... | collective-permute-start | bytes 1544 | tf_op jit(solution)/shard_map/ppermute | solution.py:817

commit v10 on v9

--- a/solution.py
+++ b/solution.py
@@ -382,48 +382,27 @@
     return lambda i, b: 2.0 * tile_of(both, REACH + i, b) * tile_of(vector, i, b)
 
 
-FETCHES = 4
-
-
-def fetch(src, dst, sems):
-    each = HIST // FETCHES
-    return [
-        pltpu.make_async_copy(src.at[pl.ds(each * n, each)], dst.at[pl.ds(each * n, each)], sems.at[n])
-        for n in range(FETCHES)
-    ]
-
-
-def side_one(both, charge, steps, inner, steps_here, ext, sems):
-    copies = fetch(steps, steps_here, sems)
-    for copy in copies:
-        copy.start()
+def side_one(both, charge, inner, ext):
     inner_residual(both, charge, inner, ext)
-    for copy in copies:
-        copy.wait()
-
-
-def side_two(vector, both, near, far, z_first, z_second, potential, steps, changes, *outs):
-    inner, grad, changes_here, rows, moments, ext, sems = outs
-    copies = fetch(changes, changes_here, sems)
-    for copy in copies:
-        copy.start()
+
+
+def side_two(vector, both, near, far, z_first, z_second, potential, steps, *outs):
+    inner, grad, rows, moments, ext = outs
     inner_basis(vector, None, inner, ext)
     lifted, rho = lifted_tile(both, vector), density_tile(both)
-    by_step = field_dots((steps,), [lifted, rho], [(rho, lifted)])
+    store(rows, 0, field_dots((steps,), [lifted, rho], [(rho, lifted)]))
     store_moments([(vector, vector)], moments)
     base_gradient(both, near, far, z_first, z_second, potential, grad, ext)
-    for copy in copies:
-        copy.wait()
-    by_change = field_dots((changes_here,), [lifted, rho])
-    store(rows, 0, by_step[:8] + by_change[:8] + by_step[16:] + by_step[8:16] + by_change[8:])
 
 
 def side_three(prior, vector, both, steps, changes, inner, rows, moments, ext):
     inner_basis(vector, prior, inner, ext)
-    lifted, rho = lifted_tile(both, vector), density_tile(both)
-    store(rows, 0, field_dots((steps, changes), [lifted], [(rho, lifted)]))
-    store(rows, 17, gram_dots(steps, changes, CROSS_PAIRS[:32]))
-    store(rows, 49, gram_dots(steps, steps, PAIRS))
+    before, lifted, rho = lifted_tile(both, prior), lifted_tile(both, vector), density_tile(both)
+    by_step = field_dots((steps,), [lifted], [(rho, lifted)])
+    by_change = field_dots((changes,), [before, rho, lifted])
+    store(rows, 0, by_step[:8] + by_change[16:] + by_step[8:] + by_change[:16])
+    store(rows, 33, gram_dots(steps, changes, CROSS_PAIRS[:32]))
+    store(rows, 65, gram_dots(steps, steps, PAIRS))
     store_moments([(prior, vector), (vector, vector)], moments)
 
 
@@ -452,14 +431,18 @@
             at = place(base + before)
             table[at : at + count - before, :] = ref[start + before : start + count, :]
 
-    put(ROW_GRAM, r3, 49, 36)
+    put(ROW_GRAM, r3, 65, 36)
     put(ROW_GRAM + 36, r4, 35, 36)
-    put(ROW_GRAM + 72, r3, 17, 32)
+    put(ROW_GRAM + 72, r3, 33, 32)
     put(ROW_GRAM + 104, r4, 71, 32)
-    put(ROW_BASE, r2, 17, 16)
+    put(ROW_BASE, r2, 8, 8)
+    put(ROW_BASE + 8, r3, 25, 8)
     put(ROW_BASE + 16, r4, 17, 18)
-    for n, rows in enumerate((r2, r3, r4)):
-        put(ROW_W + 17 * n, rows, 0, 17)
+    put(ROW_W, r2, 0, 8)
+    put(ROW_W + 8, r3, 17, 8)
+    put(ROW_W + 16, r2, 16, 1)
+    put(ROW_W + 17, r3, 0, 17)
+    put(ROW_W + 34, r4, 0, 17)
     store(table, place(ROW_W + 51), own)
 
     order = [(m2, 0), (m3, 0), (m3, 1), (m4, 0), (m4, 1), (m5, 0), (m5, 1)]
@@ -741,7 +724,9 @@
     ext = (block[0], block[1] + 16, block[2])
     face = (24, LANES)
     cells = math.prod(block)
+    history = (hist_steps, hist_changes)
     cells = math.prod(block)
+    history = (hist_steps, hist_changes)
     work = 300 * cells
     inputs = (hartree_prev, sqrt_density, ion_charge)
     halo = x_halo(hartree_prev)
@@ -769,33 +754,23 @@
         halo = x_halo(block_now)
         return halo, z_halo(*call(pack_kernel, [face, face], [block_now], flops=work))
 
-    stored = hist_steps.shape
-    inner, steps = call(
-        side_one,
-        [block, stored],
-        [both, charge, hist_steps],
-        [ext, pltpu.SemaphoreType.DMA((FETCHES,))],
-        work,
-        in_hbm=(2,),
-    )
+    (inner,) = call(side_one, [block], [both, charge], [ext], work)
     density_far = lax.ppermute(after((sqrt_density,), *faces)[0], "blk", swap("blk", 1))
     (mid,) = call(functools.partial(z_kernel, 1.0), [block], [inner, *ends], flops=work)
     density_near = lax.ppermute(after((sqrt_density,), mid)[0], "blk", swap("blk", 0))
     (v0,) = call(functools.partial(x_kernel, 1.0), [block], [mid, *halo], flops=work)
     halo, ends = exchange(v0)
-    inner, grad, changes, r2, m2 = call(
+    inner, grad, r2, m2 = call(
         side_two,
-        [block, block, stored, (40, LANES), (8, LANES)],
-        [v0, both, density_near, density_far, *density_ends, ion_potential, steps, hist_changes],
-        [ext, pltpu.SemaphoreType.DMA((FETCHES,))],
+        [block, block, (24, LANES), (8, LANES)],
+        [v0, both, density_near, density_far, *density_ends, ion_potential, hist_steps],
+        [ext],
         work,
-        in_hbm=(8,),
     )
-    history = (steps, changes)
     (v1,) = advance(-1.0 / SHIFT, inner, halo, ends)
     halo, ends = exchange(v1)
     inner, r3, m3 = call(
-        side_three, [block, (88, LANES), (8, LANES)], [v0, v1, both, *history], [ext], work
+        side_three, [block, (104, LANES), (8, LANES)], [v0, v1, both, *history], [ext], work
     )
     (v2,) = advance(-2.0 / SHIFT, inner, halo, ends)
     halo, ends = exchange(v2)

time: 74 us -> 74 us (level)
  blocking collectives: 18.5 us -> 19.8 us
  Pallas kernels: 16.7 us -> 15.4 us
    ppermute x4, starting transfers between devices: 3.52 us -> 4.95 us  [z_halo(): lax.ppermute(face_b, 'gz', swap('gz', 1))]
    all_to_all x1, blocking collectives: 18.5 us -> 19.8 us  [on_device(): lax.all_to_all(outgoing.reshape(devices, 1, LANES), ('blk', 'gz'), 0, 0,...]
    pallas_call x22, Pallas kernels: 16.7 us -> 15.4 us  [call(): pl.pallas_call(kernel, out_shape=shapes, in_specs=[pl.BlockSpec(memory_sp...]
  transfers between devices with their start and end apart: 22 -> 22, of which waited for: 5 -> 5; matrix products, arithmetic and copies ran while one was open for 0% -> 0% of each run, Pallas kernels for 19% -> 17%
where the time goes in v10:
time: 74 us; the launch traced here: 73.8 us
  starting transfers between devices  32.8 us (44%)
  blocking collectives  19.8 us (27%)
  Pallas kernels  15.4 us (21%)
  waiting for transfers between devices  4.76 us (6%)
  between operations  1.11 us (2%)
    all_to_all x1, blocking collectives, on_device(): lax.all_to_all(outgoing.reshape(devices, 1, LANES), ('blk', 'gz'), 0, 0,...  19.8 us
    ppermute x4, starting transfers between devices, x_halo(): return (lax.ppermute(block, 'blk', swap('blk', 0)), far)  16.7 us
    pallas_call x22, Pallas kernels, call(): pl.pallas_call(kernel, out_shape=shapes, in_specs=[pl.BlockSpec(memory_sp...  15.4 us
    ppermute x4, starting transfers between devices, z_halo(): lax.ppermute(face_b, 'gz', swap('gz', 1))  4.95 us
    ppermute x1, starting transfers between devices, on_device(): near = lax.ppermute(to_near, 'blk', swap('blk', 0))  3.25 us
    ppermute x4, waiting for transfers between devices, z_halo(): lax.ppermute(face_b, 'gz', swap('gz', 1))  3.24 us
    ppermute x4, starting transfers between devices, x_halo(): far = lax.ppermute(block, 'blk', swap('blk', 1))  2.97 us
    ppermute x4, starting transfers between devices, z_halo(): lax.ppermute(face_a, 'gz', swap('gz', 0))  2.62 us
  transfers between devices with their start and end apart: 22, of which 5 were waited for; matrix products, arithmetic and copies ran while one was open for 0% of the time, Pallas kernels for 17%

profile of v10, /device:TPU:1, one launch (start us, length us, event | category | flops | bytes accessed | tf_op | source)
XLA Modules:
  0.0 73.8 jit_solution(4509338696494053722)
XLA Ops:
  0.7 2.7 %collective-permute-start.3 = (f32[6,64,128]{2,1,0:T(8,128)}, f32[6,64,128]{2,1,0:T(8,128)S(1)}, u32[]{:S(2)}, u32[]{:S(2)}) collective-permute-start(f32[6,64,128]{2,1,0:T(8,128)} %hartree.1), channel_id=1, source_target_pairs={{0,252},{4,8},{8,4},{12,16},{16,12},{20,24},{24,20},{28,32},{32,28... | collective-permute-start | bytes 589832 | tf_op jit(solution)/shard_map/ppermute | solution.py:714
  3.4 6.4 %collective-permute-start.2 = (f32[6,64,128]{2,1,0:T(8,128)}, f32[6,64,128]{2,1,0:T(8,128)S(1)}, u32[]{:S(2)}, u32[]{:S(2)}) collective-permute-start(f32[6,64,128]{2,1,0:T(8,128)} %hartree.1), channel_id=1, source_target_pairs={{0,4},{4,0},{8,12},{12,8},{16,20},{20,16},{24,28},{28,24},{32,36},... | collective-permute-start | bytes 589832 | tf_op jit(solution)/shard_map/ppermute | solution.py:715
  9.7 1.3 %shard_map.77 = (f32[12,64,128]{2,1,0:T(8,128)S(1)}, f32[6,64,128]{2,1,0:T(8,128)S(1)}, f32[48,128]{1,0:T(8,128)S(1)}, f32[48,128]{1,0:T(8,128)S(1)}) custom-call(f32[6,64,128]{2,1,0:T(8,128)} %hartree.1, f32[6,64,128]{2,1,0:T(8,128)} %density.1, f32[6,64,128]{2,1,0:T(8,128)} %charge.1), custom_call_target="tpu_custom_call" | custom-call | bytes 1228800 | tf_op jit(solution)/shard_map/pallas_call | solution.py:688
  11.0 1.4 %collective-permute-start = (f32[48,128]{1,0:T(8,128)S(1)}, f32[48,128]{1,0:T(8,128)S(1)}, u32[]{:S(2)}, u32[]{:S(2)}) collective-permute-start(f32[48,128]{1,0:T(8,128)S(1)} %get-tuple-element.34), channel_id=1, source_target_pairs={{0,1},{1,0},{2,3},{3,2},{4,5},{5,4},{6,7},{7,6},{8,9},{9,8},{10,11... | collective-permute-start | bytes 73736 | tf_op jit(solution)/shard_map/ppermute | solution.py:719
  12.4 1.9 %collective-permute-start.1 = (f32[48,128]{1,0:T(8,128)S(1)}, f32[48,128]{1,0:T(8,128)S(1)}, u32[]{:S(2)}, u32[]{:S(2)}) collective-permute-start(f32[48,128]{1,0:T(8,128)S(1)} %get-tuple-element.35), channel_id=1, source_target_pairs={{0,3},{1,2},{2,1},{3,0},{4,7},{5,6},{6,5},{7,4},{8,11},{9,10},{10,... | collective-permute-start | bytes 73736 | tf_op jit(solution)/shard_map/ppermute | solution.py:719
  14.3 0.7 shard_map.78.inner
  15.0 1.3 %collective-permute-done.1.z_second = f32[48,128]{1,0:T(8,128)S(1)} collective-permute-done((f32[48,128]{1,0:T(8,128)S(1)}, f32[48,128]{1,0:T(8,128)S(1)}, u32[]{:S(2)}, u32[]{:S(2)}) %collective-permute-start.1) | collective-permute-done | bytes 24608 | tf_op jit(solution)/shard_map/ppermute | solution.py:719
  16.3 0.3 shard_map.79.inner
  16.6 1.6 %collective-permute-start.4 = (f32[6,64,128]{2,1,0:T(8,128)S(1)}, f32[6,64,128]{2,1,0:T(8,128)S(1)}, u32[]{:S(2)}, u32[]{:S(2)}) collective-permute-start(f32[6,64,128]{2,1,0:T(8,128)S(1)} %copy-done.3), channel_id=1, source_target_pairs={{0,4},{4,0},{8,12},{12,8},{16,20},{20,16},{24,28},{28,24},{32,36},... | collective-permute-start | bytes 589832 | tf_op jit(solution)/shard_map/ppermute | solution.py:760
  18.1 0.1 shard_map.80.vector.block.prior.v0
  18.3 0.1 collective-permute-start.9
  18.4 3.0 %collective-permute-start.8 = (f32[6,64,128]{2,1,0:T(8,128)S(1)}, f32[6,64,128]{2,1,0:T(8,128)S(1)}, u32[]{:S(2)}, u32[]{:S(2)}) collective-permute-start(f32[6,64,128]{2,1,0:T(8,128)S(1)} %shard_map.80.vector.block.prior.v0), channel_id=1, source_target_pairs={{0,4},{4,0},{8,12},{12,8},{16,20},{20,16},{24,28},{28,24},{32,36},... | collective-permute-start | bytes 589832 | tf_op jit(solution)/shard_map/ppermute | solution.py:715
  21.3 0.2 shard_map.82
  21.5 0.5 collective-permute-start.6
  22.0 0.5 collective-permute-start.7
  22.5 2.1 %shard_map.81 = (f32[6,64,128]{2,1,0:T(8,128)S(1)}, f32[6,64,128]{2,1,0:T(8,128)S(1)}, f32[24,128]{1,0:T(8,128)S(1)}, f32[8,128]{1,0:T(8,128)S(1)}) custom-call(f32[6,64,128]{2,1,0:T(8,128)S(1)} %shard_map.80.vector.block.prior.v0, f32[12,64,128]{2,1,0:T(8,128)S(1)} %get-tuple-element.32.both, f32[6,64,128]{2,1,0:T(8,128)S(1)} %collective-permute-done.4.near, ...), custom_call_target="tpu_custom_call" | custom-call | flops 14745600 | bytes 3211264 | tf_op jit(solution)/shard_map/pallas_call | solution.py:688
  24.6 1.4 %collective-permute-done.7.z_second = f32[24,128]{1,0:T(8,128)S(1)} collective-permute-done((f32[24,128]{1,0:T(8,128)S(1)}, f32[24,128]{1,0:T(8,128)S(1)}, u32[]{:S(2)}, u32[]{:S(2)}) %collective-permute-start.7) | collective-permute-done | bytes 12320 | tf_op jit(solution)/shard_map/ppermute | solution.py:719
  26.0 0.3 shard_map.83.inner
  26.3 0.1 shard_map.84.vector.block.prior.v1
  26.5 0.1 collective-permute-start.13
  26.6 3.4 %collective-permute-start.12 = (f32[6,64,128]{2,1,0:T(8,128)S(1)}, f32[6,64,128]{2,1,0:T(8,128)S(1)}, u32[]{:S(2)}, u32[]{:S(2)}) collective-permute-start(f32[6,64,128]{2,1,0:T(8,128)S(1)} %shard_map.84.vector.block.prior.v1), channel_id=1, source_target_pairs={{0,4},{4,0},{8,12},{12,8},{16,20},{20,16},{24,28},{28,24},{32,36},... | collective-permute-start | bytes 589832 | tf_op jit(solution)/shard_map/ppermute | solution.py:715
  30.0 0.2 shard_map.86
  30.1 0.5 collective-permute-start.10
  30.6 0.7 collective-permute-start.11
  31.3 2.5 %shard_map.85 = (f32[6,64,128]{2,1,0:T(8,128)S(1)}, f32[104,128]{1,0:T(8,128)S(1)}, f32[8,128]{1,0:T(8,128)S(1)}) custom-call(f32[6,64,128]{2,1,0:T(8,128)S(1)} %shard_map.80.vector.block.prior.v0, f32[6,64,128]{2,1,0:T(8,128)S(1)} %shard_map.84.vector.block.prior.v1, f32[12,64,128]{2,1,0:T(8,128)S(1)} %get-tuple-element.32.both, ...), custom_call_target="tpu_custom_call" | custom-call | flops 14745600 | bytes 4186112 | tf_op jit(solution)/shard_map/pallas_call | solution.py:688
  33.8 0.5 collective-permute-done.11.z_second
  34.4 0.3 shard_map.87.inner
  34.7 0.1 shard_map.88.vector.block.prior.v2
  34.9 3.9 %collective-permute-start.16 = (f32[6,64,128]{2,1,0:T(8,128)S(1)}, f32[6,64,128]{2,1,0:T(8,128)S(1)}, u32[]{:S(2)}, u32[]{:S(2)}) collective-permute-start(f32[6,64,128]{2,1,0:T(8,128)S(1)} %shard_map.88.vector.block.prior.v2), channel_id=1, source_target_pairs={{0,4},{4,0},{8,12},{12,8},{16,20},{20,16},{24,28},{28,24},{32,36},... | collective-permute-start | bytes 589832 | tf_op jit(solution)/shard_map/ppermute | solution.py:715
  38.8 0.2 shard_map.90
  39.0 0.3 collective-permute-start.14
  39.3 1.9 %collective-permute-start.15 = (f32[24,128]{1,0:T(8,128)S(1)}, f32[24,128]{1,0:T(8,128)S(1)}, u32[]{:S(2)}, u32[]{:S(2)}) collective-permute-start(f32[24,128]{1,0:T(8,128)S(1)} %get-tuple-element.47), channel_id=1, source_target_pairs={{0,3},{1,2},{2,1},{3,0},{4,7},{5,6},{6,5},{7,4},{8,11},{9,10},{10,... | collective-permute-start | bytes 36872 | tf_op jit(solution)/shard_map/ppermute | solution.py:719
  41.2 2.5 %shard_map.89 = (f32[6,64,128]{2,1,0:T(8,128)S(1)}, f32[112,128]{1,0:T(8,128)S(1)}, f32[8,128]{1,0:T(8,128)S(1)}) custom-call(f32[6,64,128]{2,1,0:T(8,128)S(1)} %shard_map.84.vector.block.prior.v1, f32[6,64,128]{2,1,0:T(8,128)S(1)} %shard_map.88.vector.block.prior.v2, f32[12,64,128]{2,1,0:T(8,128)S(1)} %get-tuple-element.32.both, ...), custom_call_target="tpu_custom_call" | custom-call | flops 14745600 | bytes 4386816 | tf_op jit(solution)/shard_map/pallas_call | solution.py:688
  43.7 0.3 shard_map.91.inner
  44.0 0.1 shard_map.92
  44.1 0.1 collective-permute-start.18
  44.2 3.3 %collective-permute-start.19 = (f32[6,32,128]{2,1,0:T(8,128)S(1)}, f32[6,32,128]{2,1,0:T(8,128)S(1)}, u32[]{:S(2)}, u32[]{:S(2)}) collective-permute-start(f32[6,32,128]{2,1,0:T(8,128)S(1)} %get-tuple-element.50), channel_id=1, source_target_pairs={{0,4},{4,0},{8,12},{12,8},{16,20},{20,16},{24,28},{28,24},{32,36},... | collective-permute-start | bytes 294920 | tf_op jit(solution)/shard_map/ppermute | solution.py:782
  47.5 0.1 shard_map.93
  47.6 0.3 collective-permute-start.20
  47.8 1.0 %shard_map.94 = (f32[1,128]{1,0:T(1,128)S(1)}, f32[1,128]{1,0:T(1,128)S(1)}) custom-call(f32[6,64,128]{2,1,0:T(8,128)S(1)} %shard_map.88.vector.block.prior.v2, f32[6,64,128]{2,1,0:T(8,128)S(1)} %get-tuple-element.58.block.vector.own.v3, f32[12,64,128]{2,1,0:T(8,128)S(1)} %get-tuple-element.32.both, f32[8,6,64,128]{3,2,1,0:T(8,128)S(1)} %copy-done, ...), custom_call_target="tpu_custom_call" | custom-call | flops 14745600 | bytes 4068352 | tf_op jit(solution)/shard_map/pallas_call | solution.py:688
  48.8 0.4 collective-permute-start.21
  49.2 0.7 %shard_map.95.inner = f32[8,128]{1,0:T(8,128)S(1)} custom-call(f32[6,64,128]{2,1,0:T(8,128)S(1)} %get-tuple-element.58.block.vector.own.v3), custom_call_target="tpu_custom_call" | custom-call | flops 14745600 | bytes 200704 | tf_op jit(solution)/shard_map/pallas_call | solution.py:688
  49.9 0.1 collective-permute-done.21.taken
  50.0 1.4 %collective-permute-done.20.z_left = f32[24,128]{1,0:T(8,128)S(1)} collective-permute-done((f32[24,128]{1,0:T(8,128)S(1)}, f32[24,128]{1,0:T(8,128)S(1)}, u32[]{:S(2)}, u32[]{:S(2)}) %collective-permute-start.20) | collective-permute-done | bytes 12320 | tf_op jit(solution)/shard_map/ppermute | solution.py:784
  51.4 0.2 shard_map.96
  51.7 0.6 shard_map.97
  52.3 19.8 %all_to_all.5 = f32[256,1,128]{2,1,0:T(1,128)S(1)} all-to-all(f32[256,1,128]{2,1,0:T(1,128)S(1)} %bitcast.5), channel_id=1, replica_groups=mesh['blk'=64,'gz'=4] {'blk','gz'}, dimensions={0} | all-to-all | bytes 262144 | tf_op jit(solution)/shard_map/all_to_all | solution.py:797
  72.1 1.6 %shard_map.98 = (f32[6,64,128]{2,1,0:T(8,128)}, f32[6,64,128]{2,1,0:T(8,128)}) custom-call(f32[256,128]{1,0:T(8,128)S(1)} %bitcast.4, f32[12,64,128]{2,1,0:T(8,128)S(1)} %get-tuple-element.32.both, f32[6,64,128]{2,1,0:T(8,128)S(1)} %get-tuple-element.44.grad, f32[6,64,128]{2,1,0:T(8,128)S(1)} %shard_map.80.vector.block.prior.v0, ...), custom_call_target="tpu_custom_call" | custom-call | flops 14745600 | bytes 5046272 | tf_op jit(solution)/shard_map/pallas_call | solution.py:688
  (27 shorter events, 0.2 us)
Async XLA Ops:
  0.6 15.9 %copy-start.3 = (f32[6,64,128]{2,1,0:T(8,128)S(1)}, f32[6,64,128]{2,1,0:T(8,128)}, u32[]{:S(2)}) copy-start(f32[6,64,128]{2,1,0:T(8,128)} %density.1) | copy-start | bytes 589828
  0.6 21.9 %copy-start = (f32[8,6,64,128]{3,2,1,0:T(8,128)S(1)}, f32[8,6,64,128]{3,2,1,0:T(8,128)}, u32[]{:S(2)}) copy-start(f32[8,6,64,128]{3,2,1,0:T(8,128)} %steps.9) | copy-start | bytes 4718596
  0.7 21.8 %copy-start.2 = (f32[6,64,128]{2,1,0:T(8,128)S(1)}, f32[6,64,128]{2,1,0:T(8,128)}, u32[]{:S(2)}) copy-start(f32[6,64,128]{2,1,0:T(8,128)} %potential.1) | copy-start | bytes 589828
  0.7 17.5 %collective-permute-start.3 = (f32[6,64,128]{2,1,0:T(8,128)}, f32[6,64,128]{2,1,0:T(8,128)S(1)}, u32[]{:S(2)}, u32[]{:S(2)}) collective-permute-start(f32[6,64,128]{2,1,0:T(8,128)} %hartree.1), channel_id=1, source_target_pairs={{0,252},{4,8},{8,4},{12,16},{16,12},{20,24},{24,20},{28,32},{32,28... | collective-permute-start | bytes 589832 | tf_op jit(solution)/shard_map/ppermute | solution.py:714
  3.4 14.8 %collective-permute-start.2 = (f32[6,64,128]{2,1,0:T(8,128)}, f32[6,64,128]{2,1,0:T(8,128)S(1)}, u32[]{:S(2)}, u32[]{:S(2)}) collective-permute-start(f32[6,64,128]{2,1,0:T(8,128)} %hartree.1), channel_id=1, source_target_pairs={{0,4},{4,0},{8,12},{12,8},{16,20},{20,16},{24,28},{28,24},{32,36},... | collective-permute-start | bytes 589832 | tf_op jit(solution)/shard_map/ppermute | solution.py:715
  11.0 4.0 %collective-permute-start = (f32[48,128]{1,0:T(8,128)S(1)}, f32[48,128]{1,0:T(8,128)S(1)}, u32[]{:S(2)}, u32[]{:S(2)}) collective-permute-start(f32[48,128]{1,0:T(8,128)S(1)} %get-tuple-element.34), channel_id=1, source_target_pairs={{0,1},{1,0},{2,3},{3,2},{4,5},{5,4},{6,7},{7,6},{8,9},{9,8},{10,11... | collective-permute-start | bytes 73736 | tf_op jit(solution)/shard_map/ppermute | solution.py:719
  12.4 3.9 %collective-permute-start.1 = (f32[48,128]{1,0:T(8,128)S(1)}, f32[48,128]{1,0:T(8,128)S(1)}, u32[]{:S(2)}, u32[]{:S(2)}) collective-permute-start(f32[48,128]{1,0:T(8,128)S(1)} %get-tuple-element.35), channel_id=1, source_target_pairs={{0,3},{1,2},{2,1},{3,0},{4,7},{5,6},{6,5},{7,4},{8,11},{9,10},{10,... | collective-permute-start | bytes 73736 | tf_op jit(solution)/shard_map/ppermute | solution.py:719
  14.3 7.7 %collective-permute-start.5 = (f32[6,64,128]{2,1,0:T(8,128)}, f32[6,64,128]{2,1,0:T(8,128)S(1)}, u32[]{:S(2)}, u32[]{:S(2)}) collective-permute-start(f32[6,64,128]{2,1,0:T(8,128)} %density.1), channel_id=1, source_target_pairs={{0,252},{4,8},{8,4},{12,16},{16,12},{20,24},{24,20},{28,32},{32,28... | collective-permute-start | bytes 589832 | tf_op jit(solution)/shard_map/ppermute | solution.py:758
  16.6 5.9 %collective-permute-start.4 = (f32[6,64,128]{2,1,0:T(8,128)S(1)}, f32[6,64,128]{2,1,0:T(8,128)S(1)}, u32[]{:S(2)}, u32[]{:S(2)}) collective-permute-start(f32[6,64,128]{2,1,0:T(8,128)S(1)} %copy-done.3), channel_id=1, source_target_pairs={{0,4},{4,0},{8,12},{12,8},{16,20},{20,16},{24,28},{28,24},{32,36},... | collective-permute-start | bytes 589832 | tf_op jit(solution)/shard_map/ppermute | solution.py:760
  18.3 8.1 %collective-permute-start.9 = (f32[6,64,128]{2,1,0:T(8,128)S(1)}, f32[6,64,128]{2,1,0:T(8,128)S(1)}, u32[]{:S(2)}, u32[]{:S(2)}) collective-permute-start(f32[6,64,128]{2,1,0:T(8,128)S(1)} %shard_map.80.vector.block.prior.v0), channel_id=1, source_target_pairs={{0,252},{4,8},{8,4},{12,16},{16,12},{20,24},{24,20},{28,32},{32,28... | collective-permute-start | bytes 589832 | tf_op jit(solution)/shard_map/ppermute | solution.py:714
  18.4 8.0 %collective-permute-start.8 = (f32[6,64,128]{2,1,0:T(8,128)S(1)}, f32[6,64,128]{2,1,0:T(8,128)S(1)}, u32[]{:S(2)}, u32[]{:S(2)}) collective-permute-start(f32[6,64,128]{2,1,0:T(8,128)S(1)} %shard_map.80.vector.block.prior.v0), channel_id=1, source_target_pairs={{0,4},{4,0},{8,12},{12,8},{16,20},{20,16},{24,28},{28,24},{32,36},... | collective-permute-start | bytes 589832 | tf_op jit(solution)/shard_map/ppermute | solution.py:715
  21.5 3.1 %collective-permute-start.6 = (f32[24,128]{1,0:T(8,128)S(1)}, f32[24,128]{1,0:T(8,128)S(1)}, u32[]{:S(2)}, u32[]{:S(2)}) collective-permute-start(f32[24,128]{1,0:T(8,128)S(1)} %get-tuple-element.39), channel_id=1, source_target_pairs={{0,1},{1,0},{2,3},{3,2},{4,5},{5,4},{6,7},{7,6},{8,9},{9,8},{10,11... | collective-permute-start | bytes 36872 | tf_op jit(solution)/shard_map/ppermute | solution.py:719
  22.0 9.3 %copy-start.1 = (f32[8,6,64,128]{3,2,1,0:T(8,128)S(1)}, f32[8,6,64,128]{3,2,1,0:T(8,128)}, u32[]{:S(2)}) copy-start(f32[8,6,64,128]{3,2,1,0:T(8,128)} %changes.7) | copy-start | bytes 4718596
  22.0 4.1 %collective-permute-start.7 = (f32[24,128]{1,0:T(8,128)S(1)}, f32[24,128]{1,0:T(8,128)S(1)}, u32[]{:S(2)}, u32[]{:S(2)}) collective-permute-start(f32[24,128]{1,0:T(8,128)S(1)} %get-tuple-element.40), channel_id=1, source_target_pairs={{0,3},{1,2},{2,1},{3,0},{4,7},{5,6},{6,5},{7,4},{8,11},{9,10},{10,... | collective-permute-start | bytes 36872 | tf_op jit(solution)/shard_map/ppermute | solution.py:719
  26.5 8.2 %collective-permute-start.13 = (f32[6,64,128]{2,1,0:T(8,128)S(1)}, f32[6,64,128]{2,1,0:T(8,128)S(1)}, u32[]{:S(2)}, u32[]{:S(2)}) collective-permute-start(f32[6,64,128]{2,1,0:T(8,128)S(1)} %shard_map.84.vector.block.prior.v1), channel_id=1, source_target_pairs={{0,252},{4,8},{8,4},{12,16},{16,12},{20,24},{24,20},{28,32},{32,28... | collective-permute-start | bytes 589832 | tf_op jit(solution)/shard_map/ppermute | solution.py:714
  26.6 8.1 %collective-permute-start.12 = (f32[6,64,128]{2,1,0:T(8,128)S(1)}, f32[6,64,128]{2,1,0:T(8,128)S(1)}, u32[]{:S(2)}, u32[]{:S(2)}) collective-permute-start(f32[6,64,128]{2,1,0:T(8,128)S(1)} %shard_map.84.vector.block.prior.v1), channel_id=1, source_target_pairs={{0,4},{4,0},{8,12},{12,8},{16,20},{20,16},{24,28},{28,24},{32,36},... | collective-permute-start | bytes 589832 | tf_op jit(solution)/shard_map/ppermute | solution.py:715
  30.1 3.7 %collective-permute-start.10 = (f32[24,128]{1,0:T(8,128)S(1)}, f32[24,128]{1,0:T(8,128)S(1)}, u32[]{:S(2)}, u32[]{:S(2)}) collective-permute-start(f32[24,128]{1,0:T(8,128)S(1)} %get-tuple-element.42), channel_id=1, source_target_pairs={{0,1},{1,0},{2,3},{3,2},{4,5},{5,4},{6,7},{7,6},{8,9},{9,8},{10,11... | collective-permute-start | bytes 36872 | tf_op jit(solution)/shard_map/ppermute | solution.py:719
  30.6 3.8 %collective-permute-start.11 = (f32[24,128]{1,0:T(8,128)S(1)}, f32[24,128]{1,0:T(8,128)S(1)}, u32[]{:S(2)}, u32[]{:S(2)}) collective-permute-start(f32[24,128]{1,0:T(8,128)S(1)} %get-tuple-element.43), channel_id=1, source_target_pairs={{0,3},{1,2},{2,1},{3,0},{4,7},{5,6},{6,5},{7,4},{8,11},{9,10},{10,... | collective-permute-start | bytes 36872 | tf_op jit(solution)/shard_map/ppermute | solution.py:719
  34.8 9.2 %collective-permute-start.17 = (f32[6,64,128]{2,1,0:T(8,128)S(1)}, f32[6,64,128]{2,1,0:T(8,128)S(1)}, u32[]{:S(2)}, u32[]{:S(2)}) collective-permute-start(f32[6,64,128]{2,1,0:T(8,128)S(1)} %shard_map.88.vector.block.prior.v2), channel_id=1, source_target_pairs={{0,252},{4,8},{8,4},{12,16},{16,12},{20,24},{24,20},{28,32},{32,28... | collective-permute-start | bytes 589832 | tf_op jit(solution)/shard_map/ppermute | solution.py:714
  34.9 9.1 %collective-permute-start.16 = (f32[6,64,128]{2,1,0:T(8,128)S(1)}, f32[6,64,128]{2,1,0:T(8,128)S(1)}, u32[]{:S(2)}, u32[]{:S(2)}) collective-permute-start(f32[6,64,128]{2,1,0:T(8,128)S(1)} %shard_map.88.vector.block.prior.v2), channel_id=1, source_target_pairs={{0,4},{4,0},{8,12},{12,8},{16,20},{20,16},{24,28},{28,24},{32,36},... | collective-permute-start | bytes 589832 | tf_op jit(solution)/shard_map/ppermute | solution.py:715
  39.0 4.7 %collective-permute-start.14 = (f32[24,128]{1,0:T(8,128)S(1)}, f32[24,128]{1,0:T(8,128)S(1)}, u32[]{:S(2)}, u32[]{:S(2)}) collective-permute-start(f32[24,128]{1,0:T(8,128)S(1)} %get-tuple-element.46), channel_id=1, source_target_pairs={{0,1},{1,0},{2,3},{3,2},{4,5},{5,4},{6,7},{7,6},{8,9},{9,8},{10,11... | collective-permute-start | bytes 36872 | tf_op jit(solution)/shard_map/ppermute | solution.py:719
  39.3 4.4 %collective-permute-start.15 = (f32[24,128]{1,0:T(8,128)S(1)}, f32[24,128]{1,0:T(8,128)S(1)}, u32[]{:S(2)}, u32[]{:S(2)}) collective-permute-start(f32[24,128]{1,0:T(8,128)S(1)} %get-tuple-element.47), channel_id=1, source_target_pairs={{0,3},{1,2},{2,1},{3,0},{4,7},{5,6},{6,5},{7,4},{8,11},{9,10},{10,... | collective-permute-start | bytes 36872 | tf_op jit(solution)/shard_map/ppermute | solution.py:719
  44.1 7.5 %collective-permute-start.18 = (f32[6,32,128]{2,1,0:T(8,128)S(1)}, f32[6,32,128]{2,1,0:T(8,128)S(1)}, u32[]{:S(2)}, u32[]{:S(2)}) collective-permute-start(f32[6,32,128]{2,1,0:T(8,128)S(1)} %get-tuple-element.49), channel_id=1, source_target_pairs={{0,252},{4,8},{8,4},{12,16},{16,12},{20,24},{24,20},{28,32},{32,28... | collective-permute-start | bytes 294920 | tf_op jit(solution)/shard_map/ppermute | solution.py:781
  44.2 7.4 %collective-permute-start.19 = (f32[6,32,128]{2,1,0:T(8,128)S(1)}, f32[6,32,128]{2,1,0:T(8,128)S(1)}, u32[]{:S(2)}, u32[]{:S(2)}) collective-permute-start(f32[6,32,128]{2,1,0:T(8,128)S(1)} %get-tuple-element.50), channel_id=1, source_target_pairs={{0,4},{4,0},{8,12},{12,8},{16,20},{20,16},{24,28},{28,24},{32,36},... | collective-permute-start | bytes 294920 | tf_op jit(solution)/shard_map/ppermute | solution.py:782
  47.6 3.8 %collective-permute-start.20 = (f32[24,128]{1,0:T(8,128)S(1)}, f32[24,128]{1,0:T(8,128)S(1)}, u32[]{:S(2)}, u32[]{:S(2)}) collective-permute-start(f32[24,128]{1,0:T(8,128)S(1)} %shard_map.93), channel_id=1, source_target_pairs={{0,1},{1,2},{2,3},{3,0},{4,5},{5,6},{6,7},{7,4},{8,9},{9,10},{10,1... | collective-permute-start | bytes 36872 | tf_op jit(solution)/shard_map/ppermute | solution.py:784
  48.8 1.2 %collective-permute-start.21 = (f32[1,128]{1,0:T(1,128)S(1)}, f32[1,128]{1,0:T(1,128)S(1)}, u32[]{:S(2)}, u32[]{:S(2)}) collective-permute-start(f32[1,128]{1,0:T(1,128)S(1)} %get-tuple-element.57), channel_id=1, source_target_pairs={{0,4},{4,0},{8,12},{12,8},{16,20},{20,16},{24,28},{28,24},{32,36},... | collective-permute-start | bytes 1544 | tf_op jit(solution)/shard_map/ppermute | solution.py:792

commit v11 on v8

--- a/solution.py
+++ b/solution.py
@@ -401,24 +401,20 @@
     store(rows, 36, field_dots((steps_here,), [density_tile(both)]))
     for copy in copies[FETCHES:]:
         copy.wait()
-    store(rows, 44, gram_dots(steps_here, changes_here, CROSS_PAIRS[:32]))
-
-
-def side_two(vector, both, steps, changes, inner, rows, moments, ext):
+
+
+def side_two(vector, inner, ext):
     inner_basis(vector, None, inner, ext)
-    lifted, rho = lifted_tile(both, vector), density_tile(both)
-    by_step = field_dots((steps,), [lifted], [(rho, lifted)])
-    by_change = field_dots((changes,), [lifted, rho])
-    store(rows, 0, by_step[:8] + by_change[:8] + by_step[8:] + by_change[8:])
-    store_moments([(vector, vector)], moments)
 
 
 def side_three(prior, vector, both, near, far, z_first, z_second, potential, steps, changes, *outs):
     inner, grad, rows, moments, ext = outs
     inner_basis(vector, prior, inner, ext)
-    lifted, rho = lifted_tile(both, vector), density_tile(both)
-    store(rows, 0, field_dots((steps, changes), [lifted], [(rho, lifted)]))
-    store_moments([(prior, vector), (vector, vector)], moments)
+    before, lifted, rho = lifted_tile(both, prior), lifted_tile(both, vector), density_tile(both)
+    values = field_dots((steps, changes), [before, lifted], [(rho, before), (rho, lifted)])
+    store(rows, 0, values[:16] + values[32:33] + values[16:32] + values[33:])
+    store(rows, 34, gram_dots(steps, changes, CROSS_PAIRS[:32]))
+    store_moments([(prior, prior), (prior, vector), (vector, vector)], moments)
     base_gradient(both, near, far, z_first, z_second, potential, grad, ext)
 
 
@@ -426,14 +422,16 @@
     inner_basis(vector, prior, inner, ext)
     lifted, rho = lifted_tile(both, vector), density_tile(both)
     slope = lambda i, b: tile_of(grad, i, b)
-    values = field_dots((steps, changes), [lifted, slope], [(rho, lifted), (rho, slope), (rho, rho)])
-    store(rows, 0, values[:16] + values[32:33] + values[16:32] + values[33:])
-    store(rows, 35, gram_dots(changes, changes, PAIRS))
-    store(rows, 71, gram_dots(steps, changes, CROSS_PAIRS[32:]))
+    by_step = field_dots((steps,), [lifted, slope], [(rho, lifted), (rho, slope), (rho, rho)])
+    by_change = field_dots((changes,), [lifted, slope, rho])
+    values = by_step[:8] + by_change[:8] + by_step[16:17] + by_step[8:16] + by_change[8:16] + by_step[17:]
+    store(rows, 0, values + by_change[16:])
+    store(rows, 43, gram_dots(changes, changes, PAIRS))
+    store(rows, 79, gram_dots(steps, changes, CROSS_PAIRS[32:]))
     store_moments([(prior, vector), (vector, vector)], moments)
 
 
-def side_five(prior, vector, both, steps, changes, r1, r2, r3, r4, m2, m3, m4, kept, given, table, m5):
+def side_five(prior, vector, both, steps, changes, r1, r3, r4, m3, m4, kept, given, table, m5):
     lifted, rho = lifted_tile(both, vector), density_tile(both)
     own = field_dots((steps, changes), [lifted], [(rho, lifted)])
     store_moments([(prior, vector), (vector, vector)], m5)
@@ -448,17 +446,17 @@
             table[at : at + count - before, :] = ref[start + before : start + count, :]
 
     put(ROW_GRAM, r1, 0, 36)
-    put(ROW_GRAM + 36, r4, 35, 36)
-    put(ROW_GRAM + 72, r1, 44, 32)
-    put(ROW_GRAM + 104, r4, 71, 32)
+    put(ROW_GRAM + 36, r4, 43, 36)
+    put(ROW_GRAM + 72, r3, 34, 32)
+    put(ROW_GRAM + 104, r4, 79, 32)
     put(ROW_BASE, r1, 36, 8)
-    put(ROW_BASE + 8, r2, 17, 8)
+    put(ROW_BASE + 8, r4, 35, 8)
     put(ROW_BASE + 16, r4, 17, 18)
-    for n, rows in enumerate((r2, r3, r4)):
-        put(ROW_W + 17 * n, rows, 0, 17)
+    put(ROW_W, r3, 0, 34)
+    put(ROW_W + 34, r4, 0, 17)
     store(table, place(ROW_W + 51), own)
 
-    order = [(m2, 0), (m3, 0), (m3, 1), (m4, 0), (m4, 1), (m5, 0), (m5, 1)]
+    order = [(m3, 0), (m3, 1), (m3, 2), (m4, 0), (m4, 1), (m5, 0), (m5, 1)]
     zero = jnp.zeros((1, LANES), jnp.float32)
     parts = [
         jnp.concatenate([ref[2 * which + low : 2 * which + low + 1, :] for ref, which in order] + [zero], axis=0)
@@ -768,7 +766,7 @@
     stored = hist_steps.shape
     inner, *history, r1 = call(
         side_one,
-        [block, stored, stored, (80, LANES)],
+        [block, stored, stored, (48, LANES)],
         [both, charge, hist_steps, hist_changes],
         [ext, pltpu.SemaphoreType.DMA((2 * FETCHES,))],
         work,
@@ -777,12 +775,12 @@
     (v0,) = advance(1.0, inner, halo, ends)
     halo, ends = exchange(v0)
     density_halo = x_halo(after((sqrt_density,), v0)[0])
-    inner, r2, m2 = call(side_two, [block, (40, LANES), (8, LANES)], [v0, both, *history], [ext], work)
+    (inner,) = call(side_two, [block], [v0], [ext], work)
     (v1,) = advance(-1.0 / SHIFT, inner, halo, ends)
     halo, ends = exchange(v1)
     inner, grad, r3, m3 = call(
         side_three,
-        [block, block, (24, LANES), (8, LANES)],
+        [block, block, (72, LANES), (8, LANES)],
         [v0, v1, both, *density_halo, *density_ends, ion_potential, *history],
         [ext],
         work,
@@ -800,7 +798,7 @@
     kept, given = call(
         side_five,
         [(1, LANES), (1, LANES)],
-        [v2, v3, both, *history, r1, r2, r3, r4, m2, m3, m4],
+        [v2, v3, both, *history, r1, r3, r4, m3, m4],
         [(2 * LANES, LANES), (8, LANES)],
         work,
     )

time: 73.3 us -> 73 us (level)
  starting transfers between devices: 32.7 us -> 34.2 us
  waiting for transfers between devices: 3.19 us -> 2.05 us
    ppermute x4, starting transfers between devices: 5.72 us -> 7.26 us  [z_halo(): lax.ppermute(face_b, 'gz', swap('gz', 1))]
    ppermute x4, waiting for transfers between devices: 1.38 us -> 0.01 us  [z_halo(): lax.ppermute(face_b, 'gz', swap('gz', 1))]
    ppermute x5, starting transfers between devices: 15.5 us -> 16.5 us  [x_halo(): return (lax.ppermute(block, 'blk', swap('blk', 0)), far)]
    ppermute x5, starting transfers between devices: 4.13 us -> 3.3 us  [x_halo(): far = lax.ppermute(block, 'blk', swap('blk', 1))]
  transfers between devices with their start and end apart: 22 -> 22, of which waited for: 4 -> 2; matrix products, arithmetic and copies ran while one was open for 0% -> 0% of each run, Pallas kernels for 20% -> 20%
where the time goes in v11:
time: 73 us; the launch traced here: 72.9 us
  starting transfers between devices  34.2 us (47%)
  blocking collectives  18.6 us (25%)
  Pallas kernels  16.9 us (23%)
  waiting for transfers between devices  2.05 us (3%)
  between operations  1.12 us (2%)
    all_to_all x1, blocking collectives, on_device(): lax.all_to_all(outgoing.reshape(devices, 1, LANES), ('blk', 'gz'), 0, 0,...  18.6 us
    pallas_call x22, Pallas kernels, call(): pl.pallas_call(kernel, out_shape=shapes, in_specs=[pl.BlockSpec(memory_sp...  16.9 us
    ppermute x5, starting transfers between devices, x_halo(): return (lax.ppermute(block, 'blk', swap('blk', 0)), far)  16.5 us
    ppermute x4, starting transfers between devices, z_halo(): lax.ppermute(face_b, 'gz', swap('gz', 1))  7.26 us
    ppermute x1, starting transfers between devices, on_device(): near = lax.ppermute(to_near, 'blk', swap('blk', 0))  3.37 us
    ppermute x5, starting transfers between devices, x_halo(): far = lax.ppermute(block, 'blk', swap('blk', 1))  3.3 us
    ppermute x4, starting transfers between devices, z_halo(): lax.ppermute(face_a, 'gz', swap('gz', 0))  3.29 us
    ppermute x1, waiting for transfers between devices, on_device(): z_left = lax.ppermute(upper, 'gz', ring('gz', 1))  1.83 us
  transfers between devices with their start and end apart: 22, of which 2 were waited for; matrix products, arithmetic and copies ran while one was open for 0% of the time, Pallas kernels for 20%

profile of v11, /device:TPU:1, one launch (start us, length us, event | category | flops | bytes accessed | tf_op | source)
XLA Modules:
  0.0 72.9 jit_solution(4634992519089940922)
XLA Ops:
  0.6 2.7 %collective-permute-start.3 = (f32[6,64,128]{2,1,0:T(8,128)}, f32[6,64,128]{2,1,0:T(8,128)S(1)}, u32[]{:S(2)}, u32[]{:S(2)}) collective-permute-start(f32[6,64,128]{2,1,0:T(8,128)} %hartree.1), channel_id=1, source_target_pairs={{0,252},{4,8},{8,4},{12,16},{16,12},{20,24},{24,20},{28,32},{32,28... | collective-permute-start | bytes 589832 | tf_op jit(solution)/shard_map/ppermute | solution.py:725
  3.3 6.4 %collective-permute-start.2 = (f32[6,64,128]{2,1,0:T(8,128)}, f32[6,64,128]{2,1,0:T(8,128)S(1)}, u32[]{:S(2)}, u32[]{:S(2)}) collective-permute-start(f32[6,64,128]{2,1,0:T(8,128)} %hartree.1), channel_id=1, source_target_pairs={{0,4},{4,0},{8,12},{12,8},{16,20},{20,16},{24,28},{28,24},{32,36},... | collective-permute-start | bytes 589832 | tf_op jit(solution)/shard_map/ppermute | solution.py:726
  9.7 1.3 %shard_map.77 = (f32[12,64,128]{2,1,0:T(8,128)S(1)}, f32[6,64,128]{2,1,0:T(8,128)S(1)}, f32[48,128]{1,0:T(8,128)S(1)}, f32[48,128]{1,0:T(8,128)S(1)}) custom-call(f32[6,64,128]{2,1,0:T(8,128)} %hartree.1, f32[6,64,128]{2,1,0:T(8,128)} %density.1, f32[6,64,128]{2,1,0:T(8,128)} %charge.1), custom_call_target="tpu_custom_call" | custom-call | bytes 1228800 | tf_op jit(solution)/shard_map/pallas_call | solution.py:699
  11.0 1.4 %collective-permute-start = (f32[48,128]{1,0:T(8,128)S(1)}, f32[48,128]{1,0:T(8,128)S(1)}, u32[]{:S(2)}, u32[]{:S(2)}) collective-permute-start(f32[48,128]{1,0:T(8,128)S(1)} %get-tuple-element.35), channel_id=1, source_target_pairs={{0,1},{1,0},{2,3},{3,2},{4,5},{5,4},{6,7},{7,6},{8,9},{9,8},{10,11... | collective-permute-start | bytes 73736 | tf_op jit(solution)/shard_map/ppermute | solution.py:730
  12.4 1.9 %collective-permute-start.1 = (f32[48,128]{1,0:T(8,128)S(1)}, f32[48,128]{1,0:T(8,128)S(1)}, u32[]{:S(2)}, u32[]{:S(2)}) collective-permute-start(f32[48,128]{1,0:T(8,128)S(1)} %get-tuple-element.36), channel_id=1, source_target_pairs={{0,3},{1,2},{2,1},{3,0},{4,7},{5,6},{6,5},{7,4},{8,11},{9,10},{10,... | collective-permute-start | bytes 73736 | tf_op jit(solution)/shard_map/ppermute | solution.py:730
  14.3 2.8 %shard_map.78 = (f32[6,64,128]{2,1,0:T(8,128)S(1)}, f32[8,6,64,128]{3,2,1,0:T(8,128)S(1)}, f32[8,6,64,128]{3,2,1,0:T(8,128)S(1)}, f32[48,128]{1,0:T(8,128)S(1)}) custom-call(f32[12,64,128]{2,1,0:T(8,128)S(1)} %get-tuple-element.32.both, f32[6,64,128]{2,1,0:T(8,128)S(1)} %get-tuple-element.33.charge, f32[8,6,64,128]{3,2,1,0:T(8,128)} %steps.1, ...), custom_call_target="tpu_custom_call" | custom-call | flops 14745600 | bytes 7102464 | tf_op jit(solution)/shard_map/pallas_call | solution.py:699
  17.0 0.0 collective-permute-done.z_first
  17.1 0.0 copy-start
  17.1 0.3 shard_map.79.inner
  17.4 0.1 shard_map.80.vector.block.prior.v0
  17.5 0.1 collective-permute-start.7
  17.6 0.9 %collective-permute-start.6 = (f32[6,64,128]{2,1,0:T(8,128)S(1)}, f32[6,64,128]{2,1,0:T(8,128)S(1)}, u32[]{:S(2)}, u32[]{:S(2)}) collective-permute-start(f32[6,64,128]{2,1,0:T(8,128)S(1)} %shard_map.80.vector.block.prior.v0), channel_id=1, source_target_pairs={{0,4},{4,0},{8,12},{12,8},{16,20},{20,16},{24,28},{28,24},{32,36},... | collective-permute-start | bytes 589832 | tf_op jit(solution)/shard_map/ppermute | solution.py:726
  18.5 0.2 shard_map.82
  18.7 1.4 %collective-permute-start.4 = (f32[24,128]{1,0:T(8,128)S(1)}, f32[24,128]{1,0:T(8,128)S(1)}, u32[]{:S(2)}, u32[]{:S(2)}) collective-permute-start(f32[24,128]{1,0:T(8,128)S(1)} %get-tuple-element.37), channel_id=1, source_target_pairs={{0,1},{1,0},{2,3},{3,2},{4,5},{5,4},{6,7},{7,6},{8,9},{9,8},{10,11... | collective-permute-start | bytes 36872 | tf_op jit(solution)/shard_map/ppermute | solution.py:730
  20.1 1.9 %collective-permute-start.5 = (f32[24,128]{1,0:T(8,128)S(1)}, f32[24,128]{1,0:T(8,128)S(1)}, u32[]{:S(2)}, u32[]{:S(2)}) collective-permute-start(f32[24,128]{1,0:T(8,128)S(1)} %get-tuple-element.38), channel_id=1, source_target_pairs={{0,3},{1,2},{2,1},{3,0},{4,7},{5,6},{6,5},{7,4},{8,11},{9,10},{10,... | collective-permute-start | bytes 36872 | tf_op jit(solution)/shard_map/ppermute | solution.py:730
  22.0 3.6 %collective-permute-start.8 = (f32[6,64,128]{2,1,0:T(8,128)S(1)}, f32[6,64,128]{2,1,0:T(8,128)S(1)}, u32[]{:S(2)}, u32[]{:S(2)}) collective-permute-start(f32[6,64,128]{2,1,0:T(8,128)S(1)} %copy-done.1), channel_id=1, source_target_pairs={{0,4},{4,0},{8,12},{12,8},{16,20},{20,16},{24,28},{28,24},{32,36},... | collective-permute-start | bytes 589832 | tf_op jit(solution)/shard_map/ppermute | solution.py:726
  25.6 0.7 shard_map.81.inner
  26.3 0.3 shard_map.83.inner
  26.6 0.1 shard_map.84.vector.block.prior.v1
  26.7 0.1 collective-permute-start.13
  26.8 2.2 %collective-permute-start.12 = (f32[6,64,128]{2,1,0:T(8,128)S(1)}, f32[6,64,128]{2,1,0:T(8,128)S(1)}, u32[]{:S(2)}, u32[]{:S(2)}) collective-permute-start(f32[6,64,128]{2,1,0:T(8,128)S(1)} %shard_map.84.vector.block.prior.v1), channel_id=1, source_target_pairs={{0,4},{4,0},{8,12},{12,8},{16,20},{20,16},{24,28},{28,24},{32,36},... | collective-permute-start | bytes 589832 | tf_op jit(solution)/shard_map/ppermute | solution.py:726
  29.0 0.2 shard_map.86
  29.2 0.4 collective-permute-start.10
  29.6 1.7 %collective-permute-start.11 = (f32[24,128]{1,0:T(8,128)S(1)}, f32[24,128]{1,0:T(8,128)S(1)}, u32[]{:S(2)}, u32[]{:S(2)}) collective-permute-start(f32[24,128]{1,0:T(8,128)S(1)} %get-tuple-element.44), channel_id=1, source_target_pairs={{0,3},{1,2},{2,1},{3,0},{4,7},{5,6},{6,5},{7,4},{8,11},{9,10},{10,... | collective-permute-start | bytes 36872 | tf_op jit(solution)/shard_map/ppermute | solution.py:730
  31.3 3.1 %shard_map.85 = (f32[6,64,128]{2,1,0:T(8,128)S(1)}, f32[6,64,128]{2,1,0:T(8,128)S(1)}, f32[72,128]{1,0:T(8,128)S(1)}, f32[8,128]{1,0:T(8,128)S(1)}) custom-call(f32[6,64,128]{2,1,0:T(8,128)S(1)} %shard_map.80.vector.block.prior.v0, f32[6,64,128]{2,1,0:T(8,128)S(1)} %shard_map.84.vector.block.prior.v1, f32[12,64,128]{2,1,0:T(8,128)S(1)} %get-tuple-element.32.both, ...), custom_call_target="tpu_custom_call" | custom-call | flops 14745600 | bytes 5005312 | tf_op jit(solution)/shard_map/pallas_call | solution.py:699
  34.4 0.3 shard_map.87.inner
  34.7 0.1 shard_map.88.vector.block.prior.v2
  34.9 0.4 collective-permute-start.17
  35.3 3.4 %collective-permute-start.16 = (f32[6,64,128]{2,1,0:T(8,128)S(1)}, f32[6,64,128]{2,1,0:T(8,128)S(1)}, u32[]{:S(2)}, u32[]{:S(2)}) collective-permute-start(f32[6,64,128]{2,1,0:T(8,128)S(1)} %shard_map.88.vector.block.prior.v2), channel_id=1, source_target_pairs={{0,4},{4,0},{8,12},{12,8},{16,20},{20,16},{24,28},{28,24},{32,36},... | collective-permute-start | bytes 589832 | tf_op jit(solution)/shard_map/ppermute | solution.py:726
  38.7 0.2 shard_map.90
  38.8 0.1 collective-permute-start.14
  38.9 1.8 %collective-permute-start.15 = (f32[24,128]{1,0:T(8,128)S(1)}, f32[24,128]{1,0:T(8,128)S(1)}, u32[]{:S(2)}, u32[]{:S(2)}) collective-permute-start(f32[24,128]{1,0:T(8,128)S(1)} %get-tuple-element.48), channel_id=1, source_target_pairs={{0,3},{1,2},{2,1},{3,0},{4,7},{5,6},{6,5},{7,4},{8,11},{9,10},{10,... | collective-permute-start | bytes 36872 | tf_op jit(solution)/shard_map/ppermute | solution.py:730
  40.7 2.6 %shard_map.89 = (f32[6,64,128]{2,1,0:T(8,128)S(1)}, f32[112,128]{1,0:T(8,128)S(1)}, f32[8,128]{1,0:T(8,128)S(1)}) custom-call(f32[6,64,128]{2,1,0:T(8,128)S(1)} %shard_map.84.vector.block.prior.v1, f32[6,64,128]{2,1,0:T(8,128)S(1)} %shard_map.88.vector.block.prior.v2, f32[12,64,128]{2,1,0:T(8,128)S(1)} %get-tuple-element.32.both, ...), custom_call_target="tpu_custom_call" | custom-call | flops 14745600 | bytes 4386816 | tf_op jit(solution)/shard_map/pallas_call | solution.py:699
  43.4 0.3 shard_map.91.inner
  43.7 0.1 shard_map.92
  43.8 0.1 collective-permute-start.18
  43.9 3.4 %collective-permute-start.19 = (f32[6,32,128]{2,1,0:T(8,128)S(1)}, f32[6,32,128]{2,1,0:T(8,128)S(1)}, u32[]{:S(2)}, u32[]{:S(2)}) collective-permute-start(f32[6,32,128]{2,1,0:T(8,128)S(1)} %get-tuple-element.51), channel_id=1, source_target_pairs={{0,4},{4,0},{8,12},{12,8},{16,20},{20,16},{24,28},{28,24},{32,36},... | collective-permute-start | bytes 294920 | tf_op jit(solution)/shard_map/ppermute | solution.py:795
  47.3 0.1 shard_map.93
  47.4 0.1 collective-permute-start.20
  47.5 1.0 %shard_map.94 = (f32[1,128]{1,0:T(1,128)S(1)}, f32[1,128]{1,0:T(1,128)S(1)}) custom-call(f32[6,64,128]{2,1,0:T(8,128)S(1)} %shard_map.88.vector.block.prior.v2, f32[6,64,128]{2,1,0:T(8,128)S(1)} %get-tuple-element.58.block.vector.own.v3, f32[12,64,128]{2,1,0:T(8,128)S(1)} %get-tuple-element.32.both, f32[8,6,64,128]{3,2,1,0:T(8,128)S(1)} %get-tuple-element.40.steps, ...), custom_call_target="tpu_custom_call" | custom-call | flops 14745600 | bytes 4060160 | tf_op jit(solution)/shard_map/pallas_call | solution.py:699
  48.5 0.3 collective-permute-start.21
  48.8 0.7 %shard_map.95.inner = f32[8,128]{1,0:T(8,128)S(1)} custom-call(f32[6,64,128]{2,1,0:T(8,128)S(1)} %get-tuple-element.58.block.vector.own.v3), custom_call_target="tpu_custom_call" | custom-call | flops 14745600 | bytes 200704 | tf_op jit(solution)/shard_map/pallas_call | solution.py:699
  49.6 0.2 collective-permute-done.21.taken
  49.7 1.8 %collective-permute-done.20.z_left = f32[24,128]{1,0:T(8,128)S(1)} collective-permute-done((f32[24,128]{1,0:T(8,128)S(1)}, f32[24,128]{1,0:T(8,128)S(1)}, u32[]{:S(2)}, u32[]{:S(2)}) %collective-permute-start.20) | collective-permute-done | bytes 12320 | tf_op jit(solution)/shard_map/ppermute | solution.py:797
  51.6 0.2 shard_map.96
  51.8 0.6 shard_map.97
  52.4 18.6 %all_to_all.5 = f32[256,1,128]{2,1,0:T(1,128)S(1)} all-to-all(f32[256,1,128]{2,1,0:T(1,128)S(1)} %bitcast.5), channel_id=1, replica_groups=mesh['blk'=64,'gz'=4] {'blk','gz'}, dimensions={0} | all-to-all | bytes 262144 | tf_op jit(solution)/shard_map/all_to_all | solution.py:810
  71.1 1.6 %shard_map.98 = (f32[6,64,128]{2,1,0:T(8,128)}, f32[6,64,128]{2,1,0:T(8,128)}) custom-call(f32[256,128]{1,0:T(8,128)S(1)} %bitcast.4, f32[12,64,128]{2,1,0:T(8,128)S(1)} %get-tuple-element.32.both, f32[6,64,128]{2,1,0:T(8,128)S(1)} %get-tuple-element.45.grad, f32[6,64,128]{2,1,0:T(8,128)S(1)} %shard_map.80.vector.block.prior.v0, ...), custom_call_target="tpu_custom_call" | custom-call | flops 14745600 | bytes 5046272 | tf_op jit(solution)/shard_map/pallas_call | solution.py:699
  (23 shorter events, 0.1 us)
Async XLA Ops:
  0.6 16.7 %collective-permute-start.3 = (f32[6,64,128]{2,1,0:T(8,128)}, f32[6,64,128]{2,1,0:T(8,128)S(1)}, u32[]{:S(2)}, u32[]{:S(2)}) collective-permute-start(f32[6,64,128]{2,1,0:T(8,128)} %hartree.1), channel_id=1, source_target_pairs={{0,252},{4,8},{8,4},{12,16},{16,12},{20,24},{24,20},{28,32},{32,28... | collective-permute-start | bytes 589832 | tf_op jit(solution)/shard_map/ppermute | solution.py:725
  3.3 14.1 %collective-permute-start.2 = (f32[6,64,128]{2,1,0:T(8,128)}, f32[6,64,128]{2,1,0:T(8,128)S(1)}, u32[]{:S(2)}, u32[]{:S(2)}) collective-permute-start(f32[6,64,128]{2,1,0:T(8,128)} %hartree.1), channel_id=1, source_target_pairs={{0,4},{4,0},{8,12},{12,8},{16,20},{20,16},{24,28},{28,24},{32,36},... | collective-permute-start | bytes 589832 | tf_op jit(solution)/shard_map/ppermute | solution.py:726
  11.0 6.1 %collective-permute-start = (f32[48,128]{1,0:T(8,128)S(1)}, f32[48,128]{1,0:T(8,128)S(1)}, u32[]{:S(2)}, u32[]{:S(2)}) collective-permute-start(f32[48,128]{1,0:T(8,128)S(1)} %get-tuple-element.35), channel_id=1, source_target_pairs={{0,1},{1,0},{2,3},{3,2},{4,5},{5,4},{6,7},{7,6},{8,9},{9,8},{10,11... | collective-permute-start | bytes 73736 | tf_op jit(solution)/shard_map/ppermute | solution.py:730
  12.4 4.7 %collective-permute-start.1 = (f32[48,128]{1,0:T(8,128)S(1)}, f32[48,128]{1,0:T(8,128)S(1)}, u32[]{:S(2)}, u32[]{:S(2)}) collective-permute-start(f32[48,128]{1,0:T(8,128)S(1)} %get-tuple-element.36), channel_id=1, source_target_pairs={{0,3},{1,2},{2,1},{3,0},{4,7},{5,6},{6,5},{7,4},{8,11},{9,10},{10,... | collective-permute-start | bytes 73736 | tf_op jit(solution)/shard_map/ppermute | solution.py:730
  14.3 7.7 %copy-start.1 = (f32[6,64,128]{2,1,0:T(8,128)S(1)}, f32[6,64,128]{2,1,0:T(8,128)}, u32[]{:S(2)}) copy-start(f32[6,64,128]{2,1,0:T(8,128)} %density.1) | copy-start | bytes 589828
  17.1 14.2 %copy-start = (f32[6,64,128]{2,1,0:T(8,128)S(1)}, f32[6,64,128]{2,1,0:T(8,128)}, u32[]{:S(2)}) copy-start(f32[6,64,128]{2,1,0:T(8,128)} %potential.1) | copy-start | bytes 589828
  17.5 9.1 %collective-permute-start.7 = (f32[6,64,128]{2,1,0:T(8,128)S(1)}, f32[6,64,128]{2,1,0:T(8,128)S(1)}, u32[]{:S(2)}, u32[]{:S(2)}) collective-permute-start(f32[6,64,128]{2,1,0:T(8,128)S(1)} %shard_map.80.vector.block.prior.v0), channel_id=1, source_target_pairs={{0,252},{4,8},{8,4},{12,16},{16,12},{20,24},{24,20},{28,32},{32,28... | collective-permute-start | bytes 589832 | tf_op jit(solution)/shard_map/ppermute | solution.py:725
  17.6 9.0 %collective-permute-start.6 = (f32[6,64,128]{2,1,0:T(8,128)S(1)}, f32[6,64,128]{2,1,0:T(8,128)S(1)}, u32[]{:S(2)}, u32[]{:S(2)}) collective-permute-start(f32[6,64,128]{2,1,0:T(8,128)S(1)} %shard_map.80.vector.block.prior.v0), channel_id=1, source_target_pairs={{0,4},{4,0},{8,12},{12,8},{16,20},{20,16},{24,28},{28,24},{32,36},... | collective-permute-start | bytes 589832 | tf_op jit(solution)/shard_map/ppermute | solution.py:726
  18.7 3.3 %collective-permute-start.4 = (f32[24,128]{1,0:T(8,128)S(1)}, f32[24,128]{1,0:T(8,128)S(1)}, u32[]{:S(2)}, u32[]{:S(2)}) collective-permute-start(f32[24,128]{1,0:T(8,128)S(1)} %get-tuple-element.37), channel_id=1, source_target_pairs={{0,1},{1,0},{2,3},{3,2},{4,5},{5,4},{6,7},{7,6},{8,9},{9,8},{10,11... | collective-permute-start | bytes 36872 | tf_op jit(solution)/shard_map/ppermute | solution.py:730
  20.1 6.2 %collective-permute-start.5 = (f32[24,128]{1,0:T(8,128)S(1)}, f32[24,128]{1,0:T(8,128)S(1)}, u32[]{:S(2)}, u32[]{:S(2)}) collective-permute-start(f32[24,128]{1,0:T(8,128)S(1)} %get-tuple-element.38), channel_id=1, source_target_pairs={{0,3},{1,2},{2,1},{3,0},{4,7},{5,6},{6,5},{7,4},{8,11},{9,10},{10,... | collective-permute-start | bytes 36872 | tf_op jit(solution)/shard_map/ppermute | solution.py:730
  22.0 7.6 %collective-permute-start.9 = (f32[6,64,128]{2,1,0:T(8,128)S(1)}, f32[6,64,128]{2,1,0:T(8,128)S(1)}, u32[]{:S(2)}, u32[]{:S(2)}) collective-permute-start(f32[6,64,128]{2,1,0:T(8,128)S(1)} %copy-done.1), channel_id=1, source_target_pairs={{0,252},{4,8},{8,4},{12,16},{16,12},{20,24},{24,20},{28,32},{32,28... | collective-permute-start | bytes 589832 | tf_op jit(solution)/shard_map/ppermute | solution.py:725
  22.0 9.3 %collective-permute-start.8 = (f32[6,64,128]{2,1,0:T(8,128)S(1)}, f32[6,64,128]{2,1,0:T(8,128)S(1)}, u32[]{:S(2)}, u32[]{:S(2)}) collective-permute-start(f32[6,64,128]{2,1,0:T(8,128)S(1)} %copy-done.1), channel_id=1, source_target_pairs={{0,4},{4,0},{8,12},{12,8},{16,20},{20,16},{24,28},{28,24},{32,36},... | collective-permute-start | bytes 589832 | tf_op jit(solution)/shard_map/ppermute | solution.py:726
  26.7 8.0 %collective-permute-start.13 = (f32[6,64,128]{2,1,0:T(8,128)S(1)}, f32[6,64,128]{2,1,0:T(8,128)S(1)}, u32[]{:S(2)}, u32[]{:S(2)}) collective-permute-start(f32[6,64,128]{2,1,0:T(8,128)S(1)} %shard_map.84.vector.block.prior.v1), channel_id=1, source_target_pairs={{0,252},{4,8},{8,4},{12,16},{16,12},{20,24},{24,20},{28,32},{32,28... | collective-permute-start | bytes 589832 | tf_op jit(solution)/shard_map/ppermute | solution.py:725
  26.8 7.9 %collective-permute-start.12 = (f32[6,64,128]{2,1,0:T(8,128)S(1)}, f32[6,64,128]{2,1,0:T(8,128)S(1)}, u32[]{:S(2)}, u32[]{:S(2)}) collective-permute-start(f32[6,64,128]{2,1,0:T(8,128)S(1)} %shard_map.84.vector.block.prior.v1), channel_id=1, source_target_pairs={{0,4},{4,0},{8,12},{12,8},{16,20},{20,16},{24,28},{28,24},{32,36},... | collective-permute-start | bytes 589832 | tf_op jit(solution)/shard_map/ppermute | solution.py:726
  29.2 5.2 %collective-permute-start.10 = (f32[24,128]{1,0:T(8,128)S(1)}, f32[24,128]{1,0:T(8,128)S(1)}, u32[]{:S(2)}, u32[]{:S(2)}) collective-permute-start(f32[24,128]{1,0:T(8,128)S(1)} %get-tuple-element.43), channel_id=1, source_target_pairs={{0,1},{1,0},{2,3},{3,2},{4,5},{5,4},{6,7},{7,6},{8,9},{9,8},{10,11... | collective-permute-start | bytes 36872 | tf_op jit(solution)/shard_map/ppermute | solution.py:730
  29.6 4.8 %collective-permute-start.11 = (f32[24,128]{1,0:T(8,128)S(1)}, f32[24,128]{1,0:T(8,128)S(1)}, u32[]{:S(2)}, u32[]{:S(2)}) collective-permute-start(f32[24,128]{1,0:T(8,128)S(1)} %get-tuple-element.44), channel_id=1, source_target_pairs={{0,3},{1,2},{2,1},{3,0},{4,7},{5,6},{6,5},{7,4},{8,11},{9,10},{10,... | collective-permute-start | bytes 36872 | tf_op jit(solution)/shard_map/ppermute | solution.py:730
  34.9 8.8 %collective-permute-start.17 = (f32[6,64,128]{2,1,0:T(8,128)S(1)}, f32[6,64,128]{2,1,0:T(8,128)S(1)}, u32[]{:S(2)}, u32[]{:S(2)}) collective-permute-start(f32[6,64,128]{2,1,0:T(8,128)S(1)} %shard_map.88.vector.block.prior.v2), channel_id=1, source_target_pairs={{0,252},{4,8},{8,4},{12,16},{16,12},{20,24},{24,20},{28,32},{32,28... | collective-permute-start | bytes 589832 | tf_op jit(solution)/shard_map/ppermute | solution.py:725
  35.3 8.4 %collective-permute-start.16 = (f32[6,64,128]{2,1,0:T(8,128)S(1)}, f32[6,64,128]{2,1,0:T(8,128)S(1)}, u32[]{:S(2)}, u32[]{:S(2)}) collective-permute-start(f32[6,64,128]{2,1,0:T(8,128)S(1)} %shard_map.88.vector.block.prior.v2), channel_id=1, source_target_pairs={{0,4},{4,0},{8,12},{12,8},{16,20},{20,16},{24,28},{28,24},{32,36},... | collective-permute-start | bytes 589832 | tf_op jit(solution)/shard_map/ppermute | solution.py:726
  38.8 4.5 %collective-permute-start.14 = (f32[24,128]{1,0:T(8,128)S(1)}, f32[24,128]{1,0:T(8,128)S(1)}, u32[]{:S(2)}, u32[]{:S(2)}) collective-permute-start(f32[24,128]{1,0:T(8,128)S(1)} %get-tuple-element.47), channel_id=1, source_target_pairs={{0,1},{1,0},{2,3},{3,2},{4,5},{5,4},{6,7},{7,6},{8,9},{9,8},{10,11... | collective-permute-start | bytes 36872 | tf_op jit(solution)/shard_map/ppermute | solution.py:730
  38.9 4.4 %collective-permute-start.15 = (f32[24,128]{1,0:T(8,128)S(1)}, f32[24,128]{1,0:T(8,128)S(1)}, u32[]{:S(2)}, u32[]{:S(2)}) collective-permute-start(f32[24,128]{1,0:T(8,128)S(1)} %get-tuple-element.48), channel_id=1, source_target_pairs={{0,3},{1,2},{2,1},{3,0},{4,7},{5,6},{6,5},{7,4},{8,11},{9,10},{10,... | collective-permute-start | bytes 36872 | tf_op jit(solution)/shard_map/ppermute | solution.py:730
  43.8 7.9 %collective-permute-start.18 = (f32[6,32,128]{2,1,0:T(8,128)S(1)}, f32[6,32,128]{2,1,0:T(8,128)S(1)}, u32[]{:S(2)}, u32[]{:S(2)}) collective-permute-start(f32[6,32,128]{2,1,0:T(8,128)S(1)} %get-tuple-element.50), channel_id=1, source_target_pairs={{0,252},{4,8},{8,4},{12,16},{16,12},{20,24},{24,20},{28,32},{32,28... | collective-permute-start | bytes 294920 | tf_op jit(solution)/shard_map/ppermute | solution.py:794
  43.9 7.9 %collective-permute-start.19 = (f32[6,32,128]{2,1,0:T(8,128)S(1)}, f32[6,32,128]{2,1,0:T(8,128)S(1)}, u32[]{:S(2)}, u32[]{:S(2)}) collective-permute-start(f32[6,32,128]{2,1,0:T(8,128)S(1)} %get-tuple-element.51), channel_id=1, source_target_pairs={{0,4},{4,0},{8,12},{12,8},{16,20},{20,16},{24,28},{28,24},{32,36},... | collective-permute-start | bytes 294920 | tf_op jit(solution)/shard_map/ppermute | solution.py:795
  47.4 4.1 %collective-permute-start.20 = (f32[24,128]{1,0:T(8,128)S(1)}, f32[24,128]{1,0:T(8,128)S(1)}, u32[]{:S(2)}, u32[]{:S(2)}) collective-permute-start(f32[24,128]{1,0:T(8,128)S(1)} %shard_map.93), channel_id=1, source_target_pairs={{0,1},{1,2},{2,3},{3,0},{4,5},{5,6},{6,7},{7,4},{8,9},{9,10},{10,1... | collective-permute-start | bytes 36872 | tf_op jit(solution)/shard_map/ppermute | solution.py:797
  48.5 1.2 %collective-permute-start.21 = (f32[1,128]{1,0:T(1,128)S(1)}, f32[1,128]{1,0:T(1,128)S(1)}, u32[]{:S(2)}, u32[]{:S(2)}) collective-permute-start(f32[1,128]{1,0:T(1,128)S(1)} %get-tuple-element.57), channel_id=1, source_target_pairs={{0,4},{4,0},{8,12},{12,8},{16,20},{20,16},{24,28},{28,24},{32,36},... | collective-permute-start | bytes 1544 | tf_op jit(solution)/shard_map/ppermute | solution.py:805

commit v12 on v11

--- a/solution.py
+++ b/solution.py
@@ -96,21 +96,35 @@
     return lax.broadcasted_iota(jnp.int32, shape, len(shape) - 1)
 
 
-def inner_plane(i, own, ext):
-    values = own[i]
-    rows = values.shape[0]
-    lane = lane_ids((rows, LANES))
-    total = (3.0 * center) * values
+def z_matrix():
+    shape = (LANES, LANES)
+    apart = jnp.abs(lax.broadcasted_iota(jnp.int32, shape, 0) - lax.broadcasted_iota(jnp.int32, shape, 1))
+    matrix = jnp.where(apart == 0, 3.0 * center, 0.0)
     for k, weight in enumerate(coeffs, 1):
-        pair = ext[i, 8 + k : 8 + k + rows, :] + ext[i, 8 - k : 8 - k + rows, :]
-        if i + k < REACH:
-            pair = pair + own[i + k]
-        if i - k >= 0:
-            pair = pair + own[i - k]
-        up = pltpu.roll(jnp.where(lane < k, 0.0, values), LANES - k, 1)
-        down = pltpu.roll(jnp.where(lane >= LANES - k, 0.0, values), k, 1)
-        total = total + weight * (pair + (up + down))
-    return total, values
+        matrix = jnp.where(apart == k, weight, matrix)
+    return matrix
+
+
+def inner_planes(own, ext):
+    fill_ext(own, ext)
+    layers, rows, lanes = own.shape
+    along_z = lax.dot_general(
+        own[...].reshape(layers * rows, lanes),
+        z_matrix(),
+        (((1,), (0,)), ((), ())),
+        precision=lax.Precision.HIGHEST,
+        preferred_element_type=jnp.float32,
+    )
+    for i in range(layers):
+        total = along_z[rows * i : rows * i + rows]
+        for k, weight in enumerate(coeffs, 1):
+            pair = ext[i, 8 + k : 8 + k + rows, :] + ext[i, 8 - k : 8 - k + rows, :]
+            if i + k < layers:
+                pair = pair + own[i + k]
+            if i - k >= 0:
+                pair = pair + own[i - k]
+            total = total + weight * pair
+        yield i, total, own[i]
 
 
 def edge_faces(z_left, z_right):
@@ -257,17 +271,13 @@
 
 def inner_residual(both, charge, out, ext):
     hartree = both.at[pl.ds(0, REACH)]
-    fill_ext(hartree, ext)
-    for i in range(REACH):
-        lap, values = inner_plane(i, hartree, ext)
+    for i, lap, values in inner_planes(hartree, ext):
         rho = both[REACH + i]
         out[i] = source_scale * (rho * rho - charge[i]) - (screen * values - lap)
 
 
 def inner_basis(own, prior, out, ext):
-    fill_ext(own, ext)
-    for i in range(REACH):
-        lap, values = inner_plane(i, own, ext)
+    for i, lap, values in inner_planes(own, ext):
         moved = (screen / SHIFT - 1.0) * values - (1.0 / SHIFT) * lap
         out[i] = moved if prior is None else 2.0 * moved - prior[i]
 
@@ -358,7 +368,6 @@
 def base_gradient(both, near, far, z_first, z_second, potential, grad, ext):
     hartree = both.at[pl.ds(0, REACH)]
     density = both.at[pl.ds(REACH, REACH)]
-    fill_ext(density, ext)
     faces = edge_faces(*by_side(z_first[24:48, :], z_second[24:48, :]))
 
     def body(near_below, far_below):
@@ -366,8 +375,7 @@
             grad[i] = side_plane(i, near, near_below) + side_plane(i, far, far_below) + z_plane(i, faces)
 
     with_sides(body)
-    for i in range(REACH):
-        lap, rho = inner_plane(i, density, ext)
+    for i, lap, rho in inner_planes(density, ext):
         power = jnp.exp(jnp.log(rho) * (4.0 / 3.0))
         grad[i] = 2.0 * rho * (hartree[i] + potential[i] + tf_scale * power) - (lap + grad[i]) * (
             1.0 / (spacing * spacing)
@@ -475,11 +483,9 @@
 
 
 def inner_moment_kernel(vector, inner, ext):
-    fill_ext(vector, ext)
     zero = jnp.zeros((8, LANES), jnp.float32)
     accs = [(zero, zero) for _ in range(2)]
-    for i in range(REACH):
-        lap, values = inner_plane(i, vector, ext)
+    for i, lap, values in inner_planes(vector, ext):
         product = values * ((screen / SHIFT - 1.0) * values - (1.0 / SHIFT) * lap)
         for b in range(8):
             accs[b % 2] = add_tile(accs[b % 2], product[8 * b : 8 * b + 8])

time: 73 us -> 73 us (level)
  Pallas kernels: 16.9 us -> 15.2 us
  starting transfers between devices: 34.2 us -> 35.3 us
    pallas_call x22, Pallas kernels: 16.9 us -> 15.2 us  [call(): pl.pallas_call(kernel, out_shape=shapes, in_specs=[pl.BlockSpec(memory_sp...]
  transfers between devices with their start and end apart: 22 -> 22, of which waited for: 2 -> 3; matrix products, arithmetic and copies ran while one was open for 0% -> 0% of each run, Pallas kernels for 20% -> 17%
where the time goes in v12:
time: 73 us; the launch traced here: 72.9 us
  starting transfers between devices  35.3 us (48%)
  blocking collectives  18.6 us (25%)
  Pallas kernels  15.2 us (21%)
  waiting for transfers between devices  2.65 us (4%)
  between operations  1.12 us (2%)
    all_to_all x1, blocking collectives, on_device(): lax.all_to_all(outgoing.reshape(devices, 1, LANES), ('blk', 'gz'), 0, 0,...  18.6 us
    ppermute x5, starting transfers between devices, x_halo(): return (lax.ppermute(block, 'blk', swap('blk', 0)), far)  17.2 us
    pallas_call x22, Pallas kernels, call(): pl.pallas_call(kernel, out_shape=shapes, in_specs=[pl.BlockSpec(memory_sp...  15.2 us
    ppermute x4, starting transfers between devices, z_halo(): lax.ppermute(face_b, 'gz', swap('gz', 1))  7.11 us
    ppermute x5, starting transfers between devices, x_halo(): far = lax.ppermute(block, 'blk', swap('blk', 1))  3.88 us
    ppermute x1, starting transfers between devices, on_device(): near = lax.ppermute(to_near, 'blk', swap('blk', 0))  3.69 us
    ppermute x4, starting transfers between devices, z_halo(): lax.ppermute(face_a, 'gz', swap('gz', 0))  3.21 us
    ppermute x1, waiting for transfers between devices, on_device(): z_left = lax.ppermute(upper, 'gz', ring('gz', 1))  1.83 us
  transfers between devices with their start and end apart: 22, of which 3 were waited for; matrix products, arithmetic and copies ran while one was open for 0% of the time, Pallas kernels for 17%

profile of v12, /device:TPU:1, one launch (start us, length us, event | category | flops | bytes accessed | tf_op | source)
XLA Modules:
  0.0 72.9 jit_solution(861324134187035932)
XLA Ops:
  0.6 2.7 %collective-permute-start.3 = (f32[6,64,128]{2,1,0:T(8,128)}, f32[6,64,128]{2,1,0:T(8,128)S(1)}, u32[]{:S(2)}, u32[]{:S(2)}) collective-permute-start(f32[6,64,128]{2,1,0:T(8,128)} %hartree.1), channel_id=1, source_target_pairs={{0,252},{4,8},{8,4},{12,16},{16,12},{20,24},{24,20},{28,32},{32,28... | collective-permute-start | bytes 589832 | tf_op jit(solution)/shard_map/ppermute | solution.py:731
  3.3 6.4 %collective-permute-start.2 = (f32[6,64,128]{2,1,0:T(8,128)}, f32[6,64,128]{2,1,0:T(8,128)S(1)}, u32[]{:S(2)}, u32[]{:S(2)}) collective-permute-start(f32[6,64,128]{2,1,0:T(8,128)} %hartree.1), channel_id=1, source_target_pairs={{0,4},{4,0},{8,12},{12,8},{16,20},{20,16},{24,28},{28,24},{32,36},... | collective-permute-start | bytes 589832 | tf_op jit(solution)/shard_map/ppermute | solution.py:732
  9.7 1.3 %shard_map.77 = (f32[12,64,128]{2,1,0:T(8,128)S(1)}, f32[6,64,128]{2,1,0:T(8,128)S(1)}, f32[48,128]{1,0:T(8,128)S(1)}, f32[48,128]{1,0:T(8,128)S(1)}) custom-call(f32[6,64,128]{2,1,0:T(8,128)} %hartree.1, f32[6,64,128]{2,1,0:T(8,128)} %density.1, f32[6,64,128]{2,1,0:T(8,128)} %charge.1), custom_call_target="tpu_custom_call" | custom-call | bytes 1228800 | tf_op jit(solution)/shard_map/pallas_call | solution.py:705
  11.0 1.4 %collective-permute-start = (f32[48,128]{1,0:T(8,128)S(1)}, f32[48,128]{1,0:T(8,128)S(1)}, u32[]{:S(2)}, u32[]{:S(2)}) collective-permute-start(f32[48,128]{1,0:T(8,128)S(1)} %get-tuple-element.35), channel_id=1, source_target_pairs={{0,1},{1,0},{2,3},{3,2},{4,5},{5,4},{6,7},{7,6},{8,9},{9,8},{10,11... | collective-permute-start | bytes 73736 | tf_op jit(solution)/shard_map/ppermute | solution.py:736
  12.4 1.9 %collective-permute-start.1 = (f32[48,128]{1,0:T(8,128)S(1)}, f32[48,128]{1,0:T(8,128)S(1)}, u32[]{:S(2)}, u32[]{:S(2)}) collective-permute-start(f32[48,128]{1,0:T(8,128)S(1)} %get-tuple-element.36), channel_id=1, source_target_pairs={{0,3},{1,2},{2,1},{3,0},{4,7},{5,6},{6,5},{7,4},{8,11},{9,10},{10,... | collective-permute-start | bytes 73736 | tf_op jit(solution)/shard_map/ppermute | solution.py:736
  14.3 2.2 %shard_map.78 = (f32[6,64,128]{2,1,0:T(8,128)S(1)}, f32[8,6,64,128]{3,2,1,0:T(8,128)S(1)}, f32[8,6,64,128]{3,2,1,0:T(8,128)S(1)}, f32[48,128]{1,0:T(8,128)S(1)}) custom-call(f32[12,64,128]{2,1,0:T(8,128)S(1)} %get-tuple-element.32.both, f32[6,64,128]{2,1,0:T(8,128)S(1)} %get-tuple-element.33.charge, f32[8,6,64,128]{3,2,1,0:T(8,128)} %steps.1, ...), custom_call_target="tpu_custom_call" | custom-call | flops 14745600 | bytes 7102464 | tf_op jit(solution)/shard_map/pallas_call | solution.py:705
  16.5 0.0 copy-start
  16.5 0.3 shard_map.79.inner
  16.8 0.1 shard_map.80.vector.block.prior.v0
  16.9 0.1 collective-permute-start.7
  17.0 1.5 %collective-permute-start.6 = (f32[6,64,128]{2,1,0:T(8,128)S(1)}, f32[6,64,128]{2,1,0:T(8,128)S(1)}, u32[]{:S(2)}, u32[]{:S(2)}) collective-permute-start(f32[6,64,128]{2,1,0:T(8,128)S(1)} %shard_map.80.vector.block.prior.v0), channel_id=1, source_target_pairs={{0,4},{4,0},{8,12},{12,8},{16,20},{20,16},{24,28},{28,24},{32,36},... | collective-permute-start | bytes 589832 | tf_op jit(solution)/shard_map/ppermute | solution.py:732
  18.5 0.2 shard_map.82
  18.7 1.4 %collective-permute-start.4 = (f32[24,128]{1,0:T(8,128)S(1)}, f32[24,128]{1,0:T(8,128)S(1)}, u32[]{:S(2)}, u32[]{:S(2)}) collective-permute-start(f32[24,128]{1,0:T(8,128)S(1)} %get-tuple-element.37), channel_id=1, source_target_pairs={{0,1},{1,0},{2,3},{3,2},{4,5},{5,4},{6,7},{7,6},{8,9},{9,8},{10,11... | collective-permute-start | bytes 36872 | tf_op jit(solution)/shard_map/ppermute | solution.py:736
  20.1 1.9 %collective-permute-start.5 = (f32[24,128]{1,0:T(8,128)S(1)}, f32[24,128]{1,0:T(8,128)S(1)}, u32[]{:S(2)}, u32[]{:S(2)}) collective-permute-start(f32[24,128]{1,0:T(8,128)S(1)} %get-tuple-element.38), channel_id=1, source_target_pairs={{0,3},{1,2},{2,1},{3,0},{4,7},{5,6},{6,5},{7,4},{8,11},{9,10},{10,... | collective-permute-start | bytes 36872 | tf_op jit(solution)/shard_map/ppermute | solution.py:736
  22.0 3.6 %collective-permute-start.8 = (f32[6,64,128]{2,1,0:T(8,128)S(1)}, f32[6,64,128]{2,1,0:T(8,128)S(1)}, u32[]{:S(2)}, u32[]{:S(2)}) collective-permute-start(f32[6,64,128]{2,1,0:T(8,128)S(1)} %copy-done.1), channel_id=1, source_target_pairs={{0,4},{4,0},{8,12},{12,8},{16,20},{20,16},{24,28},{28,24},{32,36},... | collective-permute-start | bytes 589832 | tf_op jit(solution)/shard_map/ppermute | solution.py:732
  25.6 0.4 shard_map.81.inner
  26.0 0.3 shard_map.83.inner
  26.3 0.1 shard_map.84.vector.block.prior.v1
  26.5 0.1 collective-permute-start.13
  26.6 2.2 %collective-permute-start.12 = (f32[6,64,128]{2,1,0:T(8,128)S(1)}, f32[6,64,128]{2,1,0:T(8,128)S(1)}, u32[]{:S(2)}, u32[]{:S(2)}) collective-permute-start(f32[6,64,128]{2,1,0:T(8,128)S(1)} %shard_map.84.vector.block.prior.v1), channel_id=1, source_target_pairs={{0,4},{4,0},{8,12},{12,8},{16,20},{20,16},{24,28},{28,24},{32,36},... | collective-permute-start | bytes 589832 | tf_op jit(solution)/shard_map/ppermute | solution.py:732
  28.8 0.2 shard_map.86
  28.9 0.4 collective-permute-start.10
  29.3 1.7 %collective-permute-start.11 = (f32[24,128]{1,0:T(8,128)S(1)}, f32[24,128]{1,0:T(8,128)S(1)}, u32[]{:S(2)}, u32[]{:S(2)}) collective-permute-start(f32[24,128]{1,0:T(8,128)S(1)} %get-tuple-element.44), channel_id=1, source_target_pairs={{0,3},{1,2},{2,1},{3,0},{4,7},{5,6},{6,5},{7,4},{8,11},{9,10},{10,... | collective-permute-start | bytes 36872 | tf_op jit(solution)/shard_map/ppermute | solution.py:736
  31.0 2.7 %shard_map.85 = (f32[6,64,128]{2,1,0:T(8,128)S(1)}, f32[6,64,128]{2,1,0:T(8,128)S(1)}, f32[72,128]{1,0:T(8,128)S(1)}, f32[8,128]{1,0:T(8,128)S(1)}) custom-call(f32[6,64,128]{2,1,0:T(8,128)S(1)} %shard_map.80.vector.block.prior.v0, f32[6,64,128]{2,1,0:T(8,128)S(1)} %shard_map.84.vector.block.prior.v1, f32[12,64,128]{2,1,0:T(8,128)S(1)} %get-tuple-element.32.both, ...), custom_call_target="tpu_custom_call" | custom-call | flops 14745600 | bytes 5005312 | tf_op jit(solution)/shard_map/pallas_call | solution.py:705
  33.8 0.3 shard_map.87.inner
  34.1 0.1 shard_map.88.vector.block.prior.v2
  34.2 1.0 %collective-permute-start.17 = (f32[6,64,128]{2,1,0:T(8,128)S(1)}, f32[6,64,128]{2,1,0:T(8,128)S(1)}, u32[]{:S(2)}, u32[]{:S(2)}) collective-permute-start(f32[6,64,128]{2,1,0:T(8,128)S(1)} %shard_map.88.vector.block.prior.v2), channel_id=1, source_target_pairs={{0,252},{4,8},{8,4},{12,16},{16,12},{20,24},{24,20},{28,32},{32,28... | collective-permute-start | bytes 589832 | tf_op jit(solution)/shard_map/ppermute | solution.py:731
  35.2 3.5 %collective-permute-start.16 = (f32[6,64,128]{2,1,0:T(8,128)S(1)}, f32[6,64,128]{2,1,0:T(8,128)S(1)}, u32[]{:S(2)}, u32[]{:S(2)}) collective-permute-start(f32[6,64,128]{2,1,0:T(8,128)S(1)} %shard_map.88.vector.block.prior.v2), channel_id=1, source_target_pairs={{0,4},{4,0},{8,12},{12,8},{16,20},{20,16},{24,28},{28,24},{32,36},... | collective-permute-start | bytes 589832 | tf_op jit(solution)/shard_map/ppermute | solution.py:732
  38.7 0.2 shard_map.90
  38.9 0.1 collective-permute-start.14
  39.0 1.6 %collective-permute-start.15 = (f32[24,128]{1,0:T(8,128)S(1)}, f32[24,128]{1,0:T(8,128)S(1)}, u32[]{:S(2)}, u32[]{:S(2)}) collective-permute-start(f32[24,128]{1,0:T(8,128)S(1)} %get-tuple-element.48), channel_id=1, source_target_pairs={{0,3},{1,2},{2,1},{3,0},{4,7},{5,6},{6,5},{7,4},{8,11},{9,10},{10,... | collective-permute-start | bytes 36872 | tf_op jit(solution)/shard_map/ppermute | solution.py:736
  40.5 2.4 %shard_map.89 = (f32[6,64,128]{2,1,0:T(8,128)S(1)}, f32[112,128]{1,0:T(8,128)S(1)}, f32[8,128]{1,0:T(8,128)S(1)}) custom-call(f32[6,64,128]{2,1,0:T(8,128)S(1)} %shard_map.84.vector.block.prior.v1, f32[6,64,128]{2,1,0:T(8,128)S(1)} %shard_map.88.vector.block.prior.v2, f32[12,64,128]{2,1,0:T(8,128)S(1)} %get-tuple-element.32.both, ...), custom_call_target="tpu_custom_call" | custom-call | flops 14745600 | bytes 4386816 | tf_op jit(solution)/shard_map/pallas_call | solution.py:705
  42.9 0.2 collective-permute-done.15.z_second
  43.1 0.3 shard_map.91.inner
  43.4 0.1 shard_map.92
  43.5 0.1 collective-permute-start.18
  43.6 3.7 %collective-permute-start.19 = (f32[6,32,128]{2,1,0:T(8,128)S(1)}, f32[6,32,128]{2,1,0:T(8,128)S(1)}, u32[]{:S(2)}, u32[]{:S(2)}) collective-permute-start(f32[6,32,128]{2,1,0:T(8,128)S(1)} %get-tuple-element.51), channel_id=1, source_target_pairs={{0,4},{4,0},{8,12},{12,8},{16,20},{20,16},{24,28},{28,24},{32,36},... | collective-permute-start | bytes 294920 | tf_op jit(solution)/shard_map/ppermute | solution.py:801
  47.3 0.1 shard_map.93
  47.4 0.1 collective-permute-start.20
  47.5 1.0 %shard_map.94 = (f32[1,128]{1,0:T(1,128)S(1)}, f32[1,128]{1,0:T(1,128)S(1)}) custom-call(f32[6,64,128]{2,1,0:T(8,128)S(1)} %shard_map.88.vector.block.prior.v2, f32[6,64,128]{2,1,0:T(8,128)S(1)} %get-tuple-element.58.block.vector.own.v3, f32[12,64,128]{2,1,0:T(8,128)S(1)} %get-tuple-element.32.both, f32[8,6,64,128]{3,2,1,0:T(8,128)S(1)} %get-tuple-element.40.steps, ...), custom_call_target="tpu_custom_call" | custom-call | flops 14745600 | bytes 4060160 | tf_op jit(solution)/shard_map/pallas_call | solution.py:705
  48.5 0.1 collective-permute-start.21
  48.6 0.5 shard_map.95.inner
  49.1 0.6 collective-permute-done.21.taken
  49.7 1.8 %collective-permute-done.20.z_left = f32[24,128]{1,0:T(8,128)S(1)} collective-permute-done((f32[24,128]{1,0:T(8,128)S(1)}, f32[24,128]{1,0:T(8,128)S(1)}, u32[]{:S(2)}, u32[]{:S(2)}) %collective-permute-start.20) | collective-permute-done | bytes 12320 | tf_op jit(solution)/shard_map/ppermute | solution.py:803
  51.6 0.2 shard_map.96
  51.8 0.6 shard_map.97
  52.5 18.6 %all_to_all.5 = f32[256,1,128]{2,1,0:T(1,128)S(1)} all-to-all(f32[256,1,128]{2,1,0:T(1,128)S(1)} %bitcast.5), channel_id=1, replica_groups=mesh['blk'=64,'gz'=4] {'blk','gz'}, dimensions={0} | all-to-all | bytes 262144 | tf_op jit(solution)/shard_map/all_to_all | solution.py:816
  71.1 1.6 %shard_map.98 = (f32[6,64,128]{2,1,0:T(8,128)}, f32[6,64,128]{2,1,0:T(8,128)}) custom-call(f32[256,128]{1,0:T(8,128)S(1)} %bitcast.4, f32[12,64,128]{2,1,0:T(8,128)S(1)} %get-tuple-element.32.both, f32[6,64,128]{2,1,0:T(8,128)S(1)} %get-tuple-element.45.grad, f32[6,64,128]{2,1,0:T(8,128)S(1)} %shard_map.80.vector.block.prior.v0, ...), custom_call_target="tpu_custom_call" | custom-call | flops 14745600 | bytes 5046272 | tf_op jit(solution)/shard_map/pallas_call | solution.py:705
  (23 shorter events, 0.1 us)
Async XLA Ops:
  0.6 16.1 %collective-permute-start.3 = (f32[6,64,128]{2,1,0:T(8,128)}, f32[6,64,128]{2,1,0:T(8,128)S(1)}, u32[]{:S(2)}, u32[]{:S(2)}) collective-permute-start(f32[6,64,128]{2,1,0:T(8,128)} %hartree.1), channel_id=1, source_target_pairs={{0,252},{4,8},{8,4},{12,16},{16,12},{20,24},{24,20},{28,32},{32,28... | collective-permute-start | bytes 589832 | tf_op jit(solution)/shard_map/ppermute | solution.py:731
  3.3 13.5 %collective-permute-start.2 = (f32[6,64,128]{2,1,0:T(8,128)}, f32[6,64,128]{2,1,0:T(8,128)S(1)}, u32[]{:S(2)}, u32[]{:S(2)}) collective-permute-start(f32[6,64,128]{2,1,0:T(8,128)} %hartree.1), channel_id=1, source_target_pairs={{0,4},{4,0},{8,12},{12,8},{16,20},{20,16},{24,28},{28,24},{32,36},... | collective-permute-start | bytes 589832 | tf_op jit(solution)/shard_map/ppermute | solution.py:732
  11.0 5.5 %collective-permute-start = (f32[48,128]{1,0:T(8,128)S(1)}, f32[48,128]{1,0:T(8,128)S(1)}, u32[]{:S(2)}, u32[]{:S(2)}) collective-permute-start(f32[48,128]{1,0:T(8,128)S(1)} %get-tuple-element.35), channel_id=1, source_target_pairs={{0,1},{1,0},{2,3},{3,2},{4,5},{5,4},{6,7},{7,6},{8,9},{9,8},{10,11... | collective-permute-start | bytes 73736 | tf_op jit(solution)/shard_map/ppermute | solution.py:736
  12.4 4.1 %collective-permute-start.1 = (f32[48,128]{1,0:T(8,128)S(1)}, f32[48,128]{1,0:T(8,128)S(1)}, u32[]{:S(2)}, u32[]{:S(2)}) collective-permute-start(f32[48,128]{1,0:T(8,128)S(1)} %get-tuple-element.36), channel_id=1, source_target_pairs={{0,3},{1,2},{2,1},{3,0},{4,7},{5,6},{6,5},{7,4},{8,11},{9,10},{10,... | collective-permute-start | bytes 73736 | tf_op jit(solution)/shard_map/ppermute | solution.py:736
  14.3 7.7 %copy-start.1 = (f32[6,64,128]{2,1,0:T(8,128)S(1)}, f32[6,64,128]{2,1,0:T(8,128)}, u32[]{:S(2)}) copy-start(f32[6,64,128]{2,1,0:T(8,128)} %density.1) | copy-start | bytes 589828
  16.5 14.6 %copy-start = (f32[6,64,128]{2,1,0:T(8,128)S(1)}, f32[6,64,128]{2,1,0:T(8,128)}, u32[]{:S(2)}) copy-start(f32[6,64,128]{2,1,0:T(8,128)} %potential.1) | copy-start | bytes 589828
  16.9 9.4 %collective-permute-start.7 = (f32[6,64,128]{2,1,0:T(8,128)S(1)}, f32[6,64,128]{2,1,0:T(8,128)S(1)}, u32[]{:S(2)}, u32[]{:S(2)}) collective-permute-start(f32[6,64,128]{2,1,0:T(8,128)S(1)} %shard_map.80.vector.block.prior.v0), channel_id=1, source_target_pairs={{0,252},{4,8},{8,4},{12,16},{16,12},{20,24},{24,20},{28,32},{32,28... | collective-permute-start | bytes 589832 | tf_op jit(solution)/shard_map/ppermute | solution.py:731
  17.0 9.3 %collective-permute-start.6 = (f32[6,64,128]{2,1,0:T(8,128)S(1)}, f32[6,64,128]{2,1,0:T(8,128)S(1)}, u32[]{:S(2)}, u32[]{:S(2)}) collective-permute-start(f32[6,64,128]{2,1,0:T(8,128)S(1)} %shard_map.80.vector.block.prior.v0), channel_id=1, source_target_pairs={{0,4},{4,0},{8,12},{12,8},{16,20},{20,16},{24,28},{28,24},{32,36},... | collective-permute-start | bytes 589832 | tf_op jit(solution)/shard_map/ppermute | solution.py:732
  18.7 3.3 %collective-permute-start.4 = (f32[24,128]{1,0:T(8,128)S(1)}, f32[24,128]{1,0:T(8,128)S(1)}, u32[]{:S(2)}, u32[]{:S(2)}) collective-permute-start(f32[24,128]{1,0:T(8,128)S(1)} %get-tuple-element.37), channel_id=1, source_target_pairs={{0,1},{1,0},{2,3},{3,2},{4,5},{5,4},{6,7},{7,6},{8,9},{9,8},{10,11... | collective-permute-start | bytes 36872 | tf_op jit(solution)/shard_map/ppermute | solution.py:736
  20.1 5.9 %collective-permute-start.5 = (f32[24,128]{1,0:T(8,128)S(1)}, f32[24,128]{1,0:T(8,128)S(1)}, u32[]{:S(2)}, u32[]{:S(2)}) collective-permute-start(f32[24,128]{1,0:T(8,128)S(1)} %get-tuple-element.38), channel_id=1, source_target_pairs={{0,3},{1,2},{2,1},{3,0},{4,7},{5,6},{6,5},{7,4},{8,11},{9,10},{10,... | collective-permute-start | bytes 36872 | tf_op jit(solution)/shard_map/ppermute | solution.py:736
  22.0 7.3 %collective-permute-start.9 = (f32[6,64,128]{2,1,0:T(8,128)S(1)}, f32[6,64,128]{2,1,0:T(8,128)S(1)}, u32[]{:S(2)}, u32[]{:S(2)}) collective-permute-start(f32[6,64,128]{2,1,0:T(8,128)S(1)} %copy-done.1), channel_id=1, source_target_pairs={{0,252},{4,8},{8,4},{12,16},{16,12},{20,24},{24,20},{28,32},{32,28... | collective-permute-start | bytes 589832 | tf_op jit(solution)/shard_map/ppermute | solution.py:731
  22.0 9.0 %collective-permute-start.8 = (f32[6,64,128]{2,1,0:T(8,128)S(1)}, f32[6,64,128]{2,1,0:T(8,128)S(1)}, u32[]{:S(2)}, u32[]{:S(2)}) collective-permute-start(f32[6,64,128]{2,1,0:T(8,128)S(1)} %copy-done.1), channel_id=1, source_target_pairs={{0,4},{4,0},{8,12},{12,8},{16,20},{20,16},{24,28},{28,24},{32,36},... | collective-permute-start | bytes 589832 | tf_op jit(solution)/shard_map/ppermute | solution.py:732
  26.5 7.6 %collective-permute-start.13 = (f32[6,64,128]{2,1,0:T(8,128)S(1)}, f32[6,64,128]{2,1,0:T(8,128)S(1)}, u32[]{:S(2)}, u32[]{:S(2)}) collective-permute-start(f32[6,64,128]{2,1,0:T(8,128)S(1)} %shard_map.84.vector.block.prior.v1), channel_id=1, source_target_pairs={{0,252},{4,8},{8,4},{12,16},{16,12},{20,24},{24,20},{28,32},{32,28... | collective-permute-start | bytes 589832 | tf_op jit(solution)/shard_map/ppermute | solution.py:731
  26.6 7.5 %collective-permute-start.12 = (f32[6,64,128]{2,1,0:T(8,128)S(1)}, f32[6,64,128]{2,1,0:T(8,128)S(1)}, u32[]{:S(2)}, u32[]{:S(2)}) collective-permute-start(f32[6,64,128]{2,1,0:T(8,128)S(1)} %shard_map.84.vector.block.prior.v1), channel_id=1, source_target_pairs={{0,4},{4,0},{8,12},{12,8},{16,20},{20,16},{24,28},{28,24},{32,36},... | collective-permute-start | bytes 589832 | tf_op jit(solution)/shard_map/ppermute | solution.py:732
  28.9 4.8 %collective-permute-start.10 = (f32[24,128]{1,0:T(8,128)S(1)}, f32[24,128]{1,0:T(8,128)S(1)}, u32[]{:S(2)}, u32[]{:S(2)}) collective-permute-start(f32[24,128]{1,0:T(8,128)S(1)} %get-tuple-element.43), channel_id=1, source_target_pairs={{0,1},{1,0},{2,3},{3,2},{4,5},{5,4},{6,7},{7,6},{8,9},{9,8},{10,11... | collective-permute-start | bytes 36872 | tf_op jit(solution)/shard_map/ppermute | solution.py:736
  29.3 4.5 %collective-permute-start.11 = (f32[24,128]{1,0:T(8,128)S(1)}, f32[24,128]{1,0:T(8,128)S(1)}, u32[]{:S(2)}, u32[]{:S(2)}) collective-permute-start(f32[24,128]{1,0:T(8,128)S(1)} %get-tuple-element.44), channel_id=1, source_target_pairs={{0,3},{1,2},{2,1},{3,0},{4,7},{5,6},{6,5},{7,4},{8,11},{9,10},{10,... | collective-permute-start | bytes 36872 | tf_op jit(solution)/shard_map/ppermute | solution.py:736
  34.2 9.2 %collective-permute-start.17 = (f32[6,64,128]{2,1,0:T(8,128)S(1)}, f32[6,64,128]{2,1,0:T(8,128)S(1)}, u32[]{:S(2)}, u32[]{:S(2)}) collective-permute-start(f32[6,64,128]{2,1,0:T(8,128)S(1)} %shard_map.88.vector.block.prior.v2), channel_id=1, source_target_pairs={{0,252},{4,8},{8,4},{12,16},{16,12},{20,24},{24,20},{28,32},{32,28... | collective-permute-start | bytes 589832 | tf_op jit(solution)/shard_map/ppermute | solution.py:731
  35.2 8.2 %collective-permute-start.16 = (f32[6,64,128]{2,1,0:T(8,128)S(1)}, f32[6,64,128]{2,1,0:T(8,128)S(1)}, u32[]{:S(2)}, u32[]{:S(2)}) collective-permute-start(f32[6,64,128]{2,1,0:T(8,128)S(1)} %shard_map.88.vector.block.prior.v2), channel_id=1, source_target_pairs={{0,4},{4,0},{8,12},{12,8},{16,20},{20,16},{24,28},{28,24},{32,36},... | collective-permute-start | bytes 589832 | tf_op jit(solution)/shard_map/ppermute | solution.py:732
  38.9 4.1 %collective-permute-start.14 = (f32[24,128]{1,0:T(8,128)S(1)}, f32[24,128]{1,0:T(8,128)S(1)}, u32[]{:S(2)}, u32[]{:S(2)}) collective-permute-start(f32[24,128]{1,0:T(8,128)S(1)} %get-tuple-element.47), channel_id=1, source_target_pairs={{0,1},{1,0},{2,3},{3,2},{4,5},{5,4},{6,7},{7,6},{8,9},{9,8},{10,11... | collective-permute-start | bytes 36872 | tf_op jit(solution)/shard_map/ppermute | solution.py:736
  39.0 4.1 %collective-permute-start.15 = (f32[24,128]{1,0:T(8,128)S(1)}, f32[24,128]{1,0:T(8,128)S(1)}, u32[]{:S(2)}, u32[]{:S(2)}) collective-permute-start(f32[24,128]{1,0:T(8,128)S(1)} %get-tuple-element.48), channel_id=1, source_target_pairs={{0,3},{1,2},{2,1},{3,0},{4,7},{5,6},{6,5},{7,4},{8,11},{9,10},{10,... | collective-permute-start | bytes 36872 | tf_op jit(solution)/shard_map/ppermute | solution.py:736
  43.5 8.3 %collective-permute-start.18 = (f32[6,32,128]{2,1,0:T(8,128)S(1)}, f32[6,32,128]{2,1,0:T(8,128)S(1)}, u32[]{:S(2)}, u32[]{:S(2)}) collective-permute-start(f32[6,32,128]{2,1,0:T(8,128)S(1)} %get-tuple-element.50), channel_id=1, source_target_pairs={{0,252},{4,8},{8,4},{12,16},{16,12},{20,24},{24,20},{28,32},{32,28... | collective-permute-start | bytes 294920 | tf_op jit(solution)/shard_map/ppermute | solution.py:800
  43.6 8.2 %collective-permute-start.19 = (f32[6,32,128]{2,1,0:T(8,128)S(1)}, f32[6,32,128]{2,1,0:T(8,128)S(1)}, u32[]{:S(2)}, u32[]{:S(2)}) collective-permute-start(f32[6,32,128]{2,1,0:T(8,128)S(1)} %get-tuple-element.51), channel_id=1, source_target_pairs={{0,4},{4,0},{8,12},{12,8},{16,20},{20,16},{24,28},{28,24},{32,36},... | collective-permute-start | bytes 294920 | tf_op jit(solution)/shard_map/ppermute | solution.py:801
  47.4 4.1 %collective-permute-start.20 = (f32[24,128]{1,0:T(8,128)S(1)}, f32[24,128]{1,0:T(8,128)S(1)}, u32[]{:S(2)}, u32[]{:S(2)}) collective-permute-start(f32[24,128]{1,0:T(8,128)S(1)} %shard_map.93), channel_id=1, source_target_pairs={{0,1},{1,2},{2,3},{3,0},{4,5},{5,6},{6,7},{7,4},{8,9},{9,10},{10,1... | collective-permute-start | bytes 36872 | tf_op jit(solution)/shard_map/ppermute | solution.py:803
  48.5 1.2 %collective-permute-start.21 = (f32[1,128]{1,0:T(1,128)S(1)}, f32[1,128]{1,0:T(1,128)S(1)}, u32[]{:S(2)}, u32[]{:S(2)}) collective-permute-start(f32[1,128]{1,0:T(1,128)S(1)} %get-tuple-element.57), channel_id=1, source_target_pairs={{0,4},{4,0},{8,12},{12,8},{16,20},{20,16},{24,28},{28,24},{32,36},... | collective-permute-start | bytes 1544 | tf_op jit(solution)/shard_map/ppermute | solution.py:811

commit v13 on v12

--- a/solution.py
+++ b/solution.py
@@ -409,6 +409,8 @@
     store(rows, 36, field_dots((steps_here,), [density_tile(both)]))
     for copy in copies[FETCHES:]:
         copy.wait()
+    store(rows, 44, gram_dots(changes_here, changes_here, PAIRS))
+    store(rows, 80, gram_dots(steps_here, changes_here, CROSS_PAIRS[:32]))
 
 
 def side_two(vector, inner, ext):
@@ -421,7 +423,6 @@
     before, lifted, rho = lifted_tile(both, prior), lifted_tile(both, vector), density_tile(both)
     values = field_dots((steps, changes), [before, lifted], [(rho, before), (rho, lifted)])
     store(rows, 0, values[:16] + values[32:33] + values[16:32] + values[33:])
-    store(rows, 34, gram_dots(steps, changes, CROSS_PAIRS[:32]))
     store_moments([(prior, prior), (prior, vector), (vector, vector)], moments)
     base_gradient(both, near, far, z_first, z_second, potential, grad, ext)
 
@@ -434,8 +435,7 @@
     by_change = field_dots((changes,), [lifted, slope, rho])
     values = by_step[:8] + by_change[:8] + by_step[16:17] + by_step[8:16] + by_change[8:16] + by_step[17:]
     store(rows, 0, values + by_change[16:])
-    store(rows, 43, gram_dots(changes, changes, PAIRS))
-    store(rows, 79, gram_dots(steps, changes, CROSS_PAIRS[32:]))
+    store(rows, 43, gram_dots(steps, changes, CROSS_PAIRS[32:]))
     store_moments([(prior, vector), (vector, vector)], moments)
 
 
@@ -454,9 +454,9 @@
             table[at : at + count - before, :] = ref[start + before : start + count, :]
 
     put(ROW_GRAM, r1, 0, 36)
-    put(ROW_GRAM + 36, r4, 43, 36)
-    put(ROW_GRAM + 72, r3, 34, 32)
-    put(ROW_GRAM + 104, r4, 79, 32)
+    put(ROW_GRAM + 36, r1, 44, 36)
+    put(ROW_GRAM + 72, r1, 80, 32)
+    put(ROW_GRAM + 104, r4, 43, 32)
     put(ROW_BASE, r1, 36, 8)
     put(ROW_BASE + 8, r4, 35, 8)
     put(ROW_BASE + 16, r4, 17, 18)
@@ -772,7 +772,7 @@
     stored = hist_steps.shape
     inner, *history, r1 = call(
         side_one,
-        [block, stored, stored, (48, LANES)],
+        [block, stored, stored, (112, LANES)],
         [both, charge, hist_steps, hist_changes],
         [ext, pltpu.SemaphoreType.DMA((2 * FETCHES,))],
         work,
@@ -786,7 +786,7 @@
     halo, ends = exchange(v1)
     inner, grad, r3, m3 = call(
         side_three,
-        [block, block, (72, LANES), (8, LANES)],
+        [block, block, (40, LANES), (8, LANES)],
         [v0, v1, both, *density_halo, *density_ends, ion_potential, *history],
         [ext],
         work,
@@ -794,7 +794,7 @@
     (v2,) = advance(-2.0 / SHIFT, inner, halo, ends)
     halo, ends = exchange(v2)
     inner, r4, m4 = call(
-        side_four, [block, (112, LANES), (8, LANES)], [v1, v2, both, grad, *history], [ext], work
+        side_four, [block, (80, LANES), (8, LANES)], [v1, v2, both, grad, *history], [ext], work
     )
     v3, to_near, to_far = advance(-2.0 / SHIFT, inner, halo, ends, last=True)
     far = lax.ppermute(to_far, "blk", swap("blk", 1))

time: 73 us -> 73.5 us (level)
  starting transfers between devices: 35.3 us -> 33.9 us
  waiting for transfers between devices: 2.65 us -> 3.62 us
    ppermute x4, waiting for transfers between devices: 0.18 us -> 1.35 us  [z_halo(): lax.ppermute(face_b, 'gz', swap('gz', 1))]
  transfers between devices with their start and end apart: 22 -> 22, of which waited for: 3 -> 4; matrix products, arithmetic and copies ran while one was open for 0% -> 0% of each run, Pallas kernels for 17% -> 17%
where the time goes in v13:
time: 73.5 us; the launch traced here: 73.3 us
  starting transfers between devices  33.9 us (46%)
  blocking collectives  19.3 us (26%)
  Pallas kernels  15.3 us (21%)
  waiting for transfers between devices  3.62 us (5%)
  between operations  1.1 us (1%)
    all_to_all x1, blocking collectives, on_device(): lax.all_to_all(outgoing.reshape(devices, 1, LANES), ('blk', 'gz'), 0, 0,...  19.3 us
    ppermute x5, starting transfers between devices, x_halo(): return (lax.ppermute(block, 'blk', swap('blk', 0)), far)  16.7 us
    pallas_call x22, Pallas kernels, call(): pl.pallas_call(kernel, out_shape=shapes, in_specs=[pl.BlockSpec(memory_sp...  15.3 us
    ppermute x4, starting transfers between devices, z_halo(): lax.ppermute(face_b, 'gz', swap('gz', 1))  6.57 us
    ppermute x1, starting transfers between devices, on_device(): near = lax.ppermute(to_near, 'blk', swap('blk', 0))  3.69 us
    ppermute x5, starting transfers between devices, x_halo(): far = lax.ppermute(block, 'blk', swap('blk', 1))  3.59 us
    ppermute x4, starting transfers between devices, z_halo(): lax.ppermute(face_a, 'gz', swap('gz', 0))  2.88 us
    ppermute x1, waiting for transfers between devices, on_device(): z_left = lax.ppermute(upper, 'gz', ring('gz', 1))  1.83 us
  transfers between devices with their start and end apart: 22, of which 4 were waited for; matrix products, arithmetic and copies ran while one was open for 0% of the time, Pallas kernels for 17%

profile of v13, /device:TPU:1, one launch (start us, length us, event | category | flops | bytes accessed | tf_op | source)
XLA Modules:
  0.0 73.3 jit_solution(13458557315634424166)
XLA Ops:
  0.6 2.7 %collective-permute-start.3 = (f32[6,64,128]{2,1,0:T(8,128)}, f32[6,64,128]{2,1,0:T(8,128)S(1)}, u32[]{:S(2)}, u32[]{:S(2)}) collective-permute-start(f32[6,64,128]{2,1,0:T(8,128)} %hartree.1), channel_id=1, source_target_pairs={{0,252},{4,8},{8,4},{12,16},{16,12},{20,24},{24,20},{28,32},{32,28... | collective-permute-start | bytes 589832 | tf_op jit(solution)/shard_map/ppermute | solution.py:731
  3.3 6.4 %collective-permute-start.2 = (f32[6,64,128]{2,1,0:T(8,128)}, f32[6,64,128]{2,1,0:T(8,128)S(1)}, u32[]{:S(2)}, u32[]{:S(2)}) collective-permute-start(f32[6,64,128]{2,1,0:T(8,128)} %hartree.1), channel_id=1, source_target_pairs={{0,4},{4,0},{8,12},{12,8},{16,20},{20,16},{24,28},{28,24},{32,36},... | collective-permute-start | bytes 589832 | tf_op jit(solution)/shard_map/ppermute | solution.py:732
  9.7 1.3 %shard_map.77 = (f32[12,64,128]{2,1,0:T(8,128)S(1)}, f32[6,64,128]{2,1,0:T(8,128)S(1)}, f32[48,128]{1,0:T(8,128)S(1)}, f32[48,128]{1,0:T(8,128)S(1)}) custom-call(f32[6,64,128]{2,1,0:T(8,128)} %hartree.1, f32[6,64,128]{2,1,0:T(8,128)} %density.1, f32[6,64,128]{2,1,0:T(8,128)} %charge.1), custom_call_target="tpu_custom_call" | custom-call | bytes 1228800 | tf_op jit(solution)/shard_map/pallas_call | solution.py:705
  11.0 1.4 %collective-permute-start = (f32[48,128]{1,0:T(8,128)S(1)}, f32[48,128]{1,0:T(8,128)S(1)}, u32[]{:S(2)}, u32[]{:S(2)}) collective-permute-start(f32[48,128]{1,0:T(8,128)S(1)} %get-tuple-element.35), channel_id=1, source_target_pairs={{0,1},{1,0},{2,3},{3,2},{4,5},{5,4},{6,7},{7,6},{8,9},{9,8},{10,11... | collective-permute-start | bytes 73736 | tf_op jit(solution)/shard_map/ppermute | solution.py:736
  12.4 1.9 %collective-permute-start.1 = (f32[48,128]{1,0:T(8,128)S(1)}, f32[48,128]{1,0:T(8,128)S(1)}, u32[]{:S(2)}, u32[]{:S(2)}) collective-permute-start(f32[48,128]{1,0:T(8,128)S(1)} %get-tuple-element.36), channel_id=1, source_target_pairs={{0,3},{1,2},{2,1},{3,0},{4,7},{5,6},{6,5},{7,4},{8,11},{9,10},{10,... | collective-permute-start | bytes 73736 | tf_op jit(solution)/shard_map/ppermute | solution.py:736
  14.3 3.2 %shard_map.78 = (f32[6,64,128]{2,1,0:T(8,128)S(1)}, f32[8,6,64,128]{3,2,1,0:T(8,128)S(1)}, f32[8,6,64,128]{3,2,1,0:T(8,128)S(1)}, f32[112,128]{1,0:T(8,128)S(1)}) custom-call(f32[12,64,128]{2,1,0:T(8,128)S(1)} %get-tuple-element.32.both, f32[6,64,128]{2,1,0:T(8,128)S(1)} %get-tuple-element.33.charge, f32[8,6,64,128]{3,2,1,0:T(8,128)} %steps.1, ...), custom_call_target="tpu_custom_call" | custom-call | flops 14745600 | bytes 7135232 | tf_op jit(solution)/shard_map/pallas_call | solution.py:705
  17.6 0.3 shard_map.79.inner
  17.9 0.1 shard_map.80.vector.block.prior.v0
  18.0 0.1 collective-permute-start.7
  18.1 0.9 %collective-permute-start.6 = (f32[6,64,128]{2,1,0:T(8,128)S(1)}, f32[6,64,128]{2,1,0:T(8,128)S(1)}, u32[]{:S(2)}, u32[]{:S(2)}) collective-permute-start(f32[6,64,128]{2,1,0:T(8,128)S(1)} %shard_map.80.vector.block.prior.v0), channel_id=1, source_target_pairs={{0,4},{4,0},{8,12},{12,8},{16,20},{20,16},{24,28},{28,24},{32,36},... | collective-permute-start | bytes 589832 | tf_op jit(solution)/shard_map/ppermute | solution.py:732
  19.0 0.2 shard_map.82
  19.2 0.9 %collective-permute-start.4 = (f32[24,128]{1,0:T(8,128)S(1)}, f32[24,128]{1,0:T(8,128)S(1)}, u32[]{:S(2)}, u32[]{:S(2)}) collective-permute-start(f32[24,128]{1,0:T(8,128)S(1)} %get-tuple-element.37), channel_id=1, source_target_pairs={{0,1},{1,0},{2,3},{3,2},{4,5},{5,4},{6,7},{7,6},{8,9},{9,8},{10,11... | collective-permute-start | bytes 36872 | tf_op jit(solution)/shard_map/ppermute | solution.py:736
  20.1 1.9 %collective-permute-start.5 = (f32[24,128]{1,0:T(8,128)S(1)}, f32[24,128]{1,0:T(8,128)S(1)}, u32[]{:S(2)}, u32[]{:S(2)}) collective-permute-start(f32[24,128]{1,0:T(8,128)S(1)} %get-tuple-element.38), channel_id=1, source_target_pairs={{0,3},{1,2},{2,1},{3,0},{4,7},{5,6},{6,5},{7,4},{8,11},{9,10},{10,... | collective-permute-start | bytes 36872 | tf_op jit(solution)/shard_map/ppermute | solution.py:736
  22.0 3.6 %collective-permute-start.8 = (f32[6,64,128]{2,1,0:T(8,128)S(1)}, f32[6,64,128]{2,1,0:T(8,128)S(1)}, u32[]{:S(2)}, u32[]{:S(2)}) collective-permute-start(f32[6,64,128]{2,1,0:T(8,128)S(1)} %copy-done.1), channel_id=1, source_target_pairs={{0,4},{4,0},{8,12},{12,8},{16,20},{20,16},{24,28},{28,24},{32,36},... | collective-permute-start | bytes 589832 | tf_op jit(solution)/shard_map/ppermute | solution.py:732
  25.6 0.4 shard_map.81.inner
  26.0 0.3 shard_map.83.inner
  26.3 0.1 shard_map.84.vector.block.prior.v1
  26.5 0.1 collective-permute-start.13
  26.6 2.6 %collective-permute-start.12 = (f32[6,64,128]{2,1,0:T(8,128)S(1)}, f32[6,64,128]{2,1,0:T(8,128)S(1)}, u32[]{:S(2)}, u32[]{:S(2)}) collective-permute-start(f32[6,64,128]{2,1,0:T(8,128)S(1)} %shard_map.84.vector.block.prior.v1), channel_id=1, source_target_pairs={{0,4},{4,0},{8,12},{12,8},{16,20},{20,16},{24,28},{28,24},{32,36},... | collective-permute-start | bytes 589832 | tf_op jit(solution)/shard_map/ppermute | solution.py:732
  29.2 0.2 shard_map.86
  29.3 0.5 collective-permute-start.10
  29.8 1.2 %collective-permute-start.11 = (f32[24,128]{1,0:T(8,128)S(1)}, f32[24,128]{1,0:T(8,128)S(1)}, u32[]{:S(2)}, u32[]{:S(2)}) collective-permute-start(f32[24,128]{1,0:T(8,128)S(1)} %get-tuple-element.44), channel_id=1, source_target_pairs={{0,3},{1,2},{2,1},{3,0},{4,7},{5,6},{6,5},{7,4},{8,11},{9,10},{10,... | collective-permute-start | bytes 36872 | tf_op jit(solution)/shard_map/ppermute | solution.py:736
  31.0 2.2 %shard_map.85 = (f32[6,64,128]{2,1,0:T(8,128)S(1)}, f32[6,64,128]{2,1,0:T(8,128)S(1)}, f32[40,128]{1,0:T(8,128)S(1)}, f32[8,128]{1,0:T(8,128)S(1)}) custom-call(f32[6,64,128]{2,1,0:T(8,128)S(1)} %shard_map.80.vector.block.prior.v0, f32[6,64,128]{2,1,0:T(8,128)S(1)} %shard_map.84.vector.block.prior.v1, f32[12,64,128]{2,1,0:T(8,128)S(1)} %get-tuple-element.32.both, ...), custom_call_target="tpu_custom_call" | custom-call | flops 14745600 | bytes 4988928 | tf_op jit(solution)/shard_map/pallas_call | solution.py:705
  33.2 0.6 collective-permute-done.11.z_second
  33.9 0.3 shard_map.87.inner
  34.2 0.3 shard_map.88.vector.block.prior.v2
  34.5 0.7 collective-permute-start.17
  35.2 3.2 %collective-permute-start.16 = (f32[6,64,128]{2,1,0:T(8,128)S(1)}, f32[6,64,128]{2,1,0:T(8,128)S(1)}, u32[]{:S(2)}, u32[]{:S(2)}) collective-permute-start(f32[6,64,128]{2,1,0:T(8,128)S(1)} %shard_map.88.vector.block.prior.v2), channel_id=1, source_target_pairs={{0,4},{4,0},{8,12},{12,8},{16,20},{20,16},{24,28},{28,24},{32,36},... | collective-permute-start | bytes 589832 | tf_op jit(solution)/shard_map/ppermute | solution.py:732
  38.4 0.2 shard_map.90
  38.6 0.1 collective-permute-start.14
  38.7 1.6 %collective-permute-start.15 = (f32[24,128]{1,0:T(8,128)S(1)}, f32[24,128]{1,0:T(8,128)S(1)}, u32[]{:S(2)}, u32[]{:S(2)}) collective-permute-start(f32[24,128]{1,0:T(8,128)S(1)} %get-tuple-element.48), channel_id=1, source_target_pairs={{0,3},{1,2},{2,1},{3,0},{4,7},{5,6},{6,5},{7,4},{8,11},{9,10},{10,... | collective-permute-start | bytes 36872 | tf_op jit(solution)/shard_map/ppermute | solution.py:736
  40.3 1.8 %shard_map.89 = (f32[6,64,128]{2,1,0:T(8,128)S(1)}, f32[80,128]{1,0:T(8,128)S(1)}, f32[8,128]{1,0:T(8,128)S(1)}) custom-call(f32[6,64,128]{2,1,0:T(8,128)S(1)} %shard_map.84.vector.block.prior.v1, f32[6,64,128]{2,1,0:T(8,128)S(1)} %shard_map.88.vector.block.prior.v2, f32[12,64,128]{2,1,0:T(8,128)S(1)} %get-tuple-element.32.both, ...), custom_call_target="tpu_custom_call" | custom-call | flops 14745600 | bytes 4370432 | tf_op jit(solution)/shard_map/pallas_call | solution.py:705
  42.1 0.7 collective-permute-done.15.z_second
  42.8 0.3 shard_map.91.inner
  43.1 0.1 shard_map.92
  43.3 0.1 collective-permute-start.18
  43.4 3.7 %collective-permute-start.19 = (f32[6,32,128]{2,1,0:T(8,128)S(1)}, f32[6,32,128]{2,1,0:T(8,128)S(1)}, u32[]{:S(2)}, u32[]{:S(2)}) collective-permute-start(f32[6,32,128]{2,1,0:T(8,128)S(1)} %get-tuple-element.51), channel_id=1, source_target_pairs={{0,4},{4,0},{8,12},{12,8},{16,20},{20,16},{24,28},{28,24},{32,36},... | collective-permute-start | bytes 294920 | tf_op jit(solution)/shard_map/ppermute | solution.py:801
  47.1 0.1 shard_map.93
  47.2 0.1 collective-permute-start.20
  47.3 1.0 %shard_map.94 = (f32[1,128]{1,0:T(1,128)S(1)}, f32[1,128]{1,0:T(1,128)S(1)}) custom-call(f32[6,64,128]{2,1,0:T(8,128)S(1)} %shard_map.88.vector.block.prior.v2, f32[6,64,128]{2,1,0:T(8,128)S(1)} %get-tuple-element.58.block.vector.own.v3, f32[12,64,128]{2,1,0:T(8,128)S(1)} %get-tuple-element.32.both, f32[8,6,64,128]{3,2,1,0:T(8,128)S(1)} %get-tuple-element.40.steps, ...), custom_call_target="tpu_custom_call" | custom-call | flops 14745600 | bytes 4060160 | tf_op jit(solution)/shard_map/pallas_call | solution.py:705
  48.3 0.3 collective-permute-start.21
  48.6 0.5 shard_map.95.inner
  49.1 0.4 collective-permute-done.21.taken
  49.5 1.8 %collective-permute-done.20.z_left = f32[24,128]{1,0:T(8,128)S(1)} collective-permute-done((f32[24,128]{1,0:T(8,128)S(1)}, f32[24,128]{1,0:T(8,128)S(1)}, u32[]{:S(2)}, u32[]{:S(2)}) %collective-permute-start.20) | collective-permute-done | bytes 12320 | tf_op jit(solution)/shard_map/ppermute | solution.py:803
  51.3 0.2 shard_map.96
  51.6 0.6 shard_map.97
  52.2 19.3 %all_to_all.5 = f32[256,1,128]{2,1,0:T(1,128)S(1)} all-to-all(f32[256,1,128]{2,1,0:T(1,128)S(1)} %bitcast.5), channel_id=1, replica_groups=mesh['blk'=64,'gz'=4] {'blk','gz'}, dimensions={0} | all-to-all | bytes 262144 | tf_op jit(solution)/shard_map/all_to_all | solution.py:816
  71.5 1.6 %shard_map.98 = (f32[6,64,128]{2,1,0:T(8,128)}, f32[6,64,128]{2,1,0:T(8,128)}) custom-call(f32[256,128]{1,0:T(8,128)S(1)} %bitcast.4, f32[12,64,128]{2,1,0:T(8,128)S(1)} %get-tuple-element.32.both, f32[6,64,128]{2,1,0:T(8,128)S(1)} %get-tuple-element.45.grad, f32[6,64,128]{2,1,0:T(8,128)S(1)} %shard_map.80.vector.block.prior.v0, ...), custom_call_target="tpu_custom_call" | custom-call | flops 14745600 | bytes 5046272 | tf_op jit(solution)/shard_map/pallas_call | solution.py:705
  (23 shorter events, 0.1 us)
Async XLA Ops:
  0.6 17.2 %collective-permute-start.3 = (f32[6,64,128]{2,1,0:T(8,128)}, f32[6,64,128]{2,1,0:T(8,128)S(1)}, u32[]{:S(2)}, u32[]{:S(2)}) collective-permute-start(f32[6,64,128]{2,1,0:T(8,128)} %hartree.1), channel_id=1, source_target_pairs={{0,252},{4,8},{8,4},{12,16},{16,12},{20,24},{24,20},{28,32},{32,28... | collective-permute-start | bytes 589832 | tf_op jit(solution)/shard_map/ppermute | solution.py:731
  3.3 14.5 %collective-permute-start.2 = (f32[6,64,128]{2,1,0:T(8,128)}, f32[6,64,128]{2,1,0:T(8,128)S(1)}, u32[]{:S(2)}, u32[]{:S(2)}) collective-permute-start(f32[6,64,128]{2,1,0:T(8,128)} %hartree.1), channel_id=1, source_target_pairs={{0,4},{4,0},{8,12},{12,8},{16,20},{20,16},{24,28},{28,24},{32,36},... | collective-permute-start | bytes 589832 | tf_op jit(solution)/shard_map/ppermute | solution.py:732
  11.0 6.5 %collective-permute-start = (f32[48,128]{1,0:T(8,128)S(1)}, f32[48,128]{1,0:T(8,128)S(1)}, u32[]{:S(2)}, u32[]{:S(2)}) collective-permute-start(f32[48,128]{1,0:T(8,128)S(1)} %get-tuple-element.35), channel_id=1, source_target_pairs={{0,1},{1,0},{2,3},{3,2},{4,5},{5,4},{6,7},{7,6},{8,9},{9,8},{10,11... | collective-permute-start | bytes 73736 | tf_op jit(solution)/shard_map/ppermute | solution.py:736
  12.4 5.1 %collective-permute-start.1 = (f32[48,128]{1,0:T(8,128)S(1)}, f32[48,128]{1,0:T(8,128)S(1)}, u32[]{:S(2)}, u32[]{:S(2)}) collective-permute-start(f32[48,128]{1,0:T(8,128)S(1)} %get-tuple-element.36), channel_id=1, source_target_pairs={{0,3},{1,2},{2,1},{3,0},{4,7},{5,6},{6,5},{7,4},{8,11},{9,10},{10,... | collective-permute-start | bytes 73736 | tf_op jit(solution)/shard_map/ppermute | solution.py:736
  14.3 7.7 %copy-start.1 = (f32[6,64,128]{2,1,0:T(8,128)S(1)}, f32[6,64,128]{2,1,0:T(8,128)}, u32[]{:S(2)}) copy-start(f32[6,64,128]{2,1,0:T(8,128)} %density.1) | copy-start | bytes 589828
  17.5 13.5 %copy-start = (f32[6,64,128]{2,1,0:T(8,128)S(1)}, f32[6,64,128]{2,1,0:T(8,128)}, u32[]{:S(2)}) copy-start(f32[6,64,128]{2,1,0:T(8,128)} %potential.1) | copy-start | bytes 589828
  18.0 8.3 %collective-permute-start.7 = (f32[6,64,128]{2,1,0:T(8,128)S(1)}, f32[6,64,128]{2,1,0:T(8,128)S(1)}, u32[]{:S(2)}, u32[]{:S(2)}) collective-permute-start(f32[6,64,128]{2,1,0:T(8,128)S(1)} %shard_map.80.vector.block.prior.v0), channel_id=1, source_target_pairs={{0,252},{4,8},{8,4},{12,16},{16,12},{20,24},{24,20},{28,32},{32,28... | collective-permute-start | bytes 589832 | tf_op jit(solution)/shard_map/ppermute | solution.py:731
  18.1 8.2 %collective-permute-start.6 = (f32[6,64,128]{2,1,0:T(8,128)S(1)}, f32[6,64,128]{2,1,0:T(8,128)S(1)}, u32[]{:S(2)}, u32[]{:S(2)}) collective-permute-start(f32[6,64,128]{2,1,0:T(8,128)S(1)} %shard_map.80.vector.block.prior.v0), channel_id=1, source_target_pairs={{0,4},{4,0},{8,12},{12,8},{16,20},{20,16},{24,28},{28,24},{32,36},... | collective-permute-start | bytes 589832 | tf_op jit(solution)/shard_map/ppermute | solution.py:732
  19.2 2.8 %collective-permute-start.4 = (f32[24,128]{1,0:T(8,128)S(1)}, f32[24,128]{1,0:T(8,128)S(1)}, u32[]{:S(2)}, u32[]{:S(2)}) collective-permute-start(f32[24,128]{1,0:T(8,128)S(1)} %get-tuple-element.37), channel_id=1, source_target_pairs={{0,1},{1,0},{2,3},{3,2},{4,5},{5,4},{6,7},{7,6},{8,9},{9,8},{10,11... | collective-permute-start | bytes 36872 | tf_op jit(solution)/shard_map/ppermute | solution.py:736
  20.1 5.9 %collective-permute-start.5 = (f32[24,128]{1,0:T(8,128)S(1)}, f32[24,128]{1,0:T(8,128)S(1)}, u32[]{:S(2)}, u32[]{:S(2)}) collective-permute-start(f32[24,128]{1,0:T(8,128)S(1)} %get-tuple-element.38), channel_id=1, source_target_pairs={{0,3},{1,2},{2,1},{3,0},{4,7},{5,6},{6,5},{7,4},{8,11},{9,10},{10,... | collective-permute-start | bytes 36872 | tf_op jit(solution)/shard_map/ppermute | solution.py:736
  22.0 7.8 %collective-permute-start.9 = (f32[6,64,128]{2,1,0:T(8,128)S(1)}, f32[6,64,128]{2,1,0:T(8,128)S(1)}, u32[]{:S(2)}, u32[]{:S(2)}) collective-permute-start(f32[6,64,128]{2,1,0:T(8,128)S(1)} %copy-done.1), channel_id=1, source_target_pairs={{0,252},{4,8},{8,4},{12,16},{16,12},{20,24},{24,20},{28,32},{32,28... | collective-permute-start | bytes 589832 | tf_op jit(solution)/shard_map/ppermute | solution.py:731
  22.0 9.0 %collective-permute-start.8 = (f32[6,64,128]{2,1,0:T(8,128)S(1)}, f32[6,64,128]{2,1,0:T(8,128)S(1)}, u32[]{:S(2)}, u32[]{:S(2)}) collective-permute-start(f32[6,64,128]{2,1,0:T(8,128)S(1)} %copy-done.1), channel_id=1, source_target_pairs={{0,4},{4,0},{8,12},{12,8},{16,20},{20,16},{24,28},{28,24},{32,36},... | collective-permute-start | bytes 589832 | tf_op jit(solution)/shard_map/ppermute | solution.py:732
  26.5 7.7 %collective-permute-start.13 = (f32[6,64,128]{2,1,0:T(8,128)S(1)}, f32[6,64,128]{2,1,0:T(8,128)S(1)}, u32[]{:S(2)}, u32[]{:S(2)}) collective-permute-start(f32[6,64,128]{2,1,0:T(8,128)S(1)} %shard_map.84.vector.block.prior.v1), channel_id=1, source_target_pairs={{0,252},{4,8},{8,4},{12,16},{16,12},{20,24},{24,20},{28,32},{32,28... | collective-permute-start | bytes 589832 | tf_op jit(solution)/shard_map/ppermute | solution.py:731
  26.6 7.6 %collective-permute-start.12 = (f32[6,64,128]{2,1,0:T(8,128)S(1)}, f32[6,64,128]{2,1,0:T(8,128)S(1)}, u32[]{:S(2)}, u32[]{:S(2)}) collective-permute-start(f32[6,64,128]{2,1,0:T(8,128)S(1)} %shard_map.84.vector.block.prior.v1), channel_id=1, source_target_pairs={{0,4},{4,0},{8,12},{12,8},{16,20},{20,16},{24,28},{28,24},{32,36},... | collective-permute-start | bytes 589832 | tf_op jit(solution)/shard_map/ppermute | solution.py:732
  29.3 3.9 %collective-permute-start.10 = (f32[24,128]{1,0:T(8,128)S(1)}, f32[24,128]{1,0:T(8,128)S(1)}, u32[]{:S(2)}, u32[]{:S(2)}) collective-permute-start(f32[24,128]{1,0:T(8,128)S(1)} %get-tuple-element.43), channel_id=1, source_target_pairs={{0,1},{1,0},{2,3},{3,2},{4,5},{5,4},{6,7},{7,6},{8,9},{9,8},{10,11... | collective-permute-start | bytes 36872 | tf_op jit(solution)/shard_map/ppermute | solution.py:736
  29.8 4.1 %collective-permute-start.11 = (f32[24,128]{1,0:T(8,128)S(1)}, f32[24,128]{1,0:T(8,128)S(1)}, u32[]{:S(2)}, u32[]{:S(2)}) collective-permute-start(f32[24,128]{1,0:T(8,128)S(1)} %get-tuple-element.44), channel_id=1, source_target_pairs={{0,3},{1,2},{2,1},{3,0},{4,7},{5,6},{6,5},{7,4},{8,11},{9,10},{10,... | collective-permute-start | bytes 36872 | tf_op jit(solution)/shard_map/ppermute | solution.py:736
  34.5 8.6 %collective-permute-start.17 = (f32[6,64,128]{2,1,0:T(8,128)S(1)}, f32[6,64,128]{2,1,0:T(8,128)S(1)}, u32[]{:S(2)}, u32[]{:S(2)}) collective-permute-start(f32[6,64,128]{2,1,0:T(8,128)S(1)} %shard_map.88.vector.block.prior.v2), channel_id=1, source_target_pairs={{0,252},{4,8},{8,4},{12,16},{16,12},{20,24},{24,20},{28,32},{32,28... | collective-permute-start | bytes 589832 | tf_op jit(solution)/shard_map/ppermute | solution.py:731
  35.2 7.9 %collective-permute-start.16 = (f32[6,64,128]{2,1,0:T(8,128)S(1)}, f32[6,64,128]{2,1,0:T(8,128)S(1)}, u32[]{:S(2)}, u32[]{:S(2)}) collective-permute-start(f32[6,64,128]{2,1,0:T(8,128)S(1)} %shard_map.88.vector.block.prior.v2), channel_id=1, source_target_pairs={{0,4},{4,0},{8,12},{12,8},{16,20},{20,16},{24,28},{28,24},{32,36},... | collective-permute-start | bytes 589832 | tf_op jit(solution)/shard_map/ppermute | solution.py:732
  38.6 3.5 %collective-permute-start.14 = (f32[24,128]{1,0:T(8,128)S(1)}, f32[24,128]{1,0:T(8,128)S(1)}, u32[]{:S(2)}, u32[]{:S(2)}) collective-permute-start(f32[24,128]{1,0:T(8,128)S(1)} %get-tuple-element.47), channel_id=1, source_target_pairs={{0,1},{1,0},{2,3},{3,2},{4,5},{5,4},{6,7},{7,6},{8,9},{9,8},{10,11... | collective-permute-start | bytes 36872 | tf_op jit(solution)/shard_map/ppermute | solution.py:736
  38.7 4.1 %collective-permute-start.15 = (f32[24,128]{1,0:T(8,128)S(1)}, f32[24,128]{1,0:T(8,128)S(1)}, u32[]{:S(2)}, u32[]{:S(2)}) collective-permute-start(f32[24,128]{1,0:T(8,128)S(1)} %get-tuple-element.48), channel_id=1, source_target_pairs={{0,3},{1,2},{2,1},{3,0},{4,7},{5,6},{6,5},{7,4},{8,11},{9,10},{10,... | collective-permute-start | bytes 36872 | tf_op jit(solution)/shard_map/ppermute | solution.py:736
  43.3 8.3 %collective-permute-start.18 = (f32[6,32,128]{2,1,0:T(8,128)S(1)}, f32[6,32,128]{2,1,0:T(8,128)S(1)}, u32[]{:S(2)}, u32[]{:S(2)}) collective-permute-start(f32[6,32,128]{2,1,0:T(8,128)S(1)} %get-tuple-element.50), channel_id=1, source_target_pairs={{0,252},{4,8},{8,4},{12,16},{16,12},{20,24},{24,20},{28,32},{32,28... | collective-permute-start | bytes 294920 | tf_op jit(solution)/shard_map/ppermute | solution.py:800
  43.4 8.2 %collective-permute-start.19 = (f32[6,32,128]{2,1,0:T(8,128)S(1)}, f32[6,32,128]{2,1,0:T(8,128)S(1)}, u32[]{:S(2)}, u32[]{:S(2)}) collective-permute-start(f32[6,32,128]{2,1,0:T(8,128)S(1)} %get-tuple-element.51), channel_id=1, source_target_pairs={{0,4},{4,0},{8,12},{12,8},{16,20},{20,16},{24,28},{28,24},{32,36},... | collective-permute-start | bytes 294920 | tf_op jit(solution)/shard_map/ppermute | solution.py:801
  47.2 4.1 %collective-permute-start.20 = (f32[24,128]{1,0:T(8,128)S(1)}, f32[24,128]{1,0:T(8,128)S(1)}, u32[]{:S(2)}, u32[]{:S(2)}) collective-permute-start(f32[24,128]{1,0:T(8,128)S(1)} %shard_map.93), channel_id=1, source_target_pairs={{0,1},{1,2},{2,3},{3,0},{4,5},{5,6},{6,7},{7,4},{8,9},{9,10},{10,1... | collective-permute-start | bytes 36872 | tf_op jit(solution)/shard_map/ppermute | solution.py:803
  48.3 1.2 %collective-permute-start.21 = (f32[1,128]{1,0:T(1,128)S(1)}, f32[1,128]{1,0:T(1,128)S(1)}, u32[]{:S(2)}, u32[]{:S(2)}) collective-permute-start(f32[1,128]{1,0:T(1,128)S(1)} %get-tuple-element.57), channel_id=1, source_target_pairs={{0,4},{4,0},{8,12},{12,8},{16,20},{20,16},{24,28},{28,24},{32,36},... | collective-permute-start | bytes 1544 | tf_op jit(solution)/shard_map/ppermute | solution.py:811

commit v14 on v12

--- a/solution.py
+++ b/solution.py
@@ -426,7 +426,7 @@
     base_gradient(both, near, far, z_first, z_second, potential, grad, ext)
 
 
-def side_four(prior, vector, both, grad, steps, changes, inner, rows, moments, ext):
+def side_four(prior, vector, both, grad, steps, changes, r1, r3, m3, inner, sums, rows, moments, table, ext):
     inner_basis(vector, prior, inner, ext)
     lifted, rho = lifted_tile(both, vector), density_tile(both)
     slope = lambda i, b: tile_of(grad, i, b)
@@ -438,11 +438,6 @@
     store(rows, 79, gram_dots(steps, changes, CROSS_PAIRS[32:]))
     store_moments([(prior, vector), (vector, vector)], moments)
 
-
-def side_five(prior, vector, both, steps, changes, r1, r3, r4, m3, m4, kept, given, table, m5):
-    lifted, rho = lifted_tile(both, vector), density_tile(both)
-    own = field_dots((steps, changes), [lifted], [(rho, lifted)])
-    store_moments([(prior, vector), (vector, vector)], m5)
     table[...] = jnp.zeros_like(table)
 
     def put(base, ref, start, count):
@@ -454,29 +449,40 @@
             table[at : at + count - before, :] = ref[start + before : start + count, :]
 
     put(ROW_GRAM, r1, 0, 36)
-    put(ROW_GRAM + 36, r4, 43, 36)
+    put(ROW_GRAM + 36, rows, 43, 36)
     put(ROW_GRAM + 72, r3, 34, 32)
-    put(ROW_GRAM + 104, r4, 79, 32)
+    put(ROW_GRAM + 104, rows, 79, 32)
     put(ROW_BASE, r1, 36, 8)
-    put(ROW_BASE + 8, r4, 35, 8)
-    put(ROW_BASE + 16, r4, 17, 18)
+    put(ROW_BASE + 8, rows, 35, 8)
+    put(ROW_BASE + 16, rows, 17, 18)
     put(ROW_W, r3, 0, 34)
-    put(ROW_W + 34, r4, 0, 17)
-    store(table, place(ROW_W + 51), own)
-
-    order = [(m3, 0), (m3, 1), (m3, 2), (m4, 0), (m4, 1), (m5, 0), (m5, 1)]
-    zero = jnp.zeros((1, LANES), jnp.float32)
+    put(ROW_W + 34, rows, 0, 17)
+    second = jnp.sum(jnp.transpose(table[LANES : 2 * LANES, :]), axis=0, keepdims=True)
+    sums[0:1, :] = jnp.sum(jnp.transpose(table[0:LANES, :]), axis=0, keepdims=True)
+    sums[1:2, :] = put_moments(second, [(m3, 0), (m3, 1), (m3, 2), (moments, 0), (moments, 1)], 0)
+
+
+def put_moments(row, order, start):
+    zero = jnp.zeros((8 - len(order), LANES), jnp.float32)
     parts = [
         jnp.concatenate([ref[2 * which + low : 2 * which + low + 1, :] for ref, which in order] + [zero], axis=0)
         for low in range(2)
     ]
     hi, lo = fold_lanes(*parts)
     lane = lane_ids((1, LANES))
-    first = jnp.sum(jnp.transpose(table[0:LANES, :]), axis=0, keepdims=True)
-    second = jnp.sum(jnp.transpose(table[LANES : 2 * LANES, :]), axis=0, keepdims=True)
-    for n in range(7):
-        second = jnp.where(lane == MOM_LANE + n, hi[n : n + 1], second)
-        second = jnp.where(lane == MOM_LANE + 7 + n, lo[n : n + 1], second)
+    for n in range(len(order)):
+        row = jnp.where(lane == MOM_LANE + start + n, hi[n : n + 1], row)
+        row = jnp.where(lane == MOM_LANE + 7 + start + n, lo[n : n + 1], row)
+    return row
+
+
+def side_five(prior, vector, both, steps, changes, sums, kept, given, table, m5):
+    lifted, rho = lifted_tile(both, vector), density_tile(both)
+    table[...] = jnp.zeros_like(table)
+    store(table, place(ROW_W + 51) - LANES, field_dots((steps, changes), [lifted], [(rho, lifted)]))
+    store_moments([(prior, vector), (vector, vector)], m5)
+    second = sums[1:2, :] + jnp.sum(jnp.transpose(table[...]), axis=0, keepdims=True)
+    first, second = sums[0:1, :], put_moments(second, [(m5, 0), (m5, 1)], 5)
     odd = is_odd("blk")
     kept[...] = jnp.where(odd, second, first)
     given[...] = jnp.where(odd, first, second)
@@ -502,31 +508,26 @@
     return acc
 
 
-def couple_kernel(own, z_left, inner, kept, taken, row, part):
-    zero = jnp.zeros((8, LANES), jnp.float32)
+def send_kernel(own, far, near, z_left, inner, kept, taken, out):
     faces = edge_faces(z_left[...], None)
-    acc = (zero, zero)
-    for i in range(REACH):
-        product = own[i] * z_plane(i, faces)
-        for b in range(8):
-            acc = add_tile(acc, product[8 * b : 8 * b + 8])
-    sides = df_scale(fold_rows(acc), -2.0 / SHIFT)
-    part[0:1, :], part[1:2, :] = df_add(sides, (inner[0:1, :], inner[1:2, :]))
-    lane = lane_ids((1, LANES))
-    total, err = two_sum(kept[...], taken[...])
-    low_lane = (lane >= MOM_LANE + 7) & (lane < MOM_LANE + 14) & is_odd("blk")
-    row[...] = jnp.where(low_lane, total + pltpu.roll(err, 7, 1), total)
-
-
-def send_kernel(own, far, near, part, row, out):
-    zero = jnp.zeros((8, LANES), jnp.float32)
 
     def body(near_below, far_below):
-        acc = couple(own, far, far_below, couple(own, near, near_below, (zero, zero)))
-        hi, lo = fold_lanes(*df_add(df_scale(fold_rows(acc), -2.0 / SHIFT), (part[0:1, :], part[1:2, :])))
+        zero = jnp.zeros((8, LANES), jnp.float32)
+        accs = [(zero, zero) for _ in range(2)]
+        for i in range(REACH):
+            product = own[i] * z_plane(i, faces)
+            for b in range(8):
+                accs[b % 2] = add_tile(accs[b % 2], product[8 * b : 8 * b + 8])
+        accs = [couple(own, far, far_below, accs[0]), couple(own, near, near_below, accs[1])]
+        hi, err = two_sum(accs[0][0], accs[1][0])
+        sides = fold_rows((hi, accs[0][1] + accs[1][1] + err))
+        hi, lo = fold_lanes(*df_add(df_scale(sides, -2.0 / SHIFT), (inner[0:1, :], inner[1:2, :])))
         lane = lane_ids((1, LANES))
-        value = jnp.where(lane == HALF, hi, jnp.where(lane == HALF + 1, lo, row[...]))
-        out[...] = jnp.broadcast_to(value, out.shape)
+        row, err = two_sum(kept[...], taken[...])
+        low_lane = (lane >= MOM_LANE + 7) & (lane < MOM_LANE + 14) & is_odd("blk")
+        row = jnp.where(low_lane, row + pltpu.roll(err, 7, 1), row)
+        row = jnp.where(lane == HALF, hi, jnp.where(lane == HALF + 1, lo, row))
+        out[...] = jnp.broadcast_to(row, out.shape)
 
     with_sides(body)
 
@@ -793,8 +794,12 @@
     )
     (v2,) = advance(-2.0 / SHIFT, inner, halo, ends)
     halo, ends = exchange(v2)
-    inner, r4, m4 = call(
-        side_four, [block, (112, LANES), (8, LANES)], [v1, v2, both, grad, *history], [ext], work
+    inner, sums = call(
+        side_four,
+        [block, (2, LANES)],
+        [v1, v2, both, grad, *history, r1, r3, m3],
+        [(112, LANES), (8, LANES), (2 * LANES, LANES), ext],
+        work,
     )
     v3, to_near, to_far = advance(-2.0 / SHIFT, inner, halo, ends, last=True)
     far = lax.ppermute(to_far, "blk", swap("blk", 1))
@@ -804,15 +809,14 @@
     kept, given = call(
         side_five,
         [(1, LANES), (1, LANES)],
-        [v2, v3, both, *history, r1, r3, r4, m3, m4],
-        [(2 * LANES, LANES), (8, LANES)],
+        [v2, v3, both, *history, sums],
+        [(LANES, LANES), (8, LANES)],
         work,
     )
     taken = lax.ppermute(given, "blk", swap("blk", 0))
     (inner,) = call(inner_moment_kernel, [(8, LANES)], [after((v3,), given)[0]], [ext], work)
-    row, part = call(couple_kernel, [(1, LANES), (8, LANES)], [v3, z_left, inner, kept, taken], flops=work)
     devices = lax.axis_size("blk") * lax.axis_size("gz")
-    (outgoing,) = call(send_kernel, [(devices, LANES)], [v3, far, near, part, row], flops=work)
+    (outgoing,) = call(send_kernel, [(devices, LANES)], [v3, far, near, z_left, inner, kept, taken], flops=work)
     received = lax.all_to_all(outgoing.reshape(devices, 1, LANES), ("blk", "gz"), 0, 0, tiled=True)
     return tuple(
         call(

time: 73 us -> 73 us (level)
    pallas_call x22 -> x21, Pallas kernels: 15.2 us -> 15.6 us  [call(): pl.pallas_call(kernel, out_shape=shapes, in_specs=[pl.BlockSpec(memory_sp...]
  transfers between devices with their start and end apart: 22 -> 22, of which waited for: 3 -> 2; matrix products, arithmetic and copies ran while one was open for 0% -> 0% of each run, Pallas kernels for 17% -> 18%
where the time goes in v14:
time: 73 us; the launch traced here: 72.9 us
  starting transfers between devices  35.1 us (48%)
  blocking collectives  18.7 us (26%)
  Pallas kernels  15.6 us (21%)
  waiting for transfers between devices  2.36 us (3%)
  between operations  1.1 us (2%)
    all_to_all x1, blocking collectives, on_device(): lax.all_to_all(outgoing.reshape(devices, 1, LANES), ('blk', 'gz'), 0, 0,...  18.7 us
    ppermute x5, starting transfers between devices, x_halo(): return (lax.ppermute(block, 'blk', swap('blk', 0)), far)  17.2 us
    pallas_call x21, Pallas kernels, call(): pl.pallas_call(kernel, out_shape=shapes, in_specs=[pl.BlockSpec(memory_sp...  15.6 us
    ppermute x4, starting transfers between devices, z_halo(): lax.ppermute(face_b, 'gz', swap('gz', 1))  7.11 us
    ppermute x5, starting transfers between devices, x_halo(): far = lax.ppermute(block, 'blk', swap('blk', 1))  3.88 us
    ppermute x1, starting transfers between devices, on_device(): near = lax.ppermute(to_near, 'blk', swap('blk', 0))  3.31 us
    ppermute x4, starting transfers between devices, z_halo(): lax.ppermute(face_a, 'gz', swap('gz', 0))  3.21 us
    ppermute x1, waiting for transfers between devices, on_device(): z_left = lax.ppermute(upper, 'gz', ring('gz', 1))  1.87 us
  transfers between devices with their start and end apart: 22, of which 2 were waited for; matrix products, arithmetic and copies ran while one was open for 0% of the time, Pallas kernels for 18%

profile of v14, /device:TPU:1, one launch (start us, length us, event | category | flops | bytes accessed | tf_op | source)
XLA Modules:
  0.0 72.9 jit_solution(11725875962450091625)
XLA Ops:
  0.6 2.7 %collective-permute-start.3 = (f32[6,64,128]{2,1,0:T(8,128)}, f32[6,64,128]{2,1,0:T(8,128)S(1)}, u32[]{:S(2)}, u32[]{:S(2)}) collective-permute-start(f32[6,64,128]{2,1,0:T(8,128)} %hartree.1), channel_id=1, source_target_pairs={{0,252},{4,8},{8,4},{12,16},{16,12},{20,24},{24,20},{28,32},{32,28... | collective-permute-start | bytes 589832 | tf_op jit(solution)/shard_map/ppermute | solution.py:732
  3.3 6.4 %collective-permute-start.2 = (f32[6,64,128]{2,1,0:T(8,128)}, f32[6,64,128]{2,1,0:T(8,128)S(1)}, u32[]{:S(2)}, u32[]{:S(2)}) collective-permute-start(f32[6,64,128]{2,1,0:T(8,128)} %hartree.1), channel_id=1, source_target_pairs={{0,4},{4,0},{8,12},{12,8},{16,20},{20,16},{24,28},{28,24},{32,36},... | collective-permute-start | bytes 589832 | tf_op jit(solution)/shard_map/ppermute | solution.py:733
  9.7 1.3 %shard_map.77 = (f32[12,64,128]{2,1,0:T(8,128)S(1)}, f32[6,64,128]{2,1,0:T(8,128)S(1)}, f32[48,128]{1,0:T(8,128)S(1)}, f32[48,128]{1,0:T(8,128)S(1)}) custom-call(f32[6,64,128]{2,1,0:T(8,128)} %hartree.1, f32[6,64,128]{2,1,0:T(8,128)} %density.1, f32[6,64,128]{2,1,0:T(8,128)} %charge.1), custom_call_target="tpu_custom_call" | custom-call | bytes 1228800 | tf_op jit(solution)/shard_map/pallas_call | solution.py:706
  11.0 1.4 %collective-permute-start = (f32[48,128]{1,0:T(8,128)S(1)}, f32[48,128]{1,0:T(8,128)S(1)}, u32[]{:S(2)}, u32[]{:S(2)}) collective-permute-start(f32[48,128]{1,0:T(8,128)S(1)} %get-tuple-element.32), channel_id=1, source_target_pairs={{0,1},{1,0},{2,3},{3,2},{4,5},{5,4},{6,7},{7,6},{8,9},{9,8},{10,11... | collective-permute-start | bytes 73736 | tf_op jit(solution)/shard_map/ppermute | solution.py:737
  12.4 1.9 %collective-permute-start.1 = (f32[48,128]{1,0:T(8,128)S(1)}, f32[48,128]{1,0:T(8,128)S(1)}, u32[]{:S(2)}, u32[]{:S(2)}) collective-permute-start(f32[48,128]{1,0:T(8,128)S(1)} %get-tuple-element.33), channel_id=1, source_target_pairs={{0,3},{1,2},{2,1},{3,0},{4,7},{5,6},{6,5},{7,4},{8,11},{9,10},{10,... | collective-permute-start | bytes 73736 | tf_op jit(solution)/shard_map/ppermute | solution.py:737
  14.3 2.2 %shard_map.78 = (f32[6,64,128]{2,1,0:T(8,128)S(1)}, f32[8,6,64,128]{3,2,1,0:T(8,128)S(1)}, f32[8,6,64,128]{3,2,1,0:T(8,128)S(1)}, f32[48,128]{1,0:T(8,128)S(1)}) custom-call(f32[12,64,128]{2,1,0:T(8,128)S(1)} %get-tuple-element.29.both, f32[6,64,128]{2,1,0:T(8,128)S(1)} %get-tuple-element.30.charge, f32[8,6,64,128]{3,2,1,0:T(8,128)} %steps.1, ...), custom_call_target="tpu_custom_call" | custom-call | flops 14745600 | bytes 7102464 | tf_op jit(solution)/shard_map/pallas_call | solution.py:706
  16.5 0.0 collective-permute-done.1.z_second
  16.5 0.0 copy-start
  16.5 0.3 shard_map.79.inner
  16.8 0.0 collective-permute-done.3.far
  16.8 0.1 shard_map.80.vector.block.prior.v0
  16.9 0.1 collective-permute-start.7
  17.0 1.5 %collective-permute-start.6 = (f32[6,64,128]{2,1,0:T(8,128)S(1)}, f32[6,64,128]{2,1,0:T(8,128)S(1)}, u32[]{:S(2)}, u32[]{:S(2)}) collective-permute-start(f32[6,64,128]{2,1,0:T(8,128)S(1)} %shard_map.80.vector.block.prior.v0), channel_id=1, source_target_pairs={{0,4},{4,0},{8,12},{12,8},{16,20},{20,16},{24,28},{28,24},{32,36},... | collective-permute-start | bytes 589832 | tf_op jit(solution)/shard_map/ppermute | solution.py:733
  18.5 0.2 shard_map.82
  18.7 1.4 %collective-permute-start.4 = (f32[24,128]{1,0:T(8,128)S(1)}, f32[24,128]{1,0:T(8,128)S(1)}, u32[]{:S(2)}, u32[]{:S(2)}) collective-permute-start(f32[24,128]{1,0:T(8,128)S(1)} %get-tuple-element.34), channel_id=1, source_target_pairs={{0,1},{1,0},{2,3},{3,2},{4,5},{5,4},{6,7},{7,6},{8,9},{9,8},{10,11... | collective-permute-start | bytes 36872 | tf_op jit(solution)/shard_map/ppermute | solution.py:737
  20.1 1.9 %collective-permute-start.5 = (f32[24,128]{1,0:T(8,128)S(1)}, f32[24,128]{1,0:T(8,128)S(1)}, u32[]{:S(2)}, u32[]{:S(2)}) collective-permute-start(f32[24,128]{1,0:T(8,128)S(1)} %get-tuple-element.35), channel_id=1, source_target_pairs={{0,3},{1,2},{2,1},{3,0},{4,7},{5,6},{6,5},{7,4},{8,11},{9,10},{10,... | collective-permute-start | bytes 36872 | tf_op jit(solution)/shard_map/ppermute | solution.py:737
  22.0 3.6 %collective-permute-start.8 = (f32[6,64,128]{2,1,0:T(8,128)S(1)}, f32[6,64,128]{2,1,0:T(8,128)S(1)}, u32[]{:S(2)}, u32[]{:S(2)}) collective-permute-start(f32[6,64,128]{2,1,0:T(8,128)S(1)} %copy-done.1), channel_id=1, source_target_pairs={{0,4},{4,0},{8,12},{12,8},{16,20},{20,16},{24,28},{28,24},{32,36},... | collective-permute-start | bytes 589832 | tf_op jit(solution)/shard_map/ppermute | solution.py:733
  25.6 0.4 shard_map.81.inner
  26.0 0.3 shard_map.83.inner
  26.3 0.1 shard_map.84.vector.block.prior.v1
  26.5 0.1 collective-permute-start.13
  26.6 2.2 %collective-permute-start.12 = (f32[6,64,128]{2,1,0:T(8,128)S(1)}, f32[6,64,128]{2,1,0:T(8,128)S(1)}, u32[]{:S(2)}, u32[]{:S(2)}) collective-permute-start(f32[6,64,128]{2,1,0:T(8,128)S(1)} %shard_map.84.vector.block.prior.v1), channel_id=1, source_target_pairs={{0,4},{4,0},{8,12},{12,8},{16,20},{20,16},{24,28},{28,24},{32,36},... | collective-permute-start | bytes 589832 | tf_op jit(solution)/shard_map/ppermute | solution.py:733
  28.8 0.2 shard_map.86
  28.9 0.4 collective-permute-start.10
  29.3 1.7 %collective-permute-start.11 = (f32[24,128]{1,0:T(8,128)S(1)}, f32[24,128]{1,0:T(8,128)S(1)}, u32[]{:S(2)}, u32[]{:S(2)}) collective-permute-start(f32[24,128]{1,0:T(8,128)S(1)} %get-tuple-element.41), channel_id=1, source_target_pairs={{0,3},{1,2},{2,1},{3,0},{4,7},{5,6},{6,5},{7,4},{8,11},{9,10},{10,... | collective-permute-start | bytes 36872 | tf_op jit(solution)/shard_map/ppermute | solution.py:737
  31.0 2.7 %shard_map.85 = (f32[6,64,128]{2,1,0:T(8,128)S(1)}, f32[6,64,128]{2,1,0:T(8,128)S(1)}, f32[72,128]{1,0:T(8,128)S(1)}, f32[8,128]{1,0:T(8,128)S(1)}) custom-call(f32[6,64,128]{2,1,0:T(8,128)S(1)} %shard_map.80.vector.block.prior.v0, f32[6,64,128]{2,1,0:T(8,128)S(1)} %shard_map.84.vector.block.prior.v1, f32[12,64,128]{2,1,0:T(8,128)S(1)} %get-tuple-element.29.both, ...), custom_call_target="tpu_custom_call" | custom-call | flops 14745600 | bytes 5005312 | tf_op jit(solution)/shard_map/pallas_call | solution.py:706
  33.8 0.3 shard_map.87.inner
  34.1 0.1 shard_map.88.vector.block.prior.v2
  34.2 1.0 %collective-permute-start.17 = (f32[6,64,128]{2,1,0:T(8,128)S(1)}, f32[6,64,128]{2,1,0:T(8,128)S(1)}, u32[]{:S(2)}, u32[]{:S(2)}) collective-permute-start(f32[6,64,128]{2,1,0:T(8,128)S(1)} %shard_map.88.vector.block.prior.v2), channel_id=1, source_target_pairs={{0,252},{4,8},{8,4},{12,16},{16,12},{20,24},{24,20},{28,32},{32,28... | collective-permute-start | bytes 589832 | tf_op jit(solution)/shard_map/ppermute | solution.py:732
  35.2 3.5 %collective-permute-start.16 = (f32[6,64,128]{2,1,0:T(8,128)S(1)}, f32[6,64,128]{2,1,0:T(8,128)S(1)}, u32[]{:S(2)}, u32[]{:S(2)}) collective-permute-start(f32[6,64,128]{2,1,0:T(8,128)S(1)} %shard_map.88.vector.block.prior.v2), channel_id=1, source_target_pairs={{0,4},{4,0},{8,12},{12,8},{16,20},{20,16},{24,28},{28,24},{32,36},... | collective-permute-start | bytes 589832 | tf_op jit(solution)/shard_map/ppermute | solution.py:733
  38.7 0.2 shard_map.90
  38.9 0.1 collective-permute-start.14
  39.0 1.6 %collective-permute-start.15 = (f32[24,128]{1,0:T(8,128)S(1)}, f32[24,128]{1,0:T(8,128)S(1)}, u32[]{:S(2)}, u32[]{:S(2)}) collective-permute-start(f32[24,128]{1,0:T(8,128)S(1)} %get-tuple-element.48), channel_id=1, source_target_pairs={{0,3},{1,2},{2,1},{3,0},{4,7},{5,6},{6,5},{7,4},{8,11},{9,10},{10,... | collective-permute-start | bytes 36872 | tf_op jit(solution)/shard_map/ppermute | solution.py:737
  40.5 2.9 %shard_map.89 = (f32[6,64,128]{2,1,0:T(8,128)S(1)}, f32[2,128]{1,0:T(2,128)S(1)}) custom-call(f32[6,64,128]{2,1,0:T(8,128)S(1)} %shard_map.84.vector.block.prior.v1, f32[6,64,128]{2,1,0:T(8,128)S(1)} %shard_map.88.vector.block.prior.v2, f32[12,64,128]{2,1,0:T(8,128)S(1)} %get-tuple-element.29.both, f32[6,64,128]{2,1,0:T(8,128)S(1)} %get-tuple-element.42.grad, ...), custom_call_target="tpu_custom_call" | custom-call | flops 14745600 | bytes 4391936 | tf_op jit(solution)/shard_map/pallas_call | solution.py:706
  43.5 0.3 shard_map.91.inner
  43.8 0.1 shard_map.92
  43.9 0.1 collective-permute-start.18
  44.0 3.3 %collective-permute-start.19 = (f32[6,32,128]{2,1,0:T(8,128)S(1)}, f32[6,32,128]{2,1,0:T(8,128)S(1)}, u32[]{:S(2)}, u32[]{:S(2)}) collective-permute-start(f32[6,32,128]{2,1,0:T(8,128)S(1)} %get-tuple-element.51), channel_id=1, source_target_pairs={{0,4},{4,0},{8,12},{12,8},{16,20},{20,16},{24,28},{28,24},{32,36},... | collective-permute-start | bytes 294920 | tf_op jit(solution)/shard_map/ppermute | solution.py:806
  47.3 0.1 shard_map.93
  47.4 0.1 collective-permute-start.20
  47.5 1.0 %shard_map.94 = (f32[1,128]{1,0:T(1,128)S(1)}, f32[1,128]{1,0:T(1,128)S(1)}) custom-call(f32[6,64,128]{2,1,0:T(8,128)S(1)} %shard_map.88.vector.block.prior.v2, f32[6,64,128]{2,1,0:T(8,128)S(1)} %get-tuple-element.54.block.vector.own.v3, f32[12,64,128]{2,1,0:T(8,128)S(1)} %get-tuple-element.29.both, f32[8,6,64,128]{3,2,1,0:T(8,128)S(1)} %get-tuple-element.37.steps, ...), custom_call_target="tpu_custom_call" | custom-call | flops 14745600 | bytes 3934208 | tf_op jit(solution)/shard_map/pallas_call | solution.py:706
  48.5 0.3 collective-permute-start.21
  48.8 0.5 shard_map.95.inner
  49.3 0.4 collective-permute-done.21.taken
  49.7 1.9 %collective-permute-done.20.z_left = f32[24,128]{1,0:T(8,128)S(1)} collective-permute-done((f32[24,128]{1,0:T(8,128)S(1)}, f32[24,128]{1,0:T(8,128)S(1)}, u32[]{:S(2)}, u32[]{:S(2)}) %collective-permute-start.20) | collective-permute-done | bytes 12320 | tf_op jit(solution)/shard_map/ppermute | solution.py:808
  51.6 0.8 %shard_map.96 = f32[256,128]{1,0:T(8,128)S(1)} custom-call(f32[6,64,128]{2,1,0:T(8,128)S(1)} %get-tuple-element.54.block.vector.own.v3, f32[6,32,128]{2,1,0:T(8,128)S(1)} %collective-permute-done.18.far, f32[6,32,128]{2,1,0:T(8,128)S(1)} %collective-permute-done.19.near, f32[24,128]{1,0:T(8,128)S(1)} %collective-permute-done.20.z_left, ...), custom_call_target="tpu_custom_call" | custom-call | flops 14745600 | bytes 541696 | tf_op jit(solution)/shard_map/pallas_call | solution.py:706
  52.4 18.7 %all_to_all.5 = f32[256,1,128]{2,1,0:T(1,128)S(1)} all-to-all(f32[256,1,128]{2,1,0:T(1,128)S(1)} %bitcast.5), channel_id=1, replica_groups=mesh['blk'=64,'gz'=4] {'blk','gz'}, dimensions={0} | all-to-all | bytes 262144 | tf_op jit(solution)/shard_map/all_to_all | solution.py:820
  71.1 1.6 %shard_map.97 = (f32[6,64,128]{2,1,0:T(8,128)}, f32[6,64,128]{2,1,0:T(8,128)}) custom-call(f32[256,128]{1,0:T(8,128)S(1)} %bitcast.4, f32[12,64,128]{2,1,0:T(8,128)S(1)} %get-tuple-element.29.both, f32[6,64,128]{2,1,0:T(8,128)S(1)} %get-tuple-element.42.grad, f32[6,64,128]{2,1,0:T(8,128)S(1)} %shard_map.80.vector.block.prior.v0, ...), custom_call_target="tpu_custom_call" | custom-call | flops 14745600 | bytes 5046272 | tf_op jit(solution)/shard_map/pallas_call | solution.py:706
  (22 shorter events, 0.1 us)
Async XLA Ops:
  0.6 16.1 %collective-permute-start.3 = (f32[6,64,128]{2,1,0:T(8,128)}, f32[6,64,128]{2,1,0:T(8,128)S(1)}, u32[]{:S(2)}, u32[]{:S(2)}) collective-permute-start(f32[6,64,128]{2,1,0:T(8,128)} %hartree.1), channel_id=1, source_target_pairs={{0,252},{4,8},{8,4},{12,16},{16,12},{20,24},{24,20},{28,32},{32,28... | collective-permute-start | bytes 589832 | tf_op jit(solution)/shard_map/ppermute | solution.py:732
  3.3 13.5 %collective-permute-start.2 = (f32[6,64,128]{2,1,0:T(8,128)}, f32[6,64,128]{2,1,0:T(8,128)S(1)}, u32[]{:S(2)}, u32[]{:S(2)}) collective-permute-start(f32[6,64,128]{2,1,0:T(8,128)} %hartree.1), channel_id=1, source_target_pairs={{0,4},{4,0},{8,12},{12,8},{16,20},{20,16},{24,28},{28,24},{32,36},... | collective-permute-start | bytes 589832 | tf_op jit(solution)/shard_map/ppermute | solution.py:733
  11.0 5.5 %collective-permute-start = (f32[48,128]{1,0:T(8,128)S(1)}, f32[48,128]{1,0:T(8,128)S(1)}, u32[]{:S(2)}, u32[]{:S(2)}) collective-permute-start(f32[48,128]{1,0:T(8,128)S(1)} %get-tuple-element.32), channel_id=1, source_target_pairs={{0,1},{1,0},{2,3},{3,2},{4,5},{5,4},{6,7},{7,6},{8,9},{9,8},{10,11... | collective-permute-start | bytes 73736 | tf_op jit(solution)/shard_map/ppermute | solution.py:737
  12.4 4.1 %collective-permute-start.1 = (f32[48,128]{1,0:T(8,128)S(1)}, f32[48,128]{1,0:T(8,128)S(1)}, u32[]{:S(2)}, u32[]{:S(2)}) collective-permute-start(f32[48,128]{1,0:T(8,128)S(1)} %get-tuple-element.33), channel_id=1, source_target_pairs={{0,3},{1,2},{2,1},{3,0},{4,7},{5,6},{6,5},{7,4},{8,11},{9,10},{10,... | collective-permute-start | bytes 73736 | tf_op jit(solution)/shard_map/ppermute | solution.py:737
  14.3 7.7 %copy-start.1 = (f32[6,64,128]{2,1,0:T(8,128)S(1)}, f32[6,64,128]{2,1,0:T(8,128)}, u32[]{:S(2)}) copy-start(f32[6,64,128]{2,1,0:T(8,128)} %density.1) | copy-start | bytes 589828
  16.5 14.6 %copy-start = (f32[6,64,128]{2,1,0:T(8,128)S(1)}, f32[6,64,128]{2,1,0:T(8,128)}, u32[]{:S(2)}) copy-start(f32[6,64,128]{2,1,0:T(8,128)} %potential.1) | copy-start | bytes 589828
  16.9 9.4 %collective-permute-start.7 = (f32[6,64,128]{2,1,0:T(8,128)S(1)}, f32[6,64,128]{2,1,0:T(8,128)S(1)}, u32[]{:S(2)}, u32[]{:S(2)}) collective-permute-start(f32[6,64,128]{2,1,0:T(8,128)S(1)} %shard_map.80.vector.block.prior.v0), channel_id=1, source_target_pairs={{0,252},{4,8},{8,4},{12,16},{16,12},{20,24},{24,20},{28,32},{32,28... | collective-permute-start | bytes 589832 | tf_op jit(solution)/shard_map/ppermute | solution.py:732
  17.0 9.3 %collective-permute-start.6 = (f32[6,64,128]{2,1,0:T(8,128)S(1)}, f32[6,64,128]{2,1,0:T(8,128)S(1)}, u32[]{:S(2)}, u32[]{:S(2)}) collective-permute-start(f32[6,64,128]{2,1,0:T(8,128)S(1)} %shard_map.80.vector.block.prior.v0), channel_id=1, source_target_pairs={{0,4},{4,0},{8,12},{12,8},{16,20},{20,16},{24,28},{28,24},{32,36},... | collective-permute-start | bytes 589832 | tf_op jit(solution)/shard_map/ppermute | solution.py:733
  18.7 3.3 %collective-permute-start.4 = (f32[24,128]{1,0:T(8,128)S(1)}, f32[24,128]{1,0:T(8,128)S(1)}, u32[]{:S(2)}, u32[]{:S(2)}) collective-permute-start(f32[24,128]{1,0:T(8,128)S(1)} %get-tuple-element.34), channel_id=1, source_target_pairs={{0,1},{1,0},{2,3},{3,2},{4,5},{5,4},{6,7},{7,6},{8,9},{9,8},{10,11... | collective-permute-start | bytes 36872 | tf_op jit(solution)/shard_map/ppermute | solution.py:737
  20.1 5.9 %collective-permute-start.5 = (f32[24,128]{1,0:T(8,128)S(1)}, f32[24,128]{1,0:T(8,128)S(1)}, u32[]{:S(2)}, u32[]{:S(2)}) collective-permute-start(f32[24,128]{1,0:T(8,128)S(1)} %get-tuple-element.35), channel_id=1, source_target_pairs={{0,3},{1,2},{2,1},{3,0},{4,7},{5,6},{6,5},{7,4},{8,11},{9,10},{10,... | collective-permute-start | bytes 36872 | tf_op jit(solution)/shard_map/ppermute | solution.py:737
  22.0 7.3 %collective-permute-start.9 = (f32[6,64,128]{2,1,0:T(8,128)S(1)}, f32[6,64,128]{2,1,0:T(8,128)S(1)}, u32[]{:S(2)}, u32[]{:S(2)}) collective-permute-start(f32[6,64,128]{2,1,0:T(8,128)S(1)} %copy-done.1), channel_id=1, source_target_pairs={{0,252},{4,8},{8,4},{12,16},{16,12},{20,24},{24,20},{28,32},{32,28... | collective-permute-start | bytes 589832 | tf_op jit(solution)/shard_map/ppermute | solution.py:732
  22.0 9.0 %collective-permute-start.8 = (f32[6,64,128]{2,1,0:T(8,128)S(1)}, f32[6,64,128]{2,1,0:T(8,128)S(1)}, u32[]{:S(2)}, u32[]{:S(2)}) collective-permute-start(f32[6,64,128]{2,1,0:T(8,128)S(1)} %copy-done.1), channel_id=1, source_target_pairs={{0,4},{4,0},{8,12},{12,8},{16,20},{20,16},{24,28},{28,24},{32,36},... | collective-permute-start | bytes 589832 | tf_op jit(solution)/shard_map/ppermute | solution.py:733
  26.5 7.6 %collective-permute-start.13 = (f32[6,64,128]{2,1,0:T(8,128)S(1)}, f32[6,64,128]{2,1,0:T(8,128)S(1)}, u32[]{:S(2)}, u32[]{:S(2)}) collective-permute-start(f32[6,64,128]{2,1,0:T(8,128)S(1)} %shard_map.84.vector.block.prior.v1), channel_id=1, source_target_pairs={{0,252},{4,8},{8,4},{12,16},{16,12},{20,24},{24,20},{28,32},{32,28... | collective-permute-start | bytes 589832 | tf_op jit(solution)/shard_map/ppermute | solution.py:732
  26.6 7.5 %collective-permute-start.12 = (f32[6,64,128]{2,1,0:T(8,128)S(1)}, f32[6,64,128]{2,1,0:T(8,128)S(1)}, u32[]{:S(2)}, u32[]{:S(2)}) collective-permute-start(f32[6,64,128]{2,1,0:T(8,128)S(1)} %shard_map.84.vector.block.prior.v1), channel_id=1, source_target_pairs={{0,4},{4,0},{8,12},{12,8},{16,20},{20,16},{24,28},{28,24},{32,36},... | collective-permute-start | bytes 589832 | tf_op jit(solution)/shard_map/ppermute | solution.py:733
  28.9 4.8 %collective-permute-start.10 = (f32[24,128]{1,0:T(8,128)S(1)}, f32[24,128]{1,0:T(8,128)S(1)}, u32[]{:S(2)}, u32[]{:S(2)}) collective-permute-start(f32[24,128]{1,0:T(8,128)S(1)} %get-tuple-element.40), channel_id=1, source_target_pairs={{0,1},{1,0},{2,3},{3,2},{4,5},{5,4},{6,7},{7,6},{8,9},{9,8},{10,11... | collective-permute-start | bytes 36872 | tf_op jit(solution)/shard_map/ppermute | solution.py:737
  29.3 4.5 %collective-permute-start.11 = (f32[24,128]{1,0:T(8,128)S(1)}, f32[24,128]{1,0:T(8,128)S(1)}, u32[]{:S(2)}, u32[]{:S(2)}) collective-permute-start(f32[24,128]{1,0:T(8,128)S(1)} %get-tuple-element.41), channel_id=1, source_target_pairs={{0,3},{1,2},{2,1},{3,0},{4,7},{5,6},{6,5},{7,4},{8,11},{9,10},{10,... | collective-permute-start | bytes 36872 | tf_op jit(solution)/shard_map/ppermute | solution.py:737
  34.2 9.6 %collective-permute-start.17 = (f32[6,64,128]{2,1,0:T(8,128)S(1)}, f32[6,64,128]{2,1,0:T(8,128)S(1)}, u32[]{:S(2)}, u32[]{:S(2)}) collective-permute-start(f32[6,64,128]{2,1,0:T(8,128)S(1)} %shard_map.88.vector.block.prior.v2), channel_id=1, source_target_pairs={{0,252},{4,8},{8,4},{12,16},{16,12},{20,24},{24,20},{28,32},{32,28... | collective-permute-start | bytes 589832 | tf_op jit(solution)/shard_map/ppermute | solution.py:732
  35.2 8.6 %collective-permute-start.16 = (f32[6,64,128]{2,1,0:T(8,128)S(1)}, f32[6,64,128]{2,1,0:T(8,128)S(1)}, u32[]{:S(2)}, u32[]{:S(2)}) collective-permute-start(f32[6,64,128]{2,1,0:T(8,128)S(1)} %shard_map.88.vector.block.prior.v2), channel_id=1, source_target_pairs={{0,4},{4,0},{8,12},{12,8},{16,20},{20,16},{24,28},{28,24},{32,36},... | collective-permute-start | bytes 589832 | tf_op jit(solution)/shard_map/ppermute | solution.py:733
  38.9 4.6 %collective-permute-start.14 = (f32[24,128]{1,0:T(8,128)S(1)}, f32[24,128]{1,0:T(8,128)S(1)}, u32[]{:S(2)}, u32[]{:S(2)}) collective-permute-start(f32[24,128]{1,0:T(8,128)S(1)} %get-tuple-element.47), channel_id=1, source_target_pairs={{0,1},{1,0},{2,3},{3,2},{4,5},{5,4},{6,7},{7,6},{8,9},{9,8},{10,11... | collective-permute-start | bytes 36872 | tf_op jit(solution)/shard_map/ppermute | solution.py:737
  39.0 4.5 %collective-permute-start.15 = (f32[24,128]{1,0:T(8,128)S(1)}, f32[24,128]{1,0:T(8,128)S(1)}, u32[]{:S(2)}, u32[]{:S(2)}) collective-permute-start(f32[24,128]{1,0:T(8,128)S(1)} %get-tuple-element.48), channel_id=1, source_target_pairs={{0,3},{1,2},{2,1},{3,0},{4,7},{5,6},{6,5},{7,4},{8,11},{9,10},{10,... | collective-permute-start | bytes 36872 | tf_op jit(solution)/shard_map/ppermute | solution.py:737
  43.9 7.7 %collective-permute-start.18 = (f32[6,32,128]{2,1,0:T(8,128)S(1)}, f32[6,32,128]{2,1,0:T(8,128)S(1)}, u32[]{:S(2)}, u32[]{:S(2)}) collective-permute-start(f32[6,32,128]{2,1,0:T(8,128)S(1)} %get-tuple-element.50), channel_id=1, source_target_pairs={{0,252},{4,8},{8,4},{12,16},{16,12},{20,24},{24,20},{28,32},{32,28... | collective-permute-start | bytes 294920 | tf_op jit(solution)/shard_map/ppermute | solution.py:805
  44.0 7.6 %collective-permute-start.19 = (f32[6,32,128]{2,1,0:T(8,128)S(1)}, f32[6,32,128]{2,1,0:T(8,128)S(1)}, u32[]{:S(2)}, u32[]{:S(2)}) collective-permute-start(f32[6,32,128]{2,1,0:T(8,128)S(1)} %get-tuple-element.51), channel_id=1, source_target_pairs={{0,4},{4,0},{8,12},{12,8},{16,20},{20,16},{24,28},{28,24},{32,36},... | collective-permute-start | bytes 294920 | tf_op jit(solution)/shard_map/ppermute | solution.py:806
  47.4 4.1 %collective-permute-start.20 = (f32[24,128]{1,0:T(8,128)S(1)}, f32[24,128]{1,0:T(8,128)S(1)}, u32[]{:S(2)}, u32[]{:S(2)}) collective-permute-start(f32[24,128]{1,0:T(8,128)S(1)} %shard_map.93), channel_id=1, source_target_pairs={{0,1},{1,2},{2,3},{3,0},{4,5},{5,6},{6,7},{7,4},{8,9},{9,10},{10,1... | collective-permute-start | bytes 36872 | tf_op jit(solution)/shard_map/ppermute | solution.py:808
  48.5 1.2 %collective-permute-start.21 = (f32[1,128]{1,0:T(1,128)S(1)}, f32[1,128]{1,0:T(1,128)S(1)}, u32[]{:S(2)}, u32[]{:S(2)}) collective-permute-start(f32[1,128]{1,0:T(1,128)S(1)} %get-tuple-element.53), channel_id=1, source_target_pairs={{0,4},{4,0},{8,12},{12,8},{16,20},{20,16},{24,28},{28,24},{32,36},... | collective-permute-start | bytes 1544 | tf_op jit(solution)/shard_map/ppermute | solution.py:816

commit v15 on v14

--- a/solution.py
+++ b/solution.py
@@ -409,6 +409,7 @@
     store(rows, 36, field_dots((steps_here,), [density_tile(both)]))
     for copy in copies[FETCHES:]:
         copy.wait()
+    store(rows, 44, gram_dots(changes_here, changes_here, PAIRS))
 
 
 def side_two(vector, inner, ext):
@@ -434,8 +435,7 @@
     by_change = field_dots((changes,), [lifted, slope, rho])
     values = by_step[:8] + by_change[:8] + by_step[16:17] + by_step[8:16] + by_change[8:16] + by_step[17:]
     store(rows, 0, values + by_change[16:])
-    store(rows, 43, gram_dots(changes, changes, PAIRS))
-    store(rows, 79, gram_dots(steps, changes, CROSS_PAIRS[32:]))
+    store(rows, 43, gram_dots(steps, changes, CROSS_PAIRS[32:]))
     store_moments([(prior, vector), (vector, vector)], moments)
 
     table[...] = jnp.zeros_like(table)
@@ -449,9 +449,9 @@
             table[at : at + count - before, :] = ref[start + before : start + count, :]
 
     put(ROW_GRAM, r1, 0, 36)
-    put(ROW_GRAM + 36, rows, 43, 36)
+    put(ROW_GRAM + 36, r1, 44, 36)
     put(ROW_GRAM + 72, r3, 34, 32)
-    put(ROW_GRAM + 104, rows, 79, 32)
+    put(ROW_GRAM + 104, rows, 43, 32)
     put(ROW_BASE, r1, 36, 8)
     put(ROW_BASE + 8, rows, 35, 8)
     put(ROW_BASE + 16, rows, 17, 18)
@@ -773,7 +773,7 @@
     stored = hist_steps.shape
     inner, *history, r1 = call(
         side_one,
-        [block, stored, stored, (48, LANES)],
+        [block, stored, stored, (80, LANES)],
         [both, charge, hist_steps, hist_changes],
         [ext, pltpu.SemaphoreType.DMA((2 * FETCHES,))],
         work,
@@ -798,7 +798,7 @@
         side_four,
         [block, (2, LANES)],
         [v1, v2, both, grad, *history, r1, r3, m3],
-        [(112, LANES), (8, LANES), (2 * LANES, LANES), ext],
+        [(80, LANES), (8, LANES), (2 * LANES, LANES), ext],
         work,
     )
     v3, to_near, to_far = advance(-2.0 / SHIFT, inner, halo, ends, last=True)

time: 73 us -> 73.2 us (level)
  transfers between devices with their start and end apart: 22 -> 22, of which waited for: 2 -> 3; matrix products, arithmetic and copies ran while one was open for 0% -> 0% of each run, Pallas kernels for 18% -> 18%
where the time goes in v15:
time: 73.2 us; the launch traced here: 73 us
  starting transfers between devices  34.6 us (47%)
  blocking collectives  18.8 us (26%)
  Pallas kernels  15.8 us (22%)
  waiting for transfers between devices  2.71 us (4%)
  between operations  1.1 us (2%)
    all_to_all x1, blocking collectives, on_device(): lax.all_to_all(outgoing.reshape(devices, 1, LANES), ('blk', 'gz'), 0, 0,...  18.8 us
    ppermute x5, starting transfers between devices, x_halo(): return (lax.ppermute(block, 'blk', swap('blk', 0)), far)  16.6 us
    pallas_call x21, Pallas kernels, call(): pl.pallas_call(kernel, out_shape=shapes, in_specs=[pl.BlockSpec(memory_sp...  15.8 us
    ppermute x4, starting transfers between devices, z_halo(): lax.ppermute(face_b, 'gz', swap('gz', 1))  7.06 us
    ppermute x5, starting transfers between devices, x_halo(): far = lax.ppermute(block, 'blk', swap('blk', 1))  3.7 us
    ppermute x1, starting transfers between devices, on_device(): near = lax.ppermute(to_near, 'blk', swap('blk', 0))  3.69 us
    ppermute x4, starting transfers between devices, z_halo(): lax.ppermute(face_a, 'gz', swap('gz', 0))  3.26 us
    ppermute x1, waiting for transfers between devices, on_device(): z_left = lax.ppermute(upper, 'gz', ring('gz', 1))  1.87 us
  transfers between devices with their start and end apart: 22, of which 3 were waited for; matrix products, arithmetic and copies ran while one was open for 0% of the time, Pallas kernels for 18%

profile of v15, /device:TPU:1, one launch (start us, length us, event | category | flops | bytes accessed | tf_op | source)
XLA Modules:
  0.0 73.0 jit_solution(9103058673828720444)
XLA Ops:
  0.6 2.7 %collective-permute-start.3 = (f32[6,64,128]{2,1,0:T(8,128)}, f32[6,64,128]{2,1,0:T(8,128)S(1)}, u32[]{:S(2)}, u32[]{:S(2)}) collective-permute-start(f32[6,64,128]{2,1,0:T(8,128)} %hartree.1), channel_id=1, source_target_pairs={{0,252},{4,8},{8,4},{12,16},{16,12},{20,24},{24,20},{28,32},{32,28... | collective-permute-start | bytes 589832 | tf_op jit(solution)/shard_map/ppermute | solution.py:732
  3.3 6.4 %collective-permute-start.2 = (f32[6,64,128]{2,1,0:T(8,128)}, f32[6,64,128]{2,1,0:T(8,128)S(1)}, u32[]{:S(2)}, u32[]{:S(2)}) collective-permute-start(f32[6,64,128]{2,1,0:T(8,128)} %hartree.1), channel_id=1, source_target_pairs={{0,4},{4,0},{8,12},{12,8},{16,20},{20,16},{24,28},{28,24},{32,36},... | collective-permute-start | bytes 589832 | tf_op jit(solution)/shard_map/ppermute | solution.py:733
  9.7 1.3 %shard_map.77 = (f32[12,64,128]{2,1,0:T(8,128)S(1)}, f32[6,64,128]{2,1,0:T(8,128)S(1)}, f32[48,128]{1,0:T(8,128)S(1)}, f32[48,128]{1,0:T(8,128)S(1)}) custom-call(f32[6,64,128]{2,1,0:T(8,128)} %hartree.1, f32[6,64,128]{2,1,0:T(8,128)} %density.1, f32[6,64,128]{2,1,0:T(8,128)} %charge.1), custom_call_target="tpu_custom_call" | custom-call | bytes 1228800 | tf_op jit(solution)/shard_map/pallas_call | solution.py:706
  11.0 1.4 %collective-permute-start = (f32[48,128]{1,0:T(8,128)S(1)}, f32[48,128]{1,0:T(8,128)S(1)}, u32[]{:S(2)}, u32[]{:S(2)}) collective-permute-start(f32[48,128]{1,0:T(8,128)S(1)} %get-tuple-element.32), channel_id=1, source_target_pairs={{0,1},{1,0},{2,3},{3,2},{4,5},{5,4},{6,7},{7,6},{8,9},{9,8},{10,11... | collective-permute-start | bytes 73736 | tf_op jit(solution)/shard_map/ppermute | solution.py:737
  12.4 1.9 %collective-permute-start.1 = (f32[48,128]{1,0:T(8,128)S(1)}, f32[48,128]{1,0:T(8,128)S(1)}, u32[]{:S(2)}, u32[]{:S(2)}) collective-permute-start(f32[48,128]{1,0:T(8,128)S(1)} %get-tuple-element.33), channel_id=1, source_target_pairs={{0,3},{1,2},{2,1},{3,0},{4,7},{5,6},{6,5},{7,4},{8,11},{9,10},{10,... | collective-permute-start | bytes 73736 | tf_op jit(solution)/shard_map/ppermute | solution.py:737
  14.3 2.7 %shard_map.78 = (f32[6,64,128]{2,1,0:T(8,128)S(1)}, f32[8,6,64,128]{3,2,1,0:T(8,128)S(1)}, f32[8,6,64,128]{3,2,1,0:T(8,128)S(1)}, f32[80,128]{1,0:T(8,128)S(1)}) custom-call(f32[12,64,128]{2,1,0:T(8,128)S(1)} %get-tuple-element.29.both, f32[6,64,128]{2,1,0:T(8,128)S(1)} %get-tuple-element.30.charge, f32[8,6,64,128]{3,2,1,0:T(8,128)} %steps.1, ...), custom_call_target="tpu_custom_call" | custom-call | flops 14745600 | bytes 7118848 | tf_op jit(solution)/shard_map/pallas_call | solution.py:706
  17.0 0.0 collective-permute-done.z_first
  17.0 0.0 copy-start
  17.0 0.3 shard_map.79.inner
  17.3 0.1 shard_map.80.vector.block.prior.v0
  17.5 0.1 collective-permute-start.7
  17.6 1.0 %collective-permute-start.6 = (f32[6,64,128]{2,1,0:T(8,128)S(1)}, f32[6,64,128]{2,1,0:T(8,128)S(1)}, u32[]{:S(2)}, u32[]{:S(2)}) collective-permute-start(f32[6,64,128]{2,1,0:T(8,128)S(1)} %shard_map.80.vector.block.prior.v0), channel_id=1, source_target_pairs={{0,4},{4,0},{8,12},{12,8},{16,20},{20,16},{24,28},{28,24},{32,36},... | collective-permute-start | bytes 589832 | tf_op jit(solution)/shard_map/ppermute | solution.py:733
  18.5 0.2 shard_map.82
  18.7 1.4 %collective-permute-start.4 = (f32[24,128]{1,0:T(8,128)S(1)}, f32[24,128]{1,0:T(8,128)S(1)}, u32[]{:S(2)}, u32[]{:S(2)}) collective-permute-start(f32[24,128]{1,0:T(8,128)S(1)} %get-tuple-element.34), channel_id=1, source_target_pairs={{0,1},{1,0},{2,3},{3,2},{4,5},{5,4},{6,7},{7,6},{8,9},{9,8},{10,11... | collective-permute-start | bytes 36872 | tf_op jit(solution)/shard_map/ppermute | solution.py:737
  20.1 1.9 %collective-permute-start.5 = (f32[24,128]{1,0:T(8,128)S(1)}, f32[24,128]{1,0:T(8,128)S(1)}, u32[]{:S(2)}, u32[]{:S(2)}) collective-permute-start(f32[24,128]{1,0:T(8,128)S(1)} %get-tuple-element.35), channel_id=1, source_target_pairs={{0,3},{1,2},{2,1},{3,0},{4,7},{5,6},{6,5},{7,4},{8,11},{9,10},{10,... | collective-permute-start | bytes 36872 | tf_op jit(solution)/shard_map/ppermute | solution.py:737
  22.0 3.6 %collective-permute-start.8 = (f32[6,64,128]{2,1,0:T(8,128)S(1)}, f32[6,64,128]{2,1,0:T(8,128)S(1)}, u32[]{:S(2)}, u32[]{:S(2)}) collective-permute-start(f32[6,64,128]{2,1,0:T(8,128)S(1)} %copy-done.1), channel_id=1, source_target_pairs={{0,4},{4,0},{8,12},{12,8},{16,20},{20,16},{24,28},{28,24},{32,36},... | collective-permute-start | bytes 589832 | tf_op jit(solution)/shard_map/ppermute | solution.py:733
  25.6 0.4 shard_map.81.inner
  26.0 0.3 shard_map.83.inner
  26.3 0.1 shard_map.84.vector.block.prior.v1
  26.5 0.1 collective-permute-start.13
  26.6 2.2 %collective-permute-start.12 = (f32[6,64,128]{2,1,0:T(8,128)S(1)}, f32[6,64,128]{2,1,0:T(8,128)S(1)}, u32[]{:S(2)}, u32[]{:S(2)}) collective-permute-start(f32[6,64,128]{2,1,0:T(8,128)S(1)} %shard_map.84.vector.block.prior.v1), channel_id=1, source_target_pairs={{0,4},{4,0},{8,12},{12,8},{16,20},{20,16},{24,28},{28,24},{32,36},... | collective-permute-start | bytes 589832 | tf_op jit(solution)/shard_map/ppermute | solution.py:733
  28.8 0.2 shard_map.86
  28.9 0.4 collective-permute-start.10
  29.3 1.7 %collective-permute-start.11 = (f32[24,128]{1,0:T(8,128)S(1)}, f32[24,128]{1,0:T(8,128)S(1)}, u32[]{:S(2)}, u32[]{:S(2)}) collective-permute-start(f32[24,128]{1,0:T(8,128)S(1)} %get-tuple-element.41), channel_id=1, source_target_pairs={{0,3},{1,2},{2,1},{3,0},{4,7},{5,6},{6,5},{7,4},{8,11},{9,10},{10,... | collective-permute-start | bytes 36872 | tf_op jit(solution)/shard_map/ppermute | solution.py:737
  31.0 2.7 %shard_map.85 = (f32[6,64,128]{2,1,0:T(8,128)S(1)}, f32[6,64,128]{2,1,0:T(8,128)S(1)}, f32[72,128]{1,0:T(8,128)S(1)}, f32[8,128]{1,0:T(8,128)S(1)}) custom-call(f32[6,64,128]{2,1,0:T(8,128)S(1)} %shard_map.80.vector.block.prior.v0, f32[6,64,128]{2,1,0:T(8,128)S(1)} %shard_map.84.vector.block.prior.v1, f32[12,64,128]{2,1,0:T(8,128)S(1)} %get-tuple-element.29.both, ...), custom_call_target="tpu_custom_call" | custom-call | flops 14745600 | bytes 5005312 | tf_op jit(solution)/shard_map/pallas_call | solution.py:706
  33.8 0.3 shard_map.87.inner
  34.1 0.3 shard_map.88.vector.block.prior.v2
  34.4 0.8 %collective-permute-start.17 = (f32[6,64,128]{2,1,0:T(8,128)S(1)}, f32[6,64,128]{2,1,0:T(8,128)S(1)}, u32[]{:S(2)}, u32[]{:S(2)}) collective-permute-start(f32[6,64,128]{2,1,0:T(8,128)S(1)} %shard_map.88.vector.block.prior.v2), channel_id=1, source_target_pairs={{0,252},{4,8},{8,4},{12,16},{16,12},{20,24},{24,20},{28,32},{32,28... | collective-permute-start | bytes 589832 | tf_op jit(solution)/shard_map/ppermute | solution.py:732
  35.2 3.5 %collective-permute-start.16 = (f32[6,64,128]{2,1,0:T(8,128)S(1)}, f32[6,64,128]{2,1,0:T(8,128)S(1)}, u32[]{:S(2)}, u32[]{:S(2)}) collective-permute-start(f32[6,64,128]{2,1,0:T(8,128)S(1)} %shard_map.88.vector.block.prior.v2), channel_id=1, source_target_pairs={{0,4},{4,0},{8,12},{12,8},{16,20},{20,16},{24,28},{28,24},{32,36},... | collective-permute-start | bytes 589832 | tf_op jit(solution)/shard_map/ppermute | solution.py:733
  38.7 0.2 shard_map.90
  38.9 0.1 collective-permute-start.14
  39.0 1.6 %collective-permute-start.15 = (f32[24,128]{1,0:T(8,128)S(1)}, f32[24,128]{1,0:T(8,128)S(1)}, u32[]{:S(2)}, u32[]{:S(2)}) collective-permute-start(f32[24,128]{1,0:T(8,128)S(1)} %get-tuple-element.48), channel_id=1, source_target_pairs={{0,3},{1,2},{2,1},{3,0},{4,7},{5,6},{6,5},{7,4},{8,11},{9,10},{10,... | collective-permute-start | bytes 36872 | tf_op jit(solution)/shard_map/ppermute | solution.py:737
  40.5 2.4 %shard_map.89 = (f32[6,64,128]{2,1,0:T(8,128)S(1)}, f32[2,128]{1,0:T(2,128)S(1)}) custom-call(f32[6,64,128]{2,1,0:T(8,128)S(1)} %shard_map.84.vector.block.prior.v1, f32[6,64,128]{2,1,0:T(8,128)S(1)} %shard_map.88.vector.block.prior.v2, f32[12,64,128]{2,1,0:T(8,128)S(1)} %get-tuple-element.29.both, f32[6,64,128]{2,1,0:T(8,128)S(1)} %get-tuple-element.42.grad, ...), custom_call_target="tpu_custom_call" | custom-call | flops 14745600 | bytes 4408320 | tf_op jit(solution)/shard_map/pallas_call | solution.py:706
  42.9 0.2 collective-permute-done.15.z_second
  43.1 0.3 shard_map.91.inner
  43.4 0.1 shard_map.92
  43.5 0.1 collective-permute-start.18
  43.6 3.7 %collective-permute-start.19 = (f32[6,32,128]{2,1,0:T(8,128)S(1)}, f32[6,32,128]{2,1,0:T(8,128)S(1)}, u32[]{:S(2)}, u32[]{:S(2)}) collective-permute-start(f32[6,32,128]{2,1,0:T(8,128)S(1)} %get-tuple-element.51), channel_id=1, source_target_pairs={{0,4},{4,0},{8,12},{12,8},{16,20},{20,16},{24,28},{28,24},{32,36},... | collective-permute-start | bytes 294920 | tf_op jit(solution)/shard_map/ppermute | solution.py:806
  47.3 0.1 shard_map.93
  47.4 0.1 collective-permute-start.20
  47.5 1.0 %shard_map.94 = (f32[1,128]{1,0:T(1,128)S(1)}, f32[1,128]{1,0:T(1,128)S(1)}) custom-call(f32[6,64,128]{2,1,0:T(8,128)S(1)} %shard_map.88.vector.block.prior.v2, f32[6,64,128]{2,1,0:T(8,128)S(1)} %get-tuple-element.54.block.vector.own.v3, f32[12,64,128]{2,1,0:T(8,128)S(1)} %get-tuple-element.29.both, f32[8,6,64,128]{3,2,1,0:T(8,128)S(1)} %get-tuple-element.37.steps, ...), custom_call_target="tpu_custom_call" | custom-call | flops 14745600 | bytes 3934208 | tf_op jit(solution)/shard_map/pallas_call | solution.py:706
  48.5 0.1 collective-permute-start.21
  48.6 0.5 shard_map.95.inner
  49.1 0.6 collective-permute-done.21.taken
  49.7 1.9 %collective-permute-done.20.z_left = f32[24,128]{1,0:T(8,128)S(1)} collective-permute-done((f32[24,128]{1,0:T(8,128)S(1)}, f32[24,128]{1,0:T(8,128)S(1)}, u32[]{:S(2)}, u32[]{:S(2)}) %collective-permute-start.20) | collective-permute-done | bytes 12320 | tf_op jit(solution)/shard_map/ppermute | solution.py:808
  51.6 0.8 %shard_map.96 = f32[256,128]{1,0:T(8,128)S(1)} custom-call(f32[6,64,128]{2,1,0:T(8,128)S(1)} %get-tuple-element.54.block.vector.own.v3, f32[6,32,128]{2,1,0:T(8,128)S(1)} %collective-permute-done.18.far, f32[6,32,128]{2,1,0:T(8,128)S(1)} %collective-permute-done.19.near, f32[24,128]{1,0:T(8,128)S(1)} %collective-permute-done.20.z_left, ...), custom_call_target="tpu_custom_call" | custom-call | flops 14745600 | bytes 541696 | tf_op jit(solution)/shard_map/pallas_call | solution.py:706
  52.4 18.8 %all_to_all.5 = f32[256,1,128]{2,1,0:T(1,128)S(1)} all-to-all(f32[256,1,128]{2,1,0:T(1,128)S(1)} %bitcast.5), channel_id=1, replica_groups=mesh['blk'=64,'gz'=4] {'blk','gz'}, dimensions={0} | all-to-all | bytes 262144 | tf_op jit(solution)/shard_map/all_to_all | solution.py:820
  71.2 1.6 %shard_map.97 = (f32[6,64,128]{2,1,0:T(8,128)}, f32[6,64,128]{2,1,0:T(8,128)}) custom-call(f32[256,128]{1,0:T(8,128)S(1)} %bitcast.4, f32[12,64,128]{2,1,0:T(8,128)S(1)} %get-tuple-element.29.both, f32[6,64,128]{2,1,0:T(8,128)S(1)} %get-tuple-element.42.grad, f32[6,64,128]{2,1,0:T(8,128)S(1)} %shard_map.80.vector.block.prior.v0, ...), custom_call_target="tpu_custom_call" | custom-call | flops 14745600 | bytes 5046272 | tf_op jit(solution)/shard_map/pallas_call | solution.py:706
  (22 shorter events, 0.1 us)
Async XLA Ops:
  0.6 16.7 %collective-permute-start.3 = (f32[6,64,128]{2,1,0:T(8,128)}, f32[6,64,128]{2,1,0:T(8,128)S(1)}, u32[]{:S(2)}, u32[]{:S(2)}) collective-permute-start(f32[6,64,128]{2,1,0:T(8,128)} %hartree.1), channel_id=1, source_target_pairs={{0,252},{4,8},{8,4},{12,16},{16,12},{20,24},{24,20},{28,32},{32,28... | collective-permute-start | bytes 589832 | tf_op jit(solution)/shard_map/ppermute | solution.py:732
  3.3 14.0 %collective-permute-start.2 = (f32[6,64,128]{2,1,0:T(8,128)}, f32[6,64,128]{2,1,0:T(8,128)S(1)}, u32[]{:S(2)}, u32[]{:S(2)}) collective-permute-start(f32[6,64,128]{2,1,0:T(8,128)} %hartree.1), channel_id=1, source_target_pairs={{0,4},{4,0},{8,12},{12,8},{16,20},{20,16},{24,28},{28,24},{32,36},... | collective-permute-start | bytes 589832 | tf_op jit(solution)/shard_map/ppermute | solution.py:733
  11.0 6.0 %collective-permute-start = (f32[48,128]{1,0:T(8,128)S(1)}, f32[48,128]{1,0:T(8,128)S(1)}, u32[]{:S(2)}, u32[]{:S(2)}) collective-permute-start(f32[48,128]{1,0:T(8,128)S(1)} %get-tuple-element.32), channel_id=1, source_target_pairs={{0,1},{1,0},{2,3},{3,2},{4,5},{5,4},{6,7},{7,6},{8,9},{9,8},{10,11... | collective-permute-start | bytes 73736 | tf_op jit(solution)/shard_map/ppermute | solution.py:737
  12.4 4.6 %collective-permute-start.1 = (f32[48,128]{1,0:T(8,128)S(1)}, f32[48,128]{1,0:T(8,128)S(1)}, u32[]{:S(2)}, u32[]{:S(2)}) collective-permute-start(f32[48,128]{1,0:T(8,128)S(1)} %get-tuple-element.33), channel_id=1, source_target_pairs={{0,3},{1,2},{2,1},{3,0},{4,7},{5,6},{6,5},{7,4},{8,11},{9,10},{10,... | collective-permute-start | bytes 73736 | tf_op jit(solution)/shard_map/ppermute | solution.py:737
  14.3 7.7 %copy-start.1 = (f32[6,64,128]{2,1,0:T(8,128)S(1)}, f32[6,64,128]{2,1,0:T(8,128)}, u32[]{:S(2)}) copy-start(f32[6,64,128]{2,1,0:T(8,128)} %density.1) | copy-start | bytes 589828
  17.0 14.0 %copy-start = (f32[6,64,128]{2,1,0:T(8,128)S(1)}, f32[6,64,128]{2,1,0:T(8,128)}, u32[]{:S(2)}) copy-start(f32[6,64,128]{2,1,0:T(8,128)} %potential.1) | copy-start | bytes 589828
  17.5 8.8 %collective-permute-start.7 = (f32[6,64,128]{2,1,0:T(8,128)S(1)}, f32[6,64,128]{2,1,0:T(8,128)S(1)}, u32[]{:S(2)}, u32[]{:S(2)}) collective-permute-start(f32[6,64,128]{2,1,0:T(8,128)S(1)} %shard_map.80.vector.block.prior.v0), channel_id=1, source_target_pairs={{0,252},{4,8},{8,4},{12,16},{16,12},{20,24},{24,20},{28,32},{32,28... | collective-permute-start | bytes 589832 | tf_op jit(solution)/shard_map/ppermute | solution.py:732
  17.6 8.8 %collective-permute-start.6 = (f32[6,64,128]{2,1,0:T(8,128)S(1)}, f32[6,64,128]{2,1,0:T(8,128)S(1)}, u32[]{:S(2)}, u32[]{:S(2)}) collective-permute-start(f32[6,64,128]{2,1,0:T(8,128)S(1)} %shard_map.80.vector.block.prior.v0), channel_id=1, source_target_pairs={{0,4},{4,0},{8,12},{12,8},{16,20},{20,16},{24,28},{28,24},{32,36},... | collective-permute-start | bytes 589832 | tf_op jit(solution)/shard_map/ppermute | solution.py:733
  18.7 3.3 %collective-permute-start.4 = (f32[24,128]{1,0:T(8,128)S(1)}, f32[24,128]{1,0:T(8,128)S(1)}, u32[]{:S(2)}, u32[]{:S(2)}) collective-permute-start(f32[24,128]{1,0:T(8,128)S(1)} %get-tuple-element.34), channel_id=1, source_target_pairs={{0,1},{1,0},{2,3},{3,2},{4,5},{5,4},{6,7},{7,6},{8,9},{9,8},{10,11... | collective-permute-start | bytes 36872 | tf_op jit(solution)/shard_map/ppermute | solution.py:737
  20.1 5.9 %collective-permute-start.5 = (f32[24,128]{1,0:T(8,128)S(1)}, f32[24,128]{1,0:T(8,128)S(1)}, u32[]{:S(2)}, u32[]{:S(2)}) collective-permute-start(f32[24,128]{1,0:T(8,128)S(1)} %get-tuple-element.35), channel_id=1, source_target_pairs={{0,3},{1,2},{2,1},{3,0},{4,7},{5,6},{6,5},{7,4},{8,11},{9,10},{10,... | collective-permute-start | bytes 36872 | tf_op jit(solution)/shard_map/ppermute | solution.py:737
  22.0 7.3 %collective-permute-start.9 = (f32[6,64,128]{2,1,0:T(8,128)S(1)}, f32[6,64,128]{2,1,0:T(8,128)S(1)}, u32[]{:S(2)}, u32[]{:S(2)}) collective-permute-start(f32[6,64,128]{2,1,0:T(8,128)S(1)} %copy-done.1), channel_id=1, source_target_pairs={{0,252},{4,8},{8,4},{12,16},{16,12},{20,24},{24,20},{28,32},{32,28... | collective-permute-start | bytes 589832 | tf_op jit(solution)/shard_map/ppermute | solution.py:732
  22.0 9.0 %collective-permute-start.8 = (f32[6,64,128]{2,1,0:T(8,128)S(1)}, f32[6,64,128]{2,1,0:T(8,128)S(1)}, u32[]{:S(2)}, u32[]{:S(2)}) collective-permute-start(f32[6,64,128]{2,1,0:T(8,128)S(1)} %copy-done.1), channel_id=1, source_target_pairs={{0,4},{4,0},{8,12},{12,8},{16,20},{20,16},{24,28},{28,24},{32,36},... | collective-permute-start | bytes 589832 | tf_op jit(solution)/shard_map/ppermute | solution.py:733
  26.5 7.6 %collective-permute-start.13 = (f32[6,64,128]{2,1,0:T(8,128)S(1)}, f32[6,64,128]{2,1,0:T(8,128)S(1)}, u32[]{:S(2)}, u32[]{:S(2)}) collective-permute-start(f32[6,64,128]{2,1,0:T(8,128)S(1)} %shard_map.84.vector.block.prior.v1), channel_id=1, source_target_pairs={{0,252},{4,8},{8,4},{12,16},{16,12},{20,24},{24,20},{28,32},{32,28... | collective-permute-start | bytes 589832 | tf_op jit(solution)/shard_map/ppermute | solution.py:732
  26.6 7.5 %collective-permute-start.12 = (f32[6,64,128]{2,1,0:T(8,128)S(1)}, f32[6,64,128]{2,1,0:T(8,128)S(1)}, u32[]{:S(2)}, u32[]{:S(2)}) collective-permute-start(f32[6,64,128]{2,1,0:T(8,128)S(1)} %shard_map.84.vector.block.prior.v1), channel_id=1, source_target_pairs={{0,4},{4,0},{8,12},{12,8},{16,20},{20,16},{24,28},{28,24},{32,36},... | collective-permute-start | bytes 589832 | tf_op jit(solution)/shard_map/ppermute | solution.py:733
  28.9 4.8 %collective-permute-start.10 = (f32[24,128]{1,0:T(8,128)S(1)}, f32[24,128]{1,0:T(8,128)S(1)}, u32[]{:S(2)}, u32[]{:S(2)}) collective-permute-start(f32[24,128]{1,0:T(8,128)S(1)} %get-tuple-element.40), channel_id=1, source_target_pairs={{0,1},{1,0},{2,3},{3,2},{4,5},{5,4},{6,7},{7,6},{8,9},{9,8},{10,11... | collective-permute-start | bytes 36872 | tf_op jit(solution)/shard_map/ppermute | solution.py:737
  29.3 4.4 %collective-permute-start.11 = (f32[24,128]{1,0:T(8,128)S(1)}, f32[24,128]{1,0:T(8,128)S(1)}, u32[]{:S(2)}, u32[]{:S(2)}) collective-permute-start(f32[24,128]{1,0:T(8,128)S(1)} %get-tuple-element.41), channel_id=1, source_target_pairs={{0,3},{1,2},{2,1},{3,0},{4,7},{5,6},{6,5},{7,4},{8,11},{9,10},{10,... | collective-permute-start | bytes 36872 | tf_op jit(solution)/shard_map/ppermute | solution.py:737
  34.4 9.0 %collective-permute-start.17 = (f32[6,64,128]{2,1,0:T(8,128)S(1)}, f32[6,64,128]{2,1,0:T(8,128)S(1)}, u32[]{:S(2)}, u32[]{:S(2)}) collective-permute-start(f32[6,64,128]{2,1,0:T(8,128)S(1)} %shard_map.88.vector.block.prior.v2), channel_id=1, source_target_pairs={{0,252},{4,8},{8,4},{12,16},{16,12},{20,24},{24,20},{28,32},{32,28... | collective-permute-start | bytes 589832 | tf_op jit(solution)/shard_map/ppermute | solution.py:732
  35.2 8.2 %collective-permute-start.16 = (f32[6,64,128]{2,1,0:T(8,128)S(1)}, f32[6,64,128]{2,1,0:T(8,128)S(1)}, u32[]{:S(2)}, u32[]{:S(2)}) collective-permute-start(f32[6,64,128]{2,1,0:T(8,128)S(1)} %shard_map.88.vector.block.prior.v2), channel_id=1, source_target_pairs={{0,4},{4,0},{8,12},{12,8},{16,20},{20,16},{24,28},{28,24},{32,36},... | collective-permute-start | bytes 589832 | tf_op jit(solution)/shard_map/ppermute | solution.py:733
  38.9 4.0 %collective-permute-start.14 = (f32[24,128]{1,0:T(8,128)S(1)}, f32[24,128]{1,0:T(8,128)S(1)}, u32[]{:S(2)}, u32[]{:S(2)}) collective-permute-start(f32[24,128]{1,0:T(8,128)S(1)} %get-tuple-element.47), channel_id=1, source_target_pairs={{0,1},{1,0},{2,3},{3,2},{4,5},{5,4},{6,7},{7,6},{8,9},{9,8},{10,11... | collective-permute-start | bytes 36872 | tf_op jit(solution)/shard_map/ppermute | solution.py:737
  39.0 4.1 %collective-permute-start.15 = (f32[24,128]{1,0:T(8,128)S(1)}, f32[24,128]{1,0:T(8,128)S(1)}, u32[]{:S(2)}, u32[]{:S(2)}) collective-permute-start(f32[24,128]{1,0:T(8,128)S(1)} %get-tuple-element.48), channel_id=1, source_target_pairs={{0,3},{1,2},{2,1},{3,0},{4,7},{5,6},{6,5},{7,4},{8,11},{9,10},{10,... | collective-permute-start | bytes 36872 | tf_op jit(solution)/shard_map/ppermute | solution.py:737
  43.5 8.0 %collective-permute-start.18 = (f32[6,32,128]{2,1,0:T(8,128)S(1)}, f32[6,32,128]{2,1,0:T(8,128)S(1)}, u32[]{:S(2)}, u32[]{:S(2)}) collective-permute-start(f32[6,32,128]{2,1,0:T(8,128)S(1)} %get-tuple-element.50), channel_id=1, source_target_pairs={{0,252},{4,8},{8,4},{12,16},{16,12},{20,24},{24,20},{28,32},{32,28... | collective-permute-start | bytes 294920 | tf_op jit(solution)/shard_map/ppermute | solution.py:805
  43.6 7.9 %collective-permute-start.19 = (f32[6,32,128]{2,1,0:T(8,128)S(1)}, f32[6,32,128]{2,1,0:T(8,128)S(1)}, u32[]{:S(2)}, u32[]{:S(2)}) collective-permute-start(f32[6,32,128]{2,1,0:T(8,128)S(1)} %get-tuple-element.51), channel_id=1, source_target_pairs={{0,4},{4,0},{8,12},{12,8},{16,20},{20,16},{24,28},{28,24},{32,36},... | collective-permute-start | bytes 294920 | tf_op jit(solution)/shard_map/ppermute | solution.py:806
  47.4 4.1 %collective-permute-start.20 = (f32[24,128]{1,0:T(8,128)S(1)}, f32[24,128]{1,0:T(8,128)S(1)}, u32[]{:S(2)}, u32[]{:S(2)}) collective-permute-start(f32[24,128]{1,0:T(8,128)S(1)} %shard_map.93), channel_id=1, source_target_pairs={{0,1},{1,2},{2,3},{3,0},{4,5},{5,6},{6,7},{7,4},{8,9},{9,10},{10,1... | collective-permute-start | bytes 36872 | tf_op jit(solution)/shard_map/ppermute | solution.py:808
  48.5 1.2 %collective-permute-start.21 = (f32[1,128]{1,0:T(1,128)S(1)}, f32[1,128]{1,0:T(1,128)S(1)}, u32[]{:S(2)}, u32[]{:S(2)}) collective-permute-start(f32[1,128]{1,0:T(1,128)S(1)} %get-tuple-element.53), channel_id=1, source_target_pairs={{0,4},{4,0},{8,12},{12,8},{16,20},{20,16},{24,28},{28,24},{32,36},... | collective-permute-start | bytes 1544 | tf_op jit(solution)/shard_map/ppermute | solution.py:816

commit v16 on v15

--- a/solution.py
+++ b/solution.py
@@ -409,7 +409,7 @@
     store(rows, 36, field_dots((steps_here,), [density_tile(both)]))
     for copy in copies[FETCHES:]:
         copy.wait()
-    store(rows, 44, gram_dots(changes_here, changes_here, PAIRS))
+    store(rows, 44, gram_dots(steps_here, changes_here, CROSS_PAIRS[32:]))
 
 
 def side_two(vector, inner, ext):
@@ -435,7 +435,7 @@
     by_change = field_dots((changes,), [lifted, slope, rho])
     values = by_step[:8] + by_change[:8] + by_step[16:17] + by_step[8:16] + by_change[8:16] + by_step[17:]
     store(rows, 0, values + by_change[16:])
-    store(rows, 43, gram_dots(steps, changes, CROSS_PAIRS[32:]))
+    store(rows, 43, gram_dots(changes, changes, PAIRS))
     store_moments([(prior, vector), (vector, vector)], moments)
 
     table[...] = jnp.zeros_like(table)
@@ -449,9 +449,9 @@
             table[at : at + count - before, :] = ref[start + before : start + count, :]
 
     put(ROW_GRAM, r1, 0, 36)
-    put(ROW_GRAM + 36, r1, 44, 36)
+    put(ROW_GRAM + 36, rows, 43, 36)
     put(ROW_GRAM + 72, r3, 34, 32)
-    put(ROW_GRAM + 104, rows, 43, 32)
+    put(ROW_GRAM + 104, r1, 44, 32)
     put(ROW_BASE, r1, 36, 8)
     put(ROW_BASE + 8, rows, 35, 8)
     put(ROW_BASE + 16, rows, 17, 18)

time: 73.2 us -> 73.1 us (level)
  no operation moved by 1% of the time
where the time goes in v16:
time: 73.1 us; the launch traced here: 73 us
  starting transfers between devices  34.6 us (47%)
  blocking collectives  18.8 us (26%)
  Pallas kernels  15.8 us (22%)
  waiting for transfers between devices  2.66 us (4%)
  between operations  1.1 us (2%)
    all_to_all x1, blocking collectives, on_device(): lax.all_to_all(outgoing.reshape(devices, 1, LANES), ('blk', 'gz'), 0, 0,...  18.8 us
    ppermute x5, starting transfers between devices, x_halo(): return (lax.ppermute(block, 'blk', swap('blk', 0)), far)  16.6 us
    pallas_call x21, Pallas kernels, call(): pl.pallas_call(kernel, out_shape=shapes, in_specs=[pl.BlockSpec(memory_sp...  15.8 us
    ppermute x4, starting transfers between devices, z_halo(): lax.ppermute(face_b, 'gz', swap('gz', 1))  7.11 us
    ppermute x5, starting transfers between devices, x_halo(): far = lax.ppermute(block, 'blk', swap('blk', 1))  3.7 us
    ppermute x1, starting transfers between devices, on_device(): near = lax.ppermute(to_near, 'blk', swap('blk', 0))  3.69 us
    ppermute x4, starting transfers between devices, z_halo(): lax.ppermute(face_a, 'gz', swap('gz', 0))  3.21 us
    ppermute x1, waiting for transfers between devices, on_device(): z_left = lax.ppermute(upper, 'gz', ring('gz', 1))  1.87 us
  transfers between devices with their start and end apart: 22, of which 3 were waited for; matrix products, arithmetic and copies ran while one was open for 0% of the time, Pallas kernels for 18%

profile of v16, /device:TPU:1, one launch (start us, length us, event | category | flops | bytes accessed | tf_op | source)
XLA Modules:
  0.0 73.0 jit_solution(8411546026061441557)
XLA Ops:
  0.6 2.7 %collective-permute-start.3 = (f32[6,64,128]{2,1,0:T(8,128)}, f32[6,64,128]{2,1,0:T(8,128)S(1)}, u32[]{:S(2)}, u32[]{:S(2)}) collective-permute-start(f32[6,64,128]{2,1,0:T(8,128)} %hartree.1), channel_id=1, source_target_pairs={{0,252},{4,8},{8,4},{12,16},{16,12},{20,24},{24,20},{28,32},{32,28... | collective-permute-start | bytes 589832 | tf_op jit(solution)/shard_map/ppermute | solution.py:732
  3.3 6.4 %collective-permute-start.2 = (f32[6,64,128]{2,1,0:T(8,128)}, f32[6,64,128]{2,1,0:T(8,128)S(1)}, u32[]{:S(2)}, u32[]{:S(2)}) collective-permute-start(f32[6,64,128]{2,1,0:T(8,128)} %hartree.1), channel_id=1, source_target_pairs={{0,4},{4,0},{8,12},{12,8},{16,20},{20,16},{24,28},{28,24},{32,36},... | collective-permute-start | bytes 589832 | tf_op jit(solution)/shard_map/ppermute | solution.py:733
  9.7 1.3 %shard_map.77 = (f32[12,64,128]{2,1,0:T(8,128)S(1)}, f32[6,64,128]{2,1,0:T(8,128)S(1)}, f32[48,128]{1,0:T(8,128)S(1)}, f32[48,128]{1,0:T(8,128)S(1)}) custom-call(f32[6,64,128]{2,1,0:T(8,128)} %hartree.1, f32[6,64,128]{2,1,0:T(8,128)} %density.1, f32[6,64,128]{2,1,0:T(8,128)} %charge.1), custom_call_target="tpu_custom_call" | custom-call | bytes 1228800 | tf_op jit(solution)/shard_map/pallas_call | solution.py:706
  11.0 1.4 %collective-permute-start = (f32[48,128]{1,0:T(8,128)S(1)}, f32[48,128]{1,0:T(8,128)S(1)}, u32[]{:S(2)}, u32[]{:S(2)}) collective-permute-start(f32[48,128]{1,0:T(8,128)S(1)} %get-tuple-element.32), channel_id=1, source_target_pairs={{0,1},{1,0},{2,3},{3,2},{4,5},{5,4},{6,7},{7,6},{8,9},{9,8},{10,11... | collective-permute-start | bytes 73736 | tf_op jit(solution)/shard_map/ppermute | solution.py:737
  12.4 1.9 %collective-permute-start.1 = (f32[48,128]{1,0:T(8,128)S(1)}, f32[48,128]{1,0:T(8,128)S(1)}, u32[]{:S(2)}, u32[]{:S(2)}) collective-permute-start(f32[48,128]{1,0:T(8,128)S(1)} %get-tuple-element.33), channel_id=1, source_target_pairs={{0,3},{1,2},{2,1},{3,0},{4,7},{5,6},{6,5},{7,4},{8,11},{9,10},{10,... | collective-permute-start | bytes 73736 | tf_op jit(solution)/shard_map/ppermute | solution.py:737
  14.3 2.7 %shard_map.78 = (f32[6,64,128]{2,1,0:T(8,128)S(1)}, f32[8,6,64,128]{3,2,1,0:T(8,128)S(1)}, f32[8,6,64,128]{3,2,1,0:T(8,128)S(1)}, f32[80,128]{1,0:T(8,128)S(1)}) custom-call(f32[12,64,128]{2,1,0:T(8,128)S(1)} %get-tuple-element.29.both, f32[6,64,128]{2,1,0:T(8,128)S(1)} %get-tuple-element.30.charge, f32[8,6,64,128]{3,2,1,0:T(8,128)} %steps.1, ...), custom_call_target="tpu_custom_call" | custom-call | flops 14745600 | bytes 7118848 | tf_op jit(solution)/shard_map/pallas_call | solution.py:706
  17.0 0.0 collective-permute-done.z_first
  17.0 0.0 copy-start
  17.0 0.3 shard_map.79.inner
  17.3 0.1 shard_map.80.vector.block.prior.v0
  17.4 0.1 collective-permute-start.7
  17.5 1.0 %collective-permute-start.6 = (f32[6,64,128]{2,1,0:T(8,128)S(1)}, f32[6,64,128]{2,1,0:T(8,128)S(1)}, u32[]{:S(2)}, u32[]{:S(2)}) collective-permute-start(f32[6,64,128]{2,1,0:T(8,128)S(1)} %shard_map.80.vector.block.prior.v0), channel_id=1, source_target_pairs={{0,4},{4,0},{8,12},{12,8},{16,20},{20,16},{24,28},{28,24},{32,36},... | collective-permute-start | bytes 589832 | tf_op jit(solution)/shard_map/ppermute | solution.py:733
  18.5 0.2 shard_map.82
  18.7 1.4 %collective-permute-start.4 = (f32[24,128]{1,0:T(8,128)S(1)}, f32[24,128]{1,0:T(8,128)S(1)}, u32[]{:S(2)}, u32[]{:S(2)}) collective-permute-start(f32[24,128]{1,0:T(8,128)S(1)} %get-tuple-element.34), channel_id=1, source_target_pairs={{0,1},{1,0},{2,3},{3,2},{4,5},{5,4},{6,7},{7,6},{8,9},{9,8},{10,11... | collective-permute-start | bytes 36872 | tf_op jit(solution)/shard_map/ppermute | solution.py:737
  20.1 1.9 %collective-permute-start.5 = (f32[24,128]{1,0:T(8,128)S(1)}, f32[24,128]{1,0:T(8,128)S(1)}, u32[]{:S(2)}, u32[]{:S(2)}) collective-permute-start(f32[24,128]{1,0:T(8,128)S(1)} %get-tuple-element.35), channel_id=1, source_target_pairs={{0,3},{1,2},{2,1},{3,0},{4,7},{5,6},{6,5},{7,4},{8,11},{9,10},{10,... | collective-permute-start | bytes 36872 | tf_op jit(solution)/shard_map/ppermute | solution.py:737
  22.0 3.6 %collective-permute-start.8 = (f32[6,64,128]{2,1,0:T(8,128)S(1)}, f32[6,64,128]{2,1,0:T(8,128)S(1)}, u32[]{:S(2)}, u32[]{:S(2)}) collective-permute-start(f32[6,64,128]{2,1,0:T(8,128)S(1)} %copy-done.1), channel_id=1, source_target_pairs={{0,4},{4,0},{8,12},{12,8},{16,20},{20,16},{24,28},{28,24},{32,36},... | collective-permute-start | bytes 589832 | tf_op jit(solution)/shard_map/ppermute | solution.py:733
  25.6 0.4 shard_map.81.inner
  26.0 0.3 shard_map.83.inner
  26.3 0.1 shard_map.84.vector.block.prior.v1
  26.5 0.1 collective-permute-start.13
  26.6 2.2 %collective-permute-start.12 = (f32[6,64,128]{2,1,0:T(8,128)S(1)}, f32[6,64,128]{2,1,0:T(8,128)S(1)}, u32[]{:S(2)}, u32[]{:S(2)}) collective-permute-start(f32[6,64,128]{2,1,0:T(8,128)S(1)} %shard_map.84.vector.block.prior.v1), channel_id=1, source_target_pairs={{0,4},{4,0},{8,12},{12,8},{16,20},{20,16},{24,28},{28,24},{32,36},... | collective-permute-start | bytes 589832 | tf_op jit(solution)/shard_map/ppermute | solution.py:733
  28.8 0.2 shard_map.86
  28.9 0.4 collective-permute-start.10
  29.3 1.7 %collective-permute-start.11 = (f32[24,128]{1,0:T(8,128)S(1)}, f32[24,128]{1,0:T(8,128)S(1)}, u32[]{:S(2)}, u32[]{:S(2)}) collective-permute-start(f32[24,128]{1,0:T(8,128)S(1)} %get-tuple-element.41), channel_id=1, source_target_pairs={{0,3},{1,2},{2,1},{3,0},{4,7},{5,6},{6,5},{7,4},{8,11},{9,10},{10,... | collective-permute-start | bytes 36872 | tf_op jit(solution)/shard_map/ppermute | solution.py:737
  31.0 2.7 %shard_map.85 = (f32[6,64,128]{2,1,0:T(8,128)S(1)}, f32[6,64,128]{2,1,0:T(8,128)S(1)}, f32[72,128]{1,0:T(8,128)S(1)}, f32[8,128]{1,0:T(8,128)S(1)}) custom-call(f32[6,64,128]{2,1,0:T(8,128)S(1)} %shard_map.80.vector.block.prior.v0, f32[6,64,128]{2,1,0:T(8,128)S(1)} %shard_map.84.vector.block.prior.v1, f32[12,64,128]{2,1,0:T(8,128)S(1)} %get-tuple-element.29.both, ...), custom_call_target="tpu_custom_call" | custom-call | flops 14745600 | bytes 5005312 | tf_op jit(solution)/shard_map/pallas_call | solution.py:706
  33.8 0.3 shard_map.87.inner
  34.1 0.3 shard_map.88.vector.block.prior.v2
  34.4 0.8 %collective-permute-start.17 = (f32[6,64,128]{2,1,0:T(8,128)S(1)}, f32[6,64,128]{2,1,0:T(8,128)S(1)}, u32[]{:S(2)}, u32[]{:S(2)}) collective-permute-start(f32[6,64,128]{2,1,0:T(8,128)S(1)} %shard_map.88.vector.block.prior.v2), channel_id=1, source_target_pairs={{0,252},{4,8},{8,4},{12,16},{16,12},{20,24},{24,20},{28,32},{32,28... | collective-permute-start | bytes 589832 | tf_op jit(solution)/shard_map/ppermute | solution.py:732
  35.2 3.5 %collective-permute-start.16 = (f32[6,64,128]{2,1,0:T(8,128)S(1)}, f32[6,64,128]{2,1,0:T(8,128)S(1)}, u32[]{:S(2)}, u32[]{:S(2)}) collective-permute-start(f32[6,64,128]{2,1,0:T(8,128)S(1)} %shard_map.88.vector.block.prior.v2), channel_id=1, source_target_pairs={{0,4},{4,0},{8,12},{12,8},{16,20},{20,16},{24,28},{28,24},{32,36},... | collective-permute-start | bytes 589832 | tf_op jit(solution)/shard_map/ppermute | solution.py:733
  38.7 0.2 shard_map.90
  38.9 0.1 collective-permute-start.14
  39.0 1.6 %collective-permute-start.15 = (f32[24,128]{1,0:T(8,128)S(1)}, f32[24,128]{1,0:T(8,128)S(1)}, u32[]{:S(2)}, u32[]{:S(2)}) collective-permute-start(f32[24,128]{1,0:T(8,128)S(1)} %get-tuple-element.48), channel_id=1, source_target_pairs={{0,3},{1,2},{2,1},{3,0},{4,7},{5,6},{6,5},{7,4},{8,11},{9,10},{10,... | collective-permute-start | bytes 36872 | tf_op jit(solution)/shard_map/ppermute | solution.py:737
  40.5 2.4 %shard_map.89 = (f32[6,64,128]{2,1,0:T(8,128)S(1)}, f32[2,128]{1,0:T(2,128)S(1)}) custom-call(f32[6,64,128]{2,1,0:T(8,128)S(1)} %shard_map.84.vector.block.prior.v1, f32[6,64,128]{2,1,0:T(8,128)S(1)} %shard_map.88.vector.block.prior.v2, f32[12,64,128]{2,1,0:T(8,128)S(1)} %get-tuple-element.29.both, f32[6,64,128]{2,1,0:T(8,128)S(1)} %get-tuple-element.42.grad, ...), custom_call_target="tpu_custom_call" | custom-call | flops 14745600 | bytes 4408320 | tf_op jit(solution)/shard_map/pallas_call | solution.py:706
  43.0 0.1 collective-permute-done.15.z_second
  43.1 0.3 shard_map.91.inner
  43.4 0.1 shard_map.92
  43.5 0.1 collective-permute-start.18
  43.6 3.7 %collective-permute-start.19 = (f32[6,32,128]{2,1,0:T(8,128)S(1)}, f32[6,32,128]{2,1,0:T(8,128)S(1)}, u32[]{:S(2)}, u32[]{:S(2)}) collective-permute-start(f32[6,32,128]{2,1,0:T(8,128)S(1)} %get-tuple-element.51), channel_id=1, source_target_pairs={{0,4},{4,0},{8,12},{12,8},{16,20},{20,16},{24,28},{28,24},{32,36},... | collective-permute-start | bytes 294920 | tf_op jit(solution)/shard_map/ppermute | solution.py:806
  47.3 0.1 shard_map.93
  47.4 0.1 collective-permute-start.20
  47.5 1.0 %shard_map.94 = (f32[1,128]{1,0:T(1,128)S(1)}, f32[1,128]{1,0:T(1,128)S(1)}) custom-call(f32[6,64,128]{2,1,0:T(8,128)S(1)} %shard_map.88.vector.block.prior.v2, f32[6,64,128]{2,1,0:T(8,128)S(1)} %get-tuple-element.54.block.vector.own.v3, f32[12,64,128]{2,1,0:T(8,128)S(1)} %get-tuple-element.29.both, f32[8,6,64,128]{3,2,1,0:T(8,128)S(1)} %get-tuple-element.37.steps, ...), custom_call_target="tpu_custom_call" | custom-call | flops 14745600 | bytes 3934208 | tf_op jit(solution)/shard_map/pallas_call | solution.py:706
  48.5 0.1 collective-permute-start.21
  48.6 0.5 shard_map.95.inner
  49.1 0.6 collective-permute-done.21.taken
  49.7 1.9 %collective-permute-done.20.z_left = f32[24,128]{1,0:T(8,128)S(1)} collective-permute-done((f32[24,128]{1,0:T(8,128)S(1)}, f32[24,128]{1,0:T(8,128)S(1)}, u32[]{:S(2)}, u32[]{:S(2)}) %collective-permute-start.20) | collective-permute-done | bytes 12320 | tf_op jit(solution)/shard_map/ppermute | solution.py:808
  51.6 0.8 %shard_map.96 = f32[256,128]{1,0:T(8,128)S(1)} custom-call(f32[6,64,128]{2,1,0:T(8,128)S(1)} %get-tuple-element.54.block.vector.own.v3, f32[6,32,128]{2,1,0:T(8,128)S(1)} %collective-permute-done.18.far, f32[6,32,128]{2,1,0:T(8,128)S(1)} %collective-permute-done.19.near, f32[24,128]{1,0:T(8,128)S(1)} %collective-permute-done.20.z_left, ...), custom_call_target="tpu_custom_call" | custom-call | flops 14745600 | bytes 541696 | tf_op jit(solution)/shard_map/pallas_call | solution.py:706
  52.4 18.8 %all_to_all.5 = f32[256,1,128]{2,1,0:T(1,128)S(1)} all-to-all(f32[256,1,128]{2,1,0:T(1,128)S(1)} %bitcast.5), channel_id=1, replica_groups=mesh['blk'=64,'gz'=4] {'blk','gz'}, dimensions={0} | all-to-all | bytes 262144 | tf_op jit(solution)/shard_map/all_to_all | solution.py:820
  71.2 1.6 %shard_map.97 = (f32[6,64,128]{2,1,0:T(8,128)}, f32[6,64,128]{2,1,0:T(8,128)}) custom-call(f32[256,128]{1,0:T(8,128)S(1)} %bitcast.4, f32[12,64,128]{2,1,0:T(8,128)S(1)} %get-tuple-element.29.both, f32[6,64,128]{2,1,0:T(8,128)S(1)} %get-tuple-element.42.grad, f32[6,64,128]{2,1,0:T(8,128)S(1)} %shard_map.80.vector.block.prior.v0, ...), custom_call_target="tpu_custom_call" | custom-call | flops 14745600 | bytes 5046272 | tf_op jit(solution)/shard_map/pallas_call | solution.py:706
  (22 shorter events, 0.1 us)
Async XLA Ops:
  0.6 16.7 %collective-permute-start.3 = (f32[6,64,128]{2,1,0:T(8,128)}, f32[6,64,128]{2,1,0:T(8,128)S(1)}, u32[]{:S(2)}, u32[]{:S(2)}) collective-permute-start(f32[6,64,128]{2,1,0:T(8,128)} %hartree.1), channel_id=1, source_target_pairs={{0,252},{4,8},{8,4},{12,16},{16,12},{20,24},{24,20},{28,32},{32,28... | collective-permute-start | bytes 589832 | tf_op jit(solution)/shard_map/ppermute | solution.py:732
  3.3 14.0 %collective-permute-start.2 = (f32[6,64,128]{2,1,0:T(8,128)}, f32[6,64,128]{2,1,0:T(8,128)S(1)}, u32[]{:S(2)}, u32[]{:S(2)}) collective-permute-start(f32[6,64,128]{2,1,0:T(8,128)} %hartree.1), channel_id=1, source_target_pairs={{0,4},{4,0},{8,12},{12,8},{16,20},{20,16},{24,28},{28,24},{32,36},... | collective-permute-start | bytes 589832 | tf_op jit(solution)/shard_map/ppermute | solution.py:733
  11.0 6.0 %collective-permute-start = (f32[48,128]{1,0:T(8,128)S(1)}, f32[48,128]{1,0:T(8,128)S(1)}, u32[]{:S(2)}, u32[]{:S(2)}) collective-permute-start(f32[48,128]{1,0:T(8,128)S(1)} %get-tuple-element.32), channel_id=1, source_target_pairs={{0,1},{1,0},{2,3},{3,2},{4,5},{5,4},{6,7},{7,6},{8,9},{9,8},{10,11... | collective-permute-start | bytes 73736 | tf_op jit(solution)/shard_map/ppermute | solution.py:737
  12.4 4.6 %collective-permute-start.1 = (f32[48,128]{1,0:T(8,128)S(1)}, f32[48,128]{1,0:T(8,128)S(1)}, u32[]{:S(2)}, u32[]{:S(2)}) collective-permute-start(f32[48,128]{1,0:T(8,128)S(1)} %get-tuple-element.33), channel_id=1, source_target_pairs={{0,3},{1,2},{2,1},{3,0},{4,7},{5,6},{6,5},{7,4},{8,11},{9,10},{10,... | collective-permute-start | bytes 73736 | tf_op jit(solution)/shard_map/ppermute | solution.py:737
  14.3 7.7 %copy-start.1 = (f32[6,64,128]{2,1,0:T(8,128)S(1)}, f32[6,64,128]{2,1,0:T(8,128)}, u32[]{:S(2)}) copy-start(f32[6,64,128]{2,1,0:T(8,128)} %density.1) | copy-start | bytes 589828
  17.0 14.0 %copy-start = (f32[6,64,128]{2,1,0:T(8,128)S(1)}, f32[6,64,128]{2,1,0:T(8,128)}, u32[]{:S(2)}) copy-start(f32[6,64,128]{2,1,0:T(8,128)} %potential.1) | copy-start | bytes 589828
  17.4 8.9 %collective-permute-start.7 = (f32[6,64,128]{2,1,0:T(8,128)S(1)}, f32[6,64,128]{2,1,0:T(8,128)S(1)}, u32[]{:S(2)}, u32[]{:S(2)}) collective-permute-start(f32[6,64,128]{2,1,0:T(8,128)S(1)} %shard_map.80.vector.block.prior.v0), channel_id=1, source_target_pairs={{0,252},{4,8},{8,4},{12,16},{16,12},{20,24},{24,20},{28,32},{32,28... | collective-permute-start | bytes 589832 | tf_op jit(solution)/shard_map/ppermute | solution.py:732
  17.5 8.8 %collective-permute-start.6 = (f32[6,64,128]{2,1,0:T(8,128)S(1)}, f32[6,64,128]{2,1,0:T(8,128)S(1)}, u32[]{:S(2)}, u32[]{:S(2)}) collective-permute-start(f32[6,64,128]{2,1,0:T(8,128)S(1)} %shard_map.80.vector.block.prior.v0), channel_id=1, source_target_pairs={{0,4},{4,0},{8,12},{12,8},{16,20},{20,16},{24,28},{28,24},{32,36},... | collective-permute-start | bytes 589832 | tf_op jit(solution)/shard_map/ppermute | solution.py:733
  18.7 3.3 %collective-permute-start.4 = (f32[24,128]{1,0:T(8,128)S(1)}, f32[24,128]{1,0:T(8,128)S(1)}, u32[]{:S(2)}, u32[]{:S(2)}) collective-permute-start(f32[24,128]{1,0:T(8,128)S(1)} %get-tuple-element.34), channel_id=1, source_target_pairs={{0,1},{1,0},{2,3},{3,2},{4,5},{5,4},{6,7},{7,6},{8,9},{9,8},{10,11... | collective-permute-start | bytes 36872 | tf_op jit(solution)/shard_map/ppermute | solution.py:737
  20.1 5.9 %collective-permute-start.5 = (f32[24,128]{1,0:T(8,128)S(1)}, f32[24,128]{1,0:T(8,128)S(1)}, u32[]{:S(2)}, u32[]{:S(2)}) collective-permute-start(f32[24,128]{1,0:T(8,128)S(1)} %get-tuple-element.35), channel_id=1, source_target_pairs={{0,3},{1,2},{2,1},{3,0},{4,7},{5,6},{6,5},{7,4},{8,11},{9,10},{10,... | collective-permute-start | bytes 36872 | tf_op jit(solution)/shard_map/ppermute | solution.py:737
  22.0 7.3 %collective-permute-start.9 = (f32[6,64,128]{2,1,0:T(8,128)S(1)}, f32[6,64,128]{2,1,0:T(8,128)S(1)}, u32[]{:S(2)}, u32[]{:S(2)}) collective-permute-start(f32[6,64,128]{2,1,0:T(8,128)S(1)} %copy-done.1), channel_id=1, source_target_pairs={{0,252},{4,8},{8,4},{12,16},{16,12},{20,24},{24,20},{28,32},{32,28... | collective-permute-start | bytes 589832 | tf_op jit(solution)/shard_map/ppermute | solution.py:732
  22.0 9.0 %collective-permute-start.8 = (f32[6,64,128]{2,1,0:T(8,128)S(1)}, f32[6,64,128]{2,1,0:T(8,128)S(1)}, u32[]{:S(2)}, u32[]{:S(2)}) collective-permute-start(f32[6,64,128]{2,1,0:T(8,128)S(1)} %copy-done.1), channel_id=1, source_target_pairs={{0,4},{4,0},{8,12},{12,8},{16,20},{20,16},{24,28},{28,24},{32,36},... | collective-permute-start | bytes 589832 | tf_op jit(solution)/shard_map/ppermute | solution.py:733
  26.5 7.6 %collective-permute-start.13 = (f32[6,64,128]{2,1,0:T(8,128)S(1)}, f32[6,64,128]{2,1,0:T(8,128)S(1)}, u32[]{:S(2)}, u32[]{:S(2)}) collective-permute-start(f32[6,64,128]{2,1,0:T(8,128)S(1)} %shard_map.84.vector.block.prior.v1), channel_id=1, source_target_pairs={{0,252},{4,8},{8,4},{12,16},{16,12},{20,24},{24,20},{28,32},{32,28... | collective-permute-start | bytes 589832 | tf_op jit(solution)/shard_map/ppermute | solution.py:732
  26.6 7.5 %collective-permute-start.12 = (f32[6,64,128]{2,1,0:T(8,128)S(1)}, f32[6,64,128]{2,1,0:T(8,128)S(1)}, u32[]{:S(2)}, u32[]{:S(2)}) collective-permute-start(f32[6,64,128]{2,1,0:T(8,128)S(1)} %shard_map.84.vector.block.prior.v1), channel_id=1, source_target_pairs={{0,4},{4,0},{8,12},{12,8},{16,20},{20,16},{24,28},{28,24},{32,36},... | collective-permute-start | bytes 589832 | tf_op jit(solution)/shard_map/ppermute | solution.py:733
  28.9 4.8 %collective-permute-start.10 = (f32[24,128]{1,0:T(8,128)S(1)}, f32[24,128]{1,0:T(8,128)S(1)}, u32[]{:S(2)}, u32[]{:S(2)}) collective-permute-start(f32[24,128]{1,0:T(8,128)S(1)} %get-tuple-element.40), channel_id=1, source_target_pairs={{0,1},{1,0},{2,3},{3,2},{4,5},{5,4},{6,7},{7,6},{8,9},{9,8},{10,11... | collective-permute-start | bytes 36872 | tf_op jit(solution)/shard_map/ppermute | solution.py:737
  29.3 4.5 %collective-permute-start.11 = (f32[24,128]{1,0:T(8,128)S(1)}, f32[24,128]{1,0:T(8,128)S(1)}, u32[]{:S(2)}, u32[]{:S(2)}) collective-permute-start(f32[24,128]{1,0:T(8,128)S(1)} %get-tuple-element.41), channel_id=1, source_target_pairs={{0,3},{1,2},{2,1},{3,0},{4,7},{5,6},{6,5},{7,4},{8,11},{9,10},{10,... | collective-permute-start | bytes 36872 | tf_op jit(solution)/shard_map/ppermute | solution.py:737
  34.4 9.0 %collective-permute-start.17 = (f32[6,64,128]{2,1,0:T(8,128)S(1)}, f32[6,64,128]{2,1,0:T(8,128)S(1)}, u32[]{:S(2)}, u32[]{:S(2)}) collective-permute-start(f32[6,64,128]{2,1,0:T(8,128)S(1)} %shard_map.88.vector.block.prior.v2), channel_id=1, source_target_pairs={{0,252},{4,8},{8,4},{12,16},{16,12},{20,24},{24,20},{28,32},{32,28... | collective-permute-start | bytes 589832 | tf_op jit(solution)/shard_map/ppermute | solution.py:732
  35.2 8.2 %collective-permute-start.16 = (f32[6,64,128]{2,1,0:T(8,128)S(1)}, f32[6,64,128]{2,1,0:T(8,128)S(1)}, u32[]{:S(2)}, u32[]{:S(2)}) collective-permute-start(f32[6,64,128]{2,1,0:T(8,128)S(1)} %shard_map.88.vector.block.prior.v2), channel_id=1, source_target_pairs={{0,4},{4,0},{8,12},{12,8},{16,20},{20,16},{24,28},{28,24},{32,36},... | collective-permute-start | bytes 589832 | tf_op jit(solution)/shard_map/ppermute | solution.py:733
  38.9 4.1 %collective-permute-start.14 = (f32[24,128]{1,0:T(8,128)S(1)}, f32[24,128]{1,0:T(8,128)S(1)}, u32[]{:S(2)}, u32[]{:S(2)}) collective-permute-start(f32[24,128]{1,0:T(8,128)S(1)} %get-tuple-element.47), channel_id=1, source_target_pairs={{0,1},{1,0},{2,3},{3,2},{4,5},{5,4},{6,7},{7,6},{8,9},{9,8},{10,11... | collective-permute-start | bytes 36872 | tf_op jit(solution)/shard_map/ppermute | solution.py:737
  39.0 4.1 %collective-permute-start.15 = (f32[24,128]{1,0:T(8,128)S(1)}, f32[24,128]{1,0:T(8,128)S(1)}, u32[]{:S(2)}, u32[]{:S(2)}) collective-permute-start(f32[24,128]{1,0:T(8,128)S(1)} %get-tuple-element.48), channel_id=1, source_target_pairs={{0,3},{1,2},{2,1},{3,0},{4,7},{5,6},{6,5},{7,4},{8,11},{9,10},{10,... | collective-permute-start | bytes 36872 | tf_op jit(solution)/shard_map/ppermute | solution.py:737
  43.5 8.0 %collective-permute-start.18 = (f32[6,32,128]{2,1,0:T(8,128)S(1)}, f32[6,32,128]{2,1,0:T(8,128)S(1)}, u32[]{:S(2)}, u32[]{:S(2)}) collective-permute-start(f32[6,32,128]{2,1,0:T(8,128)S(1)} %get-tuple-element.50), channel_id=1, source_target_pairs={{0,252},{4,8},{8,4},{12,16},{16,12},{20,24},{24,20},{28,32},{32,28... | collective-permute-start | bytes 294920 | tf_op jit(solution)/shard_map/ppermute | solution.py:805
  43.6 7.9 %collective-permute-start.19 = (f32[6,32,128]{2,1,0:T(8,128)S(1)}, f32[6,32,128]{2,1,0:T(8,128)S(1)}, u32[]{:S(2)}, u32[]{:S(2)}) collective-permute-start(f32[6,32,128]{2,1,0:T(8,128)S(1)} %get-tuple-element.51), channel_id=1, source_target_pairs={{0,4},{4,0},{8,12},{12,8},{16,20},{20,16},{24,28},{28,24},{32,36},... | collective-permute-start | bytes 294920 | tf_op jit(solution)/shard_map/ppermute | solution.py:806
  47.4 4.1 %collective-permute-start.20 = (f32[24,128]{1,0:T(8,128)S(1)}, f32[24,128]{1,0:T(8,128)S(1)}, u32[]{:S(2)}, u32[]{:S(2)}) collective-permute-start(f32[24,128]{1,0:T(8,128)S(1)} %shard_map.93), channel_id=1, source_target_pairs={{0,1},{1,2},{2,3},{3,0},{4,5},{5,6},{6,7},{7,4},{8,9},{9,10},{10,1... | collective-permute-start | bytes 36872 | tf_op jit(solution)/shard_map/ppermute | solution.py:808
  48.5 1.2 %collective-permute-start.21 = (f32[1,128]{1,0:T(1,128)S(1)}, f32[1,128]{1,0:T(1,128)S(1)}, u32[]{:S(2)}, u32[]{:S(2)}) collective-permute-start(f32[1,128]{1,0:T(1,128)S(1)} %get-tuple-element.53), channel_id=1, source_target_pairs={{0,4},{4,0},{8,12},{12,8},{16,20},{20,16},{24,28},{28,24},{32,36},... | collective-permute-start | bytes 1544 | tf_op jit(solution)/shard_map/ppermute | solution.py:816
